TPU v7x, 32 devices: a whole 2x2x4 slice. The times are simulated.
32 devices in a mesh: gx: 4 (over z), gy: 4 (over x, core), gz: 2 (over y).
Axes of the slice: x: 2, y: 2, z: 4, core: 2. Of those that a mesh axis runs over, the one named last changes fastest.
Arguments:
- plume_flow_variables: float32 [6, 32, 64, 256], P(None, 'gx', 'gy', 'gz'), may hold values from -6 to 6
- thermal_field: float32 [128, 64, 128], P(None, ('gx', 'gz'), 'gy'), may hold values from -6 to 6
- matter_condition: int32 [128, 64, 128], P(None, ('gx', 'gz'), 'gy'), may hold values from 0 to 2
- pool_boundary_level: int32 [32, 64], P('gx', 'gy'), may hold values from 0 to 127
- beam_focus_path: int32 [4, 2], replicated, may hold values from 0 to 127, as said below
Outputs:
- gas_out: float32 [6, 32, 64, 256], P(None, 'gx', 'gy', 'gz')
- temperature_out: float32 [128, 64, 128], P(None, ('gx', 'gz'), 'gy')
Inputs may be any that keep to these rules, and one draw needn't show every extreme that they name: `beam_focus_path`: column 0 is a position along the part's first lateral dimension, below 64; column 1 along the second, below 128.
All inputs are finite; a program needn't handle non-finite values.
Results may differ from a plain program's by a relative error of at most 0.0001.
Values sent between devices are 32-bit elements; how exact they have to be, the bound alone decides.
No kernel may reach another device: no remote copies, remote signals or barrier semaphores. Data moves between devices by JAX's collectives and lax.ppermute only.
A program may use at most 64 MiB of HBM per device.

v0:
```python
import jax
import jax.numpy as jnp
from jax import lax
from jax.sharding import PartitionSpec as P

STEPS = 2
SUBSTEPS = 2


GAS_STEP = 0.3
DRIFT_SPEED = 0.5
VAPOR_LOAD = 0.3
AMBIENT_LOAD = 0.7
STIFFNESS = 1.0
VISCOSITY = (0.2, 0.1, 0.15, 0.15, 0.15, 0.2)
HEAT_STEP = 1.0
POWDER_COND = 0.04
SOLID_COND = 0.15
LIQUID_COND = 0.09
LASER_POWER = 3.0
SPOT_RADIUS = 6.0
ABSORB_DEPTH = 4.0
BOIL_LEVEL = 1.0
BACK_PRESSURE = 0.5
LATENT_HEAT = 0.3
VAPOR_SOURCE = 0.5
RECOIL_PUSH = 0.4
RECOIL_PRESSURE = 0.6


def padded_2(value, sides, width):
    for axis, dim in sides:
        size, length = (lax.axis_size(axis), value.shape[dim])
        up = [(i, (i + 1) % size) for i in range(size - 1)]
        down = [(j, i) for i, j in up]
        last = lax.slice_in_dim(value, length - width, length, axis=dim)
        leading = lax.slice_in_dim(value, 0, width, axis=dim)
        before = lax.ppermute(last, axis, up)
        after = lax.ppermute(leading, axis, down)
        value = jnp.concatenate([before, value, after], axis=dim)
    return value


def spread_2(value, axis, source):
    kept = jnp.where(lax.axis_index(axis) == source, value, 0).astype(value.dtype)
    return lax.psum(kept, axis)


def gas_rate(padded):
    center = padded[:, 1:-1, 1:-1, 1:-1]
    east_side = padded[:, 2:, 1:-1, 1:-1]
    west_side = padded[:, :-2, 1:-1, 1:-1]
    north_side = padded[:, 1:-1, 2:, 1:-1]
    south_side = padded[:, 1:-1, :-2, 1:-1]
    upper_side = padded[:, 1:-1, 1:-1, 2:]
    lower_side = padded[:, 1:-1, 1:-1, :-2]
    slope_x = 0.5 * (east_side - west_side)
    slope_y = 0.5 * (north_side - south_side)
    slope_z = 0.5 * (upper_side - lower_side)
    laplace = (
        east_side + west_side + north_side + south_side + upper_side + lower_side - 6.0 * center
    )
    spread = slope_x[2] + slope_y[3] + slope_z[4]
    viscous = jnp.array(VISCOSITY, jnp.float32).reshape(6, 1, 1, 1)
    coupled = jnp.stack(
        [
            -VAPOR_LOAD * spread,
            -AMBIENT_LOAD * spread,
            -slope_x[5],
            -slope_y[5],
            -slope_z[5],
            -STIFFNESS * spread,
        ]
    )
    return coupled - DRIFT_SPEED * slope_z + viscous * laplace


def neighbours(padded):
    return [
        padded[2:, 1:-1, 1:-1],
        padded[:-2, 1:-1, 1:-1],
        padded[1:-1, 2:, 1:-1],
        padded[1:-1, :-2, 1:-1],
        padded[1:-1, 1:-1, 2:],
        padded[1:-1, 1:-1, :-2],
    ]


def heat_rate(padded_temp, padded_cond):
    center = padded_temp[1:-1, 1:-1, 1:-1]
    cond_center = padded_cond[1:-1, 1:-1, 1:-1]
    total = jnp.zeros_like(center)
    for temp_side, cond_side in zip(neighbours(padded_temp), neighbours(padded_cond)):
        total = total + 0.5 * (cond_center + cond_side) * (temp_side - center)
    return total


def conductivity(matter_condition):
    return jnp.where(
        matter_condition == 0,
        POWDER_COND,
        jnp.where(matter_condition == 1, SOLID_COND, LIQUID_COND),
    ).astype(jnp.float32)


def laser_heat(x_cells, y_cells, depth_cells, target):
    along_x = jnp.exp(-(((x_cells - target[0].astype(jnp.float32)) / SPOT_RADIUS) ** 2))
    along_y = jnp.exp(-(((y_cells - target[1].astype(jnp.float32)) / SPOT_RADIUS) ** 2))
    along_depth = jnp.exp(-depth_cells / ABSORB_DEPTH)
    return (
        LASER_POWER * along_depth[:, None, None] * along_x[None, :, None] * along_y[None, None, :]
    )


def evaporation(surface_temp, pressure):
    return jax.nn.softplus(surface_temp - BOIL_LEVEL - BACK_PRESSURE * pressure)


def refine(values):
    return jnp.repeat(jnp.repeat(values, 2, axis=0), 2, axis=1)


def coarsen(values):
    rows, cols = values.shape
    return 0.25 * jnp.sum(values.reshape(rows // 2, 2, cols // 2, 2), axis=(1, 3))


def global_cells(start, count):
    return (start + jnp.arange(count, dtype=jnp.int32)).astype(jnp.float32)


def valid_cycle(position, devices, count):
    global_index = position * count - 1 + jnp.arange(count + 2, dtype=jnp.int32)
    return ((global_index >= 0) & (global_index < count * devices)).astype(jnp.float32)


def advance(vapor_state):
    padded = padded_2(vapor_state, (("gx", 1), ("gy", 2), ("gz", 3)), 2)
    first_section = padded[:, 1:-1, 1:-1, 1:-1] + GAS_STEP * gas_rate(padded)
    inside_x = valid_cycle(lax.axis_index("gx"), lax.axis_size("gx"), vapor_state.shape[1])
    inside_y = valid_cycle(lax.axis_index("gy"), lax.axis_size("gy"), vapor_state.shape[2])
    inside_z = valid_cycle(lax.axis_index("gz"), lax.axis_size("gz"), vapor_state.shape[3])
    inside = inside_x[:, None, None] * inside_y[None, :, None] * inside_z[None, None, :]
    first_section = first_section * inside[None]
    return 0.5 * (
        vapor_state + first_section[:, 1:-1, 1:-1, 1:-1] + GAS_STEP * gas_rate(first_section)
    )


def shards(
    plume_flow_variables, thermal_field, matter_condition, pool_boundary_level, beam_focus_path
):
    cells_x = plume_flow_variables.shape[1]
    cells_z = plume_flow_variables.shape[3]
    height_index = lax.axis_index("gz")
    layers = lax.axis_size("gz")
    heights = height_index * cells_z + jnp.arange(cells_z, dtype=jnp.int32)
    surface_mask = (heights[None, None, :] == pool_boundary_level[:, :, None]).astype(jnp.float32)
    conduct = conductivity(matter_condition)
    workpiece_thermal_mesh = thermal_field
    depth_rim = ((1, 1), (0, 0), (0, 0))
    padded_cond = jnp.pad(padded_2(conduct, ((("gx", "gz"), 1), ("gy", 2)), 1), depth_rim)
    depth_start = jnp.int32(0)
    x_start = (lax.axis_index("gx") * layers + height_index) * workpiece_thermal_mesh.shape[1]
    on_top = jnp.float32(1.0)
    y_start = lax.axis_index("gy") * workpiece_thermal_mesh.shape[2]
    x_cells = global_cells(x_start, workpiece_thermal_mesh.shape[1])
    y_cells = global_cells(y_start, workpiece_thermal_mesh.shape[2])
    depth_cells = global_cells(depth_start, workpiece_thermal_mesh.shape[0])
    vapor_state = plume_flow_variables
    for outer_step in range(STEPS):
        vapor_state = advance(vapor_state)
        pressure = jnp.sum(vapor_state[5] * surface_mask, axis=2)
        shared = spread_2(pressure, "gz", 0)
        part_rows = cells_x // layers
        pressure_rows = lax.dynamic_slice_in_dim(shared, height_index * part_rows, part_rows, 0)
        fine_pressure = refine(pressure_rows)
        for substep in range(SUBSTEPS):
            padded = jnp.pad(
                padded_2(workpiece_thermal_mesh, ((("gx", "gz"), 1), ("gy", 2)), 1), depth_rim
            )
            target = beam_focus_path[outer_step * SUBSTEPS + substep]
            change = heat_rate(padded, padded_cond) + laser_heat(
                x_cells, y_cells, depth_cells, target
            )
            cooling = on_top * LATENT_HEAT * evaporation(workpiece_thermal_mesh[0], fine_pressure)
            change = change.at[0].add(-cooling)
            workpiece_thermal_mesh = workpiece_thermal_mesh + HEAT_STEP * change
        top_layer = lax.all_gather(workpiece_thermal_mesh[0], "gz", axis=0, tiled=True)
        surface_temp = coarsen(top_layer)
        vapor_mass = evaporation(surface_temp, pressure)[:, :, None] * surface_mask
        vapor_state = vapor_state.at[0].add(VAPOR_SOURCE * vapor_mass)
        vapor_state = vapor_state.at[4].add(RECOIL_PUSH * vapor_mass)
        vapor_state = vapor_state.at[5].add(RECOIL_PRESSURE * vapor_mass)
    return (vapor_state, workpiece_thermal_mesh)


def solution(mesh):
    return jax.shard_map(
        shards,
        mesh=mesh,
        in_specs=(
            P(None, "gx", "gy", "gz"),
            P(None, ("gx", "gz"), "gy"),
            P(None, ("gx", "gz"), "gy"),
            P("gx", "gy"),
            P(),
        ),
        out_specs=(P(None, "gx", "gy", "gz"), P(None, ("gx", "gz"), "gy")),
        check_vma=False,
    )
```

profile of v0, /device:TPU:18, one launch (start us, length us, event | category | flops | bytes accessed | tf_op | source)
XLA Modules:
  0.0 214.9 jit_solution(9522509788396882554)
XLA Ops:
  1.7 3.5 %collective-permute-start = (f32[6,2,16,128]{3,2,1,0:T(8,128)S(1)}, f32[6,2,16,128]{3,2,1,0:T(8,128)S(1)}, u32[]{:S(2)}, u32[]{:S(2)}) collective-permute-start(f32[6,2,16,128]{3,2,1,0:T(8,128)S(1)} %get-tuple-element.162), channel_id=1, source_target_pairs={{0,8},{8,16},{16,24},{1,9},{9,17},{17,25},{2,10},{10,18},{18,26},{... | collective-permute-start | bytes 294920 | tf_op jit(solution)/shard_map/ppermute | solution.py:38
  31.7 3.6 %collective-permute-start.13 = (f32[128,10,1]{0,2,1:T(1,128)S(1)}, f32[128,10,1]{0,2,1:T(1,128)S(1)}, u32[]{:S(2)}, u32[]{:S(2)}) collective-permute-start(f32[128,10,1]{0,2,1:T(1,128)S(1)} %get-tuple-element.171), channel_id=1, source_target_pairs={{2,0},{4,2},{6,4},{3,1},{5,3},{7,5},{10,8},{12,10},{14,12},{11,9},... | collective-permute-start | bytes 15368 | tf_op jit(solution)/shard_map/ppermute | solution.py:39
  45.5 4.3 %copy.271 = f32[6,12,16,128]{2,1,3,0:T(8,128)} copy(f32[6,12,16,128]{3,2,1,0:T(8,128)S(1)} %constant_dynamic-update-slice_fusion) | data formatting | bytes 1179648 | tf_op jit(solution)/shard_map/concatenate | solution.py:40
  49.9 4.2 %copy.272 = f32[6,12,2,128]{2,1,3,0:T(8,128)} copy(f32[6,12,2,128]{3,1,2,0:T(8,128)S(1)} %collective-permute-done.3) | data formatting | bytes 147456 | tf_op jit(solution)/shard_map/ppermute | solution.py:39
  54.1 4.2 %copy.270 = f32[6,12,2,128]{2,1,3,0:T(8,128)} copy(f32[6,12,2,128]{3,1,2,0:T(8,128)S(1)} %collective-permute-done.2) | data formatting | bytes 147456 | tf_op jit(solution)/shard_map/ppermute | solution.py:38
  58.2 8.2 %pad_maximum_fusion = f32[6,12,20,128]{2,1,3,0:T(8,128)S(1)} fusion(f32[6,12,2,128]{2,1,3,0:T(8,128)} %copy.272, f32[6,12,16,128]{2,1,3,0:T(8,128)} %copy.271, f32[6,12,2,128]{2,1,3,0:T(8,128)} %copy.270), kind=kLoop, calls=%fused_computation | loop fusion | flops 368640 | bytes 1474560 | tf_op jit(solution)/shard_map/concatenate | solution.py:40
  70.4 5.2 %collective-permute-start.4 = (f32[6,12,20,2]{2,1,3,0:T(8,128)S(1)}, f32[6,12,20,2]{2,1,3,0:T(8,128)}, u32[]{:S(2)}, u32[]{:S(2)}) collective-permute-start(f32[6,12,20,2]{2,1,3,0:T(8,128)S(1)} %get-tuple-element.143), channel_id=1, source_target_pairs={{0,1},{2,3},{4,5},{6,7},{8,9},{10,11},{12,13},{14,15},{16,17},{18,... | collective-permute-start | bytes 34568 | tf_op jit(solution)/shard_map/ppermute | solution.py:38
  76.5 4.4 %copy.274 = f32[6,12,20,128]{3,2,1,0:T(8,128)S(1)} copy(f32[6,12,20,128]{2,1,3,0:T(8,128)} %copy-done) | data formatting | bytes 1474560 | tf_op jit(solution)/shard_map/concatenate | solution.py:40
  91.1 4.9 %psum.14 = f32[8,16]{1,0:T(8,128)S(1)} all-reduce(f32[8,16]{1,0:T(8,128)S(1)} %broadcast_select_fusion.1), channel_id=1, replica_groups=mesh['gx'=4,'gy'=4,'gz'=2] {'gz'}, use_global_device_ids=true, to_apply=%region_1.2 | all-reduce | flops 128 | bytes 1024 | tf_op jit(solution)/shard_map/psum | solution.py:46
  98.7 3.9 %collective-permute-start.14 = (f32[128,1,32]{0,2,1:T(8,128)S(1)}, f32[128,1,32]{0,2,1:T(8,128)S(1)}, u32[]{:S(2)}, u32[]{:S(2)}) collective-permute-start(f32[128,1,32]{0,2,1:T(8,128)S(1)} %get-tuple-element.177), channel_id=1, source_target_pairs={{0,1},{1,8},{8,9},{9,16},{16,17},{17,24},{24,25},{2,3},{3,10},{10,... | collective-permute-start | bytes 49160 | tf_op jit(solution)/shard_map/ppermute | solution.py:38
  107.1 3.6 %collective-permute-start.17 = (f32[128,10,1]{0,2,1:T(1,128)S(1)}, f32[128,10,1]{0,2,1:T(1,128)S(1)}, u32[]{:S(2)}, u32[]{:S(2)}) collective-permute-start(f32[128,10,1]{0,2,1:T(1,128)S(1)} %get-tuple-element.167), channel_id=1, source_target_pairs={{2,0},{4,2},{6,4},{3,1},{5,3},{7,5},{10,8},{12,10},{14,12},{11,9},... | collective-permute-start | bytes 15368 | tf_op jit(solution)/shard_map/ppermute | solution.py:39
  113.0 4.3 %all-gather = f32[1,16,32]{2,0,1:T(1,128)S(1)} all-gather(f32[1,8,32]{2,0,1:T(1,128)S(1)} %copy.283), channel_id=2, replica_groups=mesh['gx'=4,'gy'=4,'gz'=2] {'gz'}, dimensions={1}, use_global_device_ids=true | all-gather | bytes 3072 | tf_op jit(solution)/shard_map/all_gather | solution.py:189
  127.4 3.5 %collective-permute-start.18 = (f32[6,2,16,128]{3,2,1,0:T(8,128)S(1)}, f32[6,2,16,128]{3,2,1,0:T(8,128)S(1)}, u32[]{:S(2)}, u32[]{:S(2)}) collective-permute-start(f32[6,2,16,128]{3,2,1,0:T(8,128)S(1)} %get-tuple-element.159), channel_id=1, source_target_pairs={{0,8},{8,16},{16,24},{1,9},{9,17},{17,25},{2,10},{10,18},{18,26},{... | collective-permute-start | bytes 294920 | tf_op jit(solution)/shard_map/ppermute | solution.py:38
  132.8 3.6 %collective-permute-start.27 = (f32[128,10,1]{0,2,1:T(1,128)S(1)}, f32[128,10,1]{0,2,1:T(1,128)S(1)}, u32[]{:S(2)}, u32[]{:S(2)}) collective-permute-start(f32[128,10,1]{0,2,1:T(1,128)S(1)} %get-tuple-element.165), channel_id=1, source_target_pairs={{2,0},{4,2},{6,4},{3,1},{5,3},{7,5},{10,8},{12,10},{14,12},{11,9},... | collective-permute-start | bytes 15368 | tf_op jit(solution)/shard_map/ppermute | solution.py:39
  141.5 4.3 %copy.287 = f32[6,12,16,128]{2,1,3,0:T(8,128)} copy(f32[6,12,16,128]{3,2,1,0:T(8,128)S(1)} %pad_maximum_fusion.8) | data formatting | bytes 1179648 | tf_op jit(solution)/shard_map/concatenate | solution.py:40
  145.8 4.2 %copy.288 = f32[6,12,2,128]{2,1,3,0:T(8,128)} copy(f32[6,12,2,128]{3,1,2,0:T(8,128)S(1)} %collective-permute-done.21) | data formatting | bytes 147456 | tf_op jit(solution)/shard_map/ppermute | solution.py:39
  150.0 4.2 %copy.286 = f32[6,12,2,128]{2,1,3,0:T(8,128)} copy(f32[6,12,2,128]{3,1,2,0:T(8,128)S(1)} %collective-permute-done.20) | data formatting | bytes 147456 | tf_op jit(solution)/shard_map/ppermute | solution.py:38
  154.2 8.1 %pad_maximum_fusion.1 = f32[6,12,20,128]{2,1,3,0:T(8,128)S(1)} fusion(f32[6,12,2,128]{2,1,3,0:T(8,128)} %copy.288, f32[6,12,16,128]{2,1,3,0:T(8,128)} %copy.287, f32[6,12,2,128]{2,1,3,0:T(8,128)} %copy.286), kind=kLoop, calls=%fused_computation.1 | loop fusion | flops 368640 | bytes 1474560 | tf_op jit(solution)/shard_map/concatenate | solution.py:40
  166.3 5.2 %collective-permute-start.22 = (f32[6,12,20,2]{2,1,3,0:T(8,128)S(1)}, f32[6,12,20,2]{2,1,3,0:T(8,128)}, u32[]{:S(2)}, u32[]{:S(2)}) collective-permute-start(f32[6,12,20,2]{2,1,3,0:T(8,128)S(1)} %get-tuple-element.141), channel_id=1, source_target_pairs={{0,1},{2,3},{4,5},{6,7},{8,9},{10,11},{12,13},{14,15},{16,17},{18,... | collective-permute-start | bytes 34568 | tf_op jit(solution)/shard_map/ppermute | solution.py:38
  172.3 4.4 %copy.290 = f32[6,12,20,128]{3,2,1,0:T(8,128)S(1)} copy(f32[6,12,20,128]{2,1,3,0:T(8,128)} %copy-done.1) | data formatting | bytes 1474560 | tf_op jit(solution)/shard_map/concatenate | solution.py:40
  186.7 4.9 %psum.15 = f32[8,16]{1,0:T(8,128)S(1)} all-reduce(f32[8,16]{1,0:T(8,128)S(1)} %broadcast_select_fusion), channel_id=1, replica_groups=mesh['gx'=4,'gy'=4,'gz'=2] {'gz'}, use_global_device_ids=true, to_apply=%region_4.5 | all-reduce | flops 128 | bytes 1024 | tf_op jit(solution)/shard_map/psum | solution.py:46
  194.2 3.9 %collective-permute-start.28 = (f32[128,1,32]{0,2,1:T(8,128)S(1)}, f32[128,1,32]{0,2,1:T(8,128)S(1)}, u32[]{:S(2)}, u32[]{:S(2)}) collective-permute-start(f32[128,1,32]{0,2,1:T(8,128)S(1)} %get-tuple-element.173), channel_id=1, source_target_pairs={{0,1},{1,8},{8,9},{9,16},{16,17},{17,24},{24,25},{2,3},{3,10},{10,... | collective-permute-start | bytes 49160 | tf_op jit(solution)/shard_map/ppermute | solution.py:38
  202.7 3.6 %collective-permute-start.31 = (f32[128,10,1]{0,2,1:T(1,128)S(1)}, f32[128,10,1]{0,2,1:T(1,128)S(1)}, u32[]{:S(2)}, u32[]{:S(2)}) collective-permute-start(f32[128,10,1]{0,2,1:T(1,128)S(1)} %get-tuple-element.163), channel_id=1, source_target_pairs={{2,0},{4,2},{6,4},{3,1},{5,3},{7,5},{10,8},{12,10},{14,12},{11,9},... | collective-permute-start | bytes 15368 | tf_op jit(solution)/shard_map/ppermute | solution.py:39
  208.6 4.3 %all-gather.1 = f32[1,16,32]{2,0,1:T(1,128)S(1)} all-gather(f32[1,8,32]{2,0,1:T(1,128)S(1)} %copy.299), channel_id=3, replica_groups=mesh['gx'=4,'gy'=4,'gz'=2] {'gz'}, dimensions={1}, use_global_device_ids=true | all-gather | bytes 3072 | tf_op jit(solution)/shard_map/all_gather | solution.py:189
  (258 shorter events, 98.9 us)
Async XLA Ops:
  1.7 38.3 %collective-permute-start = (f32[6,2,16,128]{3,2,1,0:T(8,128)S(1)}, f32[6,2,16,128]{3,2,1,0:T(8,128)S(1)}, u32[]{:S(2)}, u32[]{:S(2)}) collective-permute-start(f32[6,2,16,128]{3,2,1,0:T(8,128)S(1)} %get-tuple-element.162), channel_id=1, source_target_pairs={{0,8},{8,16},{16,24},{1,9},{9,17},{17,25},{2,10},{10,18},{18,26},{... | collective-permute-start | bytes 294920 | tf_op jit(solution)/shard_map/ppermute | solution.py:38
  5.1 34.9 %collective-permute-start.1 = (f32[6,2,16,128]{3,2,1,0:T(8,128)S(1)}, f32[6,2,16,128]{3,2,1,0:T(8,128)S(1)}, u32[]{:S(2)}, u32[]{:S(2)}) collective-permute-start(f32[6,2,16,128]{3,2,1,0:T(8,128)S(1)} %get-tuple-element.161), channel_id=1, source_target_pairs={{8,0},{16,8},{24,16},{9,1},{17,9},{25,17},{10,2},{18,10},{26,18},{... | collective-permute-start | bytes 294920 | tf_op jit(solution)/shard_map/ppermute | solution.py:39
  8.3 17.1 %collective-permute-start.10 = (f32[128,1,32]{0,2,1:T(8,128)S(1)}, f32[128,1,32]{0,2,1:T(8,128)S(1)}, u32[]{:S(2)}, u32[]{:S(2)}) collective-permute-start(f32[128,1,32]{0,2,1:T(8,128)S(1)} %get-tuple-element.182), channel_id=1, source_target_pairs={{0,1},{1,8},{8,9},{9,16},{16,17},{17,24},{24,25},{2,3},{3,10},{10,... | collective-permute-start | bytes 49160 | tf_op jit(solution)/shard_map/ppermute | solution.py:38
  11.7 18.0 %collective-permute-start.11 = (f32[128,1,32]{0,2,1:T(8,128)S(1)}, f32[128,1,32]{0,2,1:T(8,128)S(1)}, u32[]{:S(2)}, u32[]{:S(2)}) collective-permute-start(f32[128,1,32]{0,2,1:T(8,128)S(1)} %get-tuple-element.181), channel_id=1, source_target_pairs={{1,0},{8,1},{9,8},{16,9},{17,16},{24,17},{25,24},{3,2},{10,3},{11,... | collective-permute-start | bytes 49160 | tf_op jit(solution)/shard_map/ppermute | solution.py:39
  15.9 15.7 %collective-permute-start.7 = (f32[128,1,32]{0,2,1:T(8,128)S(1)}, f32[128,1,32]{0,2,1:T(8,128)S(1)}, u32[]{:S(2)}, u32[]{:S(2)}) collective-permute-start(f32[128,1,32]{0,2,1:T(8,128)S(1)} %get-tuple-element.180), channel_id=1, source_target_pairs={{1,0},{8,1},{9,8},{16,9},{17,16},{24,17},{25,24},{3,2},{10,3},{11,... | collective-permute-start | bytes 49160 | tf_op jit(solution)/shard_map/ppermute | solution.py:39
  25.3 10.0 %collective-permute-start.6 = (f32[128,1,32]{0,2,1:T(8,128)S(1)}, f32[128,1,32]{0,2,1:T(8,128)S(1)}, u32[]{:S(2)}, u32[]{:S(2)}) collective-permute-start(f32[128,1,32]{0,2,1:T(8,128)S(1)} %get-tuple-element.179), channel_id=1, source_target_pairs={{0,1},{1,8},{8,9},{9,16},{16,17},{17,24},{24,25},{2,3},{3,10},{10,... | collective-permute-start | bytes 49160 | tf_op jit(solution)/shard_map/ppermute | solution.py:38
  29.7 7.6 %collective-permute-start.12 = (f32[128,10,1]{0,2,1:T(1,128)S(1)}, f32[128,10,1]{0,2,1:T(1,128)S(1)}, u32[]{:S(2)}, u32[]{:S(2)}) collective-permute-start(f32[128,10,1]{0,2,1:T(1,128)S(1)} %get-tuple-element.172), channel_id=1, source_target_pairs={{0,2},{2,4},{4,6},{1,3},{3,5},{5,7},{8,10},{10,12},{12,14},{9,11},... | collective-permute-start | bytes 15368 | tf_op jit(solution)/shard_map/ppermute | solution.py:38
  31.7 8.0 %collective-permute-start.13 = (f32[128,10,1]{0,2,1:T(1,128)S(1)}, f32[128,10,1]{0,2,1:T(1,128)S(1)}, u32[]{:S(2)}, u32[]{:S(2)}) collective-permute-start(f32[128,10,1]{0,2,1:T(1,128)S(1)} %get-tuple-element.171), channel_id=1, source_target_pairs={{2,0},{4,2},{6,4},{3,1},{5,3},{7,5},{10,8},{12,10},{14,12},{11,9},... | collective-permute-start | bytes 15368 | tf_op jit(solution)/shard_map/ppermute | solution.py:39
  35.4 9.9 %collective-permute-start.9 = (f32[128,10,1]{0,2,1:T(1,128)S(1)}, f32[128,10,1]{0,2,1:T(1,128)S(1)}, u32[]{:S(2)}, u32[]{:S(2)}) collective-permute-start(f32[128,10,1]{0,2,1:T(1,128)S(1)} %get-tuple-element.170), channel_id=1, source_target_pairs={{2,0},{4,2},{6,4},{3,1},{5,3},{7,5},{10,8},{12,10},{14,12},{11,9},... | collective-permute-start | bytes 15368 | tf_op jit(solution)/shard_map/ppermute | solution.py:39
  37.3 8.0 %collective-permute-start.8 = (f32[128,10,1]{0,2,1:T(1,128)S(1)}, f32[128,10,1]{0,2,1:T(1,128)S(1)}, u32[]{:S(2)}, u32[]{:S(2)}) collective-permute-start(f32[128,10,1]{0,2,1:T(1,128)S(1)} %get-tuple-element.169), channel_id=1, source_target_pairs={{0,2},{2,4},{4,6},{1,3},{3,5},{5,7},{8,10},{10,12},{12,14},{9,11},... | collective-permute-start | bytes 15368 | tf_op jit(solution)/shard_map/ppermute | solution.py:38
  40.1 9.7 %collective-permute-start.3 = (f32[6,12,2,128]{3,1,2,0:T(8,128)S(1)}, f32[6,12,2,128]{3,1,2,0:T(8,128)S(1)}, u32[]{:S(2)}, u32[]{:S(2)}) collective-permute-start(f32[6,12,2,128]{3,1,2,0:T(8,128)S(1)} %copy.301), channel_id=1, source_target_pairs={{2,0},{4,2},{6,4},{3,1},{5,3},{7,5},{10,8},{12,10},{14,12},{11,9},... | collective-permute-start | bytes 221192 | tf_op jit(solution)/shard_map/ppermute | solution.py:39
  43.3 10.7 %collective-permute-start.2 = (f32[6,12,2,128]{3,1,2,0:T(8,128)S(1)}, f32[6,12,2,128]{3,1,2,0:T(8,128)S(1)}, u32[]{:S(2)}, u32[]{:S(2)}) collective-permute-start(f32[6,12,2,128]{3,1,2,0:T(8,128)S(1)} %copy.300), channel_id=1, source_target_pairs={{0,2},{2,4},{4,6},{1,3},{3,5},{5,7},{8,10},{10,12},{12,14},{9,11},... | collective-permute-start | bytes 221192 | tf_op jit(solution)/shard_map/ppermute | solution.py:38
  69.1 11.8 %collective-permute-start.5 = (f32[6,12,20,2]{2,1,3,0:T(8,128)S(1)}, f32[6,12,20,2]{2,1,3,0:T(8,128)S(1)}, u32[]{:S(2)}, u32[]{:S(2)}) collective-permute-start(f32[6,12,20,2]{2,1,3,0:T(8,128)S(1)} %get-tuple-element.144), channel_id=1, source_target_pairs={{1,0},{3,2},{5,4},{7,6},{9,8},{11,10},{13,12},{15,14},{17,16},{19,... | collective-permute-start | bytes 34568 | tf_op jit(solution)/shard_map/ppermute | solution.py:39
  70.4 11.1 %collective-permute-start.4 = (f32[6,12,20,2]{2,1,3,0:T(8,128)S(1)}, f32[6,12,20,2]{2,1,3,0:T(8,128)}, u32[]{:S(2)}, u32[]{:S(2)}) collective-permute-start(f32[6,12,20,2]{2,1,3,0:T(8,128)S(1)} %get-tuple-element.143), channel_id=1, source_target_pairs={{0,1},{2,3},{4,5},{6,7},{8,9},{10,11},{12,13},{14,15},{16,17},{18,... | collective-permute-start | bytes 34568 | tf_op jit(solution)/shard_map/ppermute | solution.py:38
  119.1 11.7 %collective-permute-start.25 = (f32[128,1,32]{0,2,1:T(8,128)S(1)}, f32[128,1,32]{0,2,1:T(8,128)S(1)}, u32[]{:S(2)}, u32[]{:S(2)}) collective-permute-start(f32[128,1,32]{0,2,1:T(8,128)S(1)} %get-tuple-element.176), channel_id=1, source_target_pairs={{1,0},{8,1},{9,8},{16,9},{17,16},{24,17},{25,24},{3,2},{10,3},{11,... | collective-permute-start | bytes 49160 | tf_op jit(solution)/shard_map/ppermute | solution.py:39
  122.1 8.8 %collective-permute-start.24 = (f32[128,1,32]{0,2,1:T(8,128)S(1)}, f32[128,1,32]{0,2,1:T(8,128)S(1)}, u32[]{:S(2)}, u32[]{:S(2)}) collective-permute-start(f32[128,1,32]{0,2,1:T(8,128)S(1)} %get-tuple-element.175), channel_id=1, source_target_pairs={{0,1},{1,8},{8,9},{9,16},{16,17},{17,24},{24,25},{2,3},{3,10},{10,... | collective-permute-start | bytes 49160 | tf_op jit(solution)/shard_map/ppermute | solution.py:38
  125.0 11.5 %collective-permute-start.19 = (f32[6,2,16,128]{3,2,1,0:T(8,128)S(1)}, f32[6,2,16,128]{3,2,1,0:T(8,128)S(1)}, u32[]{:S(2)}, u32[]{:S(2)}) collective-permute-start(f32[6,2,16,128]{3,2,1,0:T(8,128)S(1)} %get-tuple-element.160), channel_id=1, source_target_pairs={{8,0},{16,8},{24,16},{9,1},{17,9},{25,17},{10,2},{18,10},{26,18},{... | collective-permute-start | bytes 294920 | tf_op jit(solution)/shard_map/ppermute | solution.py:39
  127.4 9.1 %collective-permute-start.18 = (f32[6,2,16,128]{3,2,1,0:T(8,128)S(1)}, f32[6,2,16,128]{3,2,1,0:T(8,128)S(1)}, u32[]{:S(2)}, u32[]{:S(2)}) collective-permute-start(f32[6,2,16,128]{3,2,1,0:T(8,128)S(1)} %get-tuple-element.159), channel_id=1, source_target_pairs={{0,8},{8,16},{16,24},{1,9},{9,17},{17,25},{2,10},{10,18},{18,26},{... | collective-permute-start | bytes 294920 | tf_op jit(solution)/shard_map/ppermute | solution.py:38
  130.9 10.3 %collective-permute-start.26 = (f32[128,10,1]{0,2,1:T(1,128)S(1)}, f32[128,10,1]{0,2,1:T(1,128)S(1)}, u32[]{:S(2)}, u32[]{:S(2)}) collective-permute-start(f32[128,10,1]{0,2,1:T(1,128)S(1)} %get-tuple-element.166), channel_id=1, source_target_pairs={{0,2},{2,4},{4,6},{1,3},{3,5},{5,7},{8,10},{10,12},{12,14},{9,11},... | collective-permute-start | bytes 15368 | tf_op jit(solution)/shard_map/ppermute | solution.py:38
  132.8 8.4 %collective-permute-start.27 = (f32[128,10,1]{0,2,1:T(1,128)S(1)}, f32[128,10,1]{0,2,1:T(1,128)S(1)}, u32[]{:S(2)}, u32[]{:S(2)}) collective-permute-start(f32[128,10,1]{0,2,1:T(1,128)S(1)} %get-tuple-element.165), channel_id=1, source_target_pairs={{2,0},{4,2},{6,4},{3,1},{5,3},{7,5},{10,8},{12,10},{14,12},{11,9},... | collective-permute-start | bytes 15368 | tf_op jit(solution)/shard_map/ppermute | solution.py:39
  136.6 9.2 %collective-permute-start.21 = (f32[6,12,2,128]{3,1,2,0:T(8,128)S(1)}, f32[6,12,2,128]{3,1,2,0:T(8,128)S(1)}, u32[]{:S(2)}, u32[]{:S(2)}) collective-permute-start(f32[6,12,2,128]{3,1,2,0:T(8,128)S(1)} %copy.303), channel_id=1, source_target_pairs={{2,0},{4,2},{6,4},{3,1},{5,3},{7,5},{10,8},{12,10},{14,12},{11,9},... | collective-permute-start | bytes 221192 | tf_op jit(solution)/shard_map/ppermute | solution.py:39
  138.6 11.4 %collective-permute-start.20 = (f32[6,12,2,128]{3,1,2,0:T(8,128)S(1)}, f32[6,12,2,128]{3,1,2,0:T(8,128)S(1)}, u32[]{:S(2)}, u32[]{:S(2)}) collective-permute-start(f32[6,12,2,128]{3,1,2,0:T(8,128)S(1)} %copy.302), channel_id=1, source_target_pairs={{0,2},{2,4},{4,6},{1,3},{3,5},{5,7},{8,10},{10,12},{12,14},{9,11},... | collective-permute-start | bytes 221192 | tf_op jit(solution)/shard_map/ppermute | solution.py:38
  165.0 11.7 %collective-permute-start.23 = (f32[6,12,20,2]{2,1,3,0:T(8,128)S(1)}, f32[6,12,20,2]{2,1,3,0:T(8,128)S(1)}, u32[]{:S(2)}, u32[]{:S(2)}) collective-permute-start(f32[6,12,20,2]{2,1,3,0:T(8,128)S(1)} %get-tuple-element.142), channel_id=1, source_target_pairs={{1,0},{3,2},{5,4},{7,6},{9,8},{11,10},{13,12},{15,14},{17,16},{19,... | collective-permute-start | bytes 34568 | tf_op jit(solution)/shard_map/ppermute | solution.py:39
  166.3 11.0 %collective-permute-start.22 = (f32[6,12,20,2]{2,1,3,0:T(8,128)S(1)}, f32[6,12,20,2]{2,1,3,0:T(8,128)}, u32[]{:S(2)}, u32[]{:S(2)}) collective-permute-start(f32[6,12,20,2]{2,1,3,0:T(8,128)S(1)} %get-tuple-element.141), channel_id=1, source_target_pairs={{0,1},{2,3},{4,5},{6,7},{8,9},{10,11},{12,13},{14,15},{16,17},{18,... | collective-permute-start | bytes 34568 | tf_op jit(solution)/shard_map/ppermute | solution.py:38
  (43 other events, 613.6 us)
where the time goes:
time: 217 us; the launch traced here: 215 us
  starting transfers between devices  90.9 us (42%)
  local copies, waits for them, and re-layouts  52.4 us (24%)
  other arithmetic  39.1 us (18%)
  blocking collectives  18.6 us (9%)
  between operations  7.24 us (3%)
  waiting for transfers between devices  6.62 us (3%)
    ppermute x16, starting transfers between devices, padded_2(): before = lax.ppermute(last, axis, up)  49.6 us
    ppermute x16, starting transfers between devices, padded_2(): after = lax.ppermute(leading, axis, down)  41.4 us
    concatenate x13, other arithmetic, padded_2(): value = jnp.concatenate([before, value, after], axis=dim)  19 us
    concatenate x6, local copies, waits for them, and re-layouts, padded_2(): value = jnp.concatenate([before, value, after], axis=dim)  17.4 us
    ppermute x4, local copies, waits for them, and re-layouts, padded_2(): before = lax.ppermute(last, axis, up)  11.2 us
    psum x2, blocking collectives, spread_2(): return lax.psum(kept, axis)  9.89 us
    ppermute x4, local copies, waits for them, and re-layouts, padded_2(): after = lax.ppermute(leading, axis, down)  9.55 us
    all_gather x2, blocking collectives, shards(): lax.all_gather(workpiece_thermal_mesh[0], 'gz', axis=0, tiled=True)  8.68 us
  transfers between devices with their start and end apart: 32, of which 4 were waited for; matrix products, arithmetic and copies ran while one was open for 16% of the time, Pallas kernels for 0%

commit v1 on v0

v1 whole, which is shorter than its diff:
```python
import functools

import jax
import jax.numpy as jnp
from jax import lax
from jax.experimental import pallas as pl
from jax.experimental.pallas import tpu as pltpu
from jax.sharding import PartitionSpec as P

STEPS = 2
SUBSTEPS = 2
GAS_STEP = 0.3
DRIFT_SPEED = 0.5
VAPOR_LOAD = 0.3
AMBIENT_LOAD = 0.7
STIFFNESS = 1.0
VISCOSITY = (0.2, 0.1, 0.15, 0.15, 0.15, 0.2)
HEAT_STEP = 1.0
POWDER_COND = 0.04
SOLID_COND = 0.15
LIQUID_COND = 0.09
LASER_POWER = 3.0
SPOT_RADIUS = 6.0
ABSORB_DEPTH = 4.0
BOIL_LEVEL = 1.0
BACK_PRESSURE = 0.5
LATENT_HEAT = 0.3
VAPOR_SOURCE = 0.5
RECOIL_PUSH = 0.4
RECOIL_PRESSURE = 0.6

COMPS = 6
LANES = 128
SUBL = 8
F32 = jnp.float32
REACH = 6
REACH_LAST = 3
SKIN = 4
TOP = 8
GROUP = 16
LEVEL = 6
NEXT = 8


def iota(shape, axis):
    return lax.broadcasted_iota(jnp.int32, shape, axis)


def wrapped(index, own, size):
    return jnp.where(index < own + (size - own) // 2, index, index - size)


def turn(value, amount, axis):
    size = value.shape[axis]
    if isinstance(amount, int):
        amount = amount % size
        if amount == 0:
            return value
    return pltpu.roll(value, amount, axis)


def softplus(x):
    return jnp.maximum(x, 0.0) + jnp.log1p(jnp.exp(-jnp.abs(x)))


def edges(gz):
    return jnp.where(gz == 0, LANES - 1, 0), jnp.where(gz == 0, LANES - 2, 1)


def lane_turn(value, amount):
    return pltpu.roll(value, lax.rem(amount + 2 * LANES, LANES), 1)


def pack_heights(rows, base, lane, edge, behind, acc):
    for c, row in enumerate(rows):
        acc = jnp.where(lane == base + c, lane_turn(row, base + c - edge), acc)
        acc = jnp.where(lane == base + NEXT + c, lane_turn(row, base + NEXT + c - behind), acc)
    return acc


def pack_kernel(cells, meta, u, t, m, lev, out_a, out_b, out_z, out_d, out_h, own):
    rows_x, reach = cells
    gx, gz = meta[0], meta[2]
    even = lax.rem(gx, 2) == 0
    low_z = gz == 0
    tiles = u.shape[2] // SUBL
    for c in range(COMPS):
        for i in range(reach):
            for y in range(tiles):
                lo = u[c, i, y * SUBL : (y + 1) * SUBL, :]
                hi = u[c, rows_x - reach + i, y * SUBL : (y + 1) * SUBL, :]
                n = (c * reach + i) * tiles + y
                out_a[n] = jnp.where(even, hi, lo)
                out_b[n] = jnp.where(even, lo, hi)
    depth = t.shape[0]
    cols = t.shape[2]
    groups = LANES // cols
    deep = depth // groups

    def conduct(v):
        return jnp.where(v == 0, POWDER_COND, jnp.where(v == 1, SOLID_COND, LIQUID_COND)).astype(F32)

    packed_t = jnp.concatenate([t[g * deep : (g + 1) * deep] for g in range(groups)], axis=-1)
    packed_k = conduct(jnp.concatenate([m[g * deep : (g + 1) * deep] for g in range(groups)], axis=-1))
    own[:deep] = packed_t
    own[deep : 2 * deep] = packed_k
    sub = iota((1, SUBL, LANES), 1)
    half = SUBL // 2
    turned_k = pltpu.roll(packed_k, half, 1)
    low_rows = jnp.where(sub < half, packed_t, turned_k)
    high_rows = jnp.where(sub < half, turned_k, packed_t)
    out_z[:deep] = jnp.where(low_z, high_rows, low_rows)
    out_d[:deep] = jnp.where(low_z, low_rows, high_rows)
    tops = []
    for j in range(TOP // groups):
        tops.append(jnp.concatenate([t[j * groups + i] for i in range(groups)], axis=-1))
    for j in range(TOP // groups):
        tops.append(conduct(jnp.concatenate([m[j * groups + i] for i in range(groups)], axis=-1)))
    for j, top in enumerate(tops):
        own[2 * deep + j] = top
        out_z[deep + j] = top
        out_d[deep + j] = top
        out_a[COMPS * reach * tiles + j] = top
        out_b[COMPS * reach * tiles + j] = top
    edge, behind = edges(gz)
    size = u.shape[2]
    lane = iota((size, LANES), 1)
    eye = iota((size, size), 0) == iota((size, size), 1)
    levels = lev[...].astype(F32)
    acc = jnp.zeros((size, LANES), F32)
    for x in range(rows_x):
        acc = pack_heights([u[c, x] for c in range(COMPS)], x * GROUP, lane, edge, behind, acc)
        level = jnp.sum(jnp.where(eye, levels[x : x + 1, :], 0.0), axis=1, keepdims=True)
        acc = jnp.where(lane == x * GROUP + LEVEL, level, acc)
    for y in range(tiles):
        part = acc[y * SUBL : (y + 1) * SUBL]
        out_h[y] = part
        out_z[deep + len(tops) + y] = part
        out_d[deep + len(tops) + y] = part


def relay_kernel(cells, meta, u, own, in_a, in_b, in_z, in_d, in_h, out_a, out_b):
    rows_x, reach = cells
    gx, gy, gz = meta[0], meta[1], meta[2]
    even_x = lax.rem(gx, 2) == 0
    even_y = lax.rem(gy, 2) == 0
    low_z = gz == 0
    tiles = u.shape[2] // SUBL
    deep = (own.shape[0] - 4) // 2

    def put(n, hi, lo):
        out_a[n] = jnp.where(even_y, hi, lo)
        out_b[n] = jnp.where(even_y, lo, hi)

    n = 0
    for c in range(COMPS):
        for x in range(1 - reach, rows_x + reach - 1):
            pair = []
            for y in (tiles - 1, 0):
                if x < 0:
                    k = (c * reach + x + reach) * tiles + y
                    pair.append(jnp.where(even_x, in_b[k], in_a[k]))
                elif x < rows_x:
                    pair.append(u[c, x, y * SUBL : (y + 1) * SUBL, :])
                else:
                    k = (c * reach + x - rows_x) * tiles + y
                    pair.append(jnp.where(even_x, in_a[k], in_b[k]))
            put(n, *pair)
            n += 1
    base = deep + 4
    hi_y, lo_y = tiles - 1, 0
    put(
        n,
        jnp.where(low_z, in_d[base + hi_y], in_h[hi_y]),
        jnp.where(low_z, in_d[base + lo_y], in_h[lo_y]),
    )
    put(n + 1, in_z[base + hi_y], in_z[base + lo_y])
    put(
        n + 2,
        jnp.where(low_z, in_h[hi_y], in_d[base + hi_y]),
        jnp.where(low_z, in_h[lo_y], in_d[base + lo_y]),
    )
    n += 3
    half = SUBL // 2
    sub = iota((SUBL, LANES), 0)
    lane = iota((SUBL, LANES), 1)
    cols = LANES // 4
    slot = lax.rem(lane, cols) // SKIN
    per = cols // SKIN
    for j0 in range(deep // per):
        acc = [[jnp.zeros((SUBL, LANES), F32) for _ in range(4)] for _ in range(2)]
        for i in range(per):
            j = j0 * per + i
            hi = jnp.where(low_z, in_z[j], in_d[j])
            lo = jnp.where(low_z, in_d[j], in_z[j])
            four = (
                own[j],
                jnp.where(sub < half, hi, lo),
                own[deep + j],
                pltpu.roll(jnp.where(sub < half, lo, hi), half, 0),
            )
            for a in range(4):
                acc[0][a] = jnp.where(slot == i, turn(four[a], SKIN * i - (cols - SKIN), 1), acc[0][a])
                acc[1][a] = jnp.where(slot == i, turn(four[a], SKIN * i, 1), acc[1][a])
        for a in range(4):
            put(n + a * (deep // per) + j0, acc[0][a], acc[1][a])
    n += 4 * (deep // per)
    slot = lane // SUBL
    tail = in_a.shape[0] - 4
    for r in range(4):
        hi = jnp.zeros((SUBL, LANES), F32)
        lo = hi
        for j in range(4):
            if r == 0:
                src = own[2 * deep + j]
            elif r == 1:
                src = in_z[deep + j]
            elif r == 2:
                src = jnp.where(even_x, in_a[tail + j], in_b[tail + j])
            else:
                src = in_d[deep + j]
            for q in range(4):
                i = j * 4 + q
                hi = jnp.where(slot == i, turn(src, SUBL * i - cols * q - (cols - SUBL), 1), hi)
                lo = jnp.where(slot == i, turn(src, SUBL * i - cols * q, 1), lo)
        put(n + r, hi, lo)


def heat_source(row, col, beam, step):
    a = beam[step, 0].astype(F32)
    b = beam[step, 1].astype(F32)
    along_x = jnp.exp(-(((row - a) / SPOT_RADIUS) ** 2))
    along_y = jnp.exp(-(((col - b) / SPOT_RADIUS) ** 2))
    return LASER_POWER * along_x * along_y


def bulk_kernel(meta, beam, own, in_z, in_d, gy_a, gy_b, out, temp, kx, ky, kz):
    gx, gy, gz = meta[0], meta[1], meta[2]
    even_y = lax.rem(gy, 2) == 0
    low_z = gz == 0
    deep = (own.shape[0] - 4) // 2
    half = SUBL // 2
    size = 2 * SUBL
    cols = out.shape[2]
    groups = LANES // cols
    depth = out.shape[0]
    per = cols // SKIN
    sub = iota((SUBL, LANES), 0)
    lane = iota((SUBL, LANES), 1)
    base = gy_a.shape[0] - 4 - 4 * (deep // per)

    def unpack(j, carry):
        hi = jnp.where(low_z, in_z[j], in_d[j])
        lo = jnp.where(low_z, in_d[j], in_z[j])
        four = (
            own[j],
            jnp.where(sub < half, hi, lo),
            own[deep + j],
            pltpu.roll(jnp.where(sub < half, lo, hi), half, 0),
        )
        j0 = j // per
        i = lax.rem(j, per)
        for a in range(4):
            k = base + a * (deep // per) + j0
            upper = jnp.where(even_y, gy_a[k], gy_b[k])
            lower = jnp.where(even_y, gy_b[k], gy_a[k])
            for g in range(groups):
                value = turn(four[a], -cols * g, 1)
                up = lane_turn(upper, cols - (cols * g + SKIN * i))
                down = lane_turn(lower, (LANES - SKIN) - (cols * g + SKIN * i))
                value = jnp.where(
                    lane < cols,
                    value,
                    jnp.where(lane < cols + SKIN, up, jnp.where(lane >= LANES - SKIN, down, 0.0)),
                )
                rows = slice(0, SUBL) if a % 2 == 0 else slice(SUBL, size)
                if a < 2:
                    temp[0, g * deep + j, rows, :] = value
                else:
                    kz[g * deep + j, rows, :] = value
        return carry

    lax.fori_loop(0, deep, unpack, 0)

    def faces(d, k):
        nxt = jnp.where(d + 1 < depth, kz[jnp.minimum(d + 1, depth - 1)], 0.0)
        kx[d] = 0.5 * (k + turn(k, -1, 0))
        ky[d] = 0.5 * (k + turn(k, -1, 1))
        kz[d] = 0.5 * (k + nxt)
        return nxt

    first_k = kz[0]
    lax.fori_loop(0, depth, faces, first_k)

    row_l = wrapped(iota((size, LANES), 0), SUBL, size)
    col_l = wrapped(iota((size, LANES), 1), cols, LANES)
    row_g = (gx * meta[5] + gz) * SUBL + row_l
    col_g = gy * cols + col_l
    inside = (
        (row_g >= 0)
        & (row_g < meta[3] * meta[5] * SUBL)
        & (col_g >= 0)
        & (col_g < meta[4] * cols)
    )
    inside_f = jnp.where(inside, 1.0, 0.0)
    row_f, col_f = row_g.astype(F32), col_g.astype(F32)

    for s in range(STEPS * SUBSTEPS):
        src, dst = s % 2, 1 - s % 2
        beam_xy = heat_source(row_f, col_f, beam, s)
        last = s == STEPS * SUBSTEPS - 1

        def layer(d, carry):
            before = carry
            t = temp[src, d]
            below = jnp.where(d + 1 < depth, temp[src, jnp.minimum(d + 1, depth - 1)], 0.0)
            fz = kz[d] * (below - t)
            fx = kx[d] * (turn(t, -1, 0) - t)
            fy = ky[d] * (turn(t, -1, 1) - t)
            laser = beam_xy * jnp.exp(jnp.zeros((size, LANES), F32) - d.astype(F32) / ABSORB_DEPTH)
            change = (fx - turn(fx, 1, 0)) + (fy - turn(fy, 1, 1)) + (fz - before) + laser
            new = (t + HEAT_STEP * change) * inside_f
            if last:
                out[d] = new[:SUBL, :cols]
            else:
                temp[dst, d] = new
            return fz

        t0 = temp[src, 0]
        k0 = jnp.where(inside, first_k, 0.0)
        lax.fori_loop(0, depth, layer, 0.5 * k0 * t0, unroll=4)


def rates(west, mid, east, h, lane, edge):
    size = mid[0].shape[0]
    out_lap, sx, sy, sz = [], {}, {}, []
    for c in range(COMPS):
        north = turn(mid[c], -1, 0)
        south = turn(mid[c], 1, 0)
        halo = jnp.where(lane == edge, lane_turn(h, edge - c), 0.0)
        upper = jnp.where(lane == LANES - 1, halo, turn(mid[c], -1, 1))
        lower = jnp.where(lane == 0, halo, turn(mid[c], 1, 1))
        if c in (2, 5):
            sx[c] = 0.5 * (east[c] - west[c])
        if c in (3, 5):
            sy[c] = 0.5 * (north - south)
        sz.append(0.5 * (upper - lower))
        out_lap.append(east[c] + west[c] + north + south + upper + lower - 6.0 * mid[c])
    spread = sx[2] + sy[3] + sz[4]
    coupled = [-VAPOR_LOAD * spread, -AMBIENT_LOAD * spread, -sx[5], -sy[5], -sz[5], -STIFFNESS * spread]
    return [coupled[c] - DRIFT_SPEED * sz[c] + VISCOSITY[c] * out_lap[c] for c in range(COMPS)]


def halo_rates(h_west, h, h_east, mid, lane, edge, low_z):
    touch = jnp.zeros_like(h)
    for c in range(COMPS):
        touch = jnp.where(lane == c, lane_turn(mid[c], c - edge), touch)
    after = turn(h, -NEXT, 1)
    north = turn(h, -1, 0)
    south = turn(h, 1, 0)
    sx = 0.5 * (h_east - h_west)
    sy = 0.5 * (north - south)
    sz = jnp.where(low_z, 0.5, -0.5) * (after - touch)
    lap = h_east + h_west + north + south + after + touch - 6.0 * h
    q = jnp.where(lane == 2, sx, jnp.where(lane == 3, sy, jnp.where(lane == 4, sz, 0.0)))
    s = q + turn(q, -1, 1) + turn(q, -2, 1)
    coupled = jnp.where(
        lane == 0,
        -VAPOR_LOAD * turn(s, -2, 1),
        jnp.where(
            lane == 1,
            -AMBIENT_LOAD * turn(s, -1, 1),
            jnp.where(
                lane == 2,
                -turn(sx, -3, 1),
                jnp.where(
                    lane == 3,
                    -turn(sy, -2, 1),
                    jnp.where(lane == 4, -turn(sz, -1, 1), -STIFFNESS * turn(s, 3, 1)),
                ),
            ),
        ),
    )
    visc = jnp.where(
        lane == 0, VISCOSITY[0], jnp.where(lane == 1, VISCOSITY[1], jnp.where(lane == 5, VISCOSITY[5], VISCOSITY[2]))
    )
    return coupled - DRIFT_SPEED * sz + visc * lap


def advance(meta, g, h, f, fh, u1, own_x, own_y):
    n, size = g.shape[1], g.shape[2]
    gx, gy, gz = meta[0], meta[1], meta[2]
    low_z = gz == 0
    edge, _ = edges(gz)
    lane = iota((size, LANES), 1)
    y_l = wrapped(iota((size, LANES), 0), own_y, size)
    y_g = gy * own_y + y_l
    inside_y = jnp.where((y_g >= 0) & (y_g < meta[4] * own_y), 1.0, 0.0)
    before = (n - own_x) // 2

    def inside(i):
        x_g = gx * own_x + i - before
        ok = (x_g >= 0) & (x_g < meta[3] * own_x)
        return inside_y * jnp.where(ok, 1.0, 0.0)

    def one(i, carry):
        mid = [g[c, i] for c in range(COMPS)]
        rate = rates([g[c, i - 1] for c in range(COMPS)], mid, [g[c, i + 1] for c in range(COMPS)], h[i], lane, edge)
        m = inside(i)
        for c in range(COMPS):
            f[c, i - 1] = (mid[c] + GAS_STEP * rate[c]) * m
        hr = halo_rates(h[i - 1], h[i], h[i + 1], mid, lane, edge, low_z)
        fh[i - 1] = (h[i] + GAS_STEP * hr) * m
        return carry

    lax.fori_loop(1, n - 1, one, 0)

    part_rows = 4 * SUBL
    col_y = lax.div(wrapped(iota((size, LANES), 1), 2 * own_y, LANES) + LANES, 2) - LANES // 2
    spread_y = jnp.where(col_y == y_l, 1.0, 0.0)
    row_x = lax.div(wrapped(iota((part_rows, LANES), 0), 2 * own_x, part_rows) + LANES, 2) - LANES // 2
    height = iota((size, LANES), 1) + gz * LANES
    height = height.astype(F32)

    def two(i, fine):
        mid = [f[c, i - 1] for c in range(COMPS)]
        rate = rates([f[c, i - 2] for c in range(COMPS)], mid, [f[c, i] for c in range(COMPS)], fh[i - 1], lane, edge)
        m = inside(i)
        for c in range(COMPS):
            new = 0.5 * (g[c, i] + mid[c] + GAS_STEP * rate[c]) * m
            u1[c, i - 2] = new
        level = h[i][:, LEVEL : LEVEL + 1]
        at = jnp.sum(jnp.where(height == level, new, 0.0), axis=1, keepdims=True)
        line = jnp.sum(spread_y * at, axis=0, keepdims=True)
        return fine + jnp.where(row_x == i - before, line, 0.0)

    return lax.fori_loop(2, n - 2, two, jnp.zeros((part_rows, LANES), F32))


def top_heat(meta, beam, first, t, k, fine, own_rows, cols):
    gx, gy = meta[0], meta[1]
    shape = fine.shape
    row = gx * own_rows + wrapped(iota(shape, 0), own_rows, shape[0])
    col = gy * cols + wrapped(iota(shape, 1), cols, shape[1])
    row, col = row.astype(F32), col.astype(F32)
    kx = [0.5 * (v + turn(v, -1, 0)) for v in k]
    ky = [0.5 * (v + turn(v, -1, 1)) for v in k]
    kz = [0.5 * (k[d] + k[d + 1]) for d in range(TOP - 1)]
    for s in range(SUBSTEPS):
        beam_xy = heat_source(row, col, beam, first + s)
        before = 0.5 * k[0] * t[0]
        new = []
        for d in range(TOP):
            fx = kx[d] * (turn(t[d], -1, 0) - t[d])
            fy = ky[d] * (turn(t[d], -1, 1) - t[d])
            fz = kz[d] * (t[d + 1] - t[d]) if d + 1 < TOP else jnp.zeros_like(before)
            factor = jnp.exp(jnp.full(shape, -d / ABSORB_DEPTH, F32))
            change = (fx - turn(fx, 1, 0)) + (fy - turn(fy, 1, 1)) + (fz - before) + beam_xy * factor
            if d == 0:
                change = change - LATENT_HEAT * softplus(t[0] - BOIL_LEVEL - BACK_PRESSURE * fine)
            new.append(jnp.where(k[d] > 0, t[d] + HEAT_STEP * change, 0.0))
            before = fz
        t = new
    return t


def vapor_mass(t0, fine):
    four = t0 + turn(t0, -1, 1)
    four = four + turn(four, -1, 0)
    return softplus(0.25 * four - BOIL_LEVEL - BACK_PRESSURE * fine)


def mass_rows(meta, h, mass, size, own_y):
    gz = meta[2]
    y_l = wrapped(iota((size, LANES), 0), own_y, size)
    col = wrapped(iota((size, LANES), 1), 2 * own_y, LANES)
    pick = col == 2 * y_l
    height = (iota((size, LANES), 1) + gz * LANES).astype(F32)

    def row(i, x):
        r = lax.rem(2 * x + mass.shape[0], mass.shape[0])
        line = mass[pl.ds(r, 1), :]
        at = jnp.sum(jnp.where(pick, line, 0.0), axis=1, keepdims=True)
        return jnp.where(height == h[i][:, LEVEL : LEVEL + 1], at, 0.0)

    return row


def first_kernel(
    cells, meta, beam, u, own, in_a, in_b, in_z, in_d, in_h, gy_a, gy_b,
    out_g, out_m, out_t, out_k, g, h, f, fh, u1, mass,
):
    rows_x, reach = cells
    gx, gy, gz = meta[0], meta[1], meta[2]
    even_x = lax.rem(gx, 2) == 0
    even_y = lax.rem(gy, 2) == 0
    low_z = gz == 0
    own_y = u.shape[2]
    tiles = own_y // SUBL
    size = own_y + 2 * SUBL
    deep = (own.shape[0] - 4) // 2
    zero = jnp.zeros((SUBL, LANES), F32)

    def side(k):
        upper = jnp.where(even_y, gy_a[k], gy_b[k])
        lower = jnp.where(even_y, gy_b[k], gy_a[k])
        return upper, lower

    wide = rows_x + 2 * reach - 2
    for c in range(COMPS):
        for x in range(-reach, rows_x + reach):
            i = x + reach
            for y in range(tiles):
                if x < 0:
                    k = (c * reach + x + reach) * tiles + y
                    value = jnp.where(even_x, in_b[k], in_a[k])
                elif x < rows_x:
                    value = u[c, x, y * SUBL : (y + 1) * SUBL, :]
                else:
                    k = (c * reach + x - rows_x) * tiles + y
                    value = jnp.where(even_x, in_a[k], in_b[k])
                g[c, i, y * SUBL : (y + 1) * SUBL, :] = value
            if 0 < i < rows_x + 2 * reach - 1:
                upper, lower = side(c * wide + i - 1)
            else:
                upper = lower = zero
            g[c, i, own_y : own_y + SUBL, :] = upper
            g[c, i, own_y + SUBL : size, :] = lower
    base = deep + 4
    packed = []
    for b in range(3):
        parts = []
        for y in range(tiles):
            if b == 0:
                parts.append(jnp.where(low_z, in_d[base + y], in_h[y]))
            elif b == 1:
                parts.append(in_z[base + y])
            else:
                parts.append(jnp.where(low_z, in_h[y], in_d[base + y]))
        parts.extend(side(COMPS * wide + b))
        packed.append(jnp.concatenate(parts, axis=0))
    for x in range(-reach, rows_x + reach):
        b, q = divmod(x + rows_x, rows_x)
        h[x + reach] = turn(packed[b], -GROUP * q, 1)

    fine = advance(meta, g, h, f, fh, u1, rows_x, own_y)

    cols = LANES // 4
    part_rows = 4 * SUBL
    lane = iota((part_rows, LANES), 1)
    tail = in_a.shape[0] - 4
    top_at = gy_a.shape[0] - 4
    uppers, lowers = zip(*[side(top_at + r) for r in range(4)])
    uppers = jnp.concatenate(uppers, axis=0)
    lowers = jnp.concatenate(lowers, axis=0)
    layers = []
    for j in range(4):
        high = jnp.where(even_x, in_a[tail + j], in_b[tail + j])
        src = jnp.concatenate([own[2 * deep + j], in_z[deep + j], high, in_d[deep + j]], axis=0)
        for q in range(4):
            i = 4 * j + q
            layers.append(
                jnp.where(
                    lane < cols,
                    turn(src, -cols * q, 1),
                    jnp.where(
                        lane < cols + SUBL,
                        turn(uppers, cols - SUBL * i, 1),
                        jnp.where(lane >= LANES - SUBL, turn(lowers, LANES - SUBL - SUBL * i, 1), 0.0),
                    ),
                )
            )
    t, k = layers[:TOP], layers[TOP:]
    t = top_heat(meta, beam, 0, t, k, fine, 2 * rows_x, cols)
    for d in range(TOP):
        out_t[d] = t[d]
        out_k[d] = k[d]
    mass[...] = vapor_mass(t[0], fine)

    edge, behind = edges(gz)
    mass_of = mass_rows(meta, h, mass, size, own_y)
    x_from = -REACH_LAST
    count = rows_x + 2 * REACH_LAST
    half = SUBL // 2
    sub = iota((SUBL, LANES), 0)
    small = own_y + SUBL
    lane_s = iota((small, LANES), 1)
    shift = reach - 2 - REACH_LAST
    y_l = wrapped(iota((size, LANES), 0), own_y, size)
    y_g = gy * own_y + y_l
    inside_y = jnp.where((y_g >= 0) & (y_g < meta[4] * own_y), 1.0, 0.0)

    def finish(i, carry):
        x = i + x_from
        x_g = gx * rows_x + x
        ok = jnp.where((x_g >= 0) & (x_g < meta[3] * rows_x), 1.0, 0.0)
        add = mass_of(x + reach, x) * inside_y * ok
        rows = []
        for c in range(COMPS):
            value = u1[c, i + shift]
            if c == 0:
                value = value + VAPOR_SOURCE * add
            elif c == 4:
                value = value + RECOIL_PUSH * add
            elif c == 5:
                value = value + RECOIL_PRESSURE * add
            ends = jnp.where(sub < half, value[own_y : own_y + SUBL], value[own_y + SUBL : size])
            value = jnp.concatenate([value[:own_y], ends], axis=0)
            out_g[c, i] = value
            rows.append(value)
        acc = jnp.zeros((small, LANES), F32)
        for c in range(COMPS):
            acc = jnp.where(lane_s == c, lane_turn(rows[c], c - edge), acc)
            acc = jnp.where(lane_s == NEXT + c, lane_turn(rows[c], NEXT + c - behind), acc)
        level = h[x + reach][:, LEVEL : LEVEL + 1]
        ends = jnp.where(sub < half, level[own_y : own_y + SUBL], level[own_y + SUBL : size])
        level = jnp.concatenate([jnp.broadcast_to(level[:own_y], (own_y, LANES)), ends], axis=0)
        acc = jnp.where(lane_s == LEVEL, level, acc)
        acc = jnp.where(lane_s < GROUP, acc, 0.0)
        j = i // (LANES // GROUP)
        q = lax.rem(i, LANES // GROUP)
        out_m[j] = jnp.where(q == 0, 0.0, out_m[j]) + lane_turn(acc, GROUP * q)
        return carry

    out_m[...] = jnp.zeros_like(out_m)
    lax.fori_loop(0, count, finish, 0)


def last_kernel(cells, meta, beam, g, in_m, in_t, in_k, out_g, out_t, out_f, h, f, fh, u1, mass):
    rows_x, own_y = cells
    size = g.shape[2]
    n = g.shape[1]
    for i in range(n):
        j, q = divmod(i, LANES // GROUP)
        h[i] = turn(in_m[j], -GROUP * q, 1)
    fine = advance(meta, g, h, f, fh, u1, rows_x, own_y)
    cols = LANES // 4
    t = [in_t[d] for d in range(TOP)]
    k = [in_k[d] for d in range(TOP)]
    t = top_heat(meta, beam, SUBSTEPS, t, k, fine, 2 * rows_x, cols)
    for d in range(SKIN):
        out_t[d] = t[d][:SUBL]
        out_f[d] = t[d][SUBL : 2 * SUBL]
    mass[...] = vapor_mass(t[0], fine)
    mass_of = mass_rows(meta, h, mass, size, own_y)

    def finish(x, carry):
        add = mass_of(x + REACH_LAST, x)
        for c in range(COMPS):
            value = u1[c, x + REACH_LAST - 2]
            if c == 0:
                value = value + VAPOR_SOURCE * add
            elif c == 4:
                value = value + RECOIL_PUSH * add
            elif c == 5:
                value = value + RECOIL_PRESSURE * add
            out_g[c, x] = value[:own_y]
        return carry

    lax.fori_loop(0, rows_x, finish, 0)


def call(body, outs, scratch=(), scalars=1, count=0):
    vmem = pl.BlockSpec(memory_space=pltpu.VMEM)
    smem = pl.BlockSpec(memory_space=pltpu.SMEM)
    return pl.pallas_call(
        body,
        out_shape=[jax.ShapeDtypeStruct(s, F32) for s in outs],
        in_specs=[smem] * scalars + [vmem] * count,
        out_specs=[vmem] * len(outs),
        scratch_shapes=[pltpu.VMEM(s, F32) for s in scratch],
        compiler_params=pltpu.CompilerParams(vmem_limit_bytes=32 * 1024 * 1024),
    )


def pairs(count, odd):
    out = []
    for i in range(odd, count - 1, 2):
        out += [(i, i + 1), (i + 1, i)]
    return out


def cross(nx, nz, upper):
    out = []
    for i in range(nx - 1):
        a, b = i * nz + (nz - 1 if upper else 0), (i + 1) * nz + (0 if upper else nz - 1)
        out += [(a, b), (b, a)]
    return out


def shards(u, t, m, lev, beam):
    nx, ny, nz = (lax.axis_size(a) for a in ("gx", "gy", "gz"))
    gx, gy, gz = (lax.axis_index(a) for a in ("gx", "gy", "gz"))
    meta = jnp.stack([gx, gy, gz, nx, ny, nz]).astype(jnp.int32)
    _, rows_x, own_y, _ = u.shape
    tiles = own_y // SUBL
    deep = t.shape[0] * t.shape[2] // LANES
    block = (SUBL, LANES)
    n_x = COMPS * REACH * tiles + 4
    n_z = deep + 4 + tiles
    msg_a, msg_b, msg_z, msg_d, msg_h, own = call(
        functools.partial(pack_kernel, (rows_x, REACH)),
        [(n_x, *block), (n_x, *block), (n_z, *block), (n_z, *block), (tiles, *block), (2 * deep + 4, *block)],
        count=4,
    )(meta, u, t, m, lev)
    in_a = lax.ppermute(msg_a, "gx", pairs(nx, 0))
    in_b = lax.ppermute(msg_b, "gx", pairs(nx, 1))
    in_z = lax.ppermute(msg_z, "gz", pairs(nz, 0))
    in_d = lax.ppermute(msg_d, ("gx", "gz"), cross(nx, nz, True))
    in_h = lax.ppermute(msg_h, ("gx", "gz"), cross(nx, nz, False))
    n_y = COMPS * (rows_x + 2 * REACH - 2) + 3 + deep // 2 + 4
    msg_a, msg_b = call(
        functools.partial(relay_kernel, (rows_x, REACH)), [(n_y, *block), (n_y, *block)], count=7
    )(meta, u, own, in_a, in_b, in_z, in_d, in_h)
    gy_a = lax.ppermute(msg_a, "gy", pairs(ny, 0))
    gy_b = lax.ppermute(msg_b, "gy", pairs(ny, 1))

    size = own_y + 2 * SUBL
    n = rows_x + 2 * REACH
    n2 = rows_x + 2 * REACH_LAST
    small = own_y + SUBL
    part_rows = 4 * SUBL
    n_m = -(-n2 // (LANES // GROUP))
    g2, msg_m, top_t, top_k = call(
        functools.partial(first_kernel, (rows_x, REACH)),
        [(COMPS, n2, small, LANES), (n_m, small, LANES), (TOP, part_rows, LANES), (TOP, part_rows, LANES)],
        scratch=[
            (COMPS, n, size, LANES),
            (n, size, LANES),
            (COMPS, n - 2, size, LANES),
            (n - 2, size, LANES),
            (COMPS, n - 4, size, LANES),
            (part_rows, LANES),
        ],
        scalars=2,
        count=9,
    )(meta, beam, u, own, in_a, in_b, in_z, in_d, in_h, gy_a, gy_b)
    in_m = lax.ppermute(msg_m, "gz", pairs(nz, 0))
    (bulk,) = call(
        bulk_kernel,
        [t.shape],
        scratch=[
            (2, t.shape[0], 2 * SUBL, LANES),
            (t.shape[0], 2 * SUBL, LANES),
            (t.shape[0], 2 * SUBL, LANES),
            (t.shape[0], 2 * SUBL, LANES),
        ],
        scalars=2,
        count=5,
    )(meta, beam, own, in_z, in_d, gy_a, gy_b)
    gas, mine, other = call(
        functools.partial(last_kernel, (rows_x, own_y)),
        [u.shape, (SKIN, *block), (SKIN, *block)],
        scratch=[
            (n2, small, LANES),
            (COMPS, n2 - 2, small, LANES),
            (n2 - 2, small, LANES),
            (COMPS, n2 - 4, small, LANES),
            (part_rows, LANES),
        ],
        scalars=2,
        count=4,
    )(meta, beam, g2, in_m, top_t, top_k)
    given = lax.ppermute(other, "gz", pairs(nz, 0))
    skin = jnp.where(gz == 0, mine, given)[:, :, : t.shape[2]]
    return gas, lax.dynamic_update_slice(bulk, skin, (0, 0, 0))


def solution(mesh):
    return jax.shard_map(
        shards,
        mesh=mesh,
        in_specs=(
            P(None, "gx", "gy", "gz"),
            P(None, ("gx", "gz"), "gy"),
            P(None, ("gx", "gz"), "gy"),
            P("gx", "gy"),
            P(),
        ),
        out_specs=(P(None, "gx", "gy", "gz"), P(None, ("gx", "gz"), "gy")),
        check_vma=False,
    )
```

time: 217 us -> 99.3 us (0.46)
  starting transfers between devices: 90.9 us -> 13.5 us
  Pallas kernels: 0 us -> 63.5 us
  local copies, waits for them, and re-layouts: 52.4 us -> 3.11 us
  other arithmetic: 39.1 us -> 0.01 us
  blocking collectives: 18.6 us -> 0 us
  waiting for transfers between devices: 6.62 us -> 17.7 us
  between operations: 7.24 us -> 0.77 us
    ppermute x32 -> x9, starting transfers between devices: 90.9 us -> 13.5 us  [the longest x1 3.85 us: shards(): in_d = lax.ppermute(msg_d, ('gx', 'gz'), cross(nx, nz, True))]
    pallas_call x0 -> x5, Pallas kernels: none -> 63.5 us  [the longest x1 39.5 us: shards(): call(bulk_kernel, [t.shape], scratch=[(2, t.shape[0], 2 * SUBL, LANES), (...]
    ppermute x8 -> x0, local copies, waits for them, and re-layouts: 20.8 us -> none  [the longest x4 11.2 us: padded_2(): before = lax.ppermute(last, axis, up)]
    concatenate x13 -> x0, other arithmetic: 19 us -> none  [padded_2(): value = jnp.concatenate([before, value, after], axis=dim)]
    concatenate x6 -> x0, local copies, waits for them, and re-layouts: 17.4 us -> none  [padded_2(): value = jnp.concatenate([before, value, after], axis=dim)]
    mul x15 -> x0, other arithmetic: 12.9 us -> none  [the longest x2 5.21 us: advance(): first_section = first_section * inside[None]]
    ppermute x32 -> x9, waiting for transfers between devices: 6.62 us -> 17.7 us  [the longest x1 8.09 us: shards(): gy_b = lax.ppermute(msg_b, 'gy', pairs(ny, 1))]
    psum x2 -> x0, blocking collectives: 9.89 us -> none  [spread_2(): return lax.psum(kept, axis)]
  transfers between devices with their start and end apart: 32 -> 9, of which waited for: 4 -> 4; matrix products, arithmetic and copies ran while one was open for 16% -> 0% of each run, Pallas kernels for 0% -> 40%
where the time goes in v1:
time: 99.3 us; the launch traced here: 98.6 us
  Pallas kernels  63.5 us (64%)
  waiting for transfers between devices  17.7 us (18%)
  starting transfers between devices  13.5 us (14%)
  local copies, waits for them, and re-layouts  3.11 us (3%)
    pallas_call x1, Pallas kernels, shards(): call(bulk_kernel, [t.shape], scratch=[(2, t.shape[0], 2 * SUBL, LANES), (...  39.5 us
    pallas_call x1, Pallas kernels, shards(): call(functools.partial(first_kernel, (rows_x, REACH)), [(COMPS, n2, small...  13.6 us
    ppermute x1, waiting for transfers between devices, shards(): gy_b = lax.ppermute(msg_b, 'gy', pairs(ny, 1))  8.09 us
    pallas_call x1, Pallas kernels, shards(): call(functools.partial(last_kernel, (rows_x, own_y)), [u.shape, (SKIN, *b...  7.47 us
    ppermute x1, waiting for transfers between devices, shards(): in_h = lax.ppermute(msg_h, ('gx', 'gz'), cross(nx, nz, False))  4.6 us
    ppermute x1, starting transfers between devices, shards(): in_d = lax.ppermute(msg_d, ('gx', 'gz'), cross(nx, nz, True))  3.85 us
    ppermute x1, waiting for transfers between devices, shards(): in_m = lax.ppermute(msg_m, 'gz', pairs(nz, 0))  3.81 us
    unnamed x12, local copies, waits for them, and re-layouts  3.03 us
  transfers between devices with their start and end apart: 9, of which 4 were waited for; matrix products, arithmetic and copies ran while one was open for 0% of the time, Pallas kernels for 40%

profile of v1, /device:TPU:18, one launch (start us, length us, event | category | flops | bytes accessed | tf_op | source)
XLA Modules:
  0.0 98.6 jit_solution(3365480944122684791)
XLA Ops:
  0.6 1.2 %copy.7.t = f32[128,8,32]{2,1,0:T(8,128)S(1)} copy(f32[128,8,32]{0,2,1:T(8,128)} %param.6) | data formatting | bytes 262144 | tf_op args[1]
  1.8 0.0 copy-start
  1.9 0.2 copy.8.m
  2.1 0.1 stack.15.meta
  2.2 0.6 copy-done
  2.8 1.2 %shard_map.68 = (f32[76,8,128]{2,1,0:T(8,128)S(1)}, f32[76,8,128]{2,1,0:T(8,128)S(1)}, f32[38,8,128]{2,1,0:T(8,128)S(1)}, f32[38,8,128]{2,1,0:T(8,128)S(1)}, f32...) custom-call(s32[6]{0:T(128)S(1)} %stack.15.meta, f32[6,8,16,128]{3,2,1,0:T(8,128)S(1)} %copy-done, ...), custom_call_target="tpu_custom_call" | custom-call | tf_op jit(solution)/shard_map/pallas_call | solution.py:701
  4.1 1.6 %collective-permute-start = (f32[76,8,128]{2,1,0:T(8,128)S(1)}, f32[76,8,128]{2,1,0:T(8,128)S(1)}, u32[]{:S(2)}, u32[]{:S(2)}) collective-permute-start(f32[76,8,128]{2,1,0:T(8,128)S(1)} %get-tuple-element.18), channel_id=1, source_target_pairs={{0,8},{8,0},{16,24},{24,16},{1,9},{9,1},{17,25},{25,17},{2,10},{10... | collective-permute-start | bytes 933896 | tf_op jit(solution)/shard_map/ppermute | solution.py:706
  5.7 1.9 %collective-permute-start.1 = (f32[76,8,128]{2,1,0:T(8,128)S(1)}, f32[76,8,128]{2,1,0:T(8,128)S(1)}, u32[]{:S(2)}, u32[]{:S(2)}) collective-permute-start(f32[76,8,128]{2,1,0:T(8,128)S(1)} %get-tuple-element.19), channel_id=1, source_target_pairs={{8,16},{16,8},{9,17},{17,9},{10,18},{18,10},{11,19},{19,11},{12,20... | collective-permute-start | bytes 933896 | tf_op jit(solution)/shard_map/ppermute | solution.py:707
  7.6 1.6 %collective-permute-start.2 = (f32[38,8,128]{2,1,0:T(8,128)S(1)}, f32[38,8,128]{2,1,0:T(8,128)S(1)}, u32[]{:S(2)}, u32[]{:S(2)}) collective-permute-start(f32[38,8,128]{2,1,0:T(8,128)S(1)} %get-tuple-element.20), channel_id=1, source_target_pairs={{0,1},{1,0},{2,3},{3,2},{4,5},{5,4},{6,7},{7,6},{8,9},{9,8},{10,11... | collective-permute-start | bytes 466952 | tf_op jit(solution)/shard_map/ppermute | solution.py:708
  9.2 3.9 %collective-permute-start.3 = (f32[38,8,128]{2,1,0:T(8,128)S(1)}, f32[38,8,128]{2,1,0:T(8,128)S(1)}, u32[]{:S(2)}, u32[]{:S(2)}) collective-permute-start(f32[38,8,128]{2,1,0:T(8,128)S(1)} %get-tuple-element.21), channel_id=1, source_target_pairs={{1,8},{8,1},{9,16},{16,9},{17,24},{24,17},{3,10},{10,3},{11,18},{1... | collective-permute-start | bytes 466952 | tf_op jit(solution)/shard_map/ppermute | solution.py:709
  13.1 1.9 %collective-permute-start.4 = (f32[2,8,128]{2,1,0:T(8,128)S(1)}, f32[2,8,128]{2,1,0:T(8,128)S(1)}, u32[]{:S(2)}, u32[]{:S(2)}) collective-permute-start(f32[2,8,128]{2,1,0:T(8,128)S(1)} %get-tuple-element.22), channel_id=1, source_target_pairs={{0,9},{9,0},{8,17},{17,8},{16,25},{25,16},{2,11},{11,2},{10,19},{1... | collective-permute-start | bytes 24584 | tf_op jit(solution)/shard_map/ppermute | solution.py:710
  15.0 4.6 %collective-permute-done.4.in_h = f32[2,8,128]{2,1,0:T(8,128)S(1)} collective-permute-done((f32[2,8,128]{2,1,0:T(8,128)S(1)}, f32[2,8,128]{2,1,0:T(8,128)S(1)}, u32[]{:S(2)}, u32[]{:S(2)}) %collective-permute-start.4) | collective-permute-done | bytes 8224 | tf_op jit(solution)/shard_map/ppermute | solution.py:710
  19.6 1.2 %collective-permute-done.3.in_d = f32[38,8,128]{2,1,0:T(8,128)S(1)} collective-permute-done((f32[38,8,128]{2,1,0:T(8,128)S(1)}, f32[38,8,128]{2,1,0:T(8,128)S(1)}, u32[]{:S(2)}, u32[]{:S(2)}) %collective-permute-start.3) | collective-permute-done | bytes 155680 | tf_op jit(solution)/shard_map/ppermute | solution.py:709
  20.8 1.7 %shard_map.69 = (f32[131,8,128]{2,1,0:T(8,128)}, f32[131,8,128]{2,1,0:T(8,128)S(1)}) custom-call(s32[6]{0:T(128)S(1)} %stack.15.meta, f32[6,8,16,128]{3,2,1,0:T(8,128)S(1)} %copy-done, f32[68,8,128]{2,1,0:T(8,128)S(1)} %get-tuple-element.17.own, f32[76,8,128]{2,1,0:T(8,128)S(1)} %collective-permute-done.in_a, f32[76,8,128]{2,1,0:T(8,128)S(1)} %collective-permute-done.1.in_b, ...), custom_call_target="tpu_custom_call" | custom-call | tf_op jit(solution)/shard_map/pallas_call | solution.py:712
  22.5 2.5 %collective-permute-start.6 = (f32[131,8,128]{2,1,0:T(8,128)S(1)}, f32[131,8,128]{2,1,0:T(8,128)S(1)}, u32[]{:S(2)}, u32[]{:S(2)}) collective-permute-start(f32[131,8,128]{2,1,0:T(8,128)S(1)} %get-tuple-element.24), channel_id=1, source_target_pairs={{2,4},{4,2},{3,5},{5,3},{10,12},{12,10},{11,13},{13,11},{18,20},{2... | collective-permute-start | bytes 1609736 | tf_op jit(solution)/shard_map/ppermute | solution.py:716
  25.1 0.1 copy.10.beam
  25.2 8.1 %collective-permute-done.6.gy_b = f32[131,8,128]{2,1,0:T(8,128)S(1)} collective-permute-done((f32[131,8,128]{2,1,0:T(8,128)S(1)}, f32[131,8,128]{2,1,0:T(8,128)S(1)}, u32[]{:S(2)}, u32[]{:S(2)}) %collective-permute-start.6) | collective-permute-done | bytes 536608 | tf_op jit(solution)/shard_map/ppermute | solution.py:716
  33.3 13.6 %shard_map.70 = (f32[6,14,24,128]{3,2,1,0:T(8,128)S(1)}, f32[2,24,128]{2,1,0:T(8,128)S(1)}, f32[8,32,128]{2,1,0:T(8,128)S(1)}, f32[8,32,128]{2,1,0:T(8,128)S(1)}) custom-call(s32[6]{0:T(128)S(1)} %stack.15.meta, s32[4,2]{1,0:T(4,128)S(1)} %copy.10.beam, f32[6,8,16,128]{3,2,1,0:T(8,128)S(1)} %copy-done, f32[68,8,128]{2,1,0:T(8,128)S(1)} %get-tuple-element.17.own, ...), custom_call_target="tpu_custom_call" | custom-call | tf_op jit(solution)/shard_map/pallas_call | solution.py:724
  46.9 0.0 collective-permute-start.7
  46.9 3.8 %collective-permute-done.7.in_m = f32[2,24,128]{2,1,0:T(8,128)S(1)} collective-permute-done((f32[2,24,128]{2,1,0:T(8,128)S(1)}, f32[2,24,128]{2,1,0:T(8,128)S(1)}, u32[]{:S(2)}, u32[]{:S(2)}) %collective-permute-start.7) | collective-permute-done | bytes 24608 | tf_op jit(solution)/shard_map/ppermute | solution.py:738
  50.7 7.5 %shard_map.71 = (f32[6,8,16,128]{3,2,1,0:T(8,128)}, f32[4,8,128]{2,1,0:T(8,128)S(1)}, f32[4,8,128]{2,1,0:T(8,128)S(1)}) custom-call(s32[6]{0:T(128)S(1)} %stack.15.meta, s32[4,2]{1,0:T(4,128)S(1)} %copy.10.beam, f32[6,14,24,128]{3,2,1,0:T(8,128)S(1)} %get-tuple-element.25.g, f32[2,24,128]{2,1,0:T(8,128)S(1)} %collective-permute-done.7.in_m, ...), custom_call_target="tpu_custom_call" | custom-call | tf_op jit(solution)/shard_map/pallas_call | solution.py:751
  58.2 0.0 collective-permute-start.8
  58.2 39.5 %shard_map.72 = f32[128,8,32]{2,1,0:T(8,128)S(1)} custom-call(s32[6]{0:T(128)S(1)} %stack.15.meta, s32[4,2]{1,0:T(4,128)S(1)} %copy.10.beam, f32[68,8,128]{2,1,0:T(8,128)S(1)} %get-tuple-element.17.own, f32[38,8,128]{2,1,0:T(8,128)S(1)} %collective-permute-done.2.in_z, f32[38,8,128]{2,1,0:T(8,128)S(1)} %collective-permute-done.3.in_d, ...), custom_call_target="tpu_custom_call" | custom-call | tf_op jit(solution)/shard_map/pallas_call | solution.py:739
  97.7 0.9 copy.12
  (14 shorter events, 0.0 us)
Async XLA Ops:
  0.6 1.2 %copy-start.2 = (s32[128,8,32]{0,2,1:T(8,128)S(1)}, s32[128,8,32]{0,2,1:T(8,128)}, u32[]{:S(2)}) copy-start(s32[128,8,32]{0,2,1:T(8,128)} %param.7) | copy-start | bytes 393220
  1.8 1.0 %copy-start = (f32[6,8,16,128]{3,2,1,0:T(8,128)S(1)}, f32[6,8,16,128]{3,2,1,0:T(8,128)}, u32[]{:S(2)}) copy-start(f32[6,8,16,128]{3,2,1,0:T(8,128)} %u.5) | copy-start | bytes 1179652
  2.1 0.7 copy-start.1
  4.1 16.7 %collective-permute-start = (f32[76,8,128]{2,1,0:T(8,128)S(1)}, f32[76,8,128]{2,1,0:T(8,128)S(1)}, u32[]{:S(2)}, u32[]{:S(2)}) collective-permute-start(f32[76,8,128]{2,1,0:T(8,128)S(1)} %get-tuple-element.18), channel_id=1, source_target_pairs={{0,8},{8,0},{16,24},{24,16},{1,9},{9,1},{17,25},{25,17},{2,10},{10... | collective-permute-start | bytes 933896 | tf_op jit(solution)/shard_map/ppermute | solution.py:706
  5.7 15.1 %collective-permute-start.1 = (f32[76,8,128]{2,1,0:T(8,128)S(1)}, f32[76,8,128]{2,1,0:T(8,128)S(1)}, u32[]{:S(2)}, u32[]{:S(2)}) collective-permute-start(f32[76,8,128]{2,1,0:T(8,128)S(1)} %get-tuple-element.19), channel_id=1, source_target_pairs={{8,16},{16,8},{9,17},{17,9},{10,18},{18,10},{11,19},{19,11},{12,20... | collective-permute-start | bytes 933896 | tf_op jit(solution)/shard_map/ppermute | solution.py:707
  7.6 12.0 %collective-permute-start.2 = (f32[38,8,128]{2,1,0:T(8,128)S(1)}, f32[38,8,128]{2,1,0:T(8,128)S(1)}, u32[]{:S(2)}, u32[]{:S(2)}) collective-permute-start(f32[38,8,128]{2,1,0:T(8,128)S(1)} %get-tuple-element.20), channel_id=1, source_target_pairs={{0,1},{1,0},{2,3},{3,2},{4,5},{5,4},{6,7},{7,6},{8,9},{9,8},{10,11... | collective-permute-start | bytes 466952 | tf_op jit(solution)/shard_map/ppermute | solution.py:708
  9.2 11.6 %collective-permute-start.3 = (f32[38,8,128]{2,1,0:T(8,128)S(1)}, f32[38,8,128]{2,1,0:T(8,128)S(1)}, u32[]{:S(2)}, u32[]{:S(2)}) collective-permute-start(f32[38,8,128]{2,1,0:T(8,128)S(1)} %get-tuple-element.21), channel_id=1, source_target_pairs={{1,8},{8,1},{9,16},{16,9},{17,24},{24,17},{3,10},{10,3},{11,18},{1... | collective-permute-start | bytes 466952 | tf_op jit(solution)/shard_map/ppermute | solution.py:709
  13.1 6.5 %collective-permute-start.4 = (f32[2,8,128]{2,1,0:T(8,128)S(1)}, f32[2,8,128]{2,1,0:T(8,128)S(1)}, u32[]{:S(2)}, u32[]{:S(2)}) collective-permute-start(f32[2,8,128]{2,1,0:T(8,128)S(1)} %get-tuple-element.22), channel_id=1, source_target_pairs={{0,9},{9,0},{8,17},{17,8},{16,25},{25,16},{2,11},{11,2},{10,19},{1... | collective-permute-start | bytes 24584 | tf_op jit(solution)/shard_map/ppermute | solution.py:710
  22.5 2.6 %copy-start.3 = (s32[4,2]{0,1:T(2,128)S(1)}, s32[4,2]{0,1:T(2,128)}, u32[]{:S(2)}) copy-start(s32[4,2]{0,1:T(2,128)} %param.9) | copy-start | bytes 100
  22.5 2.7 %collective-permute-start.5 = (f32[131,8,128]{2,1,0:T(8,128)}, f32[131,8,128]{2,1,0:T(8,128)S(1)}, u32[]{:S(2)}, u32[]{:S(2)}) collective-permute-start(f32[131,8,128]{2,1,0:T(8,128)} %get-tuple-element.23), channel_id=1, source_target_pairs={{0,2},{2,0},{4,6},{6,4},{1,3},{3,1},{5,7},{7,5},{8,10},{10,8},{12,... | collective-permute-start | bytes 1609736 | tf_op jit(solution)/shard_map/ppermute | solution.py:715
  22.5 10.8 %collective-permute-start.6 = (f32[131,8,128]{2,1,0:T(8,128)S(1)}, f32[131,8,128]{2,1,0:T(8,128)S(1)}, u32[]{:S(2)}, u32[]{:S(2)}) collective-permute-start(f32[131,8,128]{2,1,0:T(8,128)S(1)} %get-tuple-element.24), channel_id=1, source_target_pairs={{2,4},{4,2},{3,5},{5,3},{10,12},{12,10},{11,13},{13,11},{18,20},{2... | collective-permute-start | bytes 1609736 | tf_op jit(solution)/shard_map/ppermute | solution.py:716
  46.9 3.8 %collective-permute-start.7 = (f32[2,24,128]{2,1,0:T(8,128)S(1)}, f32[2,24,128]{2,1,0:T(8,128)S(1)}, u32[]{:S(2)}, u32[]{:S(2)}) collective-permute-start(f32[2,24,128]{2,1,0:T(8,128)S(1)} %get-tuple-element.26), channel_id=1, source_target_pairs={{0,1},{1,0},{2,3},{3,2},{4,5},{5,4},{6,7},{7,6},{8,9},{9,8},{10,11... | collective-permute-start | bytes 73736 | tf_op jit(solution)/shard_map/ppermute | solution.py:738
  58.2 39.5 %collective-permute-start.8 = (f32[4,8,128]{2,1,0:T(8,128)S(1)}, f32[4,8,128]{2,1,0:T(8,128)S(1)}, u32[]{:S(2)}, u32[]{:S(2)}) collective-permute-start(f32[4,8,128]{2,1,0:T(8,128)S(1)} %get-tuple-element.31), channel_id=1, source_target_pairs={{0,1},{1,0},{2,3},{3,2},{4,5},{5,4},{6,7},{7,6},{8,9},{9,8},{10,11... | collective-permute-start | bytes 49160 | tf_op jit(solution)/shard_map/ppermute | solution.py:764

commit v2 on v1

--- a/solution.py
+++ b/solution.py
@@ -78,6 +78,41 @@
     return acc
 
 
+DEEP_5 = (2, 3, 4, 5)
+DEEP_6 = (2, 5)
+FULL = 4
+QUARTERS = (5, 3, 2, 4)
+
+
+def slab_index(c, layer, tile, tiles):
+    if layer <= FULL:
+        return (c * FULL + layer - 1) * tiles + tile
+    base = COMPS * FULL * tiles
+    if layer == FULL + 1:
+        return base + DEEP_5.index(c) * tiles + tile if c in DEEP_5 else None
+    base += len(DEEP_5) * tiles
+    return base + DEEP_6.index(c) * tiles + tile if c in DEEP_6 else None
+
+
+def slab_size(tiles):
+    return (COMPS * FULL + len(DEEP_5) + len(DEEP_6)) * tiles
+
+
+def row_tile(c, x, tile, u, in_a, in_b, even_x):
+    rows_x, tiles = u.shape[1], u.shape[2] // SUBL
+    if 0 <= x < rows_x:
+        return u[c, x, tile * SUBL : (tile + 1) * SUBL, :]
+    k = slab_index(c, -x if x < 0 else x - rows_x + 1, tile, tiles)
+    if k is None:
+        return None
+    low, high = (in_b[k], in_a[k]) if x < 0 else (in_a[k], in_b[k])
+    return jnp.where(even_x, low, high)
+
+
+def conduct(v):
+    return jnp.where(v == 0, POWDER_COND, jnp.where(v == 1, SOLID_COND, LIQUID_COND)).astype(F32)
+
+
 def pack_kernel(cells, meta, u, t, m, lev, out_a, out_b, out_z, out_d, out_h, own):
     rows_x, reach = cells
     gx, gz = meta[0], meta[2]
@@ -85,43 +120,41 @@
     low_z = gz == 0
     tiles = u.shape[2] // SUBL
     for c in range(COMPS):
-        for i in range(reach):
+        for layer in range(1, reach + 1):
             for y in range(tiles):
-                lo = u[c, i, y * SUBL : (y + 1) * SUBL, :]
-                hi = u[c, rows_x - reach + i, y * SUBL : (y + 1) * SUBL, :]
-                n = (c * reach + i) * tiles + y
+                n = slab_index(c, layer, y, tiles)
+                if n is None:
+                    continue
+                lo = u[c, layer - 1, y * SUBL : (y + 1) * SUBL, :]
+                hi = u[c, rows_x - layer, y * SUBL : (y + 1) * SUBL, :]
                 out_a[n] = jnp.where(even, hi, lo)
                 out_b[n] = jnp.where(even, lo, hi)
-    depth = t.shape[0]
-    cols = t.shape[2]
-    groups = LANES // cols
-    deep = depth // groups
-
-    def conduct(v):
-        return jnp.where(v == 0, POWDER_COND, jnp.where(v == 1, SOLID_COND, LIQUID_COND)).astype(F32)
-
-    packed_t = jnp.concatenate([t[g * deep : (g + 1) * deep] for g in range(groups)], axis=-1)
-    packed_k = conduct(jnp.concatenate([m[g * deep : (g + 1) * deep] for g in range(groups)], axis=-1))
-    own[:deep] = packed_t
-    own[deep : 2 * deep] = packed_k
-    sub = iota((1, SUBL, LANES), 1)
-    half = SUBL // 2
-    turned_k = pltpu.roll(packed_k, half, 1)
-    low_rows = jnp.where(sub < half, packed_t, turned_k)
-    high_rows = jnp.where(sub < half, turned_k, packed_t)
-    out_z[:deep] = jnp.where(low_z, high_rows, low_rows)
-    out_d[:deep] = jnp.where(low_z, low_rows, high_rows)
-    tops = []
-    for j in range(TOP // groups):
-        tops.append(jnp.concatenate([t[j * groups + i] for i in range(groups)], axis=-1))
-    for j in range(TOP // groups):
-        tops.append(conduct(jnp.concatenate([m[j * groups + i] for i in range(groups)], axis=-1)))
-    for j, top in enumerate(tops):
-        own[2 * deep + j] = top
-        out_z[deep + j] = top
-        out_d[deep + j] = top
-        out_a[COMPS * reach * tiles + j] = top
-        out_b[COMPS * reach * tiles + j] = top
+    rows, cols = t.shape[0], t.shape[1]
+    col_tiles = cols // SUBL
+    n = 0
+    for source in (lambda v: v, conduct):
+        ref = t if n == 0 else m
+        for r in range(SKIN):
+            for y in range(col_tiles):
+                lo = source(ref[r, y * SUBL : (y + 1) * SUBL, :])
+                hi = source(ref[rows - SKIN + r, y * SUBL : (y + 1) * SUBL, :])
+                out_z[n] = jnp.where(low_z, hi, lo)
+                out_d[n] = jnp.where(low_z, lo, hi)
+                n += 1
+    per = LANES // cols
+    top_a = slab_size(tiles)
+    for j in range(2 * rows // per):
+        ref, r = (t, j * per) if j < rows // per else (m, j * per - rows)
+        block = ref[r : r + per].reshape(LANES, LANES)
+        if ref is m:
+            block = conduct(block)
+        top = jnp.transpose(block)[:TOP]
+        own[j] = top
+        out_z[n + j] = top
+        out_d[n + j] = top
+        out_a[top_a + j] = top
+        out_b[top_a + j] = top
+    n += 2 * rows // per
     edge, behind = edges(gz)
     size = u.shape[2]
     lane = iota((size, LANES), 1)
@@ -135,39 +168,56 @@
     for y in range(tiles):
         part = acc[y * SUBL : (y + 1) * SUBL]
         out_h[y] = part
-        out_z[deep + len(tops) + y] = part
-        out_d[deep + len(tops) + y] = part
-
-
-def relay_kernel(cells, meta, u, own, in_a, in_b, in_z, in_d, in_h, out_a, out_b):
+        out_z[n + y] = part
+        out_d[n + y] = part
+
+
+def part_row(r, tile, ref, at, rows, in_z, in_d, low_z, col_tiles, low_part):
+    if 0 <= r < rows:
+        value = ref[r, tile * SUBL : (tile + 1) * SUBL, :]
+        return conduct(value) if at else value
+    k = (at * SKIN + (r + SKIN if r < 0 else r - rows)) * col_tiles + tile
+    low, high = (in_d[k], in_z[k]) if r < 0 else (in_z[k], in_d[k])
+    return jnp.where(low_z, low, high)
+
+
+def relay_kernel(cells, meta, u, t, m, own, in_a, in_b, in_z, in_d, in_h, out_a, out_b):
     rows_x, reach = cells
     gx, gy, gz = meta[0], meta[1], meta[2]
     even_x = lax.rem(gx, 2) == 0
     even_y = lax.rem(gy, 2) == 0
     low_z = gz == 0
     tiles = u.shape[2] // SUBL
-    deep = (own.shape[0] - 4) // 2
+    rows, cols = t.shape[0], t.shape[1]
+    col_tiles = cols // SUBL
+    half = SUBL // 2
+    sub = iota((SUBL, LANES), 0)
+    lane = iota((SUBL, LANES), 1)
+    zero = jnp.zeros((SUBL, LANES), F32)
 
     def put(n, hi, lo):
         out_a[n] = jnp.where(even_y, hi, lo)
         out_b[n] = jnp.where(even_y, lo, hi)
 
+    def both(c, x):
+        pair = [row_tile(c, x, y, u, in_a, in_b, even_x) for y in (tiles - 1, 0)]
+        return [zero if v is None else v for v in pair]
+
     n = 0
-    for c in range(COMPS):
-        for x in range(1 - reach, rows_x + reach - 1):
-            pair = []
-            for y in (tiles - 1, 0):
-                if x < 0:
-                    k = (c * reach + x + reach) * tiles + y
-                    pair.append(jnp.where(even_x, in_b[k], in_a[k]))
-                elif x < rows_x:
-                    pair.append(u[c, x, y * SUBL : (y + 1) * SUBL, :])
-                else:
-                    k = (c * reach + x - rows_x) * tiles + y
-                    pair.append(jnp.where(even_x, in_a[k], in_b[k]))
-            put(n, *pair)
+    for x in range(1 - reach, rows_x + reach - 1):
+        for c in range(0, COMPS, 2):
+            (hi0, lo0), (hi1, lo1) = both(c, x), both(c + 1, x)
+            put(n, jnp.where(sub < half, turn(hi1, half, 0), hi0), jnp.where(sub < half, lo0, turn(lo1, half, 0)))
             n += 1
-    base = deep + 4
+    for x in range(-1, rows_x + 1):
+        hi = lo = zero
+        for q, c in enumerate(QUARTERS):
+            a, b = both(c, x)
+            hi = jnp.where(sub // 2 == q, turn(a, 2 * q - 2, 0), hi)
+            lo = jnp.where(sub // 2 == q, turn(b, 2 * q - half, 0), lo)
+        put(n, hi, lo)
+        n += 1
+    base = in_z.shape[0] - tiles
     hi_y, lo_y = tiles - 1, 0
     put(
         n,
@@ -181,49 +231,35 @@
         jnp.where(low_z, in_h[lo_y], in_d[base + lo_y]),
     )
     n += 3
-    half = SUBL // 2
-    sub = iota((SUBL, LANES), 0)
-    lane = iota((SUBL, LANES), 1)
-    cols = LANES // 4
-    slot = lax.rem(lane, cols) // SKIN
-    per = cols // SKIN
-    for j0 in range(deep // per):
-        acc = [[jnp.zeros((SUBL, LANES), F32) for _ in range(4)] for _ in range(2)]
+    for r in range(-SKIN, rows + SKIN):
+        hi_t, lo_t = [part_row(r, y, t, 0, rows, in_z, in_d, low_z, col_tiles, None) for y in (col_tiles - 1, 0)]
+        hi_k, lo_k = [part_row(r, y, m, 1, rows, in_z, in_d, low_z, col_tiles, None) for y in (col_tiles - 1, 0)]
+        put(n, jnp.where(sub < half, turn(hi_k, half, 0), hi_t), jnp.where(sub < half, lo_t, turn(lo_k, half, 0)))
+        n += 1
+    sources = surface_sources(own, in_a, in_b, in_z, in_d, even_x, tiles)
+    per = LANES // cols
+    slot = lax.rem(lane, cols) // SUBL
+    for v in range(len(sources) // per):
+        hi = lo = zero
         for i in range(per):
-            j = j0 * per + i
-            hi = jnp.where(low_z, in_z[j], in_d[j])
-            lo = jnp.where(low_z, in_d[j], in_z[j])
-            four = (
-                own[j],
-                jnp.where(sub < half, hi, lo),
-                own[deep + j],
-                pltpu.roll(jnp.where(sub < half, lo, hi), half, 0),
-            )
-            for a in range(4):
-                acc[0][a] = jnp.where(slot == i, turn(four[a], SKIN * i - (cols - SKIN), 1), acc[0][a])
-                acc[1][a] = jnp.where(slot == i, turn(four[a], SKIN * i, 1), acc[1][a])
-        for a in range(4):
-            put(n + a * (deep // per) + j0, acc[0][a], acc[1][a])
-    n += 4 * (deep // per)
-    slot = lane // SUBL
-    tail = in_a.shape[0] - 4
-    for r in range(4):
-        hi = jnp.zeros((SUBL, LANES), F32)
-        lo = hi
-        for j in range(4):
-            if r == 0:
-                src = own[2 * deep + j]
-            elif r == 1:
-                src = in_z[deep + j]
-            elif r == 2:
-                src = jnp.where(even_x, in_a[tail + j], in_b[tail + j])
-            else:
-                src = in_d[deep + j]
-            for q in range(4):
-                i = j * 4 + q
-                hi = jnp.where(slot == i, turn(src, SUBL * i - cols * q - (cols - SUBL), 1), hi)
-                lo = jnp.where(slot == i, turn(src, SUBL * i - cols * q, 1), lo)
-        put(n + r, hi, lo)
+            src = sources[v * per + i]
+            hi = jnp.where(slot == i, turn(src, SUBL * i - (cols - SUBL), 1), hi)
+            lo = jnp.where(slot == i, turn(src, SUBL * i, 1), lo)
+        put(n + v, hi, lo)
+
+
+def surface_sources(own, in_a, in_b, in_z, in_d, even_x, tiles):
+    count = own.shape[0]
+    tail = in_a.shape[0] - count
+    at = in_z.shape[0] - tiles - count
+    out = []
+    for a in range(2):
+        span = range(a * count // 2, (a + 1) * count // 2)
+        out += [own[j] for j in span]
+        out += [in_z[at + j] for j in span]
+        out += [jnp.where(even_x, in_a[tail + j], in_b[tail + j]) for j in span]
+        out += [in_d[at + j] for j in span]
+    return out
 
 
 def heat_source(row, col, beam, step):
@@ -234,101 +270,86 @@
     return LASER_POWER * along_x * along_y
 
 
-def bulk_kernel(meta, beam, own, in_z, in_d, gy_a, gy_b, out, temp, kx, ky, kz):
+def bulk_kernel(meta, beam, t, m, in_z, in_d, gy_a, gy_b, out, temp, cond, kx, ky, kz):
     gx, gy, gz = meta[0], meta[1], meta[2]
     even_y = lax.rem(gy, 2) == 0
     low_z = gz == 0
-    deep = (own.shape[0] - 4) // 2
+    rows, cols, depth = t.shape
+    col_tiles = cols // SUBL
     half = SUBL // 2
-    size = 2 * SUBL
-    cols = out.shape[2]
-    groups = LANES // cols
-    depth = out.shape[0]
-    per = cols // SKIN
+    size = cols + SUBL
+    n = rows + 2 * SKIN
     sub = iota((SUBL, LANES), 0)
-    lane = iota((SUBL, LANES), 1)
-    base = gy_a.shape[0] - 4 - 4 * (deep // per)
-
-    def unpack(j, carry):
-        hi = jnp.where(low_z, in_z[j], in_d[j])
-        lo = jnp.where(low_z, in_d[j], in_z[j])
-        four = (
-            own[j],
-            jnp.where(sub < half, hi, lo),
-            own[deep + j],
-            pltpu.roll(jnp.where(sub < half, lo, hi), half, 0),
-        )
-        j0 = j // per
-        i = lax.rem(j, per)
-        for a in range(4):
-            k = base + a * (deep // per) + j0
-            upper = jnp.where(even_y, gy_a[k], gy_b[k])
-            lower = jnp.where(even_y, gy_b[k], gy_a[k])
-            for g in range(groups):
-                value = turn(four[a], -cols * g, 1)
-                up = lane_turn(upper, cols - (cols * g + SKIN * i))
-                down = lane_turn(lower, (LANES - SKIN) - (cols * g + SKIN * i))
-                value = jnp.where(
-                    lane < cols,
-                    value,
-                    jnp.where(lane < cols + SKIN, up, jnp.where(lane >= LANES - SKIN, down, 0.0)),
-                )
-                rows = slice(0, SUBL) if a % 2 == 0 else slice(SUBL, size)
-                if a < 2:
-                    temp[0, g * deep + j, rows, :] = value
-                else:
-                    kz[g * deep + j, rows, :] = value
-        return carry
-
-    lax.fori_loop(0, deep, unpack, 0)
-
-    def faces(d, k):
-        nxt = jnp.where(d + 1 < depth, kz[jnp.minimum(d + 1, depth - 1)], 0.0)
-        kx[d] = 0.5 * (k + turn(k, -1, 0))
-        ky[d] = 0.5 * (k + turn(k, -1, 1))
-        kz[d] = 0.5 * (k + nxt)
-        return nxt
-
-    first_k = kz[0]
-    lax.fori_loop(0, depth, faces, first_k)
-
-    row_l = wrapped(iota((size, LANES), 0), SUBL, size)
-    col_l = wrapped(iota((size, LANES), 1), cols, LANES)
-    row_g = (gx * meta[5] + gz) * SUBL + row_l
-    col_g = gy * cols + col_l
-    inside = (
-        (row_g >= 0)
-        & (row_g < meta[3] * meta[5] * SUBL)
-        & (col_g >= 0)
-        & (col_g < meta[4] * cols)
-    )
-    inside_f = jnp.where(inside, 1.0, 0.0)
-    row_f, col_f = row_g.astype(F32), col_g.astype(F32)
+    base = gy_a.shape[0] - 4 - n
+    for i in range(n):
+        for y in range(col_tiles):
+            span = slice(y * SUBL, (y + 1) * SUBL)
+            temp[0, i, span, :] = part_row(i - SKIN, y, t, 0, rows, in_z, in_d, low_z, col_tiles, None)
+            cond[i, span, :] = part_row(i - SKIN, y, m, 1, rows, in_z, in_d, low_z, col_tiles, None)
+        up = jnp.where(even_y, gy_a[base + i], gy_b[base + i])
+        low = jnp.where(even_y, gy_b[base + i], gy_a[base + i])
+        temp[0, i, cols:size, :] = jnp.where(sub < half, up, low)
+        cond[i, cols:size, :] = turn(jnp.where(sub < half, low, up), half, 0)
+
+    lane = iota((size, LANES), 1)
+    for i in range(n):
+        k = cond[i]
+        if i + 1 < n:
+            kx[i] = 0.5 * (k + cond[i + 1])
+        ky[i] = 0.5 * (k + turn(k, -1, 0))
+        kz[i] = 0.5 * (k + jnp.where(lane == depth - 1, 0.0, turn(k, -1, 1)))
+
+    col_g = gy * cols + wrapped(iota((size, LANES), 0), cols, size)
+    inside_y = jnp.where((col_g >= 0) & (col_g < meta[4] * cols), 1.0, 0.0)
+    col_f = col_g.astype(F32)
+    fall = jnp.exp(-lane.astype(F32) / ABSORB_DEPTH)
+    first_row = (gx * meta[5] + gz) * rows - SKIN
 
     for s in range(STEPS * SUBSTEPS):
         src, dst = s % 2, 1 - s % 2
-        beam_xy = heat_source(row_f, col_f, beam, s)
         last = s == STEPS * SUBSTEPS - 1
-
-        def layer(d, carry):
-            before = carry
-            t = temp[src, d]
-            below = jnp.where(d + 1 < depth, temp[src, jnp.minimum(d + 1, depth - 1)], 0.0)
-            fz = kz[d] * (below - t)
-            fx = kx[d] * (turn(t, -1, 0) - t)
-            fy = ky[d] * (turn(t, -1, 1) - t)
-            laser = beam_xy * jnp.exp(jnp.zeros((size, LANES), F32) - d.astype(F32) / ABSORB_DEPTH)
-            change = (fx - turn(fx, 1, 0)) + (fy - turn(fy, 1, 1)) + (fz - before) + laser
-            new = (t + HEAT_STEP * change) * inside_f
+        a = beam[s, 0].astype(F32)
+        b = beam[s, 1].astype(F32)
+        spot = LASER_POWER * fall * jnp.exp(-(((col_f - b) / SPOT_RADIUS) ** 2))
+        lo, hi = s + 1, n - 1 - s
+        fx0 = kx[lo - 1] * (temp[src, lo] - temp[src, lo - 1])
+        for i in range(lo, hi):
+            v = temp[src, i]
+            fx = kx[i] * (temp[src, i + 1] - v)
+            fy = ky[i] * (turn(v, -1, 0) - v)
+            fz = kz[i] * (jnp.where(lane == depth - 1, 0.0, turn(v, -1, 1)) - v)
+            above = jnp.where(lane == 0, 0.5 * cond[i] * v, turn(fz, 1, 1))
+            row = first_row + i
+            along_x = jnp.exp(-((jnp.full((1, LANES), row.astype(F32) - a) / SPOT_RADIUS) ** 2))
+            change = (fx - fx0) + (fy - turn(fy, 1, 0)) + (fz - above) + spot * along_x
+            new = v + HEAT_STEP * change
             if last:
-                out[d] = new[:SUBL, :cols]
+                out[i - SKIN] = new[:cols]
             else:
-                temp[dst, d] = new
-            return fz
-
-        t0 = temp[src, 0]
-        k0 = jnp.where(inside, first_k, 0.0)
-        lax.fori_loop(0, depth, layer, 0.5 * k0 * t0, unroll=4)
+                ok = (row >= 0) & (row < meta[3] * meta[5] * rows)
+                temp[dst, i] = new * (inside_y * jnp.where(ok, 1.0, 0.0))
+            fx0 = fx
+
+
+def seal_kernel(meta, bulk, mine, given, out):
+    rows, cols, depth = bulk.shape
+    per = LANES // cols
+    lane = iota((LANES, LANES), 1)
+    for j in range(mine.shape[0]):
+        skin = jnp.where(meta[2] == 0, mine[j], given[j])
+        skin = jnp.concatenate([skin, jnp.zeros((LANES - SUBL, LANES), F32)], axis=0)
+        block = jnp.where(lane < SKIN, jnp.transpose(skin), bulk[j * per : (j + 1) * per].reshape(LANES, LANES))
+        out[j * per : (j + 1) * per] = block.reshape(per, cols, LANES)
+
+
+def pack_skin(t, rows, cols, scratch, out):
+    per = LANES // cols
+    lane = iota((SUBL, LANES), 1)
+    for j in range(SUBL // per):
+        acc = jnp.zeros((SUBL, LANES), F32)
+        for q in range(per):
+            acc = jnp.where(lane // cols == q, turn(scratch[rows + j * per + q], cols * q, 1), acc)
+        out[j] = acc
 
 
 def rates(west, mid, east, h, lane, edge):
@@ -488,7 +509,7 @@
 
 def first_kernel(
     cells, meta, beam, u, own, in_a, in_b, in_z, in_d, in_h, gy_a, gy_b,
-    out_g, out_m, out_t, out_k, g, h, f, fh, u1, mass,
+    out_g, out_m, out_t, out_k, g, h, f, fh, u1, mass, skin,
 ):
     rows_x, reach = cells
     gx, gy, gz = meta[0], meta[1], meta[2]
@@ -498,7 +519,8 @@
     own_y = u.shape[2]
     tiles = own_y // SUBL
     size = own_y + 2 * SUBL
-    deep = (own.shape[0] - 4) // 2
+    half = SUBL // 2
+    sub = iota((SUBL, LANES), 0)
     zero = jnp.zeros((SUBL, LANES), F32)
 
     def side(k):
@@ -507,26 +529,27 @@
         return upper, lower
 
     wide = rows_x + 2 * reach - 2
-    for c in range(COMPS):
-        for x in range(-reach, rows_x + reach):
-            i = x + reach
+    outer = wide * COMPS // 2
+    for x in range(-reach, rows_x + reach):
+        i = x + reach
+        for c in range(COMPS):
             for y in range(tiles):
-                if x < 0:
-                    k = (c * reach + x + reach) * tiles + y
-                    value = jnp.where(even_x, in_b[k], in_a[k])
-                elif x < rows_x:
-                    value = u[c, x, y * SUBL : (y + 1) * SUBL, :]
-                else:
-                    k = (c * reach + x - rows_x) * tiles + y
-                    value = jnp.where(even_x, in_a[k], in_b[k])
-                g[c, i, y * SUBL : (y + 1) * SUBL, :] = value
-            if 0 < i < rows_x + 2 * reach - 1:
-                upper, lower = side(c * wide + i - 1)
+                value = row_tile(c, x, y, u, in_a, in_b, even_x)
+                g[c, i, y * SUBL : (y + 1) * SUBL, :] = zero if value is None else value
+            upper = lower = zero
+            if 0 < i < wide + 1:
+                upper, lower = side((i - 1) * COMPS // 2 + c // 2)
+                if c % 2:
+                    upper, lower = turn(upper, half, 0), turn(lower, half, 0)
+            if -1 <= x < rows_x + 1 and c in QUARTERS:
+                q = QUARTERS.index(c)
+                far_up, far_low = side(outer + x + 1)
+                far_up, far_low = turn(far_up, half - 2 * q, 0), turn(far_low, 2 - 2 * q, 0)
             else:
-                upper = lower = zero
-            g[c, i, own_y : own_y + SUBL, :] = upper
-            g[c, i, own_y + SUBL : size, :] = lower
-    base = deep + 4
+                far_up = far_low = zero
+            g[c, i, own_y : own_y + SUBL, :] = jnp.where(sub < half, upper, jnp.where(sub < half + 2, far_up, 0.0))
+            g[c, i, own_y + SUBL : size, :] = jnp.where(sub >= half, lower, jnp.where(sub >= half - 2, far_low, 0.0))
+    base = in_z.shape[0] - tiles
     packed = []
     for b in range(3):
         parts = []
@@ -537,7 +560,7 @@
                 parts.append(in_z[base + y])
             else:
                 parts.append(jnp.where(low_z, in_h[y], in_d[base + y]))
-        parts.extend(side(COMPS * wide + b))
+        parts.extend(side(outer + rows_x + 2 + b))
         packed.append(jnp.concatenate(parts, axis=0))
     for x in range(-reach, rows_x + reach):
         b, q = divmod(x + rows_x, rows_x)
@@ -546,30 +569,30 @@
     fine = advance(meta, g, h, f, fh, u1, rows_x, own_y)
 
     cols = LANES // 4
-    part_rows = 4 * SUBL
-    lane = iota((part_rows, LANES), 1)
-    tail = in_a.shape[0] - 4
-    top_at = gy_a.shape[0] - 4
-    uppers, lowers = zip(*[side(top_at + r) for r in range(4)])
-    uppers = jnp.concatenate(uppers, axis=0)
-    lowers = jnp.concatenate(lowers, axis=0)
+    per = LANES // cols
+    lane = iota((SUBL, LANES), 1)
+    sources = surface_sources(own, in_a, in_b, in_z, in_d, even_x, tiles)
+    count = len(sources) // 2
+    top_at = gy_a.shape[0] - len(sources) // per
     layers = []
-    for j in range(4):
-        high = jnp.where(even_x, in_a[tail + j], in_b[tail + j])
-        src = jnp.concatenate([own[2 * deep + j], in_z[deep + j], high, in_d[deep + j]], axis=0)
-        for q in range(4):
-            i = 4 * j + q
-            layers.append(
-                jnp.where(
+    for a in range(2):
+        for s in range(count):
+            src = sources[a * count + s]
+            upper, lower = side(top_at + (a * count + s) // per)
+            i = s % per
+            for q in range(per):
+                at = cols * q + SUBL * i
+                skin[s * per + q] = jnp.where(
                     lane < cols,
                     turn(src, -cols * q, 1),
                     jnp.where(
                         lane < cols + SUBL,
-                        turn(uppers, cols - SUBL * i, 1),
-                        jnp.where(lane >= LANES - SUBL, turn(lowers, LANES - SUBL - SUBL * i, 1), 0.0),
+                        turn(upper, cols - at, 1),
+                        jnp.where(lane >= LANES - SUBL, turn(lower, LANES - SUBL - at, 1), 0.0),
                     ),
                 )
-            )
+        for d in range(TOP):
+            layers.append(skin[:, d, :])
     t, k = layers[:TOP], layers[TOP:]
     t = top_heat(meta, beam, 0, t, k, fine, 2 * rows_x, cols)
     for d in range(TOP):
@@ -626,7 +649,7 @@
     lax.fori_loop(0, count, finish, 0)
 
 
-def last_kernel(cells, meta, beam, g, in_m, in_t, in_k, out_g, out_t, out_f, h, f, fh, u1, mass):
+def last_kernel(cells, meta, beam, g, in_m, in_t, in_k, out_g, out_t, out_f, h, f, fh, u1, mass, skin):
     rows_x, own_y = cells
     size = g.shape[2]
     n = g.shape[1]
@@ -638,9 +661,10 @@
     t = [in_t[d] for d in range(TOP)]
     k = [in_k[d] for d in range(TOP)]
     t = top_heat(meta, beam, SUBSTEPS, t, k, fine, 2 * rows_x, cols)
-    for d in range(SKIN):
-        out_t[d] = t[d][:SUBL]
-        out_f[d] = t[d][SUBL : 2 * SUBL]
+    for d in range(TOP):
+        skin[:, d, :] = t[d]
+    pack_skin(t, 0, cols, skin, out_t)
+    pack_skin(t, SUBL, cols, skin, out_f)
     mass[...] = vapor_mass(t[0], fine)
     mass_of = mass_rows(meta, h, mass, size, own_y)
 
@@ -693,14 +717,16 @@
     gx, gy, gz = (lax.axis_index(a) for a in ("gx", "gy", "gz"))
     meta = jnp.stack([gx, gy, gz, nx, ny, nz]).astype(jnp.int32)
     _, rows_x, own_y, _ = u.shape
+    t, m = jnp.transpose(t, (1, 2, 0)), jnp.transpose(m, (1, 2, 0))
+    rows, cols, depth = t.shape
     tiles = own_y // SUBL
-    deep = t.shape[0] * t.shape[2] // LANES
     block = (SUBL, LANES)
-    n_x = COMPS * REACH * tiles + 4
-    n_z = deep + 4 + tiles
+    n_top = 2 * rows * cols // LANES
+    n_x = slab_size(tiles) + n_top
+    n_z = 2 * SKIN * cols // SUBL + n_top + tiles
     msg_a, msg_b, msg_z, msg_d, msg_h, own = call(
         functools.partial(pack_kernel, (rows_x, REACH)),
-        [(n_x, *block), (n_x, *block), (n_z, *block), (n_z, *block), (tiles, *block), (2 * deep + 4, *block)],
+        [(n_x, *block), (n_x, *block), (n_z, *block), (n_z, *block), (tiles, *block), (n_top, *block)],
         count=4,
     )(meta, u, t, m, lev)
     in_a = lax.ppermute(msg_a, "gx", pairs(nx, 0))
@@ -708,10 +734,11 @@
     in_z = lax.ppermute(msg_z, "gz", pairs(nz, 0))
     in_d = lax.ppermute(msg_d, ("gx", "gz"), cross(nx, nz, True))
     in_h = lax.ppermute(msg_h, ("gx", "gz"), cross(nx, nz, False))
-    n_y = COMPS * (rows_x + 2 * REACH - 2) + 3 + deep // 2 + 4
+    wide = rows_x + 2 * REACH - 2
+    n_y = wide * COMPS // 2 + rows_x + 2 + 3 + rows + 2 * SKIN + n_top
     msg_a, msg_b = call(
-        functools.partial(relay_kernel, (rows_x, REACH)), [(n_y, *block), (n_y, *block)], count=7
-    )(meta, u, own, in_a, in_b, in_z, in_d, in_h)
+        functools.partial(relay_kernel, (rows_x, REACH)), [(n_y, *block), (n_y, *block)], count=9
+    )(meta, u, t, m, own, in_a, in_b, in_z, in_d, in_h)
     gy_a = lax.ppermute(msg_a, "gy", pairs(ny, 0))
     gy_b = lax.ppermute(msg_b, "gy", pairs(ny, 1))
 
@@ -731,39 +758,33 @@
             (n - 2, size, LANES),
             (COMPS, n - 4, size, LANES),
             (part_rows, LANES),
+            (part_rows, *block),
         ],
         scalars=2,
         count=9,
     )(meta, beam, u, own, in_a, in_b, in_z, in_d, in_h, gy_a, gy_b)
     in_m = lax.ppermute(msg_m, "gz", pairs(nz, 0))
+    part = (rows + 2 * SKIN, cols + SUBL, depth)
     (bulk,) = call(
-        bulk_kernel,
-        [t.shape],
-        scratch=[
-            (2, t.shape[0], 2 * SUBL, LANES),
-            (t.shape[0], 2 * SUBL, LANES),
-            (t.shape[0], 2 * SUBL, LANES),
-            (t.shape[0], 2 * SUBL, LANES),
-        ],
-        scalars=2,
-        count=5,
-    )(meta, beam, own, in_z, in_d, gy_a, gy_b)
+        bulk_kernel, [t.shape], scratch=[(2, *part), part, part, part, part], scalars=2, count=6
+    )(meta, beam, t, m, in_z, in_d, gy_a, gy_b)
     gas, mine, other = call(
         functools.partial(last_kernel, (rows_x, own_y)),
-        [u.shape, (SKIN, *block), (SKIN, *block)],
+        [u.shape, (n_top // 2, *block), (n_top // 2, *block)],
         scratch=[
             (n2, small, LANES),
             (COMPS, n2 - 2, small, LANES),
             (n2 - 2, small, LANES),
             (COMPS, n2 - 4, small, LANES),
             (part_rows, LANES),
+            (part_rows, *block),
         ],
         scalars=2,
         count=4,
     )(meta, beam, g2, in_m, top_t, top_k)
     given = lax.ppermute(other, "gz", pairs(nz, 0))
-    skin = jnp.where(gz == 0, mine, given)[:, :, : t.shape[2]]
-    return gas, lax.dynamic_update_slice(bulk, skin, (0, 0, 0))
+    (out,) = call(seal_kernel, [t.shape], count=3)(meta, bulk, mine, given)
+    return gas, jnp.transpose(out, (2, 0, 1))
 
 
 def solution(mesh):

time: 99.3 us -> 61.5 us (0.62)
  Pallas kernels: 63.5 us -> 27.8 us
  waiting for transfers between devices: 17.7 us -> 15.3 us
    pallas_call x2 -> x3, Pallas kernels: 47 us -> 11.8 us  [the longest x1 7.58 us: shards(): call(functools.partial(last_kernel, (rows_x, own_y)), [u.shape, (n_top //...]
    ppermute x1, waiting for transfers between devices: 8.09 us -> 6.05 us  [shards(): gy_b = lax.ppermute(msg_b, 'gy', pairs(ny, 1))]
    ppermute x1, waiting for transfers between devices: 1.19 us -> 0.13 us  [shards(): in_d = lax.ppermute(msg_d, ('gx', 'gz'), cross(nx, nz, True))]
    unnamed x12 -> x17, local copies, waits for them, and re-layouts: 3.03 us -> 3.5 us
  transfers between devices with their start and end apart: 9 -> 9, of which waited for: 4 -> 5; matrix products, arithmetic and copies ran while one was open for 0% -> 0% of each run, Pallas kernels for 40% -> 5%
where the time goes in v2:
time: 61.5 us; the launch traced here: 61 us
  Pallas kernels  27.8 us (45%)
  waiting for transfers between devices  15.3 us (25%)
  starting transfers between devices  13.5 us (22%)
  local copies, waits for them, and re-layouts  3.58 us (6%)
  between operations  0.76 us (1%)
    pallas_call x1, Pallas kernels, shards(): call(functools.partial(first_kernel, (rows_x, REACH)), [(COMPS, n2, small...  14.1 us
    pallas_call x1, Pallas kernels, shards(): call(functools.partial(last_kernel, (rows_x, own_y)), [u.shape, (n_top //...  7.58 us
    ppermute x1, waiting for transfers between devices, shards(): gy_b = lax.ppermute(msg_b, 'gy', pairs(ny, 1))  6.05 us
    ppermute x1, waiting for transfers between devices, shards(): in_h = lax.ppermute(msg_h, ('gx', 'gz'), cross(nx, nz, False))  4.6 us
    ppermute x1, starting transfers between devices, shards(): in_d = lax.ppermute(msg_d, ('gx', 'gz'), cross(nx, nz, True))  3.85 us
    ppermute x1, waiting for transfers between devices, shards(): in_m = lax.ppermute(msg_m, 'gz', pairs(nz, 0))  3.81 us
    unnamed x17, local copies, waits for them, and re-layouts  3.5 us
    pallas_call x1, Pallas kernels, shards(): call(bulk_kernel, [t.shape], scratch=[(2, *part), part, part, part, part]...  2.92 us
  transfers between devices with their start and end apart: 9, of which 5 were waited for; matrix products, arithmetic and copies ran while one was open for 0% of the time, Pallas kernels for 5%

profile of v2, /device:TPU:18, one launch (start us, length us, event | category | flops | bytes accessed | tf_op | source)
XLA Modules:
  0.0 61.0 jit_solution(6958525083851658253)
XLA Ops:
  0.7 0.1 stack.15.meta
  0.7 0.6 copy-done.6
  1.3 1.0 %copy-done = f32[6,8,16,128]{3,2,1,0:T(8,128)S(1)} copy-done((f32[6,8,16,128]{3,2,1,0:T(8,128)S(1)}, f32[6,8,16,128]{3,2,1,0:T(8,128)}, u32[]{:S(2)}) %copy-start) | copy-done | bytes 393240
  2.3 0.9 %copy-done.2 = f32[128,8,32]{0,2,1:T(8,128)S(1)} copy-done((f32[128,8,32]{0,2,1:T(8,128)S(1)}, f32[128,8,32]{0,2,1:T(8,128)}, u32[]{:S(2)}) %copy-start.2) | copy-done | bytes 131096
  3.2 0.9 %copy-done.4 = s32[128,8,32]{0,2,1:T(8,128)S(1)} copy-done((s32[128,8,32]{0,2,1:T(8,128)S(1)}, s32[128,8,32]{0,2,1:T(8,128)}, u32[]{:S(2)}) %copy-start.4) | copy-done | bytes 131096
  4.1 1.1 %shard_map.68 = (f32[64,8,128]{2,1,0:T(8,128)S(1)}, f32[64,8,128]{2,1,0:T(8,128)S(1)}, f32[38,8,128]{2,1,0:T(8,128)S(1)}, f32[38,8,128]{2,1,0:T(8,128)S(1)}, f32...) custom-call(s32[6]{0:T(128)S(1)} %stack.15.meta, f32[6,8,16,128]{3,2,1,0:T(8,128)S(1)} %copy-done, ...), custom_call_target="tpu_custom_call" | custom-call | tf_op jit(solution)/shard_map/pallas_call | solution.py:727
  5.2 1.6 %collective-permute-start = (f32[64,8,128]{2,1,0:T(8,128)S(1)}, f32[64,8,128]{2,1,0:T(8,128)S(1)}, u32[]{:S(2)}, u32[]{:S(2)}) collective-permute-start(f32[64,8,128]{2,1,0:T(8,128)S(1)} %get-tuple-element.18), channel_id=1, source_target_pairs={{0,8},{8,0},{16,24},{24,16},{1,9},{9,1},{17,25},{25,17},{2,10},{10... | collective-permute-start | bytes 786440 | tf_op jit(solution)/shard_map/ppermute | solution.py:732
  6.9 1.9 %collective-permute-start.1 = (f32[64,8,128]{2,1,0:T(8,128)S(1)}, f32[64,8,128]{2,1,0:T(8,128)S(1)}, u32[]{:S(2)}, u32[]{:S(2)}) collective-permute-start(f32[64,8,128]{2,1,0:T(8,128)S(1)} %get-tuple-element.19), channel_id=1, source_target_pairs={{8,16},{16,8},{9,17},{17,9},{10,18},{18,10},{11,19},{19,11},{12,20... | collective-permute-start | bytes 786440 | tf_op jit(solution)/shard_map/ppermute | solution.py:733
  8.8 1.6 %collective-permute-start.2 = (f32[38,8,128]{2,1,0:T(8,128)S(1)}, f32[38,8,128]{2,1,0:T(8,128)S(1)}, u32[]{:S(2)}, u32[]{:S(2)}) collective-permute-start(f32[38,8,128]{2,1,0:T(8,128)S(1)} %get-tuple-element.20), channel_id=1, source_target_pairs={{0,1},{1,0},{2,3},{3,2},{4,5},{5,4},{6,7},{7,6},{8,9},{9,8},{10,11... | collective-permute-start | bytes 466952 | tf_op jit(solution)/shard_map/ppermute | solution.py:734
  10.4 3.9 %collective-permute-start.3 = (f32[38,8,128]{2,1,0:T(8,128)S(1)}, f32[38,8,128]{2,1,0:T(8,128)S(1)}, u32[]{:S(2)}, u32[]{:S(2)}) collective-permute-start(f32[38,8,128]{2,1,0:T(8,128)S(1)} %get-tuple-element.21), channel_id=1, source_target_pairs={{1,8},{8,1},{9,16},{16,9},{17,24},{24,17},{3,10},{10,3},{11,18},{1... | collective-permute-start | bytes 466952 | tf_op jit(solution)/shard_map/ppermute | solution.py:735
  14.2 1.9 %collective-permute-start.4 = (f32[2,8,128]{2,1,0:T(8,128)S(1)}, f32[2,8,128]{2,1,0:T(8,128)S(1)}, u32[]{:S(2)}, u32[]{:S(2)}) collective-permute-start(f32[2,8,128]{2,1,0:T(8,128)S(1)} %get-tuple-element.22), channel_id=1, source_target_pairs={{0,9},{9,0},{8,17},{17,8},{16,25},{25,16},{2,11},{11,2},{10,19},{1... | collective-permute-start | bytes 24584 | tf_op jit(solution)/shard_map/ppermute | solution.py:736
  16.2 4.6 %collective-permute-done.4.in_h = f32[2,8,128]{2,1,0:T(8,128)S(1)} collective-permute-done((f32[2,8,128]{2,1,0:T(8,128)S(1)}, f32[2,8,128]{2,1,0:T(8,128)S(1)}, u32[]{:S(2)}, u32[]{:S(2)}) %collective-permute-start.4) | collective-permute-done | bytes 8224 | tf_op jit(solution)/shard_map/ppermute | solution.py:736
  20.8 0.1 collective-permute-done.3.in_d
  20.9 0.7 %shard_map.69 = (f32[87,8,128]{2,1,0:T(8,128)S(1)}, f32[87,8,128]{2,1,0:T(8,128)S(1)}) custom-call(s32[6]{0:T(128)S(1)} %stack.15.meta, f32[6,8,16,128]{3,2,1,0:T(8,128)S(1)} %copy-done, f32[8,32,128]{2,1,0:T(8,128)S(1)} %bitcast.7, s32[8,32,128]{2,1,0:T(8,128)S(1)} %bitcast.10, f32[4,8,128]{2,1,0:T(8,128)S(1)} %get-tuple-element.17.own, ...), custom_call_target="tpu_custom_call" | custom-call | tf_op jit(solution)/shard_map/pallas_call | solution.py:739
  21.7 0.1 collective-permute-start.5
  21.8 2.5 %collective-permute-start.6 = (f32[87,8,128]{2,1,0:T(8,128)S(1)}, f32[87,8,128]{2,1,0:T(8,128)S(1)}, u32[]{:S(2)}, u32[]{:S(2)}) collective-permute-start(f32[87,8,128]{2,1,0:T(8,128)S(1)} %get-tuple-element.24), channel_id=1, source_target_pairs={{2,4},{4,2},{3,5},{5,3},{10,12},{12,10},{11,13},{13,11},{18,20},{2... | collective-permute-start | bytes 1069064 | tf_op jit(solution)/shard_map/ppermute | solution.py:743
  24.3 0.1 copy.8.beam
  24.4 6.1 %collective-permute-done.6.gy_b = f32[87,8,128]{2,1,0:T(8,128)S(1)} collective-permute-done((f32[87,8,128]{2,1,0:T(8,128)S(1)}, f32[87,8,128]{2,1,0:T(8,128)S(1)}, u32[]{:S(2)}, u32[]{:S(2)}) %collective-permute-start.6) | collective-permute-done | bytes 356384 | tf_op jit(solution)/shard_map/ppermute | solution.py:743
  30.5 14.1 %shard_map.70 = (f32[6,14,24,128]{3,2,1,0:T(8,128)S(1)}, f32[2,24,128]{2,1,0:T(8,128)S(1)}, f32[8,32,128]{2,1,0:T(8,128)S(1)}, f32[8,32,128]{2,1,0:T(8,128)S(1)}) custom-call(s32[6]{0:T(128)S(1)} %stack.15.meta, s32[4,2]{1,0:T(4,128)S(1)} %copy.8.beam, f32[6,8,16,128]{3,2,1,0:T(8,128)S(1)} %copy-done.1, f32[4,8,128]{2,1,0:T(8,128)S(1)} %get-tuple-element.17.own, ...), custom_call_target="tpu_custom_call" | custom-call | tf_op jit(solution)/shard_map/pallas_call | solution.py:751
  44.6 3.8 %collective-permute-done.7.in_m = f32[2,24,128]{2,1,0:T(8,128)S(1)} collective-permute-done((f32[2,24,128]{2,1,0:T(8,128)S(1)}, f32[2,24,128]{2,1,0:T(8,128)S(1)}, u32[]{:S(2)}, u32[]{:S(2)}) %collective-permute-start.7) | collective-permute-done | bytes 24608 | tf_op jit(solution)/shard_map/ppermute | solution.py:766
  48.4 7.6 %shard_map.71 = (f32[6,8,16,128]{3,2,1,0:T(8,128)}, f32[2,8,128]{2,1,0:T(8,128)S(1)}, f32[2,8,128]{2,1,0:T(8,128)S(1)}) custom-call(s32[6]{0:T(128)S(1)} %stack.15.meta, s32[4,2]{1,0:T(4,128)S(1)} %copy.8.beam, f32[6,14,24,128]{3,2,1,0:T(8,128)S(1)} %get-tuple-element.25.g, f32[2,24,128]{2,1,0:T(8,128)S(1)} %collective-permute-done.7.in_m, ...), custom_call_target="tpu_custom_call" | custom-call | tf_op jit(solution)/shard_map/pallas_call | solution.py:771
  56.0 2.9 %shard_map.72.bulk = f32[8,32,128]{2,1,0:T(8,128)S(1)} custom-call(s32[6]{0:T(128)S(1)} %stack.15.meta, s32[4,2]{1,0:T(4,128)S(1)} %copy.8.beam, f32[8,32,128]{2,1,0:T(8,128)S(1)} %bitcast.8, s32[8,32,128]{2,1,0:T(8,128)S(1)} %bitcast.11, f32[38,8,128]{2,1,0:T(8,128)S(1)} %collective-permute-done.2.in_z, f32[38,8,128]{2,1,0:T(8,128)S(1)} %collective-permute-done.3.in_d, ...), custom_call_target="tpu_custom_call" | custom-call | tf_op jit(solution)/shard_map/pallas_call | solution.py:768
  59.0 0.7 %collective-permute-done.8.given = f32[2,8,128]{2,1,0:T(8,128)S(1)} collective-permute-done((f32[2,8,128]{2,1,0:T(8,128)S(1)}, f32[2,8,128]{2,1,0:T(8,128)S(1)}, u32[]{:S(2)}, u32[]{:S(2)}) %collective-permute-start.8) | collective-permute-done | bytes 8224 | tf_op jit(solution)/shard_map/ppermute | solution.py:785
  59.7 1.3 %shard_map.73 = f32[8,32,128]{2,1,0:T(8,128)} custom-call(s32[6]{0:T(128)S(1)} %stack.15.meta, f32[8,32,128]{2,1,0:T(8,128)S(1)} %shard_map.72.bulk, f32[2,8,128]{2,1,0:T(8,128)S(1)} %get-tuple-element.30.mine, f32[2,8,128]{2,1,0:T(8,128)S(1)} %collective-permute-done.8.given), custom_call_target="tpu_custom_call" | custom-call | tf_op jit(solution)/shard_map/pallas_call | solution.py:786
  (19 shorter events, 0.1 us)
Async XLA Ops:
  0.6 0.7 %copy-start.6 = (s32[8,16]{1,0:T(8,128)S(1)}, s32[8,16]{1,0:T(8,128)}, u32[]{:S(2)}) copy-start(s32[8,16]{1,0:T(8,128)} %lev.1) | copy-start | bytes 1540
  1.3 1.0 %copy-start = (f32[6,8,16,128]{3,2,1,0:T(8,128)S(1)}, f32[6,8,16,128]{3,2,1,0:T(8,128)}, u32[]{:S(2)}) copy-start(f32[6,8,16,128]{3,2,1,0:T(8,128)} %u.5) | copy-start | bytes 1179652
  2.3 0.9 %copy-start.2 = (f32[128,8,32]{0,2,1:T(8,128)S(1)}, f32[128,8,32]{0,2,1:T(8,128)}, u32[]{:S(2)}) copy-start(f32[128,8,32]{0,2,1:T(8,128)} %param.6) | copy-start | bytes 393220
  3.2 0.9 %copy-start.4 = (s32[128,8,32]{0,2,1:T(8,128)S(1)}, s32[128,8,32]{0,2,1:T(8,128)}, u32[]{:S(2)}) copy-start(s32[128,8,32]{0,2,1:T(8,128)} %param.7) | copy-start | bytes 393220
  5.2 15.7 %collective-permute-start = (f32[64,8,128]{2,1,0:T(8,128)S(1)}, f32[64,8,128]{2,1,0:T(8,128)S(1)}, u32[]{:S(2)}, u32[]{:S(2)}) collective-permute-start(f32[64,8,128]{2,1,0:T(8,128)S(1)} %get-tuple-element.18), channel_id=1, source_target_pairs={{0,8},{8,0},{16,24},{24,16},{1,9},{9,1},{17,25},{25,17},{2,10},{10... | collective-permute-start | bytes 786440 | tf_op jit(solution)/shard_map/ppermute | solution.py:732
  6.9 14.0 %collective-permute-start.1 = (f32[64,8,128]{2,1,0:T(8,128)S(1)}, f32[64,8,128]{2,1,0:T(8,128)S(1)}, u32[]{:S(2)}, u32[]{:S(2)}) collective-permute-start(f32[64,8,128]{2,1,0:T(8,128)S(1)} %get-tuple-element.19), channel_id=1, source_target_pairs={{8,16},{16,8},{9,17},{17,9},{10,18},{18,10},{11,19},{19,11},{12,20... | collective-permute-start | bytes 786440 | tf_op jit(solution)/shard_map/ppermute | solution.py:733
  8.8 12.0 %collective-permute-start.2 = (f32[38,8,128]{2,1,0:T(8,128)S(1)}, f32[38,8,128]{2,1,0:T(8,128)S(1)}, u32[]{:S(2)}, u32[]{:S(2)}) collective-permute-start(f32[38,8,128]{2,1,0:T(8,128)S(1)} %get-tuple-element.20), channel_id=1, source_target_pairs={{0,1},{1,0},{2,3},{3,2},{4,5},{5,4},{6,7},{7,6},{8,9},{9,8},{10,11... | collective-permute-start | bytes 466952 | tf_op jit(solution)/shard_map/ppermute | solution.py:734
  10.4 10.5 %collective-permute-start.3 = (f32[38,8,128]{2,1,0:T(8,128)S(1)}, f32[38,8,128]{2,1,0:T(8,128)S(1)}, u32[]{:S(2)}, u32[]{:S(2)}) collective-permute-start(f32[38,8,128]{2,1,0:T(8,128)S(1)} %get-tuple-element.21), channel_id=1, source_target_pairs={{1,8},{8,1},{9,16},{16,9},{17,24},{24,17},{3,10},{10,3},{11,18},{1... | collective-permute-start | bytes 466952 | tf_op jit(solution)/shard_map/ppermute | solution.py:735
  14.2 6.5 %collective-permute-start.4 = (f32[2,8,128]{2,1,0:T(8,128)S(1)}, f32[2,8,128]{2,1,0:T(8,128)S(1)}, u32[]{:S(2)}, u32[]{:S(2)}) collective-permute-start(f32[2,8,128]{2,1,0:T(8,128)S(1)} %get-tuple-element.22), channel_id=1, source_target_pairs={{0,9},{9,0},{8,17},{17,8},{16,25},{25,16},{2,11},{11,2},{10,19},{1... | collective-permute-start | bytes 24584 | tf_op jit(solution)/shard_map/ppermute | solution.py:736
  20.9 9.6 %copy-start.1 = (f32[6,8,16,128]{3,2,1,0:T(8,128)S(1)}, f32[6,8,16,128]{3,2,1,0:T(8,128)}, u32[]{:S(2)}) copy-start(f32[6,8,16,128]{3,2,1,0:T(8,128)} %u.5) | copy-start | bytes 1179652
  21.7 2.6 %copy-start.7 = (s32[4,2]{0,1:T(2,128)S(1)}, s32[4,2]{0,1:T(2,128)}, u32[]{:S(2)}) copy-start(s32[4,2]{0,1:T(2,128)} %param.9) | copy-start | bytes 100
  21.7 2.7 %collective-permute-start.5 = (f32[87,8,128]{2,1,0:T(8,128)S(1)}, f32[87,8,128]{2,1,0:T(8,128)S(1)}, u32[]{:S(2)}, u32[]{:S(2)}) collective-permute-start(f32[87,8,128]{2,1,0:T(8,128)S(1)} %get-tuple-element.23), channel_id=1, source_target_pairs={{0,2},{2,0},{4,6},{6,4},{1,3},{3,1},{5,7},{7,5},{8,10},{10,8},{12,... | collective-permute-start | bytes 1069064 | tf_op jit(solution)/shard_map/ppermute | solution.py:742
  21.8 8.7 %collective-permute-start.6 = (f32[87,8,128]{2,1,0:T(8,128)S(1)}, f32[87,8,128]{2,1,0:T(8,128)S(1)}, u32[]{:S(2)}, u32[]{:S(2)}) collective-permute-start(f32[87,8,128]{2,1,0:T(8,128)S(1)} %get-tuple-element.24), channel_id=1, source_target_pairs={{2,4},{4,2},{3,5},{5,3},{10,12},{12,10},{11,13},{13,11},{18,20},{2... | collective-permute-start | bytes 1069064 | tf_op jit(solution)/shard_map/ppermute | solution.py:743
  44.6 3.8 %collective-permute-start.7 = (f32[2,24,128]{2,1,0:T(8,128)S(1)}, f32[2,24,128]{2,1,0:T(8,128)S(1)}, u32[]{:S(2)}, u32[]{:S(2)}) collective-permute-start(f32[2,24,128]{2,1,0:T(8,128)S(1)} %get-tuple-element.26), channel_id=1, source_target_pairs={{0,1},{1,0},{2,3},{3,2},{4,5},{5,4},{6,7},{7,6},{8,9},{9,8},{10,11... | collective-permute-start | bytes 73736 | tf_op jit(solution)/shard_map/ppermute | solution.py:766
  48.4 7.6 %copy-start.3 = (f32[128,8,32]{0,2,1:T(8,128)S(1)}, f32[128,8,32]{0,2,1:T(8,128)}, u32[]{:S(2)}) copy-start(f32[128,8,32]{0,2,1:T(8,128)} %param.6) | copy-start | bytes 393220
  48.4 7.6 %copy-start.5 = (s32[128,8,32]{0,2,1:T(8,128)S(1)}, s32[128,8,32]{0,2,1:T(8,128)}, u32[]{:S(2)}) copy-start(s32[128,8,32]{0,2,1:T(8,128)} %param.7) | copy-start | bytes 393220
  56.0 3.7 %collective-permute-start.8 = (f32[2,8,128]{2,1,0:T(8,128)S(1)}, f32[2,8,128]{2,1,0:T(8,128)S(1)}, u32[]{:S(2)}, u32[]{:S(2)}) collective-permute-start(f32[2,8,128]{2,1,0:T(8,128)S(1)} %get-tuple-element.31), channel_id=1, source_target_pairs={{0,1},{1,0},{2,3},{3,2},{4,5},{5,4},{6,7},{7,6},{8,9},{9,8},{10,11... | collective-permute-start | bytes 24584 | tf_op jit(solution)/shard_map/ppermute | solution.py:785

commit v3 on v2

--- a/solution.py
+++ b/solution.py
@@ -38,8 +38,7 @@
 SKIN = 4
 TOP = 8
 GROUP = 16
-LEVEL = 6
-NEXT = 8
+LEVEL = 2 * COMPS
 
 
 def iota(shape, axis):
@@ -63,19 +62,18 @@
     return jnp.maximum(x, 0.0) + jnp.log1p(jnp.exp(-jnp.abs(x)))
 
 
-def edges(gz):
-    return jnp.where(gz == 0, LANES - 1, 0), jnp.where(gz == 0, LANES - 2, 1)
-
-
-def lane_turn(value, amount):
-    return pltpu.roll(value, lax.rem(amount + 2 * LANES, LANES), 1)
-
-
-def pack_heights(rows, base, lane, edge, behind, acc):
+def pack_heights(rows, base, lane, low_z, acc):
+    more = jnp.where(low_z, 2, 0)
     for c, row in enumerate(rows):
-        acc = jnp.where(lane == base + c, lane_turn(row, base + c - edge), acc)
-        acc = jnp.where(lane == base + NEXT + c, lane_turn(row, base + NEXT + c - behind), acc)
+        acc = jnp.where((lane & -2) == base + 2 * c, turn(row, base + 2 * c + more, 1), acc)
     return acc
+
+
+def unpack_heights(packed, base, low_z, h0, h1, i):
+    here = turn(packed, -base, 1)
+    other = turn(packed, -base - 1, 1)
+    h0[i] = jnp.where(low_z, here, other)
+    h1[i] = jnp.where(low_z, other, here)
 
 
 DEEP_5 = (2, 3, 4, 5)
@@ -155,16 +153,15 @@
         out_a[top_a + j] = top
         out_b[top_a + j] = top
     n += 2 * rows // per
-    edge, behind = edges(gz)
     size = u.shape[2]
     lane = iota((size, LANES), 1)
     eye = iota((size, size), 0) == iota((size, size), 1)
     levels = lev[...].astype(F32)
     acc = jnp.zeros((size, LANES), F32)
     for x in range(rows_x):
-        acc = pack_heights([u[c, x] for c in range(COMPS)], x * GROUP, lane, edge, behind, acc)
+        acc = pack_heights([u[c, x] for c in range(COMPS)], x * GROUP, lane, low_z, acc)
         level = jnp.sum(jnp.where(eye, levels[x : x + 1, :], 0.0), axis=1, keepdims=True)
-        acc = jnp.where(lane == x * GROUP + LEVEL, level, acc)
+        acc = jnp.where((lane & -2) == x * GROUP + LEVEL, level, acc)
     for y in range(tiles):
         part = acc[y * SUBL : (y + 1) * SUBL]
         out_h[y] = part
@@ -213,8 +210,8 @@
         hi = lo = zero
         for q, c in enumerate(QUARTERS):
             a, b = both(c, x)
-            hi = jnp.where(sub // 2 == q, turn(a, 2 * q - 2, 0), hi)
-            lo = jnp.where(sub // 2 == q, turn(b, 2 * q - half, 0), lo)
+            hi = jnp.where((sub & -2) == 2 * q, turn(a, 2 * q - 2, 0), hi)
+            lo = jnp.where((sub & -2) == 2 * q, turn(b, 2 * q - half, 0), lo)
         put(n, hi, lo)
         n += 1
     base = in_z.shape[0] - tiles
@@ -352,110 +349,205 @@
         out[j] = acc
 
 
-def rates(west, mid, east, h, lane, edge):
-    size = mid[0].shape[0]
-    out_lap, sx, sy, sz = [], {}, {}, []
+def split(value):
+    high = value.astype(jnp.bfloat16)
+    rest = (value - high.astype(F32)).astype(jnp.bfloat16)
+    return jnp.concatenate([high, rest], axis=1)
+
+
+def height_matrix():
+    shape = (2 * LANES, 2 * LANES)
+    k = iota(shape, 0) & (LANES - 1)
+    j = iota(shape, 1)
+    above = jnp.where(k == (j & (LANES - 1)) + 1, 1.0, 0.0)
+    below = jnp.where(k == (j & (LANES - 1)) - 1, 1.0, 0.0)
+    return (above + jnp.where(j < LANES, -below, below)).astype(jnp.bfloat16)
+
+
+def height_terms(ref, first, last, matrix, diff, total):
+    size = ref.shape[2]
     for c in range(COMPS):
-        north = turn(mid[c], -1, 0)
-        south = turn(mid[c], 1, 0)
-        halo = jnp.where(lane == edge, lane_turn(h, edge - c), 0.0)
-        upper = jnp.where(lane == LANES - 1, halo, turn(mid[c], -1, 1))
-        lower = jnp.where(lane == 0, halo, turn(mid[c], 1, 1))
-        if c in (2, 5):
-            sx[c] = 0.5 * (east[c] - west[c])
-        if c in (3, 5):
-            sy[c] = 0.5 * (north - south)
-        sz.append(0.5 * (upper - lower))
-        out_lap.append(east[c] + west[c] + north + south + upper + lower - 6.0 * mid[c])
-    spread = sx[2] + sy[3] + sz[4]
-    coupled = [-VAPOR_LOAD * spread, -AMBIENT_LOAD * spread, -sx[5], -sy[5], -sz[5], -STIFFNESS * spread]
-    return [coupled[c] - DRIFT_SPEED * sz[c] + VISCOSITY[c] * out_lap[c] for c in range(COMPS)]
-
-
-def halo_rates(h_west, h, h_east, mid, lane, edge, low_z):
-    touch = jnp.zeros_like(h)
+        rows = ref[c, first:last].reshape((last - first) * size, LANES)
+        both = jnp.dot(split(rows), matrix, preferred_element_type=F32)
+        diff[c, first:last] = both[:, :LANES].reshape(last - first, size, LANES)
+        total[c, first:last] = both[:, LANES:].reshape(last - first, size, LANES)
+
+
+def cut_weights(size, low_z):
+    lane = iota((size, LANES), 1)
+    up = (lane == LANES - 1) & low_z
+    down = (lane == 0) & jnp.logical_not(low_z)
+    sign = jnp.where(up, 1.0, jnp.where(down, -1.0, 0.0))
+    return sign, jnp.abs(sign)
+
+
+def stepped(comps, ref, i, diff, total, h, cut, scale, start, size):
+    sign, mark = cut
+    half = 0.5 * scale * GAS_STEP
+    span = pl.ds(start, size)
+
+    def dx(c):
+        return ref[c, i + 1, span, :] - ref[c, i - 1, span, :]
+
+    def dy(c):
+        return ref[c, i, pl.ds(start + 1, size), :] - ref[c, i, pl.ds(start - 1, size), :]
+
+    def dz(c):
+        return diff[c, i, span, :] + sign * h[i, span, 2 * c : 2 * c + 1]
+
+    spread = half * (dx(2) + dy(3) + dz(4))
+    out = {}
+    for c in comps:
+        v = VISCOSITY[c]
+        side = scale * GAS_STEP * v
+        drift = 0.5 * DRIFT_SPEED * scale * GAS_STEP
+        sides = (ref[c, i + 1, span, :] + ref[c, i - 1, span, :]) + (
+            ref[c, i, pl.ds(start + 1, size), :] + ref[c, i, pl.ds(start - 1, size), :]
+        )
+        across = h[i, span, 2 * c : 2 * c + 1]
+        new = (
+            scale * (1.0 - 6.0 * GAS_STEP * v) * ref[c, i, span, :]
+            + side * (sides + total[c, i, span, :])
+            - drift * diff[c, i, span, :]
+            + (side * mark - drift * sign) * across
+        )
+        if c == 2:
+            new = new - half * dx(5)
+        elif c == 3:
+            new = new - half * dy(5)
+        elif c == 4:
+            new = new - half * dz(5)
+        else:
+            new = new - {0: VAPOR_LOAD, 1: AMBIENT_LOAD, 5: STIFFNESS}[c] * spread
+        out[c] = new
+    return out
+
+
+def by_comp(lane, values):
+    out = jnp.full(lane.shape, values[-1], F32)
+    for c, v in enumerate(values[:-1]):
+        out = jnp.where(lane == 2 * c, v, out)
+    return out
+
+
+def couple_matrix():
+    shape = (6 * LANES, LANES)
+    k = iota(shape, 0)
+    j = iota(shape, 1)
+    axis = k // (2 * LANES)
+    lane = k & (LANES - 1)
+    spread = (lane == 4 + 2 * axis) & ((j == 0) | (j == 2) | (j == 10))
+    slope = (lane == 10) & (j == 4 + 2 * axis)
+    return jnp.where(spread | slope, 1.0, 0.0).astype(jnp.bfloat16)
+
+
+def halo_stepped(h0, h1, g, low_z, mask_of, out):
+    n, size = h0.shape[0], h0.shape[1]
+    rows = (n - 2) * size
+    lane = iota((1, LANES), 1)
+    more = jnp.where(low_z, 1, 0)
+    flat_lane = iota((rows, LANES), 1)
+    touch = jnp.zeros((rows, LANES), F32)
     for c in range(COMPS):
-        touch = jnp.where(lane == c, lane_turn(mid[c], c - edge), touch)
-    after = turn(h, -NEXT, 1)
-    north = turn(h, -1, 0)
-    south = turn(h, 1, 0)
-    sx = 0.5 * (h_east - h_west)
-    sy = 0.5 * (north - south)
-    sz = jnp.where(low_z, 0.5, -0.5) * (after - touch)
-    lap = h_east + h_west + north + south + after + touch - 6.0 * h
-    q = jnp.where(lane == 2, sx, jnp.where(lane == 3, sy, jnp.where(lane == 4, sz, 0.0)))
-    s = q + turn(q, -1, 1) + turn(q, -2, 1)
-    coupled = jnp.where(
-        lane == 0,
-        -VAPOR_LOAD * turn(s, -2, 1),
-        jnp.where(
-            lane == 1,
-            -AMBIENT_LOAD * turn(s, -1, 1),
-            jnp.where(
-                lane == 2,
-                -turn(sx, -3, 1),
-                jnp.where(
-                    lane == 3,
-                    -turn(sy, -2, 1),
-                    jnp.where(lane == 4, -turn(sz, -1, 1), -STIFFNESS * turn(s, 3, 1)),
-                ),
-            ),
-        ),
+        own = g[c, 1 : n - 1].reshape(rows, LANES)
+        touch = jnp.where(flat_lane == 2 * c, turn(own, 2 * c + more, 1), touch)
+    mid = h0[1 : n - 1].reshape(rows, LANES)
+    east = h0[2:n].reshape(rows, LANES)
+    west = h0[0 : n - 2].reshape(rows, LANES)
+    north = turn(mid, -1, 0)
+    south = turn(mid, 1, 0)
+    behind = h1[1 : n - 1].reshape(rows, LANES)
+    slopes = [east - west, north - south, jnp.where(low_z, 1.0, -1.0) * (behind - touch)]
+    coupled = jnp.dot(
+        jnp.concatenate([split(v) for v in slopes], axis=1), couple_matrix(), preferred_element_type=F32
     )
-    visc = jnp.where(
-        lane == 0, VISCOSITY[0], jnp.where(lane == 1, VISCOSITY[1], jnp.where(lane == 5, VISCOSITY[5], VISCOSITY[2]))
+    up = by_comp(lane, [GAS_STEP * (v - 0.5 * DRIFT_SPEED) for v in VISCOSITY])
+    down = by_comp(lane, [GAS_STEP * (v + 0.5 * DRIFT_SPEED) for v in VISCOSITY])
+    half = 0.5 * GAS_STEP
+    pull = by_comp(lane, [-half * VAPOR_LOAD, -half * AMBIENT_LOAD, -half, -half, -half, -half * STIFFNESS])
+    new = (
+        by_comp(lane, [1.0 - 6.0 * GAS_STEP * v for v in VISCOSITY]) * mid
+        + by_comp(lane, [GAS_STEP * v for v in VISCOSITY]) * ((east + west) + (north + south))
+        + jnp.where(low_z, up, down) * behind
+        + jnp.where(low_z, down, up) * touch
+        + pull * coupled
     )
-    return coupled - DRIFT_SPEED * sz + visc * lap
-
-
-def advance(meta, g, h, f, fh, u1, own_x, own_y):
+    for i in range(1, n - 1):
+        out[i - 1] = turn(new[(i - 1) * size : i * size] * mask_of(i, 0, size), -1, 0)
+
+
+def advance(meta, g, h0, h1, f, fh, diff, total, own_x, own_y, store):
     n, size = g.shape[1], g.shape[2]
     gx, gy, gz = meta[0], meta[1], meta[2]
     low_z = gz == 0
-    edge, _ = edges(gz)
-    lane = iota((size, LANES), 1)
-    y_l = wrapped(iota((size, LANES), 0), own_y, size)
-    y_g = gy * own_y + y_l
-    inside_y = jnp.where((y_g >= 0) & (y_g < meta[4] * own_y), 1.0, 0.0)
     before = (n - own_x) // 2
-
-    def inside(i):
+    before_y = (size - own_y) // 2
+    reach = before - 2
+
+    def mask_of(i, start, count):
         x_g = gx * own_x + i - before
         ok = (x_g >= 0) & (x_g < meta[3] * own_x)
-        return inside_y * jnp.where(ok, 1.0, 0.0)
-
-    def one(i, carry):
-        mid = [g[c, i] for c in range(COMPS)]
-        rate = rates([g[c, i - 1] for c in range(COMPS)], mid, [g[c, i + 1] for c in range(COMPS)], h[i], lane, edge)
-        m = inside(i)
-        for c in range(COMPS):
-            f[c, i - 1] = (mid[c] + GAS_STEP * rate[c]) * m
-        hr = halo_rates(h[i - 1], h[i], h[i + 1], mid, lane, edge, low_z)
-        fh[i - 1] = (h[i] + GAS_STEP * hr) * m
-        return carry
-
-    lax.fori_loop(1, n - 1, one, 0)
-
-    part_rows = 4 * SUBL
-    col_y = lax.div(wrapped(iota((size, LANES), 1), 2 * own_y, LANES) + LANES, 2) - LANES // 2
-    spread_y = jnp.where(col_y == y_l, 1.0, 0.0)
+        y_g = gy * own_y + iota((count, LANES), 0) + start - before_y
+        return jnp.where((y_g >= 0) & (y_g < meta[4] * own_y) & ok, 1.0, 0.0)
+
+    matrix = height_matrix()
+    halo_stepped(h0, h1, g, low_z, mask_of, fh)
+    height_terms(g, 1, n - 1, matrix, diff, total)
+    everything = tuple(range(COMPS))
+
+    def one(comps):
+        def body(i, carry):
+            count = size - 2
+            new = stepped(comps, g, i, diff, total, h0, cut_weights(count, low_z), 1.0, 1, count)
+            m = mask_of(i, 1, count)
+            for c in comps:
+                f[c, i - 1, :count, :] = new[c] * m
+            return carry
+
+        return body
+
+    lax.fori_loop(2, n - 2, one(everything), 0, unroll=2)
+    for i in (1, n - 2):
+        one((2, 5))(i, 0)
+
+    height_terms(f, 1, n - 3, matrix, diff, total)
+    start = before_y - 1 - reach
+    count = own_y + 2 * reach
+
+    def two(comps):
+        def body(i, carry):
+            cut = cut_weights(count, low_z)
+            new = stepped(comps, f, i - 1, diff, total, fh, cut, 0.5, start, count)
+            m = mask_of(i, start + 1, count)
+            for c in comps:
+                new[c] = (0.5 * g[c, i, pl.ds(start + 1, count), :] + new[c]) * m
+            store(i, new)
+            return carry
+
+        return body
+
+    lax.fori_loop(3, n - 3, two(everything), 0, unroll=2)
+    for i in (2, n - 3):
+        two((5,))(i, 0)
+
+
+def fine_pressure(meta, p, h0, own_x, own_y, part_rows):
+    n, count = p.shape[0], p.shape[1]
+    skip = (h0.shape[1] - count) // 2
+    skip_x = (h0.shape[0] - n) // 2
+    before = (n - own_x) // 2
+    y_l = iota((count, LANES), 0) - (count - own_y) // 2
+    col_y = lax.div(wrapped(iota((count, LANES), 1), 2 * own_y, LANES) + LANES, 2) - LANES // 2
+    pick = col_y == y_l
     row_x = lax.div(wrapped(iota((part_rows, LANES), 0), 2 * own_x, part_rows) + LANES, 2) - LANES // 2
-    height = iota((size, LANES), 1) + gz * LANES
-    height = height.astype(F32)
-
-    def two(i, fine):
-        mid = [f[c, i - 1] for c in range(COMPS)]
-        rate = rates([f[c, i - 2] for c in range(COMPS)], mid, [f[c, i] for c in range(COMPS)], fh[i - 1], lane, edge)
-        m = inside(i)
-        for c in range(COMPS):
-            new = 0.5 * (g[c, i] + mid[c] + GAS_STEP * rate[c]) * m
-            u1[c, i - 2] = new
-        level = h[i][:, LEVEL : LEVEL + 1]
-        at = jnp.sum(jnp.where(height == level, new, 0.0), axis=1, keepdims=True)
-        line = jnp.sum(spread_y * at, axis=0, keepdims=True)
-        return fine + jnp.where(row_x == i - before, line, 0.0)
-
-    return lax.fori_loop(2, n - 2, two, jnp.zeros((part_rows, LANES), F32))
+    height = (iota((count, LANES), 1) + meta[2] * LANES).astype(F32)
+    fine = jnp.zeros((part_rows, LANES), F32)
+    for i in range(n):
+        level = h0[i + skip_x, skip : skip + count, LEVEL : LEVEL + 1]
+        at = jnp.sum(jnp.where(height == level, p[i], 0.0), axis=1, keepdims=True)
+        line = jnp.sum(jnp.where(pick, at, 0.0), axis=0, keepdims=True)
+        fine = jnp.where(row_x == i - before, line, fine)
+    return fine
 
 
 def top_heat(meta, beam, first, t, k, fine, own_rows, cols):
@@ -491,25 +583,24 @@
     return softplus(0.25 * four - BOIL_LEVEL - BACK_PRESSURE * fine)
 
 
-def mass_rows(meta, h, mass, size, own_y):
-    gz = meta[2]
-    y_l = wrapped(iota((size, LANES), 0), own_y, size)
-    col = wrapped(iota((size, LANES), 1), 2 * own_y, LANES)
+def mass_rows(meta, h, mass, count, own_y):
+    skip = (h.shape[1] - count) // 2
+    y_l = iota((count, LANES), 0) - (count - own_y) // 2
+    col = wrapped(iota((count, LANES), 1), 2 * own_y, LANES)
     pick = col == 2 * y_l
-    height = (iota((size, LANES), 1) + gz * LANES).astype(F32)
+    height = (iota((count, LANES), 1) + meta[2] * LANES).astype(F32)
 
     def row(i, x):
-        r = lax.rem(2 * x + mass.shape[0], mass.shape[0])
-        line = mass[pl.ds(r, 1), :]
-        at = jnp.sum(jnp.where(pick, line, 0.0), axis=1, keepdims=True)
-        return jnp.where(height == h[i][:, LEVEL : LEVEL + 1], at, 0.0)
+        r = (2 * x) % mass.shape[0]
+        at = jnp.sum(jnp.where(pick, mass[r : r + 1, :], 0.0), axis=1, keepdims=True)
+        return jnp.where(height == h[i, skip : skip + count, LEVEL : LEVEL + 1], at, 0.0)
 
     return row
 
 
 def first_kernel(
     cells, meta, beam, u, own, in_a, in_b, in_z, in_d, in_h, gy_a, gy_b,
-    out_g, out_m, out_t, out_k, g, h, f, fh, u1, mass, skin,
+    out_g, out_m, out_t, out_k, g, h, h1, f, fh, diff, total, p, mass, skin,
 ):
     rows_x, reach = cells
     gx, gy, gz = meta[0], meta[1], meta[2]
@@ -535,7 +626,7 @@
         for c in range(COMPS):
             for y in range(tiles):
                 value = row_tile(c, x, y, u, in_a, in_b, even_x)
-                g[c, i, y * SUBL : (y + 1) * SUBL, :] = zero if value is None else value
+                g[c, i, (y + 1) * SUBL : (y + 2) * SUBL, :] = zero if value is None else value
             upper = lower = zero
             if 0 < i < wide + 1:
                 upper, lower = side((i - 1) * COMPS // 2 + c // 2)
@@ -547,8 +638,8 @@
                 far_up, far_low = turn(far_up, half - 2 * q, 0), turn(far_low, 2 - 2 * q, 0)
             else:
                 far_up = far_low = zero
-            g[c, i, own_y : own_y + SUBL, :] = jnp.where(sub < half, upper, jnp.where(sub < half + 2, far_up, 0.0))
-            g[c, i, own_y + SUBL : size, :] = jnp.where(sub >= half, lower, jnp.where(sub >= half - 2, far_low, 0.0))
+            g[c, i, own_y + SUBL : size, :] = jnp.where(sub < half, upper, jnp.where(sub < half + 2, far_up, 0.0))
+            g[c, i, :SUBL, :] = jnp.where(sub >= half, lower, jnp.where(sub >= half - 2, far_low, 0.0))
     base = in_z.shape[0] - tiles
     packed = []
     for b in range(3):
@@ -560,13 +651,20 @@
                 parts.append(in_z[base + y])
             else:
                 parts.append(jnp.where(low_z, in_h[y], in_d[base + y]))
-        parts.extend(side(outer + rows_x + 2 + b))
-        packed.append(jnp.concatenate(parts, axis=0))
+        upper, lower = side(outer + rows_x + 2 + b)
+        packed.append(jnp.concatenate([lower, *parts, upper], axis=0))
     for x in range(-reach, rows_x + reach):
         b, q = divmod(x + rows_x, rows_x)
-        h[x + reach] = turn(packed[b], -GROUP * q, 1)
-
-    fine = advance(meta, g, h, f, fh, u1, rows_x, own_y)
+        unpack_heights(packed[b], GROUP * q, low_z, h, h1, x + reach)
+
+    def store(i, new):
+        p[i - 2] = new[COMPS - 1]
+        if len(new) == COMPS:
+            for c in range(COMPS):
+                out_g[c, i - 3] = new[c]
+
+    advance(meta, g, h, h1, f, fh, diff, total, rows_x, own_y, store)
+    fine = fine_pressure(meta, p, h, rows_x, own_y, mass.shape[0])
 
     cols = LANES // 4
     per = LANES // cols
@@ -600,63 +698,48 @@
         out_k[d] = k[d]
     mass[...] = vapor_mass(t[0], fine)
 
-    edge, behind = edges(gz)
-    mass_of = mass_rows(meta, h, mass, size, own_y)
-    x_from = -REACH_LAST
-    count = rows_x + 2 * REACH_LAST
-    half = SUBL // 2
-    sub = iota((SUBL, LANES), 0)
-    small = own_y + SUBL
+    count, small = out_g.shape[1], out_g.shape[2]
+    mass_of = mass_rows(meta, h, mass, small, own_y)
     lane_s = iota((small, LANES), 1)
-    shift = reach - 2 - REACH_LAST
-    y_l = wrapped(iota((size, LANES), 0), own_y, size)
-    y_g = gy * own_y + y_l
+    y_g = gy * own_y + iota((small, LANES), 0) - (small - own_y) // 2
     inside_y = jnp.where((y_g >= 0) & (y_g < meta[4] * own_y), 1.0, 0.0)
-
-    def finish(i, carry):
-        x = i + x_from
+    skip = (size - small) // 2
+    per = LANES // GROUP
+    acc = jnp.zeros((small, LANES), F32)
+    for i in range(count):
+        x = i - REACH_LAST
         x_g = gx * rows_x + x
         ok = jnp.where((x_g >= 0) & (x_g < meta[3] * rows_x), 1.0, 0.0)
-        add = mass_of(x + reach, x) * inside_y * ok
-        rows = []
-        for c in range(COMPS):
-            value = u1[c, i + shift]
-            if c == 0:
-                value = value + VAPOR_SOURCE * add
-            elif c == 4:
-                value = value + RECOIL_PUSH * add
-            elif c == 5:
-                value = value + RECOIL_PRESSURE * add
-            ends = jnp.where(sub < half, value[own_y : own_y + SUBL], value[own_y + SUBL : size])
-            value = jnp.concatenate([value[:own_y], ends], axis=0)
-            out_g[c, i] = value
-            rows.append(value)
-        acc = jnp.zeros((small, LANES), F32)
-        for c in range(COMPS):
-            acc = jnp.where(lane_s == c, lane_turn(rows[c], c - edge), acc)
-            acc = jnp.where(lane_s == NEXT + c, lane_turn(rows[c], NEXT + c - behind), acc)
-        level = h[x + reach][:, LEVEL : LEVEL + 1]
-        ends = jnp.where(sub < half, level[own_y : own_y + SUBL], level[own_y + SUBL : size])
-        level = jnp.concatenate([jnp.broadcast_to(level[:own_y], (own_y, LANES)), ends], axis=0)
-        acc = jnp.where(lane_s == LEVEL, level, acc)
-        acc = jnp.where(lane_s < GROUP, acc, 0.0)
-        j = i // (LANES // GROUP)
-        q = lax.rem(i, LANES // GROUP)
-        out_m[j] = jnp.where(q == 0, 0.0, out_m[j]) + lane_turn(acc, GROUP * q)
-        return carry
-
-    out_m[...] = jnp.zeros_like(out_m)
-    lax.fori_loop(0, count, finish, 0)
-
-
-def last_kernel(cells, meta, beam, g, in_m, in_t, in_k, out_g, out_t, out_f, h, f, fh, u1, mass, skin):
+        add = mass_of(x + reach, x) * (inside_y * ok)
+        rows = [out_g[c, i] for c in range(COMPS)]
+        for c, load in ((0, VAPOR_SOURCE), (4, RECOIL_PUSH), (5, RECOIL_PRESSURE)):
+            rows[c] = rows[c] + load * add
+            out_g[c, i] = rows[c]
+        j, q = divmod(i, per)
+        acc = pack_heights(rows, GROUP * q, lane_s, low_z, acc)
+        level = h[x + reach, skip : skip + small, LEVEL : LEVEL + 1]
+        acc = jnp.where((lane_s & -2) == GROUP * q + LEVEL, level, acc)
+        if q == per - 1 or i == count - 1:
+            out_m[j] = acc
+            acc = jnp.zeros((small, LANES), F32)
+
+
+def last_kernel(
+    cells, meta, beam, g, in_m, in_t, in_k, out_g, out_t, out_f, h, h1, f, fh, diff, total, p, mass, skin
+):
     rows_x, own_y = cells
-    size = g.shape[2]
-    n = g.shape[1]
-    for i in range(n):
+    for i in range(g.shape[1]):
         j, q = divmod(i, LANES // GROUP)
-        h[i] = turn(in_m[j], -GROUP * q, 1)
-    fine = advance(meta, g, h, f, fh, u1, rows_x, own_y)
+        unpack_heights(in_m[j], GROUP * q, meta[2] == 0, h, h1, i)
+
+    def store(i, new):
+        p[i - 2] = new[COMPS - 1]
+        if len(new) == COMPS:
+            for c in range(COMPS):
+                out_g[c, i - 3] = new[c][1 : own_y + 1]
+
+    advance(meta, g, h, h1, f, fh, diff, total, rows_x, own_y, store)
+    fine = fine_pressure(meta, p, h, rows_x, own_y, mass.shape[0])
     cols = LANES // 4
     t = [in_t[d] for d in range(TOP)]
     k = [in_k[d] for d in range(TOP)]
@@ -666,22 +749,11 @@
     pack_skin(t, 0, cols, skin, out_t)
     pack_skin(t, SUBL, cols, skin, out_f)
     mass[...] = vapor_mass(t[0], fine)
-    mass_of = mass_rows(meta, h, mass, size, own_y)
-
-    def finish(x, carry):
+    mass_of = mass_rows(meta, h, mass, own_y, own_y)
+    for x in range(rows_x):
         add = mass_of(x + REACH_LAST, x)
-        for c in range(COMPS):
-            value = u1[c, x + REACH_LAST - 2]
-            if c == 0:
-                value = value + VAPOR_SOURCE * add
-            elif c == 4:
-                value = value + RECOIL_PUSH * add
-            elif c == 5:
-                value = value + RECOIL_PRESSURE * add
-            out_g[c, x] = value[:own_y]
-        return carry
-
-    lax.fori_loop(0, rows_x, finish, 0)
+        for c, load in ((0, VAPOR_SOURCE), (4, RECOIL_PUSH), (5, RECOIL_PRESSURE)):
+            out_g[c, x] = out_g[c, x] + load * add
 
 
 def call(body, outs, scratch=(), scalars=1, count=0):
@@ -695,6 +767,19 @@
         scratch_shapes=[pltpu.VMEM(s, F32) for s in scratch],
         compiler_params=pltpu.CompilerParams(vmem_limit_bytes=32 * 1024 * 1024),
     )
+
+
+def advance_scratch(n, size, count, bricks):
+    row = (size, LANES)
+    return ([(COMPS, n, *row)] if bricks else []) + [
+        (n, *row),
+        (n, *row),
+        (COMPS, n - 2, *row),
+        (n - 2, *row),
+        (COMPS, n - 1, *row),
+        (COMPS, n - 1, *row),
+        (n - 4, count, LANES),
+    ]
 
 
 def pairs(count, odd):
@@ -751,15 +836,7 @@
     g2, msg_m, top_t, top_k = call(
         functools.partial(first_kernel, (rows_x, REACH)),
         [(COMPS, n2, small, LANES), (n_m, small, LANES), (TOP, part_rows, LANES), (TOP, part_rows, LANES)],
-        scratch=[
-            (COMPS, n, size, LANES),
-            (n, size, LANES),
-            (COMPS, n - 2, size, LANES),
-            (n - 2, size, LANES),
-            (COMPS, n - 4, size, LANES),
-            (part_rows, LANES),
-            (part_rows, *block),
-        ],
+        scratch=advance_scratch(n, size, own_y + 2 * (REACH - 2), True) + [(part_rows, LANES), (part_rows, *block)],
         scalars=2,
         count=9,
     )(meta, beam, u, own, in_a, in_b, in_z, in_d, in_h, gy_a, gy_b)
@@ -771,14 +848,8 @@
     gas, mine, other = call(
         functools.partial(last_kernel, (rows_x, own_y)),
         [u.shape, (n_top // 2, *block), (n_top // 2, *block)],
-        scratch=[
-            (n2, small, LANES),
-            (COMPS, n2 - 2, small, LANES),
-            (n2 - 2, small, LANES),
-            (COMPS, n2 - 4, small, LANES),
-            (part_rows, LANES),
-            (part_rows, *block),
-        ],
+        scratch=advance_scratch(n2, small, own_y + 2 * (REACH_LAST - 2), False)
+        + [(part_rows, LANES), (part_rows, *block)],
         scalars=2,
         count=4,
     )(meta, beam, g2, in_m, top_t, top_k)

time: 61.5 us -> 55 us (0.89)
  Pallas kernels: 27.8 us -> 21.3 us
    pallas_call x1, Pallas kernels: 14.1 us -> 9.21 us  [shards(): call(functools.partial(first_kernel, (rows_x, REACH)), [(COMPS, n2, small...]
    pallas_call x1, Pallas kernels: 7.58 us -> 6.06 us  [shards(): call(functools.partial(last_kernel, (rows_x, own_y)), [u.shape, (n_top //...]
where the time goes in v3:
time: 55 us; the launch traced here: 54.5 us
  Pallas kernels  21.3 us (39%)
  waiting for transfers between devices  15.3 us (28%)
  starting transfers between devices  13.6 us (25%)
  local copies, waits for them, and re-layouts  3.58 us (7%)
  between operations  0.77 us (1%)
    pallas_call x1, Pallas kernels, shards(): call(functools.partial(first_kernel, (rows_x, REACH)), [(COMPS, n2, small...  9.21 us
    pallas_call x1, Pallas kernels, shards(): call(functools.partial(last_kernel, (rows_x, own_y)), [u.shape, (n_top //...  6.06 us
    ppermute x1, waiting for transfers between devices, shards(): gy_b = lax.ppermute(msg_b, 'gy', pairs(ny, 1))  6.05 us
    ppermute x1, waiting for transfers between devices, shards(): in_h = lax.ppermute(msg_h, ('gx', 'gz'), cross(nx, nz, False))  4.6 us
    ppermute x1, starting transfers between devices, shards(): in_d = lax.ppermute(msg_d, ('gx', 'gz'), cross(nx, nz, True))  3.85 us
    ppermute x1, waiting for transfers between devices, shards(): in_m = lax.ppermute(msg_m, 'gz', pairs(nz, 0))  3.81 us
    unnamed x17, local copies, waits for them, and re-layouts  3.5 us
    pallas_call x1, Pallas kernels, shards(): call(bulk_kernel, [t.shape], scratch=[(2, *part), part, part, part, part]...  2.92 us
  transfers between devices with their start and end apart: 9, of which 5 were waited for; matrix products, arithmetic and copies ran while one was open for 0% of the time, Pallas kernels for 5%

profile of v3, /device:TPU:18, one launch (start us, length us, event | category | flops | bytes accessed | tf_op | source)
XLA Modules:
  0.0 54.5 jit_solution(1127253839925708488)
XLA Ops:
  0.7 0.1 stack.15.meta
  0.7 0.6 %copy-done.6 = s32[8,16]{1,0:T(8,128)S(1)} copy-done((s32[8,16]{1,0:T(8,128)S(1)}, s32[8,16]{1,0:T(8,128)}, u32[]{:S(2)}) %copy-start.6) | copy-done | bytes 536
  1.3 1.0 %copy-done = f32[6,8,16,128]{3,2,1,0:T(8,128)S(1)} copy-done((f32[6,8,16,128]{3,2,1,0:T(8,128)S(1)}, f32[6,8,16,128]{3,2,1,0:T(8,128)}, u32[]{:S(2)}) %copy-start) | copy-done | bytes 393240
  2.3 0.9 %copy-done.2 = f32[128,8,32]{0,2,1:T(8,128)S(1)} copy-done((f32[128,8,32]{0,2,1:T(8,128)S(1)}, f32[128,8,32]{0,2,1:T(8,128)}, u32[]{:S(2)}) %copy-start.2) | copy-done | bytes 131096
  3.2 0.9 %copy-done.4 = s32[128,8,32]{0,2,1:T(8,128)S(1)} copy-done((s32[128,8,32]{0,2,1:T(8,128)S(1)}, s32[128,8,32]{0,2,1:T(8,128)}, u32[]{:S(2)}) %copy-start.4) | copy-done | bytes 131096
  4.1 1.0 %shard_map.68 = (f32[64,8,128]{2,1,0:T(8,128)S(1)}, f32[64,8,128]{2,1,0:T(8,128)S(1)}, f32[38,8,128]{2,1,0:T(8,128)S(1)}, f32[38,8,128]{2,1,0:T(8,128)S(1)}, f32...) custom-call(s32[6]{0:T(128)S(1)} %stack.15.meta, f32[6,8,16,128]{3,2,1,0:T(8,128)S(1)} %copy-done, ...), custom_call_target="tpu_custom_call" | custom-call | tf_op jit(solution)/shard_map/pallas_call | solution.py:812
  5.1 1.6 %collective-permute-start = (f32[64,8,128]{2,1,0:T(8,128)S(1)}, f32[64,8,128]{2,1,0:T(8,128)S(1)}, u32[]{:S(2)}, u32[]{:S(2)}) collective-permute-start(f32[64,8,128]{2,1,0:T(8,128)S(1)} %get-tuple-element.18), channel_id=1, source_target_pairs={{0,8},{8,0},{16,24},{24,16},{1,9},{9,1},{17,25},{25,17},{2,10},{10... | collective-permute-start | bytes 786440 | tf_op jit(solution)/shard_map/ppermute | solution.py:817
  6.8 1.9 %collective-permute-start.1 = (f32[64,8,128]{2,1,0:T(8,128)S(1)}, f32[64,8,128]{2,1,0:T(8,128)S(1)}, u32[]{:S(2)}, u32[]{:S(2)}) collective-permute-start(f32[64,8,128]{2,1,0:T(8,128)S(1)} %get-tuple-element.19), channel_id=1, source_target_pairs={{8,16},{16,8},{9,17},{17,9},{10,18},{18,10},{11,19},{19,11},{12,20... | collective-permute-start | bytes 786440 | tf_op jit(solution)/shard_map/ppermute | solution.py:818
  8.7 1.6 %collective-permute-start.2 = (f32[38,8,128]{2,1,0:T(8,128)S(1)}, f32[38,8,128]{2,1,0:T(8,128)S(1)}, u32[]{:S(2)}, u32[]{:S(2)}) collective-permute-start(f32[38,8,128]{2,1,0:T(8,128)S(1)} %get-tuple-element.20), channel_id=1, source_target_pairs={{0,1},{1,0},{2,3},{3,2},{4,5},{5,4},{6,7},{7,6},{8,9},{9,8},{10,11... | collective-permute-start | bytes 466952 | tf_op jit(solution)/shard_map/ppermute | solution.py:819
  10.3 3.9 %collective-permute-start.3 = (f32[38,8,128]{2,1,0:T(8,128)S(1)}, f32[38,8,128]{2,1,0:T(8,128)S(1)}, u32[]{:S(2)}, u32[]{:S(2)}) collective-permute-start(f32[38,8,128]{2,1,0:T(8,128)S(1)} %get-tuple-element.21), channel_id=1, source_target_pairs={{1,8},{8,1},{9,16},{16,9},{17,24},{24,17},{3,10},{10,3},{11,18},{1... | collective-permute-start | bytes 466952 | tf_op jit(solution)/shard_map/ppermute | solution.py:820
  14.1 1.9 %collective-permute-start.4 = (f32[2,8,128]{2,1,0:T(8,128)S(1)}, f32[2,8,128]{2,1,0:T(8,128)S(1)}, u32[]{:S(2)}, u32[]{:S(2)}) collective-permute-start(f32[2,8,128]{2,1,0:T(8,128)S(1)} %get-tuple-element.22), channel_id=1, source_target_pairs={{0,9},{9,0},{8,17},{17,8},{16,25},{25,16},{2,11},{11,2},{10,19},{1... | collective-permute-start | bytes 24584 | tf_op jit(solution)/shard_map/ppermute | solution.py:821
  16.1 4.6 %collective-permute-done.4.in_h = f32[2,8,128]{2,1,0:T(8,128)S(1)} collective-permute-done((f32[2,8,128]{2,1,0:T(8,128)S(1)}, f32[2,8,128]{2,1,0:T(8,128)S(1)}, u32[]{:S(2)}, u32[]{:S(2)}) %collective-permute-start.4) | collective-permute-done | bytes 8224 | tf_op jit(solution)/shard_map/ppermute | solution.py:821
  20.7 0.1 collective-permute-done.3.in_d
  20.8 0.7 %shard_map.69 = (f32[87,8,128]{2,1,0:T(8,128)S(1)}, f32[87,8,128]{2,1,0:T(8,128)S(1)}) custom-call(s32[6]{0:T(128)S(1)} %stack.15.meta, f32[6,8,16,128]{3,2,1,0:T(8,128)S(1)} %copy-done, f32[8,32,128]{2,1,0:T(8,128)S(1)} %bitcast.7, s32[8,32,128]{2,1,0:T(8,128)S(1)} %bitcast.10, f32[4,8,128]{2,1,0:T(8,128)S(1)} %get-tuple-element.17.own, ...), custom_call_target="tpu_custom_call" | custom-call | tf_op jit(solution)/shard_map/pallas_call | solution.py:824
  21.6 0.1 collective-permute-start.5
  21.7 2.5 %collective-permute-start.6 = (f32[87,8,128]{2,1,0:T(8,128)S(1)}, f32[87,8,128]{2,1,0:T(8,128)S(1)}, u32[]{:S(2)}, u32[]{:S(2)}) collective-permute-start(f32[87,8,128]{2,1,0:T(8,128)S(1)} %get-tuple-element.24), channel_id=1, source_target_pairs={{2,4},{4,2},{3,5},{5,3},{10,12},{12,10},{11,13},{13,11},{18,20},{2... | collective-permute-start | bytes 1069064 | tf_op jit(solution)/shard_map/ppermute | solution.py:828
  24.2 0.1 copy.8.beam
  24.3 6.1 %collective-permute-done.6.gy_b = f32[87,8,128]{2,1,0:T(8,128)S(1)} collective-permute-done((f32[87,8,128]{2,1,0:T(8,128)S(1)}, f32[87,8,128]{2,1,0:T(8,128)S(1)}, u32[]{:S(2)}, u32[]{:S(2)}) %collective-permute-start.6) | collective-permute-done | bytes 356384 | tf_op jit(solution)/shard_map/ppermute | solution.py:828
  30.4 9.2 %shard_map.70 = (f32[6,14,24,128]{3,2,1,0:T(8,128)S(1)}, f32[2,24,128]{2,1,0:T(8,128)S(1)}, f32[8,32,128]{2,1,0:T(8,128)S(1)}, f32[8,32,128]{2,1,0:T(8,128)S(1)}) custom-call(s32[6]{0:T(128)S(1)} %stack.15.meta, s32[4,2]{1,0:T(4,128)S(1)} %copy.8.beam, f32[6,8,16,128]{3,2,1,0:T(8,128)S(1)} %copy-done.1, f32[4,8,128]{2,1,0:T(8,128)S(1)} %get-tuple-element.17.own, ...), custom_call_target="tpu_custom_call" | custom-call | tf_op jit(solution)/shard_map/pallas_call | solution.py:836
  39.7 3.8 %collective-permute-done.7.in_m = f32[2,24,128]{2,1,0:T(8,128)S(1)} collective-permute-done((f32[2,24,128]{2,1,0:T(8,128)S(1)}, f32[2,24,128]{2,1,0:T(8,128)S(1)}, u32[]{:S(2)}, u32[]{:S(2)}) %collective-permute-start.7) | collective-permute-done | bytes 24608 | tf_op jit(solution)/shard_map/ppermute | solution.py:843
  43.5 6.1 %shard_map.71 = (f32[6,8,16,128]{3,2,1,0:T(8,128)}, f32[2,8,128]{2,1,0:T(8,128)S(1)}, f32[2,8,128]{2,1,0:T(8,128)S(1)}) custom-call(s32[6]{0:T(128)S(1)} %stack.15.meta, s32[4,2]{1,0:T(4,128)S(1)} %copy.8.beam, f32[6,14,24,128]{3,2,1,0:T(8,128)S(1)} %get-tuple-element.25.g, f32[2,24,128]{2,1,0:T(8,128)S(1)} %collective-permute-done.7.in_m, ...), custom_call_target="tpu_custom_call" | custom-call | tf_op jit(solution)/shard_map/pallas_call | solution.py:848
  49.6 2.9 %shard_map.72.bulk = f32[8,32,128]{2,1,0:T(8,128)S(1)} custom-call(s32[6]{0:T(128)S(1)} %stack.15.meta, s32[4,2]{1,0:T(4,128)S(1)} %copy.8.beam, f32[8,32,128]{2,1,0:T(8,128)S(1)} %bitcast.8, s32[8,32,128]{2,1,0:T(8,128)S(1)} %bitcast.11, f32[38,8,128]{2,1,0:T(8,128)S(1)} %collective-permute-done.2.in_z, f32[38,8,128]{2,1,0:T(8,128)S(1)} %collective-permute-done.3.in_d, ...), custom_call_target="tpu_custom_call" | custom-call | tf_op jit(solution)/shard_map/pallas_call | solution.py:845
  52.5 0.7 %collective-permute-done.8.given = f32[2,8,128]{2,1,0:T(8,128)S(1)} collective-permute-done((f32[2,8,128]{2,1,0:T(8,128)S(1)}, f32[2,8,128]{2,1,0:T(8,128)S(1)}, u32[]{:S(2)}, u32[]{:S(2)}) %collective-permute-start.8) | collective-permute-done | bytes 8224 | tf_op jit(solution)/shard_map/ppermute | solution.py:856
  53.2 1.3 %shard_map.73 = f32[8,32,128]{2,1,0:T(8,128)} custom-call(s32[6]{0:T(128)S(1)} %stack.15.meta, f32[8,32,128]{2,1,0:T(8,128)S(1)} %shard_map.72.bulk, f32[2,8,128]{2,1,0:T(8,128)S(1)} %get-tuple-element.30.mine, f32[2,8,128]{2,1,0:T(8,128)S(1)} %collective-permute-done.8.given), custom_call_target="tpu_custom_call" | custom-call | tf_op jit(solution)/shard_map/pallas_call | solution.py:857
  (19 shorter events, 0.1 us)
Async XLA Ops:
  0.6 0.7 %copy-start.6 = (s32[8,16]{1,0:T(8,128)S(1)}, s32[8,16]{1,0:T(8,128)}, u32[]{:S(2)}) copy-start(s32[8,16]{1,0:T(8,128)} %lev.1) | copy-start | bytes 1540
  1.3 1.0 %copy-start = (f32[6,8,16,128]{3,2,1,0:T(8,128)S(1)}, f32[6,8,16,128]{3,2,1,0:T(8,128)}, u32[]{:S(2)}) copy-start(f32[6,8,16,128]{3,2,1,0:T(8,128)} %u.5) | copy-start | bytes 1179652
  2.3 0.9 %copy-start.2 = (f32[128,8,32]{0,2,1:T(8,128)S(1)}, f32[128,8,32]{0,2,1:T(8,128)}, u32[]{:S(2)}) copy-start(f32[128,8,32]{0,2,1:T(8,128)} %param.6) | copy-start | bytes 393220
  3.2 0.9 %copy-start.4 = (s32[128,8,32]{0,2,1:T(8,128)S(1)}, s32[128,8,32]{0,2,1:T(8,128)}, u32[]{:S(2)}) copy-start(s32[128,8,32]{0,2,1:T(8,128)} %param.7) | copy-start | bytes 393220
  5.1 15.7 %collective-permute-start = (f32[64,8,128]{2,1,0:T(8,128)S(1)}, f32[64,8,128]{2,1,0:T(8,128)S(1)}, u32[]{:S(2)}, u32[]{:S(2)}) collective-permute-start(f32[64,8,128]{2,1,0:T(8,128)S(1)} %get-tuple-element.18), channel_id=1, source_target_pairs={{0,8},{8,0},{16,24},{24,16},{1,9},{9,1},{17,25},{25,17},{2,10},{10... | collective-permute-start | bytes 786440 | tf_op jit(solution)/shard_map/ppermute | solution.py:817
  6.8 14.0 %collective-permute-start.1 = (f32[64,8,128]{2,1,0:T(8,128)S(1)}, f32[64,8,128]{2,1,0:T(8,128)S(1)}, u32[]{:S(2)}, u32[]{:S(2)}) collective-permute-start(f32[64,8,128]{2,1,0:T(8,128)S(1)} %get-tuple-element.19), channel_id=1, source_target_pairs={{8,16},{16,8},{9,17},{17,9},{10,18},{18,10},{11,19},{19,11},{12,20... | collective-permute-start | bytes 786440 | tf_op jit(solution)/shard_map/ppermute | solution.py:818
  8.7 12.0 %collective-permute-start.2 = (f32[38,8,128]{2,1,0:T(8,128)S(1)}, f32[38,8,128]{2,1,0:T(8,128)S(1)}, u32[]{:S(2)}, u32[]{:S(2)}) collective-permute-start(f32[38,8,128]{2,1,0:T(8,128)S(1)} %get-tuple-element.20), channel_id=1, source_target_pairs={{0,1},{1,0},{2,3},{3,2},{4,5},{5,4},{6,7},{7,6},{8,9},{9,8},{10,11... | collective-permute-start | bytes 466952 | tf_op jit(solution)/shard_map/ppermute | solution.py:819
  10.3 10.5 %collective-permute-start.3 = (f32[38,8,128]{2,1,0:T(8,128)S(1)}, f32[38,8,128]{2,1,0:T(8,128)S(1)}, u32[]{:S(2)}, u32[]{:S(2)}) collective-permute-start(f32[38,8,128]{2,1,0:T(8,128)S(1)} %get-tuple-element.21), channel_id=1, source_target_pairs={{1,8},{8,1},{9,16},{16,9},{17,24},{24,17},{3,10},{10,3},{11,18},{1... | collective-permute-start | bytes 466952 | tf_op jit(solution)/shard_map/ppermute | solution.py:820
  14.1 6.5 %collective-permute-start.4 = (f32[2,8,128]{2,1,0:T(8,128)S(1)}, f32[2,8,128]{2,1,0:T(8,128)S(1)}, u32[]{:S(2)}, u32[]{:S(2)}) collective-permute-start(f32[2,8,128]{2,1,0:T(8,128)S(1)} %get-tuple-element.22), channel_id=1, source_target_pairs={{0,9},{9,0},{8,17},{17,8},{16,25},{25,16},{2,11},{11,2},{10,19},{1... | collective-permute-start | bytes 24584 | tf_op jit(solution)/shard_map/ppermute | solution.py:821
  20.8 9.6 %copy-start.1 = (f32[6,8,16,128]{3,2,1,0:T(8,128)S(1)}, f32[6,8,16,128]{3,2,1,0:T(8,128)}, u32[]{:S(2)}) copy-start(f32[6,8,16,128]{3,2,1,0:T(8,128)} %u.5) | copy-start | bytes 1179652
  21.6 2.6 %copy-start.7 = (s32[4,2]{0,1:T(2,128)S(1)}, s32[4,2]{0,1:T(2,128)}, u32[]{:S(2)}) copy-start(s32[4,2]{0,1:T(2,128)} %param.9) | copy-start | bytes 100
  21.6 2.7 %collective-permute-start.5 = (f32[87,8,128]{2,1,0:T(8,128)S(1)}, f32[87,8,128]{2,1,0:T(8,128)S(1)}, u32[]{:S(2)}, u32[]{:S(2)}) collective-permute-start(f32[87,8,128]{2,1,0:T(8,128)S(1)} %get-tuple-element.23), channel_id=1, source_target_pairs={{0,2},{2,0},{4,6},{6,4},{1,3},{3,1},{5,7},{7,5},{8,10},{10,8},{12,... | collective-permute-start | bytes 1069064 | tf_op jit(solution)/shard_map/ppermute | solution.py:827
  21.7 8.7 %collective-permute-start.6 = (f32[87,8,128]{2,1,0:T(8,128)S(1)}, f32[87,8,128]{2,1,0:T(8,128)S(1)}, u32[]{:S(2)}, u32[]{:S(2)}) collective-permute-start(f32[87,8,128]{2,1,0:T(8,128)S(1)} %get-tuple-element.24), channel_id=1, source_target_pairs={{2,4},{4,2},{3,5},{5,3},{10,12},{12,10},{11,13},{13,11},{18,20},{2... | collective-permute-start | bytes 1069064 | tf_op jit(solution)/shard_map/ppermute | solution.py:828
  39.6 3.9 %collective-permute-start.7 = (f32[2,24,128]{2,1,0:T(8,128)S(1)}, f32[2,24,128]{2,1,0:T(8,128)S(1)}, u32[]{:S(2)}, u32[]{:S(2)}) collective-permute-start(f32[2,24,128]{2,1,0:T(8,128)S(1)} %get-tuple-element.26), channel_id=1, source_target_pairs={{0,1},{1,0},{2,3},{3,2},{4,5},{5,4},{6,7},{7,6},{8,9},{9,8},{10,11... | collective-permute-start | bytes 73736 | tf_op jit(solution)/shard_map/ppermute | solution.py:843
  43.5 6.1 %copy-start.3 = (f32[128,8,32]{0,2,1:T(8,128)S(1)}, f32[128,8,32]{0,2,1:T(8,128)}, u32[]{:S(2)}) copy-start(f32[128,8,32]{0,2,1:T(8,128)} %param.6) | copy-start | bytes 393220
  43.5 6.1 %copy-start.5 = (s32[128,8,32]{0,2,1:T(8,128)S(1)}, s32[128,8,32]{0,2,1:T(8,128)}, u32[]{:S(2)}) copy-start(s32[128,8,32]{0,2,1:T(8,128)} %param.7) | copy-start | bytes 393220
  49.5 3.7 %collective-permute-start.8 = (f32[2,8,128]{2,1,0:T(8,128)S(1)}, f32[2,8,128]{2,1,0:T(8,128)S(1)}, u32[]{:S(2)}, u32[]{:S(2)}) collective-permute-start(f32[2,8,128]{2,1,0:T(8,128)S(1)} %get-tuple-element.31), channel_id=1, source_target_pairs={{0,1},{1,0},{2,3},{3,2},{4,5},{5,4},{6,7},{7,6},{8,9},{9,8},{10,11... | collective-permute-start | bytes 24584 | tf_op jit(solution)/shard_map/ppermute | solution.py:856

commit v4 on v3

--- a/solution.py
+++ b/solution.py
@@ -31,6 +31,7 @@
 
 COMPS = 6
 LANES = 128
+VMEM_LIMIT = 32 * 1024 * 1024
 SUBL = 8
 F32 = jnp.float32
 REACH = 6
@@ -111,12 +112,32 @@
     return jnp.where(v == 0, POWDER_COND, jnp.where(v == 1, SOLID_COND, LIQUID_COND)).astype(F32)
 
 
-def pack_kernel(cells, meta, u, t, m, lev, out_a, out_b, out_z, out_d, out_h, own):
+def surface_tops(t, m):
+    rows, cols = t.shape[0], t.shape[1]
+    per = LANES // cols
+    out = []
+    for ref in (t, m):
+        for j in range(rows // per):
+            block = ref[j * per : (j + 1) * per].reshape(LANES, LANES)
+            out.append(jnp.transpose(conduct(block) if ref is m else block)[:TOP])
+    return out
+
+
+def gas_kernel(cells, meta, u_in, t_in, m_in, out_a, out_b, u, t, m, sems):
+    copies = [
+        pltpu.make_async_copy(src, dst, sems.at[i]) for i, (src, dst) in enumerate(((t_in, t), (m_in, m), (u_in, u)))
+    ]
+    for copy in copies:
+        copy.start()
     rows_x, reach = cells
-    gx, gz = meta[0], meta[2]
-    even = lax.rem(gx, 2) == 0
-    low_z = gz == 0
+    even = lax.rem(meta[0], 2) == 0
     tiles = u.shape[2] // SUBL
+    copies[0].wait()
+    copies[1].wait()
+    for j, top in enumerate(surface_tops(t, m)):
+        out_a[slab_size(tiles) + j] = top
+        out_b[slab_size(tiles) + j] = top
+    copies[2].wait()
     for c in range(COMPS):
         for layer in range(1, reach + 1):
             for y in range(tiles):
@@ -127,6 +148,12 @@
                 hi = u[c, rows_x - layer, y * SUBL : (y + 1) * SUBL, :]
                 out_a[n] = jnp.where(even, hi, lo)
                 out_b[n] = jnp.where(even, lo, hi)
+
+
+def pack_kernel(meta, u, t, m, lev, out_h, out_z, out_d, own):
+    low_z = meta[2] == 0
+    rows_x = u.shape[1]
+    tiles = u.shape[2] // SUBL
     rows, cols = t.shape[0], t.shape[1]
     col_tiles = cols // SUBL
     n = 0
@@ -139,20 +166,12 @@
                 out_z[n] = jnp.where(low_z, hi, lo)
                 out_d[n] = jnp.where(low_z, lo, hi)
                 n += 1
-    per = LANES // cols
-    top_a = slab_size(tiles)
-    for j in range(2 * rows // per):
-        ref, r = (t, j * per) if j < rows // per else (m, j * per - rows)
-        block = ref[r : r + per].reshape(LANES, LANES)
-        if ref is m:
-            block = conduct(block)
-        top = jnp.transpose(block)[:TOP]
+    tops = surface_tops(t, m)
+    for j, top in enumerate(tops):
         own[j] = top
         out_z[n + j] = top
         out_d[n + j] = top
-        out_a[top_a + j] = top
-        out_b[top_a + j] = top
-    n += 2 * rows // per
+    n += len(tops)
     size = u.shape[2]
     lane = iota((size, LANES), 1)
     eye = iota((size, size), 0) == iota((size, size), 1)
@@ -531,6 +550,16 @@
         two((5,))(i, 0)
 
 
+def lane_sums(value):
+    high = value.astype(jnp.bfloat16)
+    rest = value - high.astype(F32)
+    middle = rest.astype(jnp.bfloat16)
+    low = (rest - middle.astype(F32)).astype(jnp.bfloat16)
+    parts = jnp.concatenate([high, middle, low], axis=1)
+    ones = jnp.ones((3 * LANES, LANES), jnp.bfloat16)
+    return jnp.dot(parts, ones, preferred_element_type=F32)
+
+
 def fine_pressure(meta, p, h0, own_x, own_y, part_rows):
     n, count = p.shape[0], p.shape[1]
     skip = (h0.shape[1] - count) // 2
@@ -542,10 +571,15 @@
     row_x = lax.div(wrapped(iota((part_rows, LANES), 0), 2 * own_x, part_rows) + LANES, 2) - LANES // 2
     height = (iota((count, LANES), 1) + meta[2] * LANES).astype(F32)
     fine = jnp.zeros((part_rows, LANES), F32)
+    full = -(-count // SUBL) * SUBL
+    pad = [jnp.zeros((full - count, LANES), F32)] if full > count else []
+    found = []
     for i in range(n):
         level = h0[i + skip_x, skip : skip + count, LEVEL : LEVEL + 1]
-        at = jnp.sum(jnp.where(height == level, p[i], 0.0), axis=1, keepdims=True)
-        line = jnp.sum(jnp.where(pick, at, 0.0), axis=0, keepdims=True)
+        found += [jnp.where(height == level, p[i], 0.0)] + pad
+    at = lane_sums(jnp.concatenate(found, axis=0))
+    for i in range(n):
+        line = jnp.sum(jnp.where(pick, at[i * full : i * full + count], 0.0), axis=0, keepdims=True)
         fine = jnp.where(row_x == i - before, line, fine)
     return fine
 
@@ -556,17 +590,18 @@
     row = gx * own_rows + wrapped(iota(shape, 0), own_rows, shape[0])
     col = gy * cols + wrapped(iota(shape, 1), cols, shape[1])
     row, col = row.astype(F32), col.astype(F32)
-    kx = [0.5 * (v + turn(v, -1, 0)) for v in k]
-    ky = [0.5 * (v + turn(v, -1, 1)) for v in k]
-    kz = [0.5 * (k[d] + k[d + 1]) for d in range(TOP - 1)]
+    deep = TOP - 1 - first
+    kx = [0.5 * (v + turn(v, -1, 0)) for v in k[:deep]]
+    ky = [0.5 * (v + turn(v, -1, 1)) for v in k[:deep]]
+    kz = [0.5 * (k[d] + k[d + 1]) for d in range(deep)]
     for s in range(SUBSTEPS):
         beam_xy = heat_source(row, col, beam, first + s)
         before = 0.5 * k[0] * t[0]
         new = []
-        for d in range(TOP):
+        for d in range(TOP - 1 - first - s):
             fx = kx[d] * (turn(t[d], -1, 0) - t[d])
             fy = ky[d] * (turn(t[d], -1, 1) - t[d])
-            fz = kz[d] * (t[d + 1] - t[d]) if d + 1 < TOP else jnp.zeros_like(before)
+            fz = kz[d] * (t[d + 1] - t[d])
             factor = jnp.exp(jnp.full(shape, -d / ABSORB_DEPTH, F32))
             change = (fx - turn(fx, 1, 0)) + (fy - turn(fy, 1, 1)) + (fz - before) + beam_xy * factor
             if d == 0:
@@ -583,19 +618,23 @@
     return softplus(0.25 * four - BOIL_LEVEL - BACK_PRESSURE * fine)
 
 
-def mass_rows(meta, h, mass, count, own_y):
+def mass_rows(meta, h, mass, first, rows, count, own_y):
     skip = (h.shape[1] - count) // 2
+    skip_x = (h.shape[0] - rows) // 2
     y_l = iota((count, LANES), 0) - (count - own_y) // 2
     col = wrapped(iota((count, LANES), 1), 2 * own_y, LANES)
     pick = col == 2 * y_l
     height = (iota((count, LANES), 1) + meta[2] * LANES).astype(F32)
-
-    def row(i, x):
-        r = (2 * x) % mass.shape[0]
-        at = jnp.sum(jnp.where(pick, mass[r : r + 1, :], 0.0), axis=1, keepdims=True)
-        return jnp.where(height == h[i, skip : skip + count, LEVEL : LEVEL + 1], at, 0.0)
-
-    return row
+    found = []
+    for i in range(rows):
+        r = (2 * (i + first)) % mass.shape[0]
+        found.append(jnp.where(pick, mass[r : r + 1, :], 0.0))
+    at = lane_sums(jnp.concatenate(found, axis=0))
+    out = []
+    for i in range(rows):
+        level = h[i + skip_x, skip : skip + count, LEVEL : LEVEL + 1]
+        out.append(jnp.where(height == level, at[i * count : (i + 1) * count], 0.0))
+    return out
 
 
 def first_kernel(
@@ -693,13 +732,13 @@
             layers.append(skin[:, d, :])
     t, k = layers[:TOP], layers[TOP:]
     t = top_heat(meta, beam, 0, t, k, fine, 2 * rows_x, cols)
-    for d in range(TOP):
+    for d in range(TOP - SUBSTEPS):
         out_t[d] = t[d]
         out_k[d] = k[d]
     mass[...] = vapor_mass(t[0], fine)
 
     count, small = out_g.shape[1], out_g.shape[2]
-    mass_of = mass_rows(meta, h, mass, small, own_y)
+    masses = mass_rows(meta, h, mass, -REACH_LAST, count, small, own_y)
     lane_s = iota((small, LANES), 1)
     y_g = gy * own_y + iota((small, LANES), 0) - (small - own_y) // 2
     inside_y = jnp.where((y_g >= 0) & (y_g < meta[4] * own_y), 1.0, 0.0)
@@ -710,7 +749,7 @@
         x = i - REACH_LAST
         x_g = gx * rows_x + x
         ok = jnp.where((x_g >= 0) & (x_g < meta[3] * rows_x), 1.0, 0.0)
-        add = mass_of(x + reach, x) * (inside_y * ok)
+        add = masses[i] * (inside_y * ok)
         rows = [out_g[c, i] for c in range(COMPS)]
         for c, load in ((0, VAPOR_SOURCE), (4, RECOIL_PUSH), (5, RECOIL_PRESSURE)):
             rows[c] = rows[c] + load * add
@@ -725,7 +764,7 @@
 
 
 def last_kernel(
-    cells, meta, beam, g, in_m, in_t, in_k, out_g, out_t, out_f, h, h1, f, fh, diff, total, p, mass, skin
+    cells, meta, beam, g, in_m, in_t, in_k, bulk, out_g, out_t, out_f, mass, h, h1, f, fh, diff, total, p, skin
 ):
     rows_x, own_y = cells
     for i in range(g.shape[1]):
@@ -741,19 +780,28 @@
     advance(meta, g, h, h1, f, fh, diff, total, rows_x, own_y, store)
     fine = fine_pressure(meta, p, h, rows_x, own_y, mass.shape[0])
     cols = LANES // 4
-    t = [in_t[d] for d in range(TOP)]
-    k = [in_k[d] for d in range(TOP)]
+    t = [in_t[d] for d in range(TOP - SUBSTEPS)]
+    k = [in_k[d] for d in range(TOP - SUBSTEPS)]
     t = top_heat(meta, beam, SUBSTEPS, t, k, fine, 2 * rows_x, cols)
-    for d in range(TOP):
+    skin[...] = jnp.zeros_like(skin)
+    for d in range(SKIN):
         skin[:, d, :] = t[d]
     pack_skin(t, 0, cols, skin, out_t)
     pack_skin(t, SUBL, cols, skin, out_f)
     mass[...] = vapor_mass(t[0], fine)
-    mass_of = mass_rows(meta, h, mass, own_y, own_y)
+
+
+def mass_kernel(meta, gas, in_m, mass, out_g, h, h1):
+    rows_x, own_y = gas.shape[1], gas.shape[2]
+    n = h.shape[0]
+    for i in range((n - rows_x) // 2, (n + rows_x) // 2):
+        j, q = divmod(i, LANES // GROUP)
+        unpack_heights(in_m[j], GROUP * q, meta[2] == 0, h, h1, i)
+    masses = mass_rows(meta, h, mass, 0, rows_x, own_y, own_y)
+    loads = {0: VAPOR_SOURCE, 4: RECOIL_PUSH, 5: RECOIL_PRESSURE}
     for x in range(rows_x):
-        add = mass_of(x + REACH_LAST, x)
-        for c, load in ((0, VAPOR_SOURCE), (4, RECOIL_PUSH), (5, RECOIL_PRESSURE)):
-            out_g[c, x] = out_g[c, x] + load * add
+        for c in range(COMPS):
+            out_g[c, x] = gas[c, x] + loads[c] * masses[x] if c in loads else gas[c, x]
 
 
 def call(body, outs, scratch=(), scalars=1, count=0):
@@ -765,7 +813,7 @@
         in_specs=[smem] * scalars + [vmem] * count,
         out_specs=[vmem] * len(outs),
         scratch_shapes=[pltpu.VMEM(s, F32) for s in scratch],
-        compiler_params=pltpu.CompilerParams(vmem_limit_bytes=32 * 1024 * 1024),
+        compiler_params=pltpu.CompilerParams(vmem_limit_bytes=VMEM_LIMIT),
     )
 
 
@@ -809,10 +857,23 @@
     n_top = 2 * rows * cols // LANES
     n_x = slab_size(tiles) + n_top
     n_z = 2 * SKIN * cols // SUBL + n_top + tiles
-    msg_a, msg_b, msg_z, msg_d, msg_h, own = call(
-        functools.partial(pack_kernel, (rows_x, REACH)),
-        [(n_x, *block), (n_x, *block), (n_z, *block), (n_z, *block), (tiles, *block), (n_top, *block)],
-        count=4,
+    vmem = pl.BlockSpec(memory_space=pltpu.VMEM)
+    hbm = pl.BlockSpec(memory_space=pltpu.HBM)
+    msg_a, msg_b = pl.pallas_call(
+        functools.partial(gas_kernel, (rows_x, REACH)),
+        out_shape=[jax.ShapeDtypeStruct((n_x, *block), F32)] * 2,
+        in_specs=[pl.BlockSpec(memory_space=pltpu.SMEM)] + [hbm] * 3,
+        out_specs=[vmem] * 2,
+        scratch_shapes=[
+            pltpu.VMEM(u.shape, F32),
+            pltpu.VMEM(t.shape, F32),
+            pltpu.VMEM(m.shape, jnp.int32),
+            pltpu.SemaphoreType.DMA((3,)),
+        ],
+        compiler_params=pltpu.CompilerParams(vmem_limit_bytes=60 * 1024 * 1024),
+    )(meta, u, t, m)
+    msg_h, msg_z, msg_d, own = call(
+        pack_kernel, [(tiles, *block), (n_z, *block), (n_z, *block), (n_top, *block)], count=4
     )(meta, u, t, m, lev)
     in_a = lax.ppermute(msg_a, "gx", pairs(nx, 0))
     in_b = lax.ppermute(msg_b, "gx", pairs(nx, 1))
@@ -824,8 +885,8 @@
     msg_a, msg_b = call(
         functools.partial(relay_kernel, (rows_x, REACH)), [(n_y, *block), (n_y, *block)], count=9
     )(meta, u, t, m, own, in_a, in_b, in_z, in_d, in_h)
+    gy_b = lax.ppermute(msg_b, "gy", pairs(ny, 1))
     gy_a = lax.ppermute(msg_a, "gy", pairs(ny, 0))
-    gy_b = lax.ppermute(msg_b, "gy", pairs(ny, 1))
 
     size = own_y + 2 * SUBL
     n = rows_x + 2 * REACH
@@ -835,7 +896,7 @@
     n_m = -(-n2 // (LANES // GROUP))
     g2, msg_m, top_t, top_k = call(
         functools.partial(first_kernel, (rows_x, REACH)),
-        [(COMPS, n2, small, LANES), (n_m, small, LANES), (TOP, part_rows, LANES), (TOP, part_rows, LANES)],
+        [(COMPS, n2, small, LANES), (n_m, small, LANES), (TOP - SUBSTEPS, part_rows, LANES), (TOP - SUBSTEPS, part_rows, LANES)],
         scratch=advance_scratch(n, size, own_y + 2 * (REACH - 2), True) + [(part_rows, LANES), (part_rows, *block)],
         scalars=2,
         count=9,
@@ -845,14 +906,14 @@
     (bulk,) = call(
         bulk_kernel, [t.shape], scratch=[(2, *part), part, part, part, part], scalars=2, count=6
     )(meta, beam, t, m, in_z, in_d, gy_a, gy_b)
-    gas, mine, other = call(
+    gas, mine, other, mass = call(
         functools.partial(last_kernel, (rows_x, own_y)),
-        [u.shape, (n_top // 2, *block), (n_top // 2, *block)],
-        scratch=advance_scratch(n2, small, own_y + 2 * (REACH_LAST - 2), False)
-        + [(part_rows, LANES), (part_rows, *block)],
+        [u.shape, (n_top // 2, *block), (n_top // 2, *block), (part_rows, LANES)],
+        scratch=advance_scratch(n2, small, own_y + 2 * (REACH_LAST - 2), False) + [(part_rows, *block)],
         scalars=2,
-        count=4,
-    )(meta, beam, g2, in_m, top_t, top_k)
+        count=5,
+    )(meta, beam, g2, in_m, top_t, top_k, bulk)
+    (gas,) = call(mass_kernel, [u.shape], scratch=[(n2, small, LANES)] * 2, count=3)(meta, gas, in_m, mass)
     given = lax.ppermute(other, "gz", pairs(nz, 0))
     (out,) = call(seal_kernel, [t.shape], count=3)(meta, bulk, mine, given)
     return gas, jnp.transpose(out, (2, 0, 1))

time: 55 us -> 49.7 us (0.904)
  local copies, waits for them, and re-layouts: 3.58 us -> 0.72 us
  waiting for transfers between devices: 15.3 us -> 12.5 us
  starting transfers between devices: 13.6 us -> 14.8 us
  Pallas kernels: 21.3 us -> 20.5 us
    pallas_call x1 -> x3, Pallas kernels: 0.99 us -> 5.25 us  [the longest x1 2.76 us: shards(): pl.pallas_call(functools.partial(gas_kernel, (rows_x, REACH)), out_shape=...]
    unnamed x17 -> x13, local copies, waits for them, and re-layouts: 3.5 us -> 0.12 us
    ppermute x1, waiting for transfers between devices: 3.81 us -> 0.88 us  [shards(): in_m = lax.ppermute(msg_m, 'gz', pairs(nz, 0))]
    pallas_call x1, Pallas kernels: 9.21 us -> 6.61 us  [shards(): call(functools.partial(first_kernel, (rows_x, REACH)), [(COMPS, n2, small...]
    pallas_call x1, Pallas kernels: 6.06 us -> 3.62 us  [shards(): call(functools.partial(last_kernel, (rows_x, own_y)), [u.shape, (n_top //...]
    ppermute x1, starting transfers between devices: 0.01 us -> 1.2 us  [shards(): given = lax.ppermute(other, 'gz', pairs(nz, 0))]
  transfers between devices with their start and end apart: 9 -> 9, of which waited for: 5 -> 4; matrix products, arithmetic and copies ran while one was open for 0% -> 0% of each run, Pallas kernels for 5% -> 11%
where the time goes in v4:
time: 49.7 us; the launch traced here: 49.3 us
  Pallas kernels  20.5 us (41%)
  starting transfers between devices  14.8 us (30%)
  waiting for transfers between devices  12.5 us (25%)
  between operations  0.83 us (2%)
  local copies, waits for them, and re-layouts  0.72 us (1%)
    pallas_call x1, Pallas kernels, shards(): call(functools.partial(first_kernel, (rows_x, REACH)), [(COMPS, n2, small...  6.61 us
    ppermute x1, waiting for transfers between devices, shards(): gy_b = lax.ppermute(msg_b, 'gy', pairs(ny, 1))  6.05 us
    ppermute x1, waiting for transfers between devices, shards(): in_h = lax.ppermute(msg_h, ('gx', 'gz'), cross(nx, nz, False))  4.52 us
    ppermute x1, starting transfers between devices, shards(): in_d = lax.ppermute(msg_d, ('gx', 'gz'), cross(nx, nz, True))  3.85 us
    pallas_call x1, Pallas kernels, shards(): call(functools.partial(last_kernel, (rows_x, own_y)), [u.shape, (n_top //...  3.62 us
    pallas_call x1, Pallas kernels, shards(): call(bulk_kernel, [t.shape], scratch=[(2, *part), part, part, part, part]...  2.92 us
    pallas_call x1, Pallas kernels, shards(): pl.pallas_call(functools.partial(gas_kernel, (rows_x, REACH)), out_shape=...  2.76 us
    ppermute x1, starting transfers between devices, shards(): gy_b = lax.ppermute(msg_b, 'gy', pairs(ny, 1))  2.53 us
  transfers between devices with their start and end apart: 9, of which 4 were waited for; matrix products, arithmetic and copies ran while one was open for 0% of the time, Pallas kernels for 11%

profile of v4, /device:TPU:18, one launch (start us, length us, event | category | flops | bytes accessed | tf_op | source)
XLA Modules:
  0.0 49.3 jit_solution(11911813041440206988)
XLA Ops:
  0.6 0.0 copy-start
  0.7 0.6 %stack.15.meta = s32[6]{0:T(128)} concatenate(s32[1]{0:T(128)} %bitcast, s32[1]{0:T(128)} %bitcast.1, s32[1]{0:T(128)} %bitcast.2, s32[2]{0:T(128)S(1)} %broadcast.3, s32[1]{0:T(128)} %constant.14.clone.1), dimensions={0} | concatenate | bytes 48 | tf_op jit(solution)/shard_map/stack | solution.py:851
  1.3 2.8 %shard_map.69 = (f32[64,8,128]{2,1,0:T(8,128)}, f32[64,8,128]{2,1,0:T(8,128)}) custom-call(s32[6]{0:T(128)} %stack.15.meta, f32[6,8,16,128]{3,2,1,0:T(8,128)} %u.5, f32[8,32,128]{2,1,0:T(8,128)} %bitcast.6, s32[8,32,128]{2,1,0:T(8,128)} %bitcast.10), custom_call_target="tpu_custom_call" | custom-call | tf_op jit(solution)/shard_map/pallas_call | solution.py:862
  4.0 1.6 %collective-permute-start = (f32[64,8,128]{2,1,0:T(8,128)}, f32[64,8,128]{2,1,0:T(8,128)S(1)}, u32[]{:S(2)}, u32[]{:S(2)}) collective-permute-start(f32[64,8,128]{2,1,0:T(8,128)} %get-tuple-element.19), channel_id=1, source_target_pairs={{0,8},{8,0},{16,24},{24,16},{1,9},{9,1},{17,25},{25,17},{2,10},{10... | collective-permute-start | bytes 786440 | tf_op jit(solution)/shard_map/ppermute | solution.py:878
  5.7 1.9 %collective-permute-start.1 = (f32[64,8,128]{2,1,0:T(8,128)}, f32[64,8,128]{2,1,0:T(8,128)S(1)}, u32[]{:S(2)}, u32[]{:S(2)}) collective-permute-start(f32[64,8,128]{2,1,0:T(8,128)} %get-tuple-element.20), channel_id=1, source_target_pairs={{8,16},{16,8},{9,17},{17,9},{10,18},{18,10},{11,19},{19,11},{12,20... | collective-permute-start | bytes 786440 | tf_op jit(solution)/shard_map/ppermute | solution.py:879
  7.6 1.0 %shard_map.68 = (f32[2,8,128]{2,1,0:T(8,128)S(1)}, f32[38,8,128]{2,1,0:T(8,128)S(1)}, f32[38,8,128]{2,1,0:T(8,128)S(1)}, f32[4,8,128]{2,1,0:T(8,128)S(1)}) custom-call(s32[6]{0:T(128)S(1)} %copy-done.3, f32[6,8,16,128]{3,2,1,0:T(8,128)S(1)} %copy-done, f32[8,32,128]{2,1,0:T(8,128)S(1)} %bitcast.7, s32[8,32,128]{2,1,0:T(8,128)S(1)} %bitcast.11, ...), custom_call_target="tpu_custom_call" | custom-call | tf_op jit(solution)/shard_map/pallas_call | solution.py:875
  8.7 1.6 %collective-permute-start.2 = (f32[38,8,128]{2,1,0:T(8,128)S(1)}, f32[38,8,128]{2,1,0:T(8,128)S(1)}, u32[]{:S(2)}, u32[]{:S(2)}) collective-permute-start(f32[38,8,128]{2,1,0:T(8,128)S(1)} %get-tuple-element.21), channel_id=1, source_target_pairs={{0,1},{1,0},{2,3},{3,2},{4,5},{5,4},{6,7},{7,6},{8,9},{9,8},{10,11... | collective-permute-start | bytes 466952 | tf_op jit(solution)/shard_map/ppermute | solution.py:880
  10.2 3.9 %collective-permute-start.3 = (f32[38,8,128]{2,1,0:T(8,128)S(1)}, f32[38,8,128]{2,1,0:T(8,128)S(1)}, u32[]{:S(2)}, u32[]{:S(2)}) collective-permute-start(f32[38,8,128]{2,1,0:T(8,128)S(1)} %get-tuple-element.22), channel_id=1, source_target_pairs={{1,8},{8,1},{9,16},{16,9},{17,24},{24,17},{3,10},{10,3},{11,18},{1... | collective-permute-start | bytes 466952 | tf_op jit(solution)/shard_map/ppermute | solution.py:881
  14.1 1.9 %collective-permute-start.4 = (f32[2,8,128]{2,1,0:T(8,128)S(1)}, f32[2,8,128]{2,1,0:T(8,128)S(1)}, u32[]{:S(2)}, u32[]{:S(2)}) collective-permute-start(f32[2,8,128]{2,1,0:T(8,128)S(1)} %get-tuple-element.23), channel_id=1, source_target_pairs={{0,9},{9,0},{8,17},{17,8},{16,25},{25,16},{2,11},{11,2},{10,19},{1... | collective-permute-start | bytes 24584 | tf_op jit(solution)/shard_map/ppermute | solution.py:882
  16.0 4.5 %collective-permute-done.4.in_h = f32[2,8,128]{2,1,0:T(8,128)S(1)} collective-permute-done((f32[2,8,128]{2,1,0:T(8,128)S(1)}, f32[2,8,128]{2,1,0:T(8,128)S(1)}, u32[]{:S(2)}, u32[]{:S(2)}) %collective-permute-start.4) | collective-permute-done | bytes 8224 | tf_op jit(solution)/shard_map/ppermute | solution.py:882
  20.6 0.7 %shard_map.70 = (f32[87,8,128]{2,1,0:T(8,128)S(1)}, f32[87,8,128]{2,1,0:T(8,128)S(1)}) custom-call(s32[6]{0:T(128)S(1)} %copy-done.3, f32[6,8,16,128]{3,2,1,0:T(8,128)S(1)} %copy-done, f32[8,32,128]{2,1,0:T(8,128)S(1)} %bitcast.8, s32[8,32,128]{2,1,0:T(8,128)S(1)} %bitcast.12, f32[4,8,128]{2,1,0:T(8,128)S(1)} %get-tuple-element.18.own, ...), custom_call_target="tpu_custom_call" | custom-call | tf_op jit(solution)/shard_map/pallas_call | solution.py:885
  21.3 0.1 collective-permute-start.5
  21.4 2.5 %collective-permute-start.6 = (f32[87,8,128]{2,1,0:T(8,128)S(1)}, f32[87,8,128]{2,1,0:T(8,128)S(1)}, u32[]{:S(2)}, u32[]{:S(2)}) collective-permute-start(f32[87,8,128]{2,1,0:T(8,128)S(1)} %get-tuple-element.25), channel_id=1, source_target_pairs={{2,4},{4,2},{3,5},{5,3},{10,12},{12,10},{11,13},{13,11},{18,20},{2... | collective-permute-start | bytes 1069064 | tf_op jit(solution)/shard_map/ppermute | solution.py:888
  24.0 0.1 copy.9.beam
  24.1 6.1 %collective-permute-done.6.gy_b = f32[87,8,128]{2,1,0:T(8,128)S(1)} collective-permute-done((f32[87,8,128]{2,1,0:T(8,128)S(1)}, f32[87,8,128]{2,1,0:T(8,128)S(1)}, u32[]{:S(2)}, u32[]{:S(2)}) %collective-permute-start.6) | collective-permute-done | bytes 356384 | tf_op jit(solution)/shard_map/ppermute | solution.py:888
  30.1 6.6 %shard_map.71 = (f32[6,14,24,128]{3,2,1,0:T(8,128)S(1)}, f32[2,24,128]{2,1,0:T(8,128)S(1)}, f32[6,32,128]{2,1,0:T(8,128)S(1)}, f32[6,32,128]{2,1,0:T(8,128)S(1)}) custom-call(s32[6]{0:T(128)S(1)} %copy-done.3, s32[4,2]{1,0:T(4,128)S(1)} %copy.9.beam, f32[6,8,16,128]{3,2,1,0:T(8,128)S(1)} %copy-done, f32[4,8,128]{2,1,0:T(8,128)S(1)} %get-tuple-element.18.own, ...), custom_call_target="tpu_custom_call" | custom-call | tf_op jit(solution)/shard_map/pallas_call | solution.py:897
  36.7 0.1 collective-permute-start.7
  36.8 2.9 %shard_map.72.bulk = f32[8,32,128]{2,1,0:T(8,128)S(1)} custom-call(s32[6]{0:T(128)S(1)} %copy-done.3, s32[4,2]{1,0:T(4,128)S(1)} %copy.9.beam, f32[8,32,128]{2,1,0:T(8,128)S(1)} %bitcast.9, s32[8,32,128]{2,1,0:T(8,128)S(1)} %bitcast.13, f32[38,8,128]{2,1,0:T(8,128)S(1)} %collective-permute-done.2.in_z, f32[38,8,128]{2,1,0:T(8,128)S(1)} %collective-permute-done.3.in_d, ...), custom_call_target="tpu_custom_call" | custom-call | tf_op jit(solution)/shard_map/pallas_call | solution.py:906
  39.7 0.9 %collective-permute-done.7.in_m = f32[2,24,128]{2,1,0:T(8,128)S(1)} collective-permute-done((f32[2,24,128]{2,1,0:T(8,128)S(1)}, f32[2,24,128]{2,1,0:T(8,128)S(1)}, u32[]{:S(2)}, u32[]{:S(2)}) %collective-permute-start.7) | collective-permute-done | bytes 24608 | tf_op jit(solution)/shard_map/ppermute | solution.py:904
  40.6 3.6 %shard_map.73 = (f32[6,8,16,128]{3,2,1,0:T(8,128)S(1)}, f32[2,8,128]{2,1,0:T(8,128)S(1)}, f32[2,8,128]{2,1,0:T(8,128)S(1)}, f32[32,128]{1,0:T(8,128)S(1)}) custom-call(s32[6]{0:T(128)S(1)} %copy-done.3, s32[4,2]{1,0:T(4,128)S(1)} %copy.9.beam, f32[6,14,24,128]{3,2,1,0:T(8,128)S(1)} %get-tuple-element.26.g, f32[2,24,128]{2,1,0:T(8,128)S(1)} %collective-permute-done.7.in_m, ...), custom_call_target="tpu_custom_call" | custom-call | tf_op jit(solution)/shard_map/pallas_call | solution.py:909
  44.2 1.2 %collective-permute-start.8 = (f32[2,8,128]{2,1,0:T(8,128)S(1)}, f32[2,8,128]{2,1,0:T(8,128)S(1)}, u32[]{:S(2)}, u32[]{:S(2)}) collective-permute-start(f32[2,8,128]{2,1,0:T(8,128)S(1)} %get-tuple-element.33), channel_id=1, source_target_pairs={{0,1},{1,0},{2,3},{3,2},{4,5},{5,4},{6,7},{7,6},{8,9},{9,8},{10,11... | collective-permute-start | bytes 24584 | tf_op jit(solution)/shard_map/ppermute | solution.py:917
  45.5 1.5 %shard_map.74 = f32[6,8,16,128]{3,2,1,0:T(8,128)} custom-call(s32[6]{0:T(128)S(1)} %copy-done.3, f32[6,8,16,128]{3,2,1,0:T(8,128)S(1)} %get-tuple-element.30.gas, f32[2,24,128]{2,1,0:T(8,128)S(1)} %collective-permute-done.7.in_m, f32[32,128]{1,0:T(8,128)S(1)} %get-tuple-element.31.mass), custom_call_target="tpu_custom_call" | custom-call | tf_op jit(solution)/shard_map/pallas_call | solution.py:916
  46.9 1.0 %collective-permute-done.8.given = f32[2,8,128]{2,1,0:T(8,128)S(1)} collective-permute-done((f32[2,8,128]{2,1,0:T(8,128)S(1)}, f32[2,8,128]{2,1,0:T(8,128)S(1)}, u32[]{:S(2)}, u32[]{:S(2)}) %collective-permute-start.8) | collective-permute-done | bytes 8224 | tf_op jit(solution)/shard_map/ppermute | solution.py:917
  48.0 1.3 %shard_map.75 = f32[8,32,128]{2,1,0:T(8,128)} custom-call(s32[6]{0:T(128)S(1)} %copy-done.3, f32[8,32,128]{2,1,0:T(8,128)S(1)} %shard_map.72.bulk, f32[2,8,128]{2,1,0:T(8,128)S(1)} %get-tuple-element.32.mine, f32[2,8,128]{2,1,0:T(8,128)S(1)} %collective-permute-done.8.given), custom_call_target="tpu_custom_call" | custom-call | tf_op jit(solution)/shard_map/pallas_call | solution.py:918
  (17 shorter events, 0.0 us)
Async XLA Ops:
  0.6 7.0 %copy-start = (f32[6,8,16,128]{3,2,1,0:T(8,128)S(1)}, f32[6,8,16,128]{3,2,1,0:T(8,128)}, u32[]{:S(2)}) copy-start(f32[6,8,16,128]{3,2,1,0:T(8,128)} %u.5) | copy-start | bytes 1179652
  1.3 6.4 %copy-start.1 = (f32[128,8,32]{0,2,1:T(8,128)S(1)}, f32[128,8,32]{0,2,1:T(8,128)}, u32[]{:S(2)}) copy-start(f32[128,8,32]{0,2,1:T(8,128)} %param.6) | copy-start | bytes 393220
  1.3 6.4 %copy-start.2 = (s32[128,8,32]{0,2,1:T(8,128)S(1)}, s32[128,8,32]{0,2,1:T(8,128)}, u32[]{:S(2)}) copy-start(s32[128,8,32]{0,2,1:T(8,128)} %param.7) | copy-start | bytes 393220
  1.3 6.4 %copy-start.4 = (s32[8,16]{1,0:T(8,128)S(1)}, s32[8,16]{1,0:T(8,128)}, u32[]{:S(2)}) copy-start(s32[8,16]{1,0:T(8,128)} %lev.1) | copy-start | bytes 1540
  4.0 3.6 %copy-start.3 = (s32[6]{0:T(128)S(1)}, s32[6]{0:T(128)}, u32[]{:S(2)}) copy-start(s32[6]{0:T(128)} %stack.15.meta) | copy-start | bytes 76
  4.0 16.5 %collective-permute-start = (f32[64,8,128]{2,1,0:T(8,128)}, f32[64,8,128]{2,1,0:T(8,128)S(1)}, u32[]{:S(2)}, u32[]{:S(2)}) collective-permute-start(f32[64,8,128]{2,1,0:T(8,128)} %get-tuple-element.19), channel_id=1, source_target_pairs={{0,8},{8,0},{16,24},{24,16},{1,9},{9,1},{17,25},{25,17},{2,10},{10... | collective-permute-start | bytes 786440 | tf_op jit(solution)/shard_map/ppermute | solution.py:878
  5.7 14.9 %collective-permute-start.1 = (f32[64,8,128]{2,1,0:T(8,128)}, f32[64,8,128]{2,1,0:T(8,128)S(1)}, u32[]{:S(2)}, u32[]{:S(2)}) collective-permute-start(f32[64,8,128]{2,1,0:T(8,128)} %get-tuple-element.20), channel_id=1, source_target_pairs={{8,16},{16,8},{9,17},{17,9},{10,18},{18,10},{11,19},{19,11},{12,20... | collective-permute-start | bytes 786440 | tf_op jit(solution)/shard_map/ppermute | solution.py:879
  8.7 11.9 %collective-permute-start.2 = (f32[38,8,128]{2,1,0:T(8,128)S(1)}, f32[38,8,128]{2,1,0:T(8,128)S(1)}, u32[]{:S(2)}, u32[]{:S(2)}) collective-permute-start(f32[38,8,128]{2,1,0:T(8,128)S(1)} %get-tuple-element.21), channel_id=1, source_target_pairs={{0,1},{1,0},{2,3},{3,2},{4,5},{5,4},{6,7},{7,6},{8,9},{9,8},{10,11... | collective-permute-start | bytes 466952 | tf_op jit(solution)/shard_map/ppermute | solution.py:880
  10.2 10.3 %collective-permute-start.3 = (f32[38,8,128]{2,1,0:T(8,128)S(1)}, f32[38,8,128]{2,1,0:T(8,128)S(1)}, u32[]{:S(2)}, u32[]{:S(2)}) collective-permute-start(f32[38,8,128]{2,1,0:T(8,128)S(1)} %get-tuple-element.22), channel_id=1, source_target_pairs={{1,8},{8,1},{9,16},{16,9},{17,24},{24,17},{3,10},{10,3},{11,18},{1... | collective-permute-start | bytes 466952 | tf_op jit(solution)/shard_map/ppermute | solution.py:881
  14.1 6.4 %collective-permute-start.4 = (f32[2,8,128]{2,1,0:T(8,128)S(1)}, f32[2,8,128]{2,1,0:T(8,128)S(1)}, u32[]{:S(2)}, u32[]{:S(2)}) collective-permute-start(f32[2,8,128]{2,1,0:T(8,128)S(1)} %get-tuple-element.23), channel_id=1, source_target_pairs={{0,9},{9,0},{8,17},{17,8},{16,25},{25,16},{2,11},{11,2},{10,19},{1... | collective-permute-start | bytes 24584 | tf_op jit(solution)/shard_map/ppermute | solution.py:882
  21.3 2.6 %copy-start.5 = (s32[4,2]{0,1:T(2,128)S(1)}, s32[4,2]{0,1:T(2,128)}, u32[]{:S(2)}) copy-start(s32[4,2]{0,1:T(2,128)} %param.9) | copy-start | bytes 100
  21.3 2.7 %collective-permute-start.5 = (f32[87,8,128]{2,1,0:T(8,128)S(1)}, f32[87,8,128]{2,1,0:T(8,128)S(1)}, u32[]{:S(2)}, u32[]{:S(2)}) collective-permute-start(f32[87,8,128]{2,1,0:T(8,128)S(1)} %get-tuple-element.24), channel_id=1, source_target_pairs={{0,2},{2,0},{4,6},{6,4},{1,3},{3,1},{5,7},{7,5},{8,10},{10,8},{12,... | collective-permute-start | bytes 1069064 | tf_op jit(solution)/shard_map/ppermute | solution.py:889
  21.4 8.7 %collective-permute-start.6 = (f32[87,8,128]{2,1,0:T(8,128)S(1)}, f32[87,8,128]{2,1,0:T(8,128)S(1)}, u32[]{:S(2)}, u32[]{:S(2)}) collective-permute-start(f32[87,8,128]{2,1,0:T(8,128)S(1)} %get-tuple-element.25), channel_id=1, source_target_pairs={{2,4},{4,2},{3,5},{5,3},{10,12},{12,10},{11,13},{13,11},{18,20},{2... | collective-permute-start | bytes 1069064 | tf_op jit(solution)/shard_map/ppermute | solution.py:888
  36.7 3.9 %collective-permute-start.7 = (f32[2,24,128]{2,1,0:T(8,128)S(1)}, f32[2,24,128]{2,1,0:T(8,128)S(1)}, u32[]{:S(2)}, u32[]{:S(2)}) collective-permute-start(f32[2,24,128]{2,1,0:T(8,128)S(1)} %get-tuple-element.27), channel_id=1, source_target_pairs={{0,1},{1,0},{2,3},{3,2},{4,5},{5,4},{6,7},{7,6},{8,9},{9,8},{10,11... | collective-permute-start | bytes 73736 | tf_op jit(solution)/shard_map/ppermute | solution.py:904
  44.2 3.7 %collective-permute-start.8 = (f32[2,8,128]{2,1,0:T(8,128)S(1)}, f32[2,8,128]{2,1,0:T(8,128)S(1)}, u32[]{:S(2)}, u32[]{:S(2)}) collective-permute-start(f32[2,8,128]{2,1,0:T(8,128)S(1)} %get-tuple-element.33), channel_id=1, source_target_pairs={{0,1},{1,0},{2,3},{3,2},{4,5},{5,4},{6,7},{7,6},{8,9},{9,8},{10,11... | collective-permute-start | bytes 24584 | tf_op jit(solution)/shard_map/ppermute | solution.py:917

commit v5 on v4

--- a/solution.py
+++ b/solution.py
@@ -83,29 +83,29 @@
 QUARTERS = (5, 3, 2, 4)
 
 
-def slab_index(c, layer, tile, tiles):
+def slab_index(c, layer, below):
     if layer <= FULL:
-        return (c * FULL + layer - 1) * tiles + tile
-    base = COMPS * FULL * tiles
+        return c * FULL + (FULL - layer if below else layer - 1)
+    base = COMPS * FULL
     if layer == FULL + 1:
-        return base + DEEP_5.index(c) * tiles + tile if c in DEEP_5 else None
-    base += len(DEEP_5) * tiles
-    return base + DEEP_6.index(c) * tiles + tile if c in DEEP_6 else None
-
-
-def slab_size(tiles):
-    return (COMPS * FULL + len(DEEP_5) + len(DEEP_6)) * tiles
+        return base + DEEP_5.index(c) if c in DEEP_5 else None
+    return base + len(DEEP_5) + DEEP_6.index(c) if c in DEEP_6 else None
+
+
+def slab_size():
+    return COMPS * FULL + len(DEEP_5) + len(DEEP_6)
 
 
 def row_tile(c, x, tile, u, in_a, in_b, even_x):
-    rows_x, tiles = u.shape[1], u.shape[2] // SUBL
+    rows_x = u.shape[1]
+    span = slice(tile * SUBL, (tile + 1) * SUBL)
     if 0 <= x < rows_x:
-        return u[c, x, tile * SUBL : (tile + 1) * SUBL, :]
-    k = slab_index(c, -x if x < 0 else x - rows_x + 1, tile, tiles)
+        return u[c, x, span, :]
+    k = slab_index(c, -x if x < 0 else x - rows_x + 1, x < 0)
     if k is None:
         return None
-    low, high = (in_b[k], in_a[k]) if x < 0 else (in_a[k], in_b[k])
-    return jnp.where(even_x, low, high)
+    low, high = (in_b, in_a) if x < 0 else (in_a, in_b)
+    return jnp.where(even_x, low[k, span, :], high[k, span, :])
 
 
 def conduct(v):
@@ -123,31 +123,40 @@
     return out
 
 
-def gas_kernel(cells, meta, u_in, t_in, m_in, out_a, out_b, u, t, m, sems):
-    copies = [
-        pltpu.make_async_copy(src, dst, sems.at[i]) for i, (src, dst) in enumerate(((t_in, t), (m_in, m), (u_in, u)))
-    ]
+def gas_kernel(reach, meta, u_in, t_in, m_in, out_a, out_b, u, t, m, top, sems):
+    pairs_in = ((u_in, u), (t_in, t), (m_in, m))
+    fetches = [pltpu.make_async_copy(src, dst, sems.at[i]) for i, (src, dst) in enumerate(pairs_in)]
+    for copy in fetches:
+        copy.start()
+    rows_x, own_y = u.shape[1], u.shape[2]
+    even = lax.rem(meta[0], 2) == 0
+    copies = []
+
+    def send(src, dst):
+        copy = pltpu.make_async_copy(src, dst, sems.at[len(fetches) + len(copies)])
+        copy.start()
+        copies.append(copy)
+
+    fetches[0].wait()
+    for out, high in ((out_a, even), (out_b, jnp.logical_not(even))):
+        first = jnp.where(high, rows_x - FULL, 0)
+        for c in range(COMPS):
+            send(u.at[c, pl.ds(first, FULL)], out.at[pl.ds(c * FULL, FULL)])
+        base = COMPS * FULL
+        row = jnp.where(high, rows_x - FULL - 1, FULL)
+        send(u.at[pl.ds(DEEP_5[0], len(DEEP_5)), row], out.at[pl.ds(base, len(DEEP_5))])
+        row = jnp.where(high, rows_x - reach, reach - 1)
+        for j, c in enumerate(DEEP_6):
+            send(u.at[c, row], out.at[base + len(DEEP_5) + j])
+    for copy in fetches[1:]:
+        copy.wait()
+    for j, value in enumerate(surface_tops(t, m)):
+        span = j * SUBL
+        top[span // own_y, span % own_y : span % own_y + SUBL, :] = value
+    for out in (out_a, out_b):
+        send(top, out.at[pl.ds(slab_size(), top.shape[0])])
     for copy in copies:
-        copy.start()
-    rows_x, reach = cells
-    even = lax.rem(meta[0], 2) == 0
-    tiles = u.shape[2] // SUBL
-    copies[0].wait()
-    copies[1].wait()
-    for j, top in enumerate(surface_tops(t, m)):
-        out_a[slab_size(tiles) + j] = top
-        out_b[slab_size(tiles) + j] = top
-    copies[2].wait()
-    for c in range(COMPS):
-        for layer in range(1, reach + 1):
-            for y in range(tiles):
-                n = slab_index(c, layer, y, tiles)
-                if n is None:
-                    continue
-                lo = u[c, layer - 1, y * SUBL : (y + 1) * SUBL, :]
-                hi = u[c, rows_x - layer, y * SUBL : (y + 1) * SUBL, :]
-                out_a[n] = jnp.where(even, hi, lo)
-                out_b[n] = jnp.where(even, lo, hi)
+        copy.wait()
 
 
 def pack_kernel(meta, u, t, m, lev, out_h, out_z, out_d, own):
@@ -197,7 +206,7 @@
     return jnp.where(low_z, low, high)
 
 
-def relay_kernel(cells, meta, u, t, m, own, in_a, in_b, in_z, in_d, in_h, out_a, out_b):
+def relay_kernel(cells, meta, u, t, m, own, in_a, in_b, in_z, in_d, in_h, out_a, out_b, part_a, part_b):
     rows_x, reach = cells
     gx, gy, gz = meta[0], meta[1], meta[2]
     even_x = lax.rem(gx, 2) == 0
@@ -250,8 +259,10 @@
     for r in range(-SKIN, rows + SKIN):
         hi_t, lo_t = [part_row(r, y, t, 0, rows, in_z, in_d, low_z, col_tiles, None) for y in (col_tiles - 1, 0)]
         hi_k, lo_k = [part_row(r, y, m, 1, rows, in_z, in_d, low_z, col_tiles, None) for y in (col_tiles - 1, 0)]
-        put(n, jnp.where(sub < half, turn(hi_k, half, 0), hi_t), jnp.where(sub < half, lo_t, turn(lo_k, half, 0)))
-        n += 1
+        hi = jnp.where(sub < half, turn(hi_k, half, 0), hi_t)
+        lo = jnp.where(sub < half, lo_t, turn(lo_k, half, 0))
+        part_a[r + SKIN] = jnp.where(even_y, hi, lo)
+        part_b[r + SKIN] = jnp.where(even_y, lo, hi)
     sources = surface_sources(own, in_a, in_b, in_z, in_d, even_x, tiles)
     per = LANES // cols
     slot = lax.rem(lane, cols) // SUBL
@@ -266,14 +277,18 @@
 
 def surface_sources(own, in_a, in_b, in_z, in_d, even_x, tiles):
     count = own.shape[0]
-    tail = in_a.shape[0] - count
     at = in_z.shape[0] - tiles - count
+
+    def high(j):
+        k, span = slab_size() + j // tiles, slice(j % tiles * SUBL, (j % tiles + 1) * SUBL)
+        return jnp.where(even_x, in_a[k, span, :], in_b[k, span, :])
+
     out = []
     for a in range(2):
         span = range(a * count // 2, (a + 1) * count // 2)
         out += [own[j] for j in span]
         out += [in_z[at + j] for j in span]
-        out += [jnp.where(even_x, in_a[tail + j], in_b[tail + j]) for j in span]
+        out += [high(j) for j in span]
         out += [in_d[at + j] for j in span]
     return out
 
@@ -296,14 +311,13 @@
     size = cols + SUBL
     n = rows + 2 * SKIN
     sub = iota((SUBL, LANES), 0)
-    base = gy_a.shape[0] - 4 - n
     for i in range(n):
         for y in range(col_tiles):
             span = slice(y * SUBL, (y + 1) * SUBL)
             temp[0, i, span, :] = part_row(i - SKIN, y, t, 0, rows, in_z, in_d, low_z, col_tiles, None)
             cond[i, span, :] = part_row(i - SKIN, y, m, 1, rows, in_z, in_d, low_z, col_tiles, None)
-        up = jnp.where(even_y, gy_a[base + i], gy_b[base + i])
-        low = jnp.where(even_y, gy_b[base + i], gy_a[base + i])
+        up = jnp.where(even_y, gy_a[i], gy_b[i])
+        low = jnp.where(even_y, gy_b[i], gy_a[i])
         temp[0, i, cols:size, :] = jnp.where(sub < half, up, low)
         cond[i, cols:size, :] = turn(jnp.where(sub < half, low, up), half, 0)
 
@@ -392,16 +406,20 @@
         total[c, first:last] = both[:, LANES:].reshape(last - first, size, LANES)
 
 
-def cut_weights(size, low_z):
-    lane = iota((size, LANES), 1)
+def cut_weights(low_z, scale):
+    lane = iota((1, LANES), 1)
     up = (lane == LANES - 1) & low_z
     down = (lane == 0) & jnp.logical_not(low_z)
-    sign = jnp.where(up, 1.0, jnp.where(down, -1.0, 0.0))
-    return sign, jnp.abs(sign)
+    weight = {}
+    for v in sorted(set(VISCOSITY)):
+        side = scale * GAS_STEP * v
+        drift = 0.5 * DRIFT_SPEED * scale * GAS_STEP
+        weight[v] = jnp.where(up, side - drift, jnp.where(down, side + drift, 0.0))
+    return jnp.where(up, 1.0, jnp.where(down, -1.0, 0.0)), weight
 
 
 def stepped(comps, ref, i, diff, total, h, cut, scale, start, size):
-    sign, mark = cut
+    sign, weight = cut
     half = 0.5 * scale * GAS_STEP
     span = pl.ds(start, size)
 
@@ -428,7 +446,7 @@
             scale * (1.0 - 6.0 * GAS_STEP * v) * ref[c, i, span, :]
             + side * (sides + total[c, i, span, :])
             - drift * diff[c, i, span, :]
-            + (side * mark - drift * sign) * across
+            + weight[v] * across
         )
         if c == 2:
             new = new - half * dx(5)
@@ -495,7 +513,7 @@
         out[i - 1] = turn(new[(i - 1) * size : i * size] * mask_of(i, 0, size), -1, 0)
 
 
-def advance(meta, g, h0, h1, f, fh, diff, total, own_x, own_y, store):
+def advance(meta, g, h0, h1, f, fh, diff, total, own_x, own_y, store, unroll):
     n, size = g.shape[1], g.shape[2]
     gx, gy, gz = meta[0], meta[1], meta[2]
     low_z = gz == 0
@@ -503,21 +521,26 @@
     before_y = (size - own_y) // 2
     reach = before - 2
 
+    def mask_y(start, count):
+        y_g = gy * own_y + iota((count, LANES), 0) + start - before_y
+        return jnp.where((y_g >= 0) & (y_g < meta[4] * own_y), 1.0, 0.0)
+
     def mask_of(i, start, count):
         x_g = gx * own_x + i - before
         ok = (x_g >= 0) & (x_g < meta[3] * own_x)
-        y_g = gy * own_y + iota((count, LANES), 0) + start - before_y
-        return jnp.where((y_g >= 0) & (y_g < meta[4] * own_y) & ok, 1.0, 0.0)
+        return mask_y(start, count) * jnp.where(ok, 1.0, 0.0)
 
     matrix = height_matrix()
     halo_stepped(h0, h1, g, low_z, mask_of, fh)
     height_terms(g, 1, n - 1, matrix, diff, total)
     everything = tuple(range(COMPS))
 
+    cut = cut_weights(low_z, 1.0)
+
     def one(comps):
         def body(i, carry):
             count = size - 2
-            new = stepped(comps, g, i, diff, total, h0, cut_weights(count, low_z), 1.0, 1, count)
+            new = stepped(comps, g, i, diff, total, h0, cut, 1.0, 1, count)
             m = mask_of(i, 1, count)
             for c in comps:
                 f[c, i - 1, :count, :] = new[c] * m
@@ -525,7 +548,7 @@
 
         return body
 
-    lax.fori_loop(2, n - 2, one(everything), 0, unroll=2)
+    lax.fori_loop(2, n - 2, one(everything), 0, unroll=unroll)
     for i in (1, n - 2):
         one((2, 5))(i, 0)
 
@@ -533,10 +556,11 @@
     start = before_y - 1 - reach
     count = own_y + 2 * reach
 
+    half_cut = cut_weights(low_z, 0.5)
+
     def two(comps):
         def body(i, carry):
-            cut = cut_weights(count, low_z)
-            new = stepped(comps, f, i - 1, diff, total, fh, cut, 0.5, start, count)
+            new = stepped(comps, f, i - 1, diff, total, fh, half_cut, 0.5, start, count)
             m = mask_of(i, start + 1, count)
             for c in comps:
                 new[c] = (0.5 * g[c, i, pl.ds(start + 1, count), :] + new[c]) * m
@@ -545,9 +569,13 @@
 
         return body
 
-    lax.fori_loop(3, n - 3, two(everything), 0, unroll=2)
+    outer = 1 if reach > 1 else 0
+    lax.fori_loop(3 + outer, n - 3 - outer, two(everything), 0, unroll=unroll)
     for i in (2, n - 3):
         two((5,))(i, 0)
+    if outer:
+        for i in (3, n - 4):
+            two((2, 5))(i, 0)
 
 
 def lane_sums(value):
@@ -698,11 +726,11 @@
 
     def store(i, new):
         p[i - 2] = new[COMPS - 1]
-        if len(new) == COMPS:
+        if len(new) > 1:
             for c in range(COMPS):
-                out_g[c, i - 3] = new[c]
-
-    advance(meta, g, h, h1, f, fh, diff, total, rows_x, own_y, store)
+                out_g[c, i - 3] = new[c] if c in new else jnp.zeros_like(new[COMPS - 1])
+
+    advance(meta, g, h, h1, f, fh, diff, total, rows_x, own_y, store, 4)
     fine = fine_pressure(meta, p, h, rows_x, own_y, mass.shape[0])
 
     cols = LANES // 4
@@ -777,7 +805,7 @@
             for c in range(COMPS):
                 out_g[c, i - 3] = new[c][1 : own_y + 1]
 
-    advance(meta, g, h, h1, f, fh, diff, total, rows_x, own_y, store)
+    advance(meta, g, h, h1, f, fh, diff, total, rows_x, own_y, store, True)
     fine = fine_pressure(meta, p, h, rows_x, own_y, mass.shape[0])
     cols = LANES // 4
     t = [in_t[d] for d in range(TOP - SUBSTEPS)]
@@ -804,11 +832,19 @@
             out_g[c, x] = gas[c, x] + loads[c] * masses[x] if c in loads else gas[c, x]
 
 
-def call(body, outs, scratch=(), scalars=1, count=0):
+def places():
+    axes = ("gx", "gy", "gz")
+    return [lax.axis_index(a) for a in axes] + [lax.axis_size(a) for a in axes]
+
+
+def call(body, outs, scratch=(), scalars=0, count=0):
+    def kernel(*refs):
+        body(places(), *refs)
+
     vmem = pl.BlockSpec(memory_space=pltpu.VMEM)
     smem = pl.BlockSpec(memory_space=pltpu.SMEM)
     return pl.pallas_call(
-        body,
+        kernel,
         out_shape=[jax.ShapeDtypeStruct(s, F32) for s in outs],
         in_specs=[smem] * scalars + [vmem] * count,
         out_specs=[vmem] * len(outs),
@@ -847,46 +883,55 @@
 
 def shards(u, t, m, lev, beam):
     nx, ny, nz = (lax.axis_size(a) for a in ("gx", "gy", "gz"))
-    gx, gy, gz = (lax.axis_index(a) for a in ("gx", "gy", "gz"))
-    meta = jnp.stack([gx, gy, gz, nx, ny, nz]).astype(jnp.int32)
     _, rows_x, own_y, _ = u.shape
     t, m = jnp.transpose(t, (1, 2, 0)), jnp.transpose(m, (1, 2, 0))
     rows, cols, depth = t.shape
     tiles = own_y // SUBL
     block = (SUBL, LANES)
     n_top = 2 * rows * cols // LANES
-    n_x = slab_size(tiles) + n_top
+    top = (n_top // tiles, own_y, LANES)
+    n_x = slab_size() + top[0]
     n_z = 2 * SKIN * cols // SUBL + n_top + tiles
     vmem = pl.BlockSpec(memory_space=pltpu.VMEM)
     hbm = pl.BlockSpec(memory_space=pltpu.HBM)
+    hbm = pl.BlockSpec(memory_space=pltpu.HBM)
+
+    def gas_pack(*refs):
+        gas_kernel(REACH, places(), *refs)
+
+    copies = 5 + 2 * (COMPS + 1 + len(DEEP_6))
     msg_a, msg_b = pl.pallas_call(
-        functools.partial(gas_kernel, (rows_x, REACH)),
-        out_shape=[jax.ShapeDtypeStruct((n_x, *block), F32)] * 2,
-        in_specs=[pl.BlockSpec(memory_space=pltpu.SMEM)] + [hbm] * 3,
-        out_specs=[vmem] * 2,
+        gas_pack,
+        out_shape=[jax.ShapeDtypeStruct((n_x, own_y, LANES), F32)] * 2,
+        in_specs=[hbm] * 3,
+        out_specs=[hbm] * 2,
         scratch_shapes=[
             pltpu.VMEM(u.shape, F32),
             pltpu.VMEM(t.shape, F32),
             pltpu.VMEM(m.shape, jnp.int32),
-            pltpu.SemaphoreType.DMA((3,)),
+            pltpu.VMEM(top, F32),
+            pltpu.SemaphoreType.DMA((copies,)),
         ],
         compiler_params=pltpu.CompilerParams(vmem_limit_bytes=60 * 1024 * 1024),
-    )(meta, u, t, m)
+    )(u, t, m)
     msg_h, msg_z, msg_d, own = call(
         pack_kernel, [(tiles, *block), (n_z, *block), (n_z, *block), (n_top, *block)], count=4
-    )(meta, u, t, m, lev)
+    )(u, t, m, lev)
     in_a = lax.ppermute(msg_a, "gx", pairs(nx, 0))
     in_b = lax.ppermute(msg_b, "gx", pairs(nx, 1))
     in_z = lax.ppermute(msg_z, "gz", pairs(nz, 0))
     in_d = lax.ppermute(msg_d, ("gx", "gz"), cross(nx, nz, True))
     in_h = lax.ppermute(msg_h, ("gx", "gz"), cross(nx, nz, False))
     wide = rows_x + 2 * REACH - 2
-    n_y = wide * COMPS // 2 + rows_x + 2 + 3 + rows + 2 * SKIN + n_top
-    msg_a, msg_b = call(
-        functools.partial(relay_kernel, (rows_x, REACH)), [(n_y, *block), (n_y, *block)], count=9
-    )(meta, u, t, m, own, in_a, in_b, in_z, in_d, in_h)
+    n_y = wide * COMPS // 2 + rows_x + 2 + 3 + n_top
+    n_part = rows + 2 * SKIN
+    msg_a, msg_b, part_a, part_b = call(
+        functools.partial(relay_kernel, (rows_x, REACH)), [(n_y, *block)] * 2 + [(n_part, *block)] * 2, count=9
+    )(u, t, m, own, in_a, in_b, in_z, in_d, in_h)
     gy_b = lax.ppermute(msg_b, "gy", pairs(ny, 1))
     gy_a = lax.ppermute(msg_a, "gy", pairs(ny, 0))
+    part_b = lax.ppermute(part_b, "gy", pairs(ny, 1))
+    part_a = lax.ppermute(part_a, "gy", pairs(ny, 0))
 
     size = own_y + 2 * SUBL
     n = rows_x + 2 * REACH
@@ -898,24 +943,24 @@
         functools.partial(first_kernel, (rows_x, REACH)),
         [(COMPS, n2, small, LANES), (n_m, small, LANES), (TOP - SUBSTEPS, part_rows, LANES), (TOP - SUBSTEPS, part_rows, LANES)],
         scratch=advance_scratch(n, size, own_y + 2 * (REACH - 2), True) + [(part_rows, LANES), (part_rows, *block)],
-        scalars=2,
+        scalars=1,
         count=9,
-    )(meta, beam, u, own, in_a, in_b, in_z, in_d, in_h, gy_a, gy_b)
+    )(beam, u, own, in_a, in_b, in_z, in_d, in_h, gy_a, gy_b)
     in_m = lax.ppermute(msg_m, "gz", pairs(nz, 0))
     part = (rows + 2 * SKIN, cols + SUBL, depth)
     (bulk,) = call(
-        bulk_kernel, [t.shape], scratch=[(2, *part), part, part, part, part], scalars=2, count=6
-    )(meta, beam, t, m, in_z, in_d, gy_a, gy_b)
+        bulk_kernel, [t.shape], scratch=[(2, *part), part, part, part, part], scalars=1, count=6
+    )(beam, t, m, in_z, in_d, part_a, part_b)
     gas, mine, other, mass = call(
         functools.partial(last_kernel, (rows_x, own_y)),
         [u.shape, (n_top // 2, *block), (n_top // 2, *block), (part_rows, LANES)],
         scratch=advance_scratch(n2, small, own_y + 2 * (REACH_LAST - 2), False) + [(part_rows, *block)],
-        scalars=2,
+        scalars=1,
         count=5,
-    )(meta, beam, g2, in_m, top_t, top_k, bulk)
-    (gas,) = call(mass_kernel, [u.shape], scratch=[(n2, small, LANES)] * 2, count=3)(meta, gas, in_m, mass)
+    )(beam, g2, in_m, top_t, top_k, bulk)
+    (gas,) = call(mass_kernel, [u.shape], scratch=[(n2, small, LANES)] * 2, count=3)(gas, in_m, mass)
     given = lax.ppermute(other, "gz", pairs(nz, 0))
-    (out,) = call(seal_kernel, [t.shape], count=3)(meta, bulk, mine, given)
+    (out,) = call(seal_kernel, [t.shape], count=3)(bulk, mine, given)
     return gas, jnp.transpose(out, (2, 0, 1))
 
 

time: 49.7 us -> 44.9 us (0.903)
  Pallas kernels: 20.5 us -> 16.4 us
  waiting for transfers between devices: 12.5 us -> 9.2 us
  starting transfers between devices: 14.8 us -> 17.9 us
  local copies, waits for them, and re-layouts: 0.72 us -> 0.12 us
    ppermute x1, waiting for transfers between devices: 6.05 us -> 2.22 us  [shards(): gy_b = lax.ppermute(msg_b, 'gy', pairs(ny, 1))]
    ppermute x0 -> x2, starting transfers between devices: none -> 3.1 us  [the longest x1 3.03 us: shards(): part_b = lax.ppermute(part_b, 'gy', pairs(ny, 1))]
    pallas_call x3, Pallas kernels: 4.84 us -> 3.06 us  [the longest x1 2.06 us: shards(): pl.pallas_call(gas_pack, out_shape=[jax.ShapeDtypeStruct((n_x, own_y, LAN...]
    pallas_call x1, Pallas kernels: 3.62 us -> 2.77 us  [shards(): call(functools.partial(last_kernel, (rows_x, own_y)), [u.shape, (n_top //...]
    another operation x2 -> x0, local copies, waits for them, and re-layouts: 0.6 us -> none  [the longest x1 0.6 us: shards(): meta = jnp.stack([gx, gy, gz, nx, ny, nz]).astype(jnp.int32)]
    ppermute x1, waiting for transfers between devices: 1.02 us -> 1.56 us  [shards(): given = lax.ppermute(other, 'gz', pairs(nz, 0))]
    pallas_call x1, Pallas kernels: 1 us -> 0.46 us  [shards(): call(pack_kernel, [(tiles, *block), (n_z, *block), (n_z, *block), (n_top,...]
    pallas_call x1, Pallas kernels: 1.49 us -> 0.96 us  [shards(): call(mass_kernel, [u.shape], scratch=[(n2, small, LANES)] * 2, count=3)]
  transfers between devices with their start and end apart: 9 -> 11, of which waited for: 4 -> 4; matrix products, arithmetic and copies ran while one was open for 0% -> 0% of each run, Pallas kernels for 11% -> 24%
where the time goes in v5:
time: 44.9 us; the launch traced here: 44.5 us
  starting transfers between devices  17.9 us (40%)
  Pallas kernels  16.4 us (37%)
  waiting for transfers between devices  9.2 us (20%)
  between operations  0.85 us (2%)
    pallas_call x1, Pallas kernels, shards(): call(functools.partial(first_kernel, (rows_x, REACH)), [(COMPS, n2, small...  6.26 us
    ppermute x1, waiting for transfers between devices, shards(): in_h = lax.ppermute(msg_h, ('gx', 'gz'), cross(nx, nz, False))  4.52 us
    ppermute x1, starting transfers between devices, shards(): in_d = lax.ppermute(msg_d, ('gx', 'gz'), cross(nx, nz, True))  3.85 us
    ppermute x1, starting transfers between devices, shards(): part_b = lax.ppermute(part_b, 'gy', pairs(ny, 1))  3.03 us
    pallas_call x1, Pallas kernels, shards(): call(bulk_kernel, [t.shape], scratch=[(2, *part), part, part, part, part]...  2.9 us
    pallas_call x1, Pallas kernels, shards(): call(functools.partial(last_kernel, (rows_x, own_y)), [u.shape, (n_top //...  2.77 us
    ppermute x1, starting transfers between devices, shards(): gy_b = lax.ppermute(msg_b, 'gy', pairs(ny, 1))  2.53 us
    ppermute x1, waiting for transfers between devices, shards(): gy_b = lax.ppermute(msg_b, 'gy', pairs(ny, 1))  2.22 us
  transfers between devices with their start and end apart: 11, of which 4 were waited for; matrix products, arithmetic and copies ran while one was open for 0% of the time, Pallas kernels for 24%

profile of v5, /device:TPU:18, one launch (start us, length us, event | category | flops | bytes accessed | tf_op | source)
XLA Modules:
  0.0 44.5 jit_solution(6475958857860525185)
XLA Ops:
  0.7 2.1 %shard_map.69 = (f32[32,16,128]{2,1,0:T(8,128)}, f32[32,16,128]{2,1,0:T(8,128)}) custom-call(f32[6,8,16,128]{3,2,1,0:T(8,128)} %refs_1_.1, f32[8,32,128]{2,1,0:T(8,128)} %bitcast.3, s32[8,32,128]{2,1,0:T(8,128)} %bitcast.7), custom_call_target="tpu_custom_call" | custom-call | tf_op jit(solution)/shard_map/pallas_call | solution.py:903
  2.7 1.6 %collective-permute-start = (f32[32,16,128]{2,1,0:T(8,128)}, f32[32,16,128]{2,1,0:T(8,128)S(1)}, u32[]{:S(2)}, u32[]{:S(2)}) collective-permute-start(f32[32,16,128]{2,1,0:T(8,128)} %get-tuple-element.21), channel_id=1, source_target_pairs={{0,8},{8,0},{16,24},{24,16},{1,9},{9,1},{17,25},{25,17},{2,10},{10... | collective-permute-start | bytes 786440 | tf_op jit(solution)/shard_map/ppermute | solution.py:920
  4.4 1.9 %collective-permute-start.1 = (f32[32,16,128]{2,1,0:T(8,128)}, f32[32,16,128]{2,1,0:T(8,128)S(1)}, u32[]{:S(2)}, u32[]{:S(2)}) collective-permute-start(f32[32,16,128]{2,1,0:T(8,128)} %get-tuple-element.22), channel_id=1, source_target_pairs={{8,16},{16,8},{9,17},{17,9},{10,18},{18,10},{11,19},{19,11},{12,20... | collective-permute-start | bytes 786440 | tf_op jit(solution)/shard_map/ppermute | solution.py:921
  6.3 0.5 %shard_map.68 = (f32[2,8,128]{2,1,0:T(8,128)S(1)}, f32[38,8,128]{2,1,0:T(8,128)S(1)}, f32[38,8,128]{2,1,0:T(8,128)S(1)}, f32[4,8,128]{2,1,0:T(8,128)S(1)}) custom-call(f32[6,8,16,128]{3,2,1,0:T(8,128)S(1)} %copy-done, f32[8,32,128]{2,1,0:T(8,128)S(1)} %bitcast.4, s32[8,32,128]{2,1,0:T(8,128)S(1)} %bitcast.8, s32[8,16]{1,0:T(8,128)S(1)} %copy-done.3), custom_call_target="tpu_custom_call" | custom-call | tf_op jit(solution)/shard_map/pallas_call | solution.py:917
  6.8 1.6 %collective-permute-start.2 = (f32[38,8,128]{2,1,0:T(8,128)S(1)}, f32[38,8,128]{2,1,0:T(8,128)S(1)}, u32[]{:S(2)}, u32[]{:S(2)}) collective-permute-start(f32[38,8,128]{2,1,0:T(8,128)S(1)} %get-tuple-element.23), channel_id=1, source_target_pairs={{0,1},{1,0},{2,3},{3,2},{4,5},{5,4},{6,7},{7,6},{8,9},{9,8},{10,11... | collective-permute-start | bytes 466952 | tf_op jit(solution)/shard_map/ppermute | solution.py:922
  8.4 3.9 %collective-permute-start.3 = (f32[38,8,128]{2,1,0:T(8,128)S(1)}, f32[38,8,128]{2,1,0:T(8,128)S(1)}, u32[]{:S(2)}, u32[]{:S(2)}) collective-permute-start(f32[38,8,128]{2,1,0:T(8,128)S(1)} %get-tuple-element.24), channel_id=1, source_target_pairs={{1,8},{8,1},{9,16},{16,9},{17,24},{24,17},{3,10},{10,3},{11,18},{1... | collective-permute-start | bytes 466952 | tf_op jit(solution)/shard_map/ppermute | solution.py:923
  12.2 1.9 %collective-permute-start.4 = (f32[2,8,128]{2,1,0:T(8,128)S(1)}, f32[2,8,128]{2,1,0:T(8,128)S(1)}, u32[]{:S(2)}, u32[]{:S(2)}) collective-permute-start(f32[2,8,128]{2,1,0:T(8,128)S(1)} %get-tuple-element.25), channel_id=1, source_target_pairs={{0,9},{9,0},{8,17},{17,8},{16,25},{25,16},{2,11},{11,2},{10,19},{1... | collective-permute-start | bytes 24584 | tf_op jit(solution)/shard_map/ppermute | solution.py:924
  14.2 4.5 %collective-permute-done.4.refs_8_.refs_7_ = f32[2,8,128]{2,1,0:T(8,128)S(1)} collective-permute-done((f32[2,8,128]{2,1,0:T(8,128)S(1)}, f32[2,8,128]{2,1,0:T(8,128)S(1)}, u32[]{:S(2)}, u32[]{:S(2)}) %collective-permute-start.4) | collective-permute-done | bytes 8224 | tf_op jit(solution)/shard_map/ppermute | solution.py:924
  18.7 0.2 shard_map.70
  18.9 0.1 collective-permute-start.5
  19.0 2.5 %collective-permute-start.6 = (f32[71,8,128]{2,1,0:T(8,128)S(1)}, f32[71,8,128]{2,1,0:T(8,128)S(1)}, u32[]{:S(2)}, u32[]{:S(2)}) collective-permute-start(f32[71,8,128]{2,1,0:T(8,128)S(1)} %get-tuple-element.27), channel_id=1, source_target_pairs={{2,4},{4,2},{3,5},{5,3},{10,12},{12,10},{11,13},{13,11},{18,20},{2... | collective-permute-start | bytes 872456 | tf_op jit(solution)/shard_map/ppermute | solution.py:931
  21.6 0.1 collective-permute-start.8
  21.6 3.0 %collective-permute-start.9 = (f32[16,8,128]{2,1,0:T(8,128)S(1)}, f32[16,8,128]{2,1,0:T(8,128)S(1)}, u32[]{:S(2)}, u32[]{:S(2)}) collective-permute-start(f32[16,8,128]{2,1,0:T(8,128)S(1)} %get-tuple-element.33), channel_id=1, source_target_pairs={{2,4},{4,2},{3,5},{5,3},{10,12},{12,10},{11,13},{13,11},{18,20},{2... | collective-permute-start | bytes 196616 | tf_op jit(solution)/shard_map/ppermute | solution.py:933
  24.7 0.1 copy.9.refs_0_
  24.8 2.2 %collective-permute-done.6.refs_9_ = f32[71,8,128]{2,1,0:T(8,128)S(1)} collective-permute-done((f32[71,8,128]{2,1,0:T(8,128)S(1)}, f32[71,8,128]{2,1,0:T(8,128)S(1)}, u32[]{:S(2)}, u32[]{:S(2)}) %collective-permute-start.6) | collective-permute-done | bytes 290848 | tf_op jit(solution)/shard_map/ppermute | solution.py:931
  27.0 6.3 %shard_map.71 = (f32[6,14,24,128]{3,2,1,0:T(8,128)S(1)}, f32[2,24,128]{2,1,0:T(8,128)S(1)}, f32[6,32,128]{2,1,0:T(8,128)S(1)}, f32[6,32,128]{2,1,0:T(8,128)S(1)}) custom-call(s32[4,2]{1,0:T(4,128)S(1)} %copy.9.refs_0_, f32[6,8,16,128]{3,2,1,0:T(8,128)S(1)} %copy-done, f32[4,8,128]{2,1,0:T(8,128)S(1)} %get-tuple-element.20.refs_3_.refs_2_, ...), custom_call_target="tpu_custom_call" | custom-call | tf_op jit(solution)/shard_map/pallas_call | solution.py:942
  33.3 0.1 collective-permute-start.7
  33.4 2.9 %shard_map.72.refs_5_.refs_0_ = f32[8,32,128]{2,1,0:T(8,128)S(1)} custom-call(s32[4,2]{1,0:T(4,128)S(1)} %copy.9.refs_0_, f32[8,32,128]{2,1,0:T(8,128)S(1)} %bitcast.6, s32[8,32,128]{2,1,0:T(8,128)S(1)} %bitcast.10, f32[38,8,128]{2,1,0:T(8,128)S(1)} %collective-permute-done.2.refs_6_.refs_5_.refs_3_, ...), custom_call_target="tpu_custom_call" | custom-call | tf_op jit(solution)/shard_map/pallas_call | solution.py:951
  36.3 0.9 %collective-permute-done.7.refs_2_.refs_1_ = f32[2,24,128]{2,1,0:T(8,128)S(1)} collective-permute-done((f32[2,24,128]{2,1,0:T(8,128)S(1)}, f32[2,24,128]{2,1,0:T(8,128)S(1)}, u32[]{:S(2)}, u32[]{:S(2)}) %collective-permute-start.7) | collective-permute-done | bytes 24608 | tf_op jit(solution)/shard_map/ppermute | solution.py:949
  37.2 2.8 %shard_map.73 = (f32[6,8,16,128]{3,2,1,0:T(8,128)S(1)}, f32[2,8,128]{2,1,0:T(8,128)S(1)}, f32[2,8,128]{2,1,0:T(8,128)S(1)}, f32[32,128]{1,0:T(8,128)S(1)}) custom-call(s32[4,2]{1,0:T(4,128)S(1)} %copy.9.refs_0_, f32[6,14,24,128]{3,2,1,0:T(8,128)S(1)} %get-tuple-element.28.refs_1_, f32[2,24,128]{2,1,0:T(8,128)S(1)} %collective-permute-done.7.refs_2_.refs_1_, ...), custom_call_target="tpu_custom_call" | custom-call | tf_op jit(solution)/shard_map/pallas_call | solution.py:954
  39.9 1.2 %collective-permute-start.10 = (f32[2,8,128]{2,1,0:T(8,128)S(1)}, f32[2,8,128]{2,1,0:T(8,128)S(1)}, u32[]{:S(2)}, u32[]{:S(2)}) collective-permute-start(f32[2,8,128]{2,1,0:T(8,128)S(1)} %get-tuple-element.37), channel_id=1, source_target_pairs={{0,1},{1,0},{2,3},{3,2},{4,5},{5,4},{6,7},{7,6},{8,9},{9,8},{10,11... | collective-permute-start | bytes 24584 | tf_op jit(solution)/shard_map/ppermute | solution.py:962
  41.1 1.0 %shard_map.74 = f32[6,8,16,128]{3,2,1,0:T(8,128)} custom-call(f32[6,8,16,128]{3,2,1,0:T(8,128)S(1)} %get-tuple-element.34.refs_0_, f32[2,24,128]{2,1,0:T(8,128)S(1)} %collective-permute-done.7.refs_2_.refs_1_, f32[32,128]{1,0:T(8,128)S(1)} %get-tuple-element.35.refs_2_), custom_call_target="tpu_custom_call" | custom-call | tf_op jit(solution)/shard_map/pallas_call | solution.py:961
  42.1 1.6 %collective-permute-done.10.refs_2_ = f32[2,8,128]{2,1,0:T(8,128)S(1)} collective-permute-done((f32[2,8,128]{2,1,0:T(8,128)S(1)}, f32[2,8,128]{2,1,0:T(8,128)S(1)}, u32[]{:S(2)}, u32[]{:S(2)}) %collective-permute-start.10) | collective-permute-done | bytes 8224 | tf_op jit(solution)/shard_map/ppermute | solution.py:962
  43.7 0.8 %shard_map.75 = f32[8,32,128]{2,1,0:T(8,128)} custom-call(f32[8,32,128]{2,1,0:T(8,128)S(1)} %shard_map.72.refs_5_.refs_0_, f32[2,8,128]{2,1,0:T(8,128)S(1)} %get-tuple-element.36.refs_1_, f32[2,8,128]{2,1,0:T(8,128)S(1)} %collective-permute-done.10.refs_2_), custom_call_target="tpu_custom_call" | custom-call | tf_op jit(solution)/shard_map/pallas_call | solution.py:963
  (17 shorter events, 0.0 us)
Async XLA Ops:
  0.6 5.7 %copy-start = (f32[6,8,16,128]{3,2,1,0:T(8,128)S(1)}, f32[6,8,16,128]{3,2,1,0:T(8,128)}, u32[]{:S(2)}) copy-start(f32[6,8,16,128]{3,2,1,0:T(8,128)} %refs_1_.1) | copy-start | bytes 1179652
  0.6 5.7 %copy-start.1 = (f32[128,8,32]{0,2,1:T(8,128)S(1)}, f32[128,8,32]{0,2,1:T(8,128)}, u32[]{:S(2)}) copy-start(f32[128,8,32]{0,2,1:T(8,128)} %param.6) | copy-start | bytes 393220
  0.7 5.7 %copy-start.2 = (s32[128,8,32]{0,2,1:T(8,128)S(1)}, s32[128,8,32]{0,2,1:T(8,128)}, u32[]{:S(2)}) copy-start(s32[128,8,32]{0,2,1:T(8,128)} %param.7) | copy-start | bytes 393220
  0.7 5.7 %copy-start.3 = (s32[8,16]{1,0:T(8,128)S(1)}, s32[8,16]{1,0:T(8,128)}, u32[]{:S(2)}) copy-start(s32[8,16]{1,0:T(8,128)} %refs_3_.1) | copy-start | bytes 1540
  2.7 16.0 %collective-permute-start = (f32[32,16,128]{2,1,0:T(8,128)}, f32[32,16,128]{2,1,0:T(8,128)S(1)}, u32[]{:S(2)}, u32[]{:S(2)}) collective-permute-start(f32[32,16,128]{2,1,0:T(8,128)} %get-tuple-element.21), channel_id=1, source_target_pairs={{0,8},{8,0},{16,24},{24,16},{1,9},{9,1},{17,25},{25,17},{2,10},{10... | collective-permute-start | bytes 786440 | tf_op jit(solution)/shard_map/ppermute | solution.py:920
  4.4 14.3 %collective-permute-start.1 = (f32[32,16,128]{2,1,0:T(8,128)}, f32[32,16,128]{2,1,0:T(8,128)S(1)}, u32[]{:S(2)}, u32[]{:S(2)}) collective-permute-start(f32[32,16,128]{2,1,0:T(8,128)} %get-tuple-element.22), channel_id=1, source_target_pairs={{8,16},{16,8},{9,17},{17,9},{10,18},{18,10},{11,19},{19,11},{12,20... | collective-permute-start | bytes 786440 | tf_op jit(solution)/shard_map/ppermute | solution.py:921
  6.8 11.9 %collective-permute-start.2 = (f32[38,8,128]{2,1,0:T(8,128)S(1)}, f32[38,8,128]{2,1,0:T(8,128)S(1)}, u32[]{:S(2)}, u32[]{:S(2)}) collective-permute-start(f32[38,8,128]{2,1,0:T(8,128)S(1)} %get-tuple-element.23), channel_id=1, source_target_pairs={{0,1},{1,0},{2,3},{3,2},{4,5},{5,4},{6,7},{7,6},{8,9},{9,8},{10,11... | collective-permute-start | bytes 466952 | tf_op jit(solution)/shard_map/ppermute | solution.py:922
  8.4 10.3 %collective-permute-start.3 = (f32[38,8,128]{2,1,0:T(8,128)S(1)}, f32[38,8,128]{2,1,0:T(8,128)S(1)}, u32[]{:S(2)}, u32[]{:S(2)}) collective-permute-start(f32[38,8,128]{2,1,0:T(8,128)S(1)} %get-tuple-element.24), channel_id=1, source_target_pairs={{1,8},{8,1},{9,16},{16,9},{17,24},{24,17},{3,10},{10,3},{11,18},{1... | collective-permute-start | bytes 466952 | tf_op jit(solution)/shard_map/ppermute | solution.py:923
  12.2 6.4 %collective-permute-start.4 = (f32[2,8,128]{2,1,0:T(8,128)S(1)}, f32[2,8,128]{2,1,0:T(8,128)S(1)}, u32[]{:S(2)}, u32[]{:S(2)}) collective-permute-start(f32[2,8,128]{2,1,0:T(8,128)S(1)} %get-tuple-element.25), channel_id=1, source_target_pairs={{0,9},{9,0},{8,17},{17,8},{16,25},{25,16},{2,11},{11,2},{10,19},{1... | collective-permute-start | bytes 24584 | tf_op jit(solution)/shard_map/ppermute | solution.py:924
  18.9 5.9 %collective-permute-start.5 = (f32[71,8,128]{2,1,0:T(8,128)S(1)}, f32[71,8,128]{2,1,0:T(8,128)S(1)}, u32[]{:S(2)}, u32[]{:S(2)}) collective-permute-start(f32[71,8,128]{2,1,0:T(8,128)S(1)} %get-tuple-element.26), channel_id=1, source_target_pairs={{0,2},{2,0},{4,6},{6,4},{1,3},{3,1},{5,7},{7,5},{8,10},{10,8},{12,... | collective-permute-start | bytes 872456 | tf_op jit(solution)/shard_map/ppermute | solution.py:932
  19.0 8.0 %collective-permute-start.6 = (f32[71,8,128]{2,1,0:T(8,128)S(1)}, f32[71,8,128]{2,1,0:T(8,128)S(1)}, u32[]{:S(2)}, u32[]{:S(2)}) collective-permute-start(f32[71,8,128]{2,1,0:T(8,128)S(1)} %get-tuple-element.27), channel_id=1, source_target_pairs={{2,4},{4,2},{3,5},{5,3},{10,12},{12,10},{11,13},{13,11},{18,20},{2... | collective-permute-start | bytes 872456 | tf_op jit(solution)/shard_map/ppermute | solution.py:931
  21.5 3.1 %copy-start.4 = (s32[4,2]{0,1:T(2,128)S(1)}, s32[4,2]{0,1:T(2,128)}, u32[]{:S(2)}) copy-start(s32[4,2]{0,1:T(2,128)} %param.9) | copy-start | bytes 100
  21.6 11.8 %collective-permute-start.8 = (f32[16,8,128]{2,1,0:T(8,128)S(1)}, f32[16,8,128]{2,1,0:T(8,128)S(1)}, u32[]{:S(2)}, u32[]{:S(2)}) collective-permute-start(f32[16,8,128]{2,1,0:T(8,128)S(1)} %get-tuple-element.32), channel_id=1, source_target_pairs={{0,2},{2,0},{4,6},{6,4},{1,3},{3,1},{5,7},{7,5},{8,10},{10,8},{12,... | collective-permute-start | bytes 196616 | tf_op jit(solution)/shard_map/ppermute | solution.py:934
  21.6 11.7 %collective-permute-start.9 = (f32[16,8,128]{2,1,0:T(8,128)S(1)}, f32[16,8,128]{2,1,0:T(8,128)S(1)}, u32[]{:S(2)}, u32[]{:S(2)}) collective-permute-start(f32[16,8,128]{2,1,0:T(8,128)S(1)} %get-tuple-element.33), channel_id=1, source_target_pairs={{2,4},{4,2},{3,5},{5,3},{10,12},{12,10},{11,13},{13,11},{18,20},{2... | collective-permute-start | bytes 196616 | tf_op jit(solution)/shard_map/ppermute | solution.py:933
  33.3 3.9 %collective-permute-start.7 = (f32[2,24,128]{2,1,0:T(8,128)S(1)}, f32[2,24,128]{2,1,0:T(8,128)S(1)}, u32[]{:S(2)}, u32[]{:S(2)}) collective-permute-start(f32[2,24,128]{2,1,0:T(8,128)S(1)} %get-tuple-element.29), channel_id=1, source_target_pairs={{0,1},{1,0},{2,3},{3,2},{4,5},{5,4},{6,7},{7,6},{8,9},{9,8},{10,11... | collective-permute-start | bytes 73736 | tf_op jit(solution)/shard_map/ppermute | solution.py:949
  39.9 3.7 %collective-permute-start.10 = (f32[2,8,128]{2,1,0:T(8,128)S(1)}, f32[2,8,128]{2,1,0:T(8,128)S(1)}, u32[]{:S(2)}, u32[]{:S(2)}) collective-permute-start(f32[2,8,128]{2,1,0:T(8,128)S(1)} %get-tuple-element.37), channel_id=1, source_target_pairs={{0,1},{1,0},{2,3},{3,2},{4,5},{5,4},{6,7},{7,6},{8,9},{9,8},{10,11... | collective-permute-start | bytes 24584 | tf_op jit(solution)/shard_map/ppermute | solution.py:962

commit v6 on v5

--- a/solution.py
+++ b/solution.py
@@ -81,6 +81,12 @@
 DEEP_6 = (2, 5)
 FULL = 4
 QUARTERS = (5, 3, 2, 4)
+NEAR = 3
+
+
+def quarter_rows(rows_x, reach):
+    far = [x for d in range(NEAR + 1, reach) for x in (-d, rows_x + d - 1)]
+    return [(x, 0) for x in far] + [(x, FULL) for x in range(-1, rows_x + 1)]
 
 
 def slab_index(c, layer, below):
@@ -119,17 +125,24 @@
     for ref in (t, m):
         for j in range(rows // per):
             block = ref[j * per : (j + 1) * per].reshape(LANES, LANES)
-            out.append(jnp.transpose(conduct(block) if ref is m else block)[:TOP])
+            out.append(jnp.transpose(block)[:TOP])
     return out
 
 
-def gas_kernel(reach, meta, u_in, t_in, m_in, out_a, out_b, u, t, m, top, sems):
-    pairs_in = ((u_in, u), (t_in, t), (m_in, m))
+def pack_kernel(
+    reach, meta, u_in, t_in, m_in, lev_in, to_a, to_b, to_z, to_d, to_h, to_part,
+    u, m, lev, out_z, out_d, out_h, part, sems,
+):
+    rows_x, own_y = u.shape[1], u.shape[2]
+    rows, cols = m.shape[0], m.shape[1]
+    t, k = part.at[0:rows], part.at[rows : 2 * rows]
+    pairs_in = ((u_in, u), (t_in, t), (m_in, m), (lev_in, lev))
     fetches = [pltpu.make_async_copy(src, dst, sems.at[i]) for i, (src, dst) in enumerate(pairs_in)]
     for copy in fetches:
         copy.start()
-    rows_x, own_y = u.shape[1], u.shape[2]
     even = lax.rem(meta[0], 2) == 0
+    low_z = meta[2] == 0
+    tiles = own_y // SUBL
     copies = []
 
     def send(src, dst):
@@ -138,7 +151,7 @@
         copies.append(copy)
 
     fetches[0].wait()
-    for out, high in ((out_a, even), (out_b, jnp.logical_not(even))):
+    for out, high in ((to_a, even), (to_b, jnp.logical_not(even))):
         first = jnp.where(high, rows_x - FULL, 0)
         for c in range(COMPS):
             send(u.at[c, pl.ds(first, FULL)], out.at[pl.ds(c * FULL, FULL)])
@@ -150,36 +163,27 @@
             send(u.at[c, row], out.at[base + len(DEEP_5) + j])
     for copy in fetches[1:]:
         copy.wait()
-    for j, value in enumerate(surface_tops(t, m)):
-        span = j * SUBL
-        top[span // own_y, span % own_y : span % own_y + SUBL, :] = value
-    for out in (out_a, out_b):
-        send(top, out.at[pl.ds(slab_size(), top.shape[0])])
-    for copy in copies:
-        copy.wait()
-
-
-def pack_kernel(meta, u, t, m, lev, out_h, out_z, out_d, own):
-    low_z = meta[2] == 0
-    rows_x = u.shape[1]
-    tiles = u.shape[2] // SUBL
-    rows, cols = t.shape[0], t.shape[1]
+    k[...] = conduct(m[...])
+    tops = surface_tops(t, k)
+    for j, value in enumerate(tops):
+        part[2 * rows, j * SUBL : (j + 1) * SUBL, :] = value
+    for out in (to_a, to_b):
+        for j in range(cols // own_y):
+            send(part.at[2 * rows, pl.ds(j * own_y, own_y)], out.at[slab_size() + j])
+    send(part, to_part)
     col_tiles = cols // SUBL
     n = 0
-    for source in (lambda v: v, conduct):
-        ref = t if n == 0 else m
+    for ref in (t, k):
         for r in range(SKIN):
             for y in range(col_tiles):
-                lo = source(ref[r, y * SUBL : (y + 1) * SUBL, :])
-                hi = source(ref[rows - SKIN + r, y * SUBL : (y + 1) * SUBL, :])
+                lo = ref[r, y * SUBL : (y + 1) * SUBL, :]
+                hi = ref[rows - SKIN + r, y * SUBL : (y + 1) * SUBL, :]
                 out_z[n] = jnp.where(low_z, hi, lo)
                 out_d[n] = jnp.where(low_z, lo, hi)
                 n += 1
-    tops = surface_tops(t, m)
-    for j, top in enumerate(tops):
-        own[j] = top
-        out_z[n + j] = top
-        out_d[n + j] = top
+    for j, value in enumerate(tops):
+        out_z[n + j] = value
+        out_d[n + j] = value
     n += len(tops)
     size = u.shape[2]
     lane = iota((size, LANES), 1)
@@ -195,18 +199,28 @@
         out_h[y] = part
         out_z[n + y] = part
         out_d[n + y] = part
+    for src, dst in ((out_z, to_z), (out_d, to_d), (out_h, to_h)):
+        send(src, dst)
+    for copy in copies:
+        copy.wait()
+
+
+def hold_kernel(meta, u_in, part_in, u, part):
+    u[...] = u_in[...]
+    part[...] = part_in[...]
 
 
 def part_row(r, tile, ref, at, rows, in_z, in_d, low_z, col_tiles, low_part):
     if 0 <= r < rows:
-        value = ref[r, tile * SUBL : (tile + 1) * SUBL, :]
-        return conduct(value) if at else value
+        return ref[r, tile * SUBL : (tile + 1) * SUBL, :]
     k = (at * SKIN + (r + SKIN if r < 0 else r - rows)) * col_tiles + tile
     low, high = (in_d[k], in_z[k]) if r < 0 else (in_z[k], in_d[k])
     return jnp.where(low_z, low, high)
 
 
-def relay_kernel(cells, meta, u, t, m, own, in_a, in_b, in_z, in_d, in_h, out_a, out_b, part_a, part_b):
+def relay_kernel(cells, meta, u, part, in_a, in_b, in_z, in_d, in_h, out_a, out_b, part_a, part_b):
+    rows = part.shape[0] // 2
+    t, m = part.at[0:rows], part.at[rows : 2 * rows]
     rows_x, reach = cells
     gx, gy, gz = meta[0], meta[1], meta[2]
     even_x = lax.rem(gx, 2) == 0
@@ -229,17 +243,17 @@
         return [zero if v is None else v for v in pair]
 
     n = 0
-    for x in range(1 - reach, rows_x + reach - 1):
+    for x in range(-NEAR, rows_x + NEAR):
         for c in range(0, COMPS, 2):
             (hi0, lo0), (hi1, lo1) = both(c, x), both(c + 1, x)
             put(n, jnp.where(sub < half, turn(hi1, half, 0), hi0), jnp.where(sub < half, lo0, turn(lo1, half, 0)))
             n += 1
-    for x in range(-1, rows_x + 1):
+    for x, skip in quarter_rows(rows_x, reach):
         hi = lo = zero
         for q, c in enumerate(QUARTERS):
             a, b = both(c, x)
-            hi = jnp.where((sub & -2) == 2 * q, turn(a, 2 * q - 2, 0), hi)
-            lo = jnp.where((sub & -2) == 2 * q, turn(b, 2 * q - half, 0), lo)
+            hi = jnp.where((sub & -2) == 2 * q, turn(a, 2 * q - (SUBL - 2 - skip), 0), hi)
+            lo = jnp.where((sub & -2) == 2 * q, turn(b, 2 * q - skip, 0), lo)
         put(n, hi, lo)
         n += 1
     base = in_z.shape[0] - tiles
@@ -263,7 +277,7 @@
         lo = jnp.where(sub < half, lo_t, turn(lo_k, half, 0))
         part_a[r + SKIN] = jnp.where(even_y, hi, lo)
         part_b[r + SKIN] = jnp.where(even_y, lo, hi)
-    sources = surface_sources(own, in_a, in_b, in_z, in_d, even_x, tiles)
+    sources = surface_sources(part, in_a, in_b, in_z, in_d, even_x, tiles)
     per = LANES // cols
     slot = lax.rem(lane, cols) // SUBL
     for v in range(len(sources) // per):
@@ -275,8 +289,8 @@
         put(n + v, hi, lo)
 
 
-def surface_sources(own, in_a, in_b, in_z, in_d, even_x, tiles):
-    count = own.shape[0]
+def surface_sources(part, in_a, in_b, in_z, in_d, even_x, tiles):
+    count = part.shape[1] // SUBL
     at = in_z.shape[0] - tiles - count
 
     def high(j):
@@ -286,7 +300,7 @@
     out = []
     for a in range(2):
         span = range(a * count // 2, (a + 1) * count // 2)
-        out += [own[j] for j in span]
+        out += [part[part.shape[0] - 1, j * SUBL : (j + 1) * SUBL, :] for j in span]
         out += [in_z[at + j] for j in span]
         out += [high(j) for j in span]
         out += [in_d[at + j] for j in span]
@@ -301,7 +315,9 @@
     return LASER_POWER * along_x * along_y
 
 
-def bulk_kernel(meta, beam, t, m, in_z, in_d, gy_a, gy_b, out, temp, cond, kx, ky, kz):
+def bulk_kernel(meta, beam, part, in_z, in_d, gy_a, gy_b, out, temp, cond, kx, ky, kz):
+    rows = part.shape[0] // 2
+    t, m = part.at[0:rows], part.at[rows : 2 * rows]
     gx, gy, gz = meta[0], meta[1], meta[2]
     even_y = lax.rem(gy, 2) == 0
     low_z = gz == 0
@@ -397,10 +413,10 @@
     return (above + jnp.where(j < LANES, -below, below)).astype(jnp.bfloat16)
 
 
-def height_terms(ref, first, last, matrix, diff, total):
-    size = ref.shape[2]
+def height_terms(ref, first, last, matrix, diff, total, start=0):
+    size = diff.shape[2]
     for c in range(COMPS):
-        rows = ref[c, first:last].reshape((last - first) * size, LANES)
+        rows = ref[c, first:last, start : start + size].reshape((last - first) * size, LANES)
         both = jnp.dot(split(rows), matrix, preferred_element_type=F32)
         diff[c, first:last] = both[:, :LANES].reshape(last - first, size, LANES)
         total[c, first:last] = both[:, LANES:].reshape(last - first, size, LANES)
@@ -418,10 +434,11 @@
     return jnp.where(up, 1.0, jnp.where(down, -1.0, 0.0)), weight
 
 
-def stepped(comps, ref, i, diff, total, h, cut, scale, start, size):
+def stepped(comps, ref, i, diff, total, h, cut, scale, start, size, skip=0):
     sign, weight = cut
     half = 0.5 * scale * GAS_STEP
     span = pl.ds(start, size)
+    terms = pl.ds(start - skip, size)
 
     def dx(c):
         return ref[c, i + 1, span, :] - ref[c, i - 1, span, :]
@@ -430,7 +447,7 @@
         return ref[c, i, pl.ds(start + 1, size), :] - ref[c, i, pl.ds(start - 1, size), :]
 
     def dz(c):
-        return diff[c, i, span, :] + sign * h[i, span, 2 * c : 2 * c + 1]
+        return diff[c, i, terms, :] + sign * h[i, span, 2 * c : 2 * c + 1]
 
     spread = half * (dx(2) + dy(3) + dz(4))
     out = {}
@@ -444,8 +461,8 @@
         across = h[i, span, 2 * c : 2 * c + 1]
         new = (
             scale * (1.0 - 6.0 * GAS_STEP * v) * ref[c, i, span, :]
-            + side * (sides + total[c, i, span, :])
-            - drift * diff[c, i, span, :]
+            + side * (sides + total[c, i, terms, :])
+            - drift * diff[c, i, terms, :]
             + weight[v] * across
         )
         if c == 2:
@@ -478,22 +495,26 @@
     return jnp.where(spread | slope, 1.0, 0.0).astype(jnp.bfloat16)
 
 
-def halo_stepped(h0, h1, g, low_z, mask_of, out):
-    n, size = h0.shape[0], h0.shape[1]
+def halo_stepped(h0, h1, g, low_z, mask_of, start, size, out, at):
+    n = h0.shape[0]
+    span = slice(start, start + size)
     rows = (n - 2) * size
     lane = iota((1, LANES), 1)
     more = jnp.where(low_z, 1, 0)
     flat_lane = iota((rows, LANES), 1)
     touch = jnp.zeros((rows, LANES), F32)
     for c in range(COMPS):
-        own = g[c, 1 : n - 1].reshape(rows, LANES)
+        own = g[c, 1 : n - 1, span].reshape(rows, LANES)
         touch = jnp.where(flat_lane == 2 * c, turn(own, 2 * c + more, 1), touch)
-    mid = h0[1 : n - 1].reshape(rows, LANES)
-    east = h0[2:n].reshape(rows, LANES)
-    west = h0[0 : n - 2].reshape(rows, LANES)
-    north = turn(mid, -1, 0)
-    south = turn(mid, 1, 0)
-    behind = h1[1 : n - 1].reshape(rows, LANES)
+    mid = h0[1 : n - 1, span].reshape(rows, LANES)
+    east = h0[2:n, span].reshape(rows, LANES)
+    west = h0[0 : n - 2, span].reshape(rows, LANES)
+    if start:
+        north = h0[1 : n - 1, start + 1 : start + size + 1].reshape(rows, LANES)
+        south = h0[1 : n - 1, start - 1 : start + size - 1].reshape(rows, LANES)
+    else:
+        north, south = turn(mid, -1, 0), turn(mid, 1, 0)
+    behind = h1[1 : n - 1, span].reshape(rows, LANES)
     slopes = [east - west, north - south, jnp.where(low_z, 1.0, -1.0) * (behind - touch)]
     coupled = jnp.dot(
         jnp.concatenate([split(v) for v in slopes], axis=1), couple_matrix(), preferred_element_type=F32
@@ -510,67 +531,66 @@
         + pull * coupled
     )
     for i in range(1, n - 1):
-        out[i - 1] = turn(new[(i - 1) * size : i * size] * mask_of(i, 0, size), -1, 0)
-
-
-def advance(meta, g, h0, h1, f, fh, diff, total, own_x, own_y, store, unroll):
-    n, size = g.shape[1], g.shape[2]
-    gx, gy, gz = meta[0], meta[1], meta[2]
-    low_z = gz == 0
-    before = (n - own_x) // 2
-    before_y = (size - own_y) // 2
-    reach = before - 2
-
-    def mask_y(start, count):
-        y_g = gy * own_y + iota((count, LANES), 0) + start - before_y
-        return jnp.where((y_g >= 0) & (y_g < meta[4] * own_y), 1.0, 0.0)
+        row = new[(i - 1) * size : i * size] * mask_of(i, start, size)
+        if at < 0:
+            row, at_row = turn(row, at, 0), 0
+        else:
+            at_row = at
+        out[i - 1, at_row : at_row + size] = row
+
+
+def grid_masks(meta, n, size, own_x, own_y):
+    before, before_y = (n - own_x) // 2, (size - own_y) // 2
 
     def mask_of(i, start, count):
-        x_g = gx * own_x + i - before
+        x_g = meta[0] * own_x + i - before
         ok = (x_g >= 0) & (x_g < meta[3] * own_x)
-        return mask_y(start, count) * jnp.where(ok, 1.0, 0.0)
-
-    matrix = height_matrix()
-    halo_stepped(h0, h1, g, low_z, mask_of, fh)
-    height_terms(g, 1, n - 1, matrix, diff, total)
-    everything = tuple(range(COMPS))
-
-    cut = cut_weights(low_z, 1.0)
+        y_g = meta[1] * own_y + iota((count, LANES), 0) + start - before_y
+        return jnp.where((y_g >= 0) & (y_g < meta[4] * own_y), 1.0, 0.0) * jnp.where(ok, 1.0, 0.0)
+
+    return mask_of
+
+
+def first_stage(meta, g, h0, windows, f, mask_of, unroll):
+    n = g.shape[1]
+    cut = cut_weights(meta[2] == 0, 1.0)
 
     def one(comps):
         def body(i, carry):
-            count = size - 2
-            new = stepped(comps, g, i, diff, total, h0, cut, 1.0, 1, count)
-            m = mask_of(i, 1, count)
-            for c in comps:
-                f[c, i - 1, :count, :] = new[c] * m
+            for start, size, diff, total, skip, at in windows:
+                new = stepped(comps, g, i, diff, total, h0, cut, 1.0, start, size, skip)
+                m = mask_of(i, start, size)
+                for c in comps:
+                    f[c, i - 1, at : at + size, :] = new[c] * m
             return carry
 
         return body
 
-    lax.fori_loop(2, n - 2, one(everything), 0, unroll=unroll)
+    lax.fori_loop(2, n - 2, one(tuple(range(COMPS))), 0, unroll=unroll)
     for i in (1, n - 2):
         one((2, 5))(i, 0)
 
-    height_terms(f, 1, n - 3, matrix, diff, total)
-    start = before_y - 1 - reach
+
+def second_stage(meta, g, f, fh, diff, total, skip, reach, own_y, mask_of, store, unroll):
+    n = g.shape[1]
+    height_terms(f, 1, n - 3, height_matrix(), diff, total)
+    start = (g.shape[2] - own_y) // 2 - reach
     count = own_y + 2 * reach
-
-    half_cut = cut_weights(low_z, 0.5)
+    cut = cut_weights(meta[2] == 0, 0.5)
 
     def two(comps):
         def body(i, carry):
-            new = stepped(comps, f, i - 1, diff, total, fh, half_cut, 0.5, start, count)
-            m = mask_of(i, start + 1, count)
+            new = stepped(comps, f, i - 1, diff, total, fh, cut, 0.5, start - skip, count)
+            m = mask_of(i, start, count)
             for c in comps:
-                new[c] = (0.5 * g[c, i, pl.ds(start + 1, count), :] + new[c]) * m
+                new[c] = (0.5 * g[c, i, pl.ds(start, count), :] + new[c]) * m
             store(i, new)
             return carry
 
         return body
 
     outer = 1 if reach > 1 else 0
-    lax.fori_loop(3 + outer, n - 3 - outer, two(everything), 0, unroll=unroll)
+    lax.fori_loop(3 + outer, n - 3 - outer, two(tuple(range(COMPS))), 0, unroll=unroll)
     for i in (2, n - 3):
         two((5,))(i, 0)
     if outer:
@@ -665,50 +685,21 @@
     return out
 
 
-def first_kernel(
-    cells, meta, beam, u, own, in_a, in_b, in_z, in_d, in_h, gy_a, gy_b,
-    out_g, out_m, out_t, out_k, g, h, h1, f, fh, diff, total, p, mass, skin,
-):
+def inner_kernel(cells, meta, u, in_a, in_b, in_z, in_d, in_h, g, f, h0, h1, fh, diff, total):
     rows_x, reach = cells
-    gx, gy, gz = meta[0], meta[1], meta[2]
-    even_x = lax.rem(gx, 2) == 0
-    even_y = lax.rem(gy, 2) == 0
-    low_z = gz == 0
+    even_x = lax.rem(meta[0], 2) == 0
+    low_z = meta[2] == 0
     own_y = u.shape[2]
     tiles = own_y // SUBL
-    size = own_y + 2 * SUBL
-    half = SUBL // 2
-    sub = iota((SUBL, LANES), 0)
+    size = g.shape[2]
+    n = g.shape[1]
     zero = jnp.zeros((SUBL, LANES), F32)
-
-    def side(k):
-        upper = jnp.where(even_y, gy_a[k], gy_b[k])
-        lower = jnp.where(even_y, gy_b[k], gy_a[k])
-        return upper, lower
-
-    wide = rows_x + 2 * reach - 2
-    outer = wide * COMPS // 2
     for x in range(-reach, rows_x + reach):
-        i = x + reach
         for c in range(COMPS):
             for y in range(tiles):
                 value = row_tile(c, x, y, u, in_a, in_b, even_x)
-                g[c, i, (y + 1) * SUBL : (y + 2) * SUBL, :] = zero if value is None else value
-            upper = lower = zero
-            if 0 < i < wide + 1:
-                upper, lower = side((i - 1) * COMPS // 2 + c // 2)
-                if c % 2:
-                    upper, lower = turn(upper, half, 0), turn(lower, half, 0)
-            if -1 <= x < rows_x + 1 and c in QUARTERS:
-                q = QUARTERS.index(c)
-                far_up, far_low = side(outer + x + 1)
-                far_up, far_low = turn(far_up, half - 2 * q, 0), turn(far_low, 2 - 2 * q, 0)
-            else:
-                far_up = far_low = zero
-            g[c, i, own_y + SUBL : size, :] = jnp.where(sub < half, upper, jnp.where(sub < half + 2, far_up, 0.0))
-            g[c, i, :SUBL, :] = jnp.where(sub >= half, lower, jnp.where(sub >= half - 2, far_low, 0.0))
+                g[c, x + reach, (y + 1) * SUBL : (y + 2) * SUBL, :] = zero if value is None else value
     base = in_z.shape[0] - tiles
-    packed = []
     for b in range(3):
         parts = []
         for y in range(tiles):
@@ -718,11 +709,73 @@
                 parts.append(in_z[base + y])
             else:
                 parts.append(jnp.where(low_z, in_h[y], in_d[base + y]))
-        upper, lower = side(outer + rows_x + 2 + b)
-        packed.append(jnp.concatenate([lower, *parts, upper], axis=0))
+        unpack_group(jnp.concatenate(parts, axis=0), b, rows_x, reach, low_z, h0, h1, SUBL, own_y)
+    mask_of = grid_masks(meta, n, size, rows_x, own_y)
+    halo_stepped(h0, h1, g, low_z, mask_of, SUBL, own_y, fh, 0)
+    height_terms(g, 1, n - 1, height_matrix(), diff, total, SUBL)
+    first_stage(meta, g, h0, [(SUBL, own_y, diff, total, SUBL, 0)], f, mask_of, 4)
+
+
+def unpack_group(packed, b, rows_x, reach, low_z, h0, h1, start, size):
     for x in range(-reach, rows_x + reach):
-        b, q = divmod(x + rows_x, rows_x)
-        unpack_heights(packed[b], GROUP * q, low_z, h, h1, x + reach)
+        if (x + rows_x) // rows_x == b:
+            base = GROUP * ((x + rows_x) % rows_x)
+            here, other = turn(packed, -base, 1), turn(packed, -base - 1, 1)
+            h0[x + reach, start : start + size] = jnp.where(low_z, here, other)
+            h1[x + reach, start : start + size] = jnp.where(low_z, other, here)
+
+
+def first_kernel(
+    cells, meta, beam, part, in_a, in_b, in_z, in_d, gy_a, gy_b, g_in, f_in, h0_in, h1_in, fh_in,
+    out_g, out_m, out_t, out_k, g, h, h1, f, fh, diff_lo, total_lo, diff_hi, total_hi, diff, total, p, mass, skin,
+):
+    rows_x, reach = cells
+    gx, gy, gz = meta[0], meta[1], meta[2]
+    even_x = lax.rem(gx, 2) == 0
+    even_y = lax.rem(gy, 2) == 0
+    low_z = gz == 0
+    n, size = g.shape[1], g.shape[2]
+    own_y = size - 2 * SUBL
+    tiles = own_y // SUBL
+    half = SUBL // 2
+    sub = iota((SUBL, LANES), 0)
+    zero = jnp.zeros((SUBL, LANES), F32)
+    inner = slice(SUBL, SUBL + own_y)
+
+    def side(k):
+        upper = jnp.where(even_y, gy_a[k], gy_b[k])
+        lower = jnp.where(even_y, gy_b[k], gy_a[k])
+        return upper, lower
+
+    quarter = (rows_x + 2 * NEAR) * COMPS // 2
+    places_of = {}
+    for k, (x, skip) in enumerate(quarter_rows(rows_x, reach)):
+        places_of[x, skip] = quarter + k
+    for x in range(-reach, rows_x + reach):
+        i = x + reach
+        for c in range(COMPS):
+            g[c, i, inner, :] = g_in[c, i, inner, :]
+            upper = lower = zero
+            if -NEAR <= x < rows_x + NEAR:
+                near_up, near_low = side((x + NEAR) * COMPS // 2 + c // 2)
+                if c % 2:
+                    near_up, near_low = turn(near_up, half, 0), turn(near_low, half, 0)
+                upper = jnp.where(sub < half, near_up, 0.0)
+                lower = jnp.where(sub >= half, near_low, 0.0)
+            for skip in (0, FULL):
+                if (x, skip) in places_of and c in QUARTERS:
+                    q = 2 * QUARTERS.index(c)
+                    up, low = side(places_of[x, skip])
+                    upper = jnp.where((sub & -2) == skip, turn(up, skip - q, 0), upper)
+                    lower = jnp.where((sub & -2) == SUBL - 2 - skip, turn(low, SUBL - 2 - skip - q, 0), lower)
+            g[c, i, own_y + SUBL : size, :] = upper
+            g[c, i, :SUBL, :] = lower
+    h[:, inner, :] = h0_in[:, inner, :]
+    h1[:, inner, :] = h1_in[:, inner, :]
+    for b in range(3):
+        upper, lower = side(quarter + len(places_of) + b)
+        unpack_group(lower, b, rows_x, reach, low_z, h, h1, 0, SUBL)
+        unpack_group(upper, b, rows_x, reach, low_z, h, h1, own_y + SUBL, SUBL)
 
     def store(i, new):
         p[i - 2] = new[COMPS - 1]
@@ -730,13 +783,23 @@
             for c in range(COMPS):
                 out_g[c, i - 3] = new[c] if c in new else jnp.zeros_like(new[COMPS - 1])
 
-    advance(meta, g, h, h1, f, fh, diff, total, rows_x, own_y, store, 4)
+    mask_of = grid_masks(meta, n, size, rows_x, own_y)
+    f[:, :, inner, :] = f_in[...]
+    fh[:, inner, :] = fh_in[...]
+    upper_at = size - SUBL - 1
+    windows = []
+    for start, d, t in ((1, diff_lo, total_lo), (upper_at, diff_hi, total_hi)):
+        halo_stepped(h, h1, g, low_z, mask_of, start, SUBL, fh, start)
+        height_terms(g, 1, n - 1, height_matrix(), d, t, start)
+        windows.append((start, SUBL, d, t, start, start))
+    first_stage(meta, g, h, windows, f, mask_of, 4)
+    second_stage(meta, g, f, fh, diff, total, 0, reach - 2, own_y, mask_of, store, 4)
     fine = fine_pressure(meta, p, h, rows_x, own_y, mass.shape[0])
 
     cols = LANES // 4
     per = LANES // cols
     lane = iota((SUBL, LANES), 1)
-    sources = surface_sources(own, in_a, in_b, in_z, in_d, even_x, tiles)
+    sources = surface_sources(part, in_a, in_b, in_z, in_d, even_x, tiles)
     count = len(sources) // 2
     top_at = gy_a.shape[0] - len(sources) // per
     layers = []
@@ -805,7 +868,12 @@
             for c in range(COMPS):
                 out_g[c, i - 3] = new[c][1 : own_y + 1]
 
-    advance(meta, g, h, h1, f, fh, diff, total, rows_x, own_y, store, True)
+    n, size = g.shape[1], g.shape[2]
+    mask_of = grid_masks(meta, n, size, rows_x, own_y)
+    halo_stepped(h, h1, g, meta[2] == 0, mask_of, 0, size, fh, -1)
+    height_terms(g, 1, n - 1, height_matrix(), diff, total)
+    first_stage(meta, g, h, [(1, size - 2, diff, total, 0, 0)], f, mask_of, True)
+    second_stage(meta, g, f, fh, diff, total, 1, REACH_LAST - 2, own_y, mask_of, store, True)
     fine = fine_pressure(meta, p, h, rows_x, own_y, mass.shape[0])
     cols = LANES // 4
     t = [in_t[d] for d in range(TOP - SUBSTEPS)]
@@ -851,19 +919,6 @@
         scratch_shapes=[pltpu.VMEM(s, F32) for s in scratch],
         compiler_params=pltpu.CompilerParams(vmem_limit_bytes=VMEM_LIMIT),
     )
-
-
-def advance_scratch(n, size, count, bricks):
-    row = (size, LANES)
-    return ([(COMPS, n, *row)] if bricks else []) + [
-        (n, *row),
-        (n, *row),
-        (COMPS, n - 2, *row),
-        (n - 2, *row),
-        (COMPS, n - 1, *row),
-        (COMPS, n - 1, *row),
-        (n - 4, count, LANES),
-    ]
 
 
 def pairs(count, odd):
@@ -894,40 +949,34 @@
     n_z = 2 * SKIN * cols // SUBL + n_top + tiles
     vmem = pl.BlockSpec(memory_space=pltpu.VMEM)
     hbm = pl.BlockSpec(memory_space=pltpu.HBM)
-    hbm = pl.BlockSpec(memory_space=pltpu.HBM)
-
-    def gas_pack(*refs):
-        gas_kernel(REACH, places(), *refs)
-
-    copies = 5 + 2 * (COMPS + 1 + len(DEEP_6))
-    msg_a, msg_b = pl.pallas_call(
-        gas_pack,
-        out_shape=[jax.ShapeDtypeStruct((n_x, own_y, LANES), F32)] * 2,
-        in_specs=[hbm] * 3,
-        out_specs=[hbm] * 2,
-        scratch_shapes=[
-            pltpu.VMEM(u.shape, F32),
-            pltpu.VMEM(t.shape, F32),
-            pltpu.VMEM(m.shape, jnp.int32),
-            pltpu.VMEM(top, F32),
-            pltpu.SemaphoreType.DMA((copies,)),
-        ],
+
+    def pack(*refs):
+        pack_kernel(REACH, places(), *refs)
+
+    whole = (2 * rows + 1, cols, depth)
+    copies = 4 + 2 * (COMPS + 1 + len(DEEP_6) + top[0]) + 4
+    shapes = [(n_x, own_y, LANES)] * 2 + [(n_z, *block)] * 2 + [(tiles, *block), whole]
+    msg_a, msg_b, msg_z, msg_d, msg_h, part = pl.pallas_call(
+        pack,
+        out_shape=[jax.ShapeDtypeStruct(v, F32) for v in shapes],
+        in_specs=[hbm] * 4,
+        out_specs=[hbm] * 6,
+        scratch_shapes=[pltpu.VMEM(u.shape, F32), pltpu.VMEM(m.shape, jnp.int32), pltpu.VMEM(lev.shape, jnp.int32)]
+        + [pltpu.VMEM(v, F32) for v in shapes[2:]]
+        + [pltpu.SemaphoreType.DMA((copies,))],
         compiler_params=pltpu.CompilerParams(vmem_limit_bytes=60 * 1024 * 1024),
-    )(u, t, m)
-    msg_h, msg_z, msg_d, own = call(
-        pack_kernel, [(tiles, *block), (n_z, *block), (n_z, *block), (n_top, *block)], count=4
     )(u, t, m, lev)
+    u, part = call(hold_kernel, [u.shape, whole], count=2)(u, part)
     in_a = lax.ppermute(msg_a, "gx", pairs(nx, 0))
     in_b = lax.ppermute(msg_b, "gx", pairs(nx, 1))
     in_z = lax.ppermute(msg_z, "gz", pairs(nz, 0))
     in_d = lax.ppermute(msg_d, ("gx", "gz"), cross(nx, nz, True))
     in_h = lax.ppermute(msg_h, ("gx", "gz"), cross(nx, nz, False))
-    wide = rows_x + 2 * REACH - 2
-    n_y = wide * COMPS // 2 + rows_x + 2 + 3 + n_top
+    n_y = (rows_x + 2 * NEAR) * COMPS // 2 + len(quarter_rows(rows_x, REACH)) + 3 + n_top
     n_part = rows + 2 * SKIN
     msg_a, msg_b, part_a, part_b = call(
-        functools.partial(relay_kernel, (rows_x, REACH)), [(n_y, *block)] * 2 + [(n_part, *block)] * 2, count=9
-    )(u, t, m, own, in_a, in_b, in_z, in_d, in_h)
+        functools.partial(relay_kernel, (rows_x, REACH)), [(n_y, *block)] * 2 + [(n_part, *block)] * 2, count=7
+    )(u, part, in_a, in_b, in_z, in_d, in_h)
     gy_b = lax.ppermute(msg_b, "gy", pairs(ny, 1))
     gy_a = lax.ppermute(msg_a, "gy", pairs(ny, 0))
     part_b = lax.ppermute(part_b, "gy", pairs(ny, 1))
@@ -939,22 +988,41 @@
     small = own_y + SUBL
     part_rows = 4 * SUBL
     n_m = -(-n2 // (LANES // GROUP))
+    row = (size, LANES)
+    own_row = (own_y, LANES)
+    g1, f1, h0, h1, fh1 = call(
+        functools.partial(inner_kernel, (rows_x, REACH)),
+        [(COMPS, n, *row), (COMPS, n - 2, *own_row), (n, *row), (n, *row), (n - 2, *own_row)],
+        scratch=[(COMPS, n - 1, *own_row)] * 2,
+        count=6,
+    )(u, in_a, in_b, in_z, in_d, in_h)
     g2, msg_m, top_t, top_k = call(
         functools.partial(first_kernel, (rows_x, REACH)),
-        [(COMPS, n2, small, LANES), (n_m, small, LANES), (TOP - SUBSTEPS, part_rows, LANES), (TOP - SUBSTEPS, part_rows, LANES)],
-        scratch=advance_scratch(n, size, own_y + 2 * (REACH - 2), True) + [(part_rows, LANES), (part_rows, *block)],
+        [
+            (COMPS, n2, small, LANES),
+            (n_m, small, LANES),
+            (TOP - SUBSTEPS, part_rows, LANES),
+            (TOP - SUBSTEPS, part_rows, LANES),
+        ],
+        scratch=[(COMPS, n, *row), (n, *row), (n, *row), (COMPS, n - 2, *row), (n - 2, *row)]
+        + [(COMPS, n - 1, *block)] * 4
+        + [(COMPS, n - 3, *row)] * 2
+        + [(n - 4, own_y + 2 * (REACH - 2), LANES), (part_rows, LANES), (part_rows, *block)],
         scalars=1,
-        count=9,
-    )(beam, u, own, in_a, in_b, in_z, in_d, in_h, gy_a, gy_b)
+        count=12,
+    )(beam, part, in_a, in_b, in_z, in_d, gy_a, gy_b, g1, f1, h0, h1, fh1)
     in_m = lax.ppermute(msg_m, "gz", pairs(nz, 0))
-    part = (rows + 2 * SKIN, cols + SUBL, depth)
+    field = (rows + 2 * SKIN, cols + SUBL, depth)
     (bulk,) = call(
-        bulk_kernel, [t.shape], scratch=[(2, *part), part, part, part, part], scalars=1, count=6
-    )(beam, t, m, in_z, in_d, part_a, part_b)
+        bulk_kernel, [t.shape], scratch=[(2, *field), field, field, field, field], scalars=1, count=5
+    )(beam, part, in_z, in_d, part_a, part_b)
     gas, mine, other, mass = call(
         functools.partial(last_kernel, (rows_x, own_y)),
         [u.shape, (n_top // 2, *block), (n_top // 2, *block), (part_rows, LANES)],
-        scratch=advance_scratch(n2, small, own_y + 2 * (REACH_LAST - 2), False) + [(part_rows, *block)],
+        scratch=[(n2, small, LANES)] * 2
+        + [(COMPS, n2 - 2, small, LANES), (n2 - 2, small, LANES)]
+        + [(COMPS, n2 - 1, small, LANES)] * 2
+        + [(n2 - 4, own_y + 2 * (REACH_LAST - 2), LANES), (part_rows, *block)],
         scalars=1,
         count=5,
     )(beam, g2, in_m, top_t, top_k, bulk)

time: 44.9 us -> 44 us (0.980)
  waiting for transfers between devices: 9.2 us -> 5.73 us
  local copies, waits for them, and re-layouts: 0.12 us -> 2.04 us
  Pallas kernels: 16.4 us -> 17.2 us
    unnamed x11 -> x7, local copies, waits for them, and re-layouts: 0.12 us -> 2.04 us
    ppermute x1, waiting for transfers between devices: 2.22 us -> 0.32 us  [shards(): gy_b = lax.ppermute(msg_b, 'gy', pairs(ny, 1))]
    ppermute x1, waiting for transfers between devices: 4.52 us -> 2.81 us  [shards(): in_h = lax.ppermute(msg_h, ('gx', 'gz'), cross(nx, nz, False))]
    pallas_call x3 -> x4, Pallas kernels: 5.42 us -> 7.04 us  [the longest x1 2.9 us: shards(): call(bulk_kernel, [t.shape], scratch=[(2, *field), field, field, field, f...]
    pallas_call x1, Pallas kernels: 6.26 us -> 5.46 us  [shards(): call(functools.partial(first_kernel, (rows_x, REACH)), [(COMPS, n2, small...]
  transfers between devices with their start and end apart: 11 -> 11, of which waited for: 4 -> 5; matrix products, arithmetic and copies ran while one was open for 0% -> 0% of each run, Pallas kernels for 24% -> 25%
where the time goes in v6:
time: 44 us; the launch traced here: 43.7 us
  starting transfers between devices  17.9 us (41%)
  Pallas kernels  17.2 us (39%)
  waiting for transfers between devices  5.73 us (13%)
  local copies, waits for them, and re-layouts  2.04 us (5%)
  between operations  0.79 us (2%)
    pallas_call x1, Pallas kernels, shards(): call(functools.partial(first_kernel, (rows_x, REACH)), [(COMPS, n2, small...  5.46 us
    ppermute x1, starting transfers between devices, shards(): in_d = lax.ppermute(msg_d, ('gx', 'gz'), cross(nx, nz, True))  3.85 us
    ppermute x1, starting transfers between devices, shards(): part_b = lax.ppermute(part_b, 'gy', pairs(ny, 1))  3.03 us
    pallas_call x1, Pallas kernels, shards(): call(bulk_kernel, [t.shape], scratch=[(2, *field), field, field, field, f...  2.9 us
    ppermute x1, waiting for transfers between devices, shards(): in_h = lax.ppermute(msg_h, ('gx', 'gz'), cross(nx, nz, False))  2.81 us
    pallas_call x1, Pallas kernels, shards(): call(functools.partial(last_kernel, (rows_x, own_y)), [u.shape, (n_top //...  2.78 us
    pallas_call x1, Pallas kernels, shards(): pl.pallas_call(pack, out_shape=[jax.ShapeDtypeStruct(v, F32) for v in sha...  2.55 us
    ppermute x1, starting transfers between devices, shards(): gy_b = lax.ppermute(msg_b, 'gy', pairs(ny, 1))  2.53 us
  transfers between devices with their start and end apart: 11, of which 5 were waited for; matrix products, arithmetic and copies ran while one was open for 0% of the time, Pallas kernels for 25%

profile of v6, /device:TPU:18, one launch (start us, length us, event | category | flops | bytes accessed | tf_op | source)
XLA Modules:
  0.0 43.7 jit_solution(6109296464899988575)
XLA Ops:
  0.6 2.5 %shard_map.68 = (f32[32,16,128]{2,1,0:T(8,128)}, f32[32,16,128]{2,1,0:T(8,128)}, f32[38,8,128]{2,1,0:T(8,128)}, f32[38,8,128]{2,1,0:T(8,128)}, f32[2,8,128]{2,1,0:T(8,128)}, /*index=5*/f32[17,32,128]{2,1,0:T(8,128)}) custom-call(f32[6,8,16,128]{3,2,1,0:T(8,128)} %refs_0_.6, f32[8,32,128]{2,1,0:T(8,128)} %bitcast.3, s32[8,32,128]{2,1,0:T(8,128)} %bitcast.4, ...), custom_call_target="tpu_custom_call" | custom-call | tf_op jit(solution)/shard_map/pallas_call | solution.py:959
  3.2 1.6 %collective-permute-start = (f32[32,16,128]{2,1,0:T(8,128)}, f32[32,16,128]{2,1,0:T(8,128)S(1)}, u32[]{:S(2)}, u32[]{:S(2)}) collective-permute-start(f32[32,16,128]{2,1,0:T(8,128)} %get-tuple-element.29), channel_id=1, source_target_pairs={{0,8},{8,0},{16,24},{24,16},{1,9},{9,1},{17,25},{25,17},{2,10},{10... | collective-permute-start | bytes 786440 | tf_op jit(solution)/shard_map/ppermute | solution.py:970
  4.8 1.9 %collective-permute-start.1 = (f32[32,16,128]{2,1,0:T(8,128)}, f32[32,16,128]{2,1,0:T(8,128)S(1)}, u32[]{:S(2)}, u32[]{:S(2)}) collective-permute-start(f32[32,16,128]{2,1,0:T(8,128)} %get-tuple-element.30), channel_id=1, source_target_pairs={{8,16},{16,8},{9,17},{17,9},{10,18},{18,10},{11,19},{19,11},{12,20... | collective-permute-start | bytes 786440 | tf_op jit(solution)/shard_map/ppermute | solution.py:971
  6.8 1.6 %collective-permute-start.2 = (f32[38,8,128]{2,1,0:T(8,128)}, f32[38,8,128]{2,1,0:T(8,128)S(1)}, u32[]{:S(2)}, u32[]{:S(2)}) collective-permute-start(f32[38,8,128]{2,1,0:T(8,128)} %get-tuple-element.31), channel_id=1, source_target_pairs={{0,1},{1,0},{2,3},{3,2},{4,5},{5,4},{6,7},{7,6},{8,9},{9,8},{10,11... | collective-permute-start | bytes 466952 | tf_op jit(solution)/shard_map/ppermute | solution.py:972
  8.3 3.9 %collective-permute-start.3 = (f32[38,8,128]{2,1,0:T(8,128)}, f32[38,8,128]{2,1,0:T(8,128)S(1)}, u32[]{:S(2)}, u32[]{:S(2)}) collective-permute-start(f32[38,8,128]{2,1,0:T(8,128)} %get-tuple-element.32), channel_id=1, source_target_pairs={{1,8},{8,1},{9,16},{16,9},{17,24},{24,17},{3,10},{10,3},{11,18},{1... | collective-permute-start | bytes 466952 | tf_op jit(solution)/shard_map/ppermute | solution.py:973
  12.2 1.9 %collective-permute-start.4 = (f32[2,8,128]{2,1,0:T(8,128)}, f32[2,8,128]{2,1,0:T(8,128)S(1)}, u32[]{:S(2)}, u32[]{:S(2)}) collective-permute-start(f32[2,8,128]{2,1,0:T(8,128)} %get-tuple-element.34), channel_id=1, source_target_pairs={{0,9},{9,0},{8,17},{17,8},{16,25},{25,16},{2,11},{11,2},{10,19},{1... | collective-permute-start | bytes 24584 | tf_op jit(solution)/shard_map/ppermute | solution.py:974
  14.1 1.0 %copy-done = f32[6,8,16,128]{3,2,1,0:T(8,128)S(1)} copy-done((f32[6,8,16,128]{3,2,1,0:T(8,128)S(1)}, f32[6,8,16,128]{3,2,1,0:T(8,128)}, u32[]{:S(2)}) %copy-start) | copy-done | bytes 393240
  15.1 1.0 %copy-done.1 = f32[17,32,128]{2,1,0:T(8,128)S(1)} copy-done((f32[17,32,128]{2,1,0:T(8,128)S(1)}, f32[17,32,128]{2,1,0:T(8,128)}, u32[]{:S(2)}) %copy-start.1) | copy-done | bytes 278552
  16.1 2.8 %collective-permute-done.4.refs_6_.refs_5_ = f32[2,8,128]{2,1,0:T(8,128)S(1)} collective-permute-done((f32[2,8,128]{2,1,0:T(8,128)}, f32[2,8,128]{2,1,0:T(8,128)S(1)}, u32[]{:S(2)}, u32[]{:S(2)}) %collective-permute-start.4) | collective-permute-done | bytes 8224 | tf_op jit(solution)/shard_map/ppermute | solution.py:974
  18.9 0.1 collective-permute-done.3.refs_5_.refs_4_.refs_3_
  19.1 0.2 shard_map.70
  19.4 2.5 %collective-permute-start.6 = (f32[63,8,128]{2,1,0:T(8,128)S(1)}, f32[63,8,128]{2,1,0:T(8,128)S(1)}, u32[]{:S(2)}, u32[]{:S(2)}) collective-permute-start(f32[63,8,128]{2,1,0:T(8,128)S(1)} %get-tuple-element.36), channel_id=1, source_target_pairs={{2,4},{4,2},{3,5},{5,3},{10,12},{12,10},{11,13},{13,11},{18,20},{2... | collective-permute-start | bytes 774152 | tf_op jit(solution)/shard_map/ppermute | solution.py:980
  22.0 3.0 %collective-permute-start.9 = (f32[16,8,128]{2,1,0:T(8,128)S(1)}, f32[16,8,128]{2,1,0:T(8,128)S(1)}, u32[]{:S(2)}, u32[]{:S(2)}) collective-permute-start(f32[16,8,128]{2,1,0:T(8,128)S(1)} %get-tuple-element.47), channel_id=1, source_target_pairs={{2,4},{4,2},{3,5},{5,3},{10,12},{12,10},{11,13},{13,11},{18,20},{2... | collective-permute-start | bytes 196616 | tf_op jit(solution)/shard_map/ppermute | solution.py:982
  25.0 0.1 copy.9.refs_0_
  25.1 1.5 %shard_map.71 = (f32[6,20,32,128]{3,2,1,0:T(8,128)S(1)}, f32[6,18,16,128]{3,2,1,0:T(8,128)S(1)}, f32[20,32,128]{2,1,0:T(8,128)S(1)}, f32[20,32,128]{2,1,0:T(8,128)S(1)}, f32[18,16,128]{2,1,0:T(8,128)S(1)}) custom-call(f32[6,8,16,128]{3,2,1,0:T(8,128)S(1)} %get-tuple-element.33.refs_0_, f32[32,16,128]{2,1,0:T(8,128)S(1)} %collective-permute-done.refs_2_.refs_1_, ...), custom_call_target="tpu_custom_call" | custom-call | tf_op jit(solution)/shard_map/pallas_call | solution.py:993
  26.7 0.3 collective-permute-done.6.refs_7_
  27.0 5.5 %shard_map.72 = (f32[6,14,24,128]{3,2,1,0:T(8,128)S(1)}, f32[2,24,128]{2,1,0:T(8,128)S(1)}, f32[6,32,128]{2,1,0:T(8,128)S(1)}, f32[6,32,128]{2,1,0:T(8,128)S(1)}) custom-call(s32[4,2]{1,0:T(4,128)S(1)} %copy.9.refs_0_, f32[17,32,128]{2,1,0:T(8,128)S(1)} %get-tuple-element.28.refs_1_, f32[32,16,128]{2,1,0:T(8,128)S(1)} %collective-permute-done.refs_2_.refs_1_, ...), custom_call_target="tpu_custom_call" | custom-call | tf_op jit(solution)/shard_map/pallas_call | solution.py:999
  32.6 2.9 %shard_map.73.refs_5_.refs_0_ = f32[8,32,128]{2,1,0:T(8,128)S(1)} custom-call(s32[4,2]{1,0:T(4,128)S(1)} %copy.9.refs_0_, f32[17,32,128]{2,1,0:T(8,128)S(1)} %get-tuple-element.28.refs_1_, f32[38,8,128]{2,1,0:T(8,128)S(1)} %collective-permute-done.2.refs_4_.refs_3_.refs_2_, f32[38,8,128]{2,1,0:T(8,128)S(1)} %collective-permute-done.3.refs_5_.refs_4_.refs_3_, ...), custom_call_target="tpu_custom_call" | custom-call | tf_op jit(solution)/shard_map/pallas_call | solution.py:1016
  35.5 0.9 %collective-permute-done.7.refs_2_.refs_1_ = f32[2,24,128]{2,1,0:T(8,128)S(1)} collective-permute-done((f32[2,24,128]{2,1,0:T(8,128)S(1)}, f32[2,24,128]{2,1,0:T(8,128)S(1)}, u32[]{:S(2)}, u32[]{:S(2)}) %collective-permute-start.7) | collective-permute-done | bytes 24608 | tf_op jit(solution)/shard_map/ppermute | solution.py:1014
  36.4 2.8 %shard_map.74 = (f32[6,8,16,128]{3,2,1,0:T(8,128)S(1)}, f32[2,8,128]{2,1,0:T(8,128)S(1)}, f32[2,8,128]{2,1,0:T(8,128)S(1)}, f32[32,128]{1,0:T(8,128)S(1)}) custom-call(s32[4,2]{1,0:T(4,128)S(1)} %copy.9.refs_0_, f32[6,14,24,128]{3,2,1,0:T(8,128)S(1)} %get-tuple-element.42.refs_1_, f32[2,24,128]{2,1,0:T(8,128)S(1)} %collective-permute-done.7.refs_2_.refs_1_, ...), custom_call_target="tpu_custom_call" | custom-call | tf_op jit(solution)/shard_map/pallas_call | solution.py:1019
  39.1 1.2 %collective-permute-start.10 = (f32[2,8,128]{2,1,0:T(8,128)S(1)}, f32[2,8,128]{2,1,0:T(8,128)S(1)}, u32[]{:S(2)}, u32[]{:S(2)}) collective-permute-start(f32[2,8,128]{2,1,0:T(8,128)S(1)} %get-tuple-element.51), channel_id=1, source_target_pairs={{0,1},{1,0},{2,3},{3,2},{4,5},{5,4},{6,7},{7,6},{8,9},{9,8},{10,11... | collective-permute-start | bytes 24584 | tf_op jit(solution)/shard_map/ppermute | solution.py:1030
  40.3 1.0 %shard_map.75 = f32[6,8,16,128]{3,2,1,0:T(8,128)} custom-call(f32[6,8,16,128]{3,2,1,0:T(8,128)S(1)} %get-tuple-element.48.refs_0_, f32[2,24,128]{2,1,0:T(8,128)S(1)} %collective-permute-done.7.refs_2_.refs_1_, f32[32,128]{1,0:T(8,128)S(1)} %get-tuple-element.49.refs_2_), custom_call_target="tpu_custom_call" | custom-call | tf_op jit(solution)/shard_map/pallas_call | solution.py:1029
  41.3 1.6 %collective-permute-done.10.refs_2_ = f32[2,8,128]{2,1,0:T(8,128)S(1)} collective-permute-done((f32[2,8,128]{2,1,0:T(8,128)S(1)}, f32[2,8,128]{2,1,0:T(8,128)S(1)}, u32[]{:S(2)}, u32[]{:S(2)}) %collective-permute-start.10) | collective-permute-done | bytes 8224 | tf_op jit(solution)/shard_map/ppermute | solution.py:1030
  42.9 0.8 %shard_map.76 = f32[8,32,128]{2,1,0:T(8,128)} custom-call(f32[8,32,128]{2,1,0:T(8,128)S(1)} %shard_map.73.refs_5_.refs_0_, f32[2,8,128]{2,1,0:T(8,128)S(1)} %get-tuple-element.50.refs_1_, f32[2,8,128]{2,1,0:T(8,128)S(1)} %collective-permute-done.10.refs_2_), custom_call_target="tpu_custom_call" | custom-call | tf_op jit(solution)/shard_map/pallas_call | solution.py:1031
  (14 shorter events, 0.3 us)
Async XLA Ops:
  0.6 24.4 %copy-start.2 = (s32[4,2]{0,1:T(2,128)S(1)}, s32[4,2]{0,1:T(2,128)}, u32[]{:S(2)}) copy-start(s32[4,2]{0,1:T(2,128)} %param.9) | copy-start | bytes 100
  3.2 15.9 %collective-permute-start = (f32[32,16,128]{2,1,0:T(8,128)}, f32[32,16,128]{2,1,0:T(8,128)S(1)}, u32[]{:S(2)}, u32[]{:S(2)}) collective-permute-start(f32[32,16,128]{2,1,0:T(8,128)} %get-tuple-element.29), channel_id=1, source_target_pairs={{0,8},{8,0},{16,24},{24,16},{1,9},{9,1},{17,25},{25,17},{2,10},{10... | collective-permute-start | bytes 786440 | tf_op jit(solution)/shard_map/ppermute | solution.py:970
  4.8 14.2 %collective-permute-start.1 = (f32[32,16,128]{2,1,0:T(8,128)}, f32[32,16,128]{2,1,0:T(8,128)S(1)}, u32[]{:S(2)}, u32[]{:S(2)}) collective-permute-start(f32[32,16,128]{2,1,0:T(8,128)} %get-tuple-element.30), channel_id=1, source_target_pairs={{8,16},{16,8},{9,17},{17,9},{10,18},{18,10},{11,19},{19,11},{12,20... | collective-permute-start | bytes 786440 | tf_op jit(solution)/shard_map/ppermute | solution.py:971
  6.8 12.2 %collective-permute-start.2 = (f32[38,8,128]{2,1,0:T(8,128)}, f32[38,8,128]{2,1,0:T(8,128)S(1)}, u32[]{:S(2)}, u32[]{:S(2)}) collective-permute-start(f32[38,8,128]{2,1,0:T(8,128)} %get-tuple-element.31), channel_id=1, source_target_pairs={{0,1},{1,0},{2,3},{3,2},{4,5},{5,4},{6,7},{7,6},{8,9},{9,8},{10,11... | collective-permute-start | bytes 466952 | tf_op jit(solution)/shard_map/ppermute | solution.py:972
  8.3 10.7 %collective-permute-start.3 = (f32[38,8,128]{2,1,0:T(8,128)}, f32[38,8,128]{2,1,0:T(8,128)S(1)}, u32[]{:S(2)}, u32[]{:S(2)}) collective-permute-start(f32[38,8,128]{2,1,0:T(8,128)} %get-tuple-element.32), channel_id=1, source_target_pairs={{1,8},{8,1},{9,16},{16,9},{17,24},{24,17},{3,10},{10,3},{11,18},{1... | collective-permute-start | bytes 466952 | tf_op jit(solution)/shard_map/ppermute | solution.py:973
  12.2 6.7 %collective-permute-start.4 = (f32[2,8,128]{2,1,0:T(8,128)}, f32[2,8,128]{2,1,0:T(8,128)S(1)}, u32[]{:S(2)}, u32[]{:S(2)}) collective-permute-start(f32[2,8,128]{2,1,0:T(8,128)} %get-tuple-element.34), channel_id=1, source_target_pairs={{0,9},{9,0},{8,17},{17,8},{16,25},{25,16},{2,11},{11,2},{10,19},{1... | collective-permute-start | bytes 24584 | tf_op jit(solution)/shard_map/ppermute | solution.py:974
  14.1 1.0 %copy-start = (f32[6,8,16,128]{3,2,1,0:T(8,128)S(1)}, f32[6,8,16,128]{3,2,1,0:T(8,128)}, u32[]{:S(2)}) copy-start(f32[6,8,16,128]{3,2,1,0:T(8,128)} %refs_0_.6) | copy-start | bytes 1179652
  15.1 1.0 %copy-start.1 = (f32[17,32,128]{2,1,0:T(8,128)S(1)}, f32[17,32,128]{2,1,0:T(8,128)}, u32[]{:S(2)}) copy-start(f32[17,32,128]{2,1,0:T(8,128)} %get-tuple-element.27.refs_1_) | copy-start | bytes 835588
  19.3 7.4 %collective-permute-start.5 = (f32[63,8,128]{2,1,0:T(8,128)S(1)}, f32[63,8,128]{2,1,0:T(8,128)S(1)}, u32[]{:S(2)}, u32[]{:S(2)}) collective-permute-start(f32[63,8,128]{2,1,0:T(8,128)S(1)} %get-tuple-element.35), channel_id=1, source_target_pairs={{0,2},{2,0},{4,6},{6,4},{1,3},{3,1},{5,7},{7,5},{8,10},{10,8},{12,... | collective-permute-start | bytes 774152 | tf_op jit(solution)/shard_map/ppermute | solution.py:981
  19.4 7.6 %collective-permute-start.6 = (f32[63,8,128]{2,1,0:T(8,128)S(1)}, f32[63,8,128]{2,1,0:T(8,128)S(1)}, u32[]{:S(2)}, u32[]{:S(2)}) collective-permute-start(f32[63,8,128]{2,1,0:T(8,128)S(1)} %get-tuple-element.36), channel_id=1, source_target_pairs={{2,4},{4,2},{3,5},{5,3},{10,12},{12,10},{11,13},{13,11},{18,20},{2... | collective-permute-start | bytes 774152 | tf_op jit(solution)/shard_map/ppermute | solution.py:980
  21.9 10.7 %collective-permute-start.8 = (f32[16,8,128]{2,1,0:T(8,128)S(1)}, f32[16,8,128]{2,1,0:T(8,128)S(1)}, u32[]{:S(2)}, u32[]{:S(2)}) collective-permute-start(f32[16,8,128]{2,1,0:T(8,128)S(1)} %get-tuple-element.46), channel_id=1, source_target_pairs={{0,2},{2,0},{4,6},{6,4},{1,3},{3,1},{5,7},{7,5},{8,10},{10,8},{12,... | collective-permute-start | bytes 196616 | tf_op jit(solution)/shard_map/ppermute | solution.py:983
  22.0 10.6 %collective-permute-start.9 = (f32[16,8,128]{2,1,0:T(8,128)S(1)}, f32[16,8,128]{2,1,0:T(8,128)S(1)}, u32[]{:S(2)}, u32[]{:S(2)}) collective-permute-start(f32[16,8,128]{2,1,0:T(8,128)S(1)} %get-tuple-element.47), channel_id=1, source_target_pairs={{2,4},{4,2},{3,5},{5,3},{10,12},{12,10},{11,13},{13,11},{18,20},{2... | collective-permute-start | bytes 196616 | tf_op jit(solution)/shard_map/ppermute | solution.py:982
  32.5 3.9 %collective-permute-start.7 = (f32[2,24,128]{2,1,0:T(8,128)S(1)}, f32[2,24,128]{2,1,0:T(8,128)S(1)}, u32[]{:S(2)}, u32[]{:S(2)}) collective-permute-start(f32[2,24,128]{2,1,0:T(8,128)S(1)} %get-tuple-element.43), channel_id=1, source_target_pairs={{0,1},{1,0},{2,3},{3,2},{4,5},{5,4},{6,7},{7,6},{8,9},{9,8},{10,11... | collective-permute-start | bytes 73736 | tf_op jit(solution)/shard_map/ppermute | solution.py:1014
  39.1 3.7 %collective-permute-start.10 = (f32[2,8,128]{2,1,0:T(8,128)S(1)}, f32[2,8,128]{2,1,0:T(8,128)S(1)}, u32[]{:S(2)}, u32[]{:S(2)}) collective-permute-start(f32[2,8,128]{2,1,0:T(8,128)S(1)} %get-tuple-element.51), channel_id=1, source_target_pairs={{0,1},{1,0},{2,3},{3,2},{4,5},{5,4},{6,7},{7,6},{8,9},{9,8},{10,11... | collective-permute-start | bytes 24584 | tf_op jit(solution)/shard_map/ppermute | solution.py:1030

commit v7 on v6

--- a/solution.py
+++ b/solution.py
@@ -413,9 +413,9 @@
     return (above + jnp.where(j < LANES, -below, below)).astype(jnp.bfloat16)
 
 
-def height_terms(ref, first, last, matrix, diff, total, start=0):
+def height_terms(ref, first, last, matrix, diff, total, start=0, comps=tuple(range(COMPS))):
     size = diff.shape[2]
-    for c in range(COMPS):
+    for c in comps:
         rows = ref[c, first:last, start : start + size].reshape((last - first) * size, LANES)
         both = jnp.dot(split(rows), matrix, preferred_element_type=F32)
         diff[c, first:last] = both[:, :LANES].reshape(last - first, size, LANES)
@@ -551,7 +551,7 @@
     return mask_of
 
 
-def first_stage(meta, g, h0, windows, f, mask_of, unroll):
+def first_stage(meta, g, h0, windows, f, mask_of, unroll, comps=tuple(range(COMPS)), edge=(2, 5)):
     n = g.shape[1]
     cut = cut_weights(meta[2] == 0, 1.0)
 
@@ -566,14 +566,12 @@
 
         return body
 
-    lax.fori_loop(2, n - 2, one(tuple(range(COMPS))), 0, unroll=unroll)
-    for i in (1, n - 2):
-        one((2, 5))(i, 0)
-
-
-def second_stage(meta, g, f, fh, diff, total, skip, reach, own_y, mask_of, store, unroll):
-    n = g.shape[1]
-    height_terms(f, 1, n - 3, height_matrix(), diff, total)
+    lax.fori_loop(2, n - 2, one(comps), 0, unroll=unroll)
+    for i in (1, n - 2) if edge else ():
+        one(edge)(i, 0)
+
+
+def second_stage(meta, g, f, fh, diff, total, skip, reach, own_y, mask_of, store):
     start = (g.shape[2] - own_y) // 2 - reach
     count = own_y + 2 * reach
     cut = cut_weights(meta[2] == 0, 0.5)
@@ -589,13 +587,15 @@
 
         return body
 
-    outer = 1 if reach > 1 else 0
-    lax.fori_loop(3 + outer, n - 3 - outer, two(tuple(range(COMPS))), 0, unroll=unroll)
-    for i in (2, n - 3):
-        two((5,))(i, 0)
-    if outer:
-        for i in (3, n - 4):
-            two((2, 5))(i, 0)
+    return two
+
+
+class Joined:
+    def __init__(self, low, high):
+        self.low, self.high = low, high
+
+    def __getitem__(self, key):
+        return (self.low if key[0] < self.low.shape[0] else self.high)[key]
 
 
 def lane_sums(value):
@@ -793,7 +793,13 @@
         height_terms(g, 1, n - 1, height_matrix(), d, t, start)
         windows.append((start, SUBL, d, t, start, start))
     first_stage(meta, g, h, windows, f, mask_of, 4)
-    second_stage(meta, g, f, fh, diff, total, 0, reach - 2, own_y, mask_of, store, 4)
+    height_terms(f, 1, n - 3, height_matrix(), diff, total)
+    two = second_stage(meta, g, f, fh, diff, total, 0, reach - 2, own_y, mask_of, store)
+    lax.fori_loop(4, n - 4, two(tuple(range(COMPS))), 0, unroll=4)
+    for i in (2, n - 3):
+        two((5,))(i, 0)
+    for i in (3, n - 4):
+        two((2, 5))(i, 0)
     fine = fine_pressure(meta, p, h, rows_x, own_y, mass.shape[0])
 
     cols = LANES // 4
@@ -855,25 +861,26 @@
 
 
 def last_kernel(
-    cells, meta, beam, g, in_m, in_t, in_k, bulk, out_g, out_t, out_f, mass, h, h1, f, fh, diff, total, p, skin
+    cells, meta, beam, g, in_m, in_t, in_k, bulk, out_t, out_f, mass, p, h, f, fh, h1, diff, total, skin
 ):
     rows_x, own_y = cells
-    for i in range(g.shape[1]):
+    n, size = g.shape[1], g.shape[2]
+    for i in range(n):
         j, q = divmod(i, LANES // GROUP)
         unpack_heights(in_m[j], GROUP * q, meta[2] == 0, h, h1, i)
+    mask_of = grid_masks(meta, n, size, rows_x, own_y)
+    matrix = height_matrix()
+    halo_stepped(h, h1, g, meta[2] == 0, mask_of, 0, size, fh, -1)
+    flow = tuple(range(2, COMPS))
+    height_terms(g, 1, n - 1, matrix, diff, total, 0, flow)
+    first_stage(meta, g, h, [(1, size - 2, diff, total, 0, 0)], f, mask_of, True, flow)
+    height_terms(f, 1, n - 3, matrix, diff, total, 0, (4, 5))
 
     def store(i, new):
         p[i - 2] = new[COMPS - 1]
-        if len(new) == COMPS:
-            for c in range(COMPS):
-                out_g[c, i - 3] = new[c][1 : own_y + 1]
-
-    n, size = g.shape[1], g.shape[2]
-    mask_of = grid_masks(meta, n, size, rows_x, own_y)
-    halo_stepped(h, h1, g, meta[2] == 0, mask_of, 0, size, fh, -1)
-    height_terms(g, 1, n - 1, height_matrix(), diff, total)
-    first_stage(meta, g, h, [(1, size - 2, diff, total, 0, 0)], f, mask_of, True)
-    second_stage(meta, g, f, fh, diff, total, 1, REACH_LAST - 2, own_y, mask_of, store, True)
+
+    two = second_stage(meta, g, f, fh, diff, total, 1, REACH_LAST - 2, own_y, mask_of, store)
+    lax.fori_loop(2, n - 2, two((COMPS - 1,)), 0, unroll=True)
     fine = fine_pressure(meta, p, h, rows_x, own_y, mass.shape[0])
     cols = LANES // 4
     t = [in_t[d] for d in range(TOP - SUBSTEPS)]
@@ -887,17 +894,28 @@
     mass[...] = vapor_mass(t[0], fine)
 
 
-def mass_kernel(meta, gas, in_m, mass, out_g, h, h1):
-    rows_x, own_y = gas.shape[1], gas.shape[2]
-    n = h.shape[0]
-    for i in range((n - rows_x) // 2, (n + rows_x) // 2):
-        j, q = divmod(i, LANES // GROUP)
-        unpack_heights(in_m[j], GROUP * q, meta[2] == 0, h, h1, i)
+def gas_kernel(meta, g, mass, p, h, flow, fh, out_g, f, diff, total):
+    rows_x, own_y = out_g.shape[1], out_g.shape[2]
+    n, size = g.shape[1], g.shape[2]
+    matrix = height_matrix()
+    height_terms(g, 1, n - 1, matrix, diff, total, 0, (0, 1, 4))
+    mask_of = grid_masks(meta, n, size, rows_x, own_y)
+    first_stage(meta, g, h, [(1, size - 2, diff, total, 0, 0)], f, mask_of, True, (0, 1), ())
+    both = Joined(f, flow)
+    height_terms(both, 2, n - 4, matrix, diff, total, 0, tuple(range(COMPS)))
     masses = mass_rows(meta, h, mass, 0, rows_x, own_y, own_y)
     loads = {0: VAPOR_SOURCE, 4: RECOIL_PUSH, 5: RECOIL_PRESSURE}
-    for x in range(rows_x):
-        for c in range(COMPS):
-            out_g[c, x] = gas[c, x] + loads[c] * masses[x] if c in loads else gas[c, x]
+
+    def store(i, new):
+        x = i - (n - rows_x) // 2
+        for c in new:
+            out_g[c, x] = new[c] + loads[c] * masses[x] if c in loads else new[c]
+
+    two = second_stage(meta, g, both, fh, diff, total, 1, 0, own_y, lambda i, start, count: 1.0, store)
+    for i in range(REACH_LAST, n - REACH_LAST):
+        two(tuple(range(COMPS - 1)))(i, 0)
+        x = i - (n - rows_x) // 2
+        out_g[COMPS - 1, x] = p[i - 2, 1 : own_y + 1] + RECOIL_PRESSURE * masses[x]
 
 
 def places():
@@ -1016,17 +1034,28 @@
     (bulk,) = call(
         bulk_kernel, [t.shape], scratch=[(2, *field), field, field, field, field], scalars=1, count=5
     )(beam, part, in_z, in_d, part_a, part_b)
-    gas, mine, other, mass = call(
+    low_row = (small, LANES)
+    mine, other, mass, p, h, f, fh = call(
         functools.partial(last_kernel, (rows_x, own_y)),
-        [u.shape, (n_top // 2, *block), (n_top // 2, *block), (part_rows, LANES)],
-        scratch=[(n2, small, LANES)] * 2
-        + [(COMPS, n2 - 2, small, LANES), (n2 - 2, small, LANES)]
-        + [(COMPS, n2 - 1, small, LANES)] * 2
-        + [(n2 - 4, own_y + 2 * (REACH_LAST - 2), LANES), (part_rows, *block)],
+        [
+            (n_top // 2, *block),
+            (n_top // 2, *block),
+            (part_rows, LANES),
+            (n2 - 4, own_y + 2 * (REACH_LAST - 2), LANES),
+            (n2, *low_row),
+            (COMPS, n2 - 2, *low_row),
+            (n2 - 2, *low_row),
+        ],
+        scratch=[(n2, *low_row)] + [(COMPS, n2 - 1, *low_row)] * 2 + [(part_rows, *block)],
         scalars=1,
         count=5,
     )(beam, g2, in_m, top_t, top_k, bulk)
-    (gas,) = call(mass_kernel, [u.shape], scratch=[(n2, small, LANES)] * 2, count=3)(gas, in_m, mass)
+    (gas,) = call(
+        gas_kernel,
+        [u.shape],
+        scratch=[(2, n2 - 2, *low_row)] + [(COMPS, n2 - 1, *low_row)] * 2,
+        count=6,
+    )(g2, mass, p, h, f, fh)
     given = lax.ppermute(other, "gz", pairs(nz, 0))
     (out,) = call(seal_kernel, [t.shape], count=3)(bulk, mine, given)
     return gas, jnp.transpose(out, (2, 0, 1))

time: 44 us -> 43.4 us (0.986)
  waiting for transfers between devices: 5.73 us -> 5.05 us
    ppermute x1, waiting for transfers between devices: 1.57 us -> 0.89 us  [shards(): given = lax.ppermute(other, 'gz', pairs(nz, 0))]
  transfers between devices with their start and end apart: 11 -> 11, of which waited for: 5 -> 5; matrix products, arithmetic and copies ran while one was open for 0% -> 0% of each run, Pallas kernels for 25% -> 27%
where the time goes in v7:
time: 43.4 us; the launch traced here: 43.1 us
  starting transfers between devices  17.9 us (41%)
  Pallas kernels  17.3 us (40%)
  waiting for transfers between devices  5.05 us (12%)
  local copies, waits for them, and re-layouts  2.04 us (5%)
  between operations  0.79 us (2%)
    pallas_call x1, Pallas kernels, shards(): call(functools.partial(first_kernel, (rows_x, REACH)), [(COMPS, n2, small...  5.46 us
    ppermute x1, starting transfers between devices, shards(): in_d = lax.ppermute(msg_d, ('gx', 'gz'), cross(nx, nz, True))  3.85 us
    ppermute x1, starting transfers between devices, shards(): part_b = lax.ppermute(part_b, 'gy', pairs(ny, 1))  3.03 us
    pallas_call x1, Pallas kernels, shards(): call(bulk_kernel, [t.shape], scratch=[(2, *field), field, field, field, f...  2.9 us
    ppermute x1, waiting for transfers between devices, shards(): in_h = lax.ppermute(msg_h, ('gx', 'gz'), cross(nx, nz, False))  2.81 us
    pallas_call x1, Pallas kernels, shards(): pl.pallas_call(pack, out_shape=[jax.ShapeDtypeStruct(v, F32) for v in sha...  2.55 us
    ppermute x1, starting transfers between devices, shards(): gy_b = lax.ppermute(msg_b, 'gy', pairs(ny, 1))  2.53 us
    pallas_call x1, Pallas kernels, shards(): call(functools.partial(last_kernel, (rows_x, own_y)), [(n_top // 2, *bloc...  2.21 us
  transfers between devices with their start and end apart: 11, of which 5 were waited for; matrix products, arithmetic and copies ran while one was open for 0% of the time, Pallas kernels for 27%

profile of v7, /device:TPU:18, one launch (start us, length us, event | category | flops | bytes accessed | tf_op | source)
XLA Modules:
  0.0 43.1 jit_solution(7993483757888678727)
XLA Ops:
  0.6 2.5 %shard_map.68 = (f32[32,16,128]{2,1,0:T(8,128)}, f32[32,16,128]{2,1,0:T(8,128)}, f32[38,8,128]{2,1,0:T(8,128)}, f32[38,8,128]{2,1,0:T(8,128)}, f32[2,8,128]{2,1,0:T(8,128)}, /*index=5*/f32[17,32,128]{2,1,0:T(8,128)}) custom-call(f32[6,8,16,128]{3,2,1,0:T(8,128)} %refs_0_.6, f32[8,32,128]{2,1,0:T(8,128)} %bitcast.3, s32[8,32,128]{2,1,0:T(8,128)} %bitcast.4, ...), custom_call_target="tpu_custom_call" | custom-call | tf_op jit(solution)/shard_map/pallas_call | solution.py:977
  3.2 1.6 %collective-permute-start = (f32[32,16,128]{2,1,0:T(8,128)}, f32[32,16,128]{2,1,0:T(8,128)S(1)}, u32[]{:S(2)}, u32[]{:S(2)}) collective-permute-start(f32[32,16,128]{2,1,0:T(8,128)} %get-tuple-element.32), channel_id=1, source_target_pairs={{0,8},{8,0},{16,24},{24,16},{1,9},{9,1},{17,25},{25,17},{2,10},{10... | collective-permute-start | bytes 786440 | tf_op jit(solution)/shard_map/ppermute | solution.py:988
  4.8 1.9 %collective-permute-start.1 = (f32[32,16,128]{2,1,0:T(8,128)}, f32[32,16,128]{2,1,0:T(8,128)S(1)}, u32[]{:S(2)}, u32[]{:S(2)}) collective-permute-start(f32[32,16,128]{2,1,0:T(8,128)} %get-tuple-element.33), channel_id=1, source_target_pairs={{8,16},{16,8},{9,17},{17,9},{10,18},{18,10},{11,19},{19,11},{12,20... | collective-permute-start | bytes 786440 | tf_op jit(solution)/shard_map/ppermute | solution.py:989
  6.8 1.6 %collective-permute-start.2 = (f32[38,8,128]{2,1,0:T(8,128)}, f32[38,8,128]{2,1,0:T(8,128)S(1)}, u32[]{:S(2)}, u32[]{:S(2)}) collective-permute-start(f32[38,8,128]{2,1,0:T(8,128)} %get-tuple-element.34), channel_id=1, source_target_pairs={{0,1},{1,0},{2,3},{3,2},{4,5},{5,4},{6,7},{7,6},{8,9},{9,8},{10,11... | collective-permute-start | bytes 466952 | tf_op jit(solution)/shard_map/ppermute | solution.py:990
  8.3 3.9 %collective-permute-start.3 = (f32[38,8,128]{2,1,0:T(8,128)}, f32[38,8,128]{2,1,0:T(8,128)S(1)}, u32[]{:S(2)}, u32[]{:S(2)}) collective-permute-start(f32[38,8,128]{2,1,0:T(8,128)} %get-tuple-element.35), channel_id=1, source_target_pairs={{1,8},{8,1},{9,16},{16,9},{17,24},{24,17},{3,10},{10,3},{11,18},{1... | collective-permute-start | bytes 466952 | tf_op jit(solution)/shard_map/ppermute | solution.py:991
  12.2 1.9 %collective-permute-start.4 = (f32[2,8,128]{2,1,0:T(8,128)}, f32[2,8,128]{2,1,0:T(8,128)S(1)}, u32[]{:S(2)}, u32[]{:S(2)}) collective-permute-start(f32[2,8,128]{2,1,0:T(8,128)} %get-tuple-element.37), channel_id=1, source_target_pairs={{0,9},{9,0},{8,17},{17,8},{16,25},{25,16},{2,11},{11,2},{10,19},{1... | collective-permute-start | bytes 24584 | tf_op jit(solution)/shard_map/ppermute | solution.py:992
  14.1 1.0 %copy-done = f32[6,8,16,128]{3,2,1,0:T(8,128)S(1)} copy-done((f32[6,8,16,128]{3,2,1,0:T(8,128)S(1)}, f32[6,8,16,128]{3,2,1,0:T(8,128)}, u32[]{:S(2)}) %copy-start) | copy-done | bytes 393240
  15.1 1.0 %copy-done.1 = f32[17,32,128]{2,1,0:T(8,128)S(1)} copy-done((f32[17,32,128]{2,1,0:T(8,128)S(1)}, f32[17,32,128]{2,1,0:T(8,128)}, u32[]{:S(2)}) %copy-start.1) | copy-done | bytes 278552
  16.1 2.8 %collective-permute-done.4.refs_6_.refs_5_ = f32[2,8,128]{2,1,0:T(8,128)S(1)} collective-permute-done((f32[2,8,128]{2,1,0:T(8,128)}, f32[2,8,128]{2,1,0:T(8,128)S(1)}, u32[]{:S(2)}, u32[]{:S(2)}) %collective-permute-start.4) | collective-permute-done | bytes 8224 | tf_op jit(solution)/shard_map/ppermute | solution.py:992
  18.9 0.1 collective-permute-done.3.refs_5_.refs_4_.refs_3_
  19.1 0.2 shard_map.70
  19.4 2.5 %collective-permute-start.6 = (f32[63,8,128]{2,1,0:T(8,128)S(1)}, f32[63,8,128]{2,1,0:T(8,128)S(1)}, u32[]{:S(2)}, u32[]{:S(2)}) collective-permute-start(f32[63,8,128]{2,1,0:T(8,128)S(1)} %get-tuple-element.39), channel_id=1, source_target_pairs={{2,4},{4,2},{3,5},{5,3},{10,12},{12,10},{11,13},{13,11},{18,20},{2... | collective-permute-start | bytes 774152 | tf_op jit(solution)/shard_map/ppermute | solution.py:998
  22.0 3.0 %collective-permute-start.9 = (f32[16,8,128]{2,1,0:T(8,128)S(1)}, f32[16,8,128]{2,1,0:T(8,128)S(1)}, u32[]{:S(2)}, u32[]{:S(2)}) collective-permute-start(f32[16,8,128]{2,1,0:T(8,128)S(1)} %get-tuple-element.50), channel_id=1, source_target_pairs={{2,4},{4,2},{3,5},{5,3},{10,12},{12,10},{11,13},{13,11},{18,20},{2... | collective-permute-start | bytes 196616 | tf_op jit(solution)/shard_map/ppermute | solution.py:1000
  25.0 0.1 copy.7.refs_0_
  25.1 1.5 %shard_map.71 = (f32[6,20,32,128]{3,2,1,0:T(8,128)S(1)}, f32[6,18,16,128]{3,2,1,0:T(8,128)S(1)}, f32[20,32,128]{2,1,0:T(8,128)S(1)}, f32[20,32,128]{2,1,0:T(8,128)S(1)}, f32[18,16,128]{2,1,0:T(8,128)S(1)}) custom-call(f32[6,8,16,128]{3,2,1,0:T(8,128)S(1)} %get-tuple-element.36.refs_0_, f32[32,16,128]{2,1,0:T(8,128)S(1)} %collective-permute-done.refs_2_.refs_1_, ...), custom_call_target="tpu_custom_call" | custom-call | tf_op jit(solution)/shard_map/pallas_call | solution.py:1011
  26.7 0.3 collective-permute-done.6.refs_7_
  27.0 5.5 %shard_map.72 = (f32[6,14,24,128]{3,2,1,0:T(8,128)S(1)}, f32[2,24,128]{2,1,0:T(8,128)S(1)}, f32[6,32,128]{2,1,0:T(8,128)S(1)}, f32[6,32,128]{2,1,0:T(8,128)S(1)}) custom-call(s32[4,2]{1,0:T(4,128)S(1)} %copy.7.refs_0_, f32[17,32,128]{2,1,0:T(8,128)S(1)} %get-tuple-element.31.refs_1_, f32[32,16,128]{2,1,0:T(8,128)S(1)} %collective-permute-done.refs_2_.refs_1_, ...), custom_call_target="tpu_custom_call" | custom-call | tf_op jit(solution)/shard_map/pallas_call | solution.py:1017
  32.6 2.9 %shard_map.73.refs_5_.refs_0_ = f32[8,32,128]{2,1,0:T(8,128)S(1)} custom-call(s32[4,2]{1,0:T(4,128)S(1)} %copy.7.refs_0_, f32[17,32,128]{2,1,0:T(8,128)S(1)} %get-tuple-element.31.refs_1_, f32[38,8,128]{2,1,0:T(8,128)S(1)} %collective-permute-done.2.refs_4_.refs_3_.refs_2_, f32[38,8,128]{2,1,0:T(8,128)S(1)} %collective-permute-done.3.refs_5_.refs_4_.refs_3_, ...), custom_call_target="tpu_custom_call" | custom-call | tf_op jit(solution)/shard_map/pallas_call | solution.py:1034
  35.5 0.9 %collective-permute-done.7.refs_2_ = f32[2,24,128]{2,1,0:T(8,128)S(1)} collective-permute-done((f32[2,24,128]{2,1,0:T(8,128)S(1)}, f32[2,24,128]{2,1,0:T(8,128)S(1)}, u32[]{:S(2)}, u32[]{:S(2)}) %collective-permute-start.7) | collective-permute-done | bytes 24608 | tf_op jit(solution)/shard_map/ppermute | solution.py:1032
  36.4 2.2 %shard_map.74 = (f32[2,8,128]{2,1,0:T(8,128)S(1)}, f32[2,8,128]{2,1,0:T(8,128)S(1)}, f32[32,128]{1,0:T(8,128)S(1)}, f32[10,18,128]{2,1,0:T(8,128)S(1)}, f32[14,2...) custom-call(s32[4,2]{1,0:T(4,128)S(1)} %copy.7.refs_0_, ...), custom_call_target="tpu_custom_call" | custom-call | tf_op jit(solution)/shard_map/pallas_call | solution.py:1038
  38.6 1.2 %collective-permute-start.10 = (f32[2,8,128]{2,1,0:T(8,128)S(1)}, f32[2,8,128]{2,1,0:T(8,128)S(1)}, u32[]{:S(2)}, u32[]{:S(2)}) collective-permute-start(f32[2,8,128]{2,1,0:T(8,128)S(1)} %get-tuple-element.57), channel_id=1, source_target_pairs={{0,1},{1,0},{2,3},{3,2},{4,5},{5,4},{6,7},{7,6},{8,9},{9,8},{10,11... | collective-permute-start | bytes 24584 | tf_op jit(solution)/shard_map/ppermute | solution.py:1059
  39.8 1.6 %shard_map.75 = f32[6,8,16,128]{3,2,1,0:T(8,128)} custom-call(f32[6,14,24,128]{3,2,1,0:T(8,128)S(1)} %get-tuple-element.45.refs_1_.refs_0_, f32[32,128]{1,0:T(8,128)S(1)} %get-tuple-element.51.refs_1_, f32[10,18,128]{2,1,0:T(8,128)S(1)} %get-tuple-element.52.refs_2_, f32[14,24,128]{2,1,0:T(8,128)S(1)} %get-tuple-element.53.refs_3_, ...), custom_call_target="tpu_custom_call" | custom-call | tf_op jit(solution)/shard_map/pallas_call | solution.py:1053
  41.4 0.9 %collective-permute-done.10.refs_2_ = f32[2,8,128]{2,1,0:T(8,128)S(1)} collective-permute-done((f32[2,8,128]{2,1,0:T(8,128)S(1)}, f32[2,8,128]{2,1,0:T(8,128)S(1)}, u32[]{:S(2)}, u32[]{:S(2)}) %collective-permute-start.10) | collective-permute-done | bytes 8224 | tf_op jit(solution)/shard_map/ppermute | solution.py:1059
  42.3 0.8 %shard_map.76 = f32[8,32,128]{2,1,0:T(8,128)} custom-call(f32[8,32,128]{2,1,0:T(8,128)S(1)} %shard_map.73.refs_5_.refs_0_, f32[2,8,128]{2,1,0:T(8,128)S(1)} %get-tuple-element.56.refs_1_, f32[2,8,128]{2,1,0:T(8,128)S(1)} %collective-permute-done.10.refs_2_), custom_call_target="tpu_custom_call" | custom-call | tf_op jit(solution)/shard_map/pallas_call | solution.py:1060
  (14 shorter events, 0.3 us)
Async XLA Ops:
  0.6 24.4 %copy-start.2 = (s32[4,2]{0,1:T(2,128)S(1)}, s32[4,2]{0,1:T(2,128)}, u32[]{:S(2)}) copy-start(s32[4,2]{0,1:T(2,128)} %param.9) | copy-start | bytes 100
  3.2 15.9 %collective-permute-start = (f32[32,16,128]{2,1,0:T(8,128)}, f32[32,16,128]{2,1,0:T(8,128)S(1)}, u32[]{:S(2)}, u32[]{:S(2)}) collective-permute-start(f32[32,16,128]{2,1,0:T(8,128)} %get-tuple-element.32), channel_id=1, source_target_pairs={{0,8},{8,0},{16,24},{24,16},{1,9},{9,1},{17,25},{25,17},{2,10},{10... | collective-permute-start | bytes 786440 | tf_op jit(solution)/shard_map/ppermute | solution.py:988
  4.8 14.2 %collective-permute-start.1 = (f32[32,16,128]{2,1,0:T(8,128)}, f32[32,16,128]{2,1,0:T(8,128)S(1)}, u32[]{:S(2)}, u32[]{:S(2)}) collective-permute-start(f32[32,16,128]{2,1,0:T(8,128)} %get-tuple-element.33), channel_id=1, source_target_pairs={{8,16},{16,8},{9,17},{17,9},{10,18},{18,10},{11,19},{19,11},{12,20... | collective-permute-start | bytes 786440 | tf_op jit(solution)/shard_map/ppermute | solution.py:989
  6.8 12.2 %collective-permute-start.2 = (f32[38,8,128]{2,1,0:T(8,128)}, f32[38,8,128]{2,1,0:T(8,128)S(1)}, u32[]{:S(2)}, u32[]{:S(2)}) collective-permute-start(f32[38,8,128]{2,1,0:T(8,128)} %get-tuple-element.34), channel_id=1, source_target_pairs={{0,1},{1,0},{2,3},{3,2},{4,5},{5,4},{6,7},{7,6},{8,9},{9,8},{10,11... | collective-permute-start | bytes 466952 | tf_op jit(solution)/shard_map/ppermute | solution.py:990
  8.3 10.7 %collective-permute-start.3 = (f32[38,8,128]{2,1,0:T(8,128)}, f32[38,8,128]{2,1,0:T(8,128)S(1)}, u32[]{:S(2)}, u32[]{:S(2)}) collective-permute-start(f32[38,8,128]{2,1,0:T(8,128)} %get-tuple-element.35), channel_id=1, source_target_pairs={{1,8},{8,1},{9,16},{16,9},{17,24},{24,17},{3,10},{10,3},{11,18},{1... | collective-permute-start | bytes 466952 | tf_op jit(solution)/shard_map/ppermute | solution.py:991
  12.2 6.7 %collective-permute-start.4 = (f32[2,8,128]{2,1,0:T(8,128)}, f32[2,8,128]{2,1,0:T(8,128)S(1)}, u32[]{:S(2)}, u32[]{:S(2)}) collective-permute-start(f32[2,8,128]{2,1,0:T(8,128)} %get-tuple-element.37), channel_id=1, source_target_pairs={{0,9},{9,0},{8,17},{17,8},{16,25},{25,16},{2,11},{11,2},{10,19},{1... | collective-permute-start | bytes 24584 | tf_op jit(solution)/shard_map/ppermute | solution.py:992
  14.1 1.0 %copy-start = (f32[6,8,16,128]{3,2,1,0:T(8,128)S(1)}, f32[6,8,16,128]{3,2,1,0:T(8,128)}, u32[]{:S(2)}) copy-start(f32[6,8,16,128]{3,2,1,0:T(8,128)} %refs_0_.6) | copy-start | bytes 1179652
  15.1 1.0 %copy-start.1 = (f32[17,32,128]{2,1,0:T(8,128)S(1)}, f32[17,32,128]{2,1,0:T(8,128)}, u32[]{:S(2)}) copy-start(f32[17,32,128]{2,1,0:T(8,128)} %get-tuple-element.30.refs_1_) | copy-start | bytes 835588
  19.3 7.4 %collective-permute-start.5 = (f32[63,8,128]{2,1,0:T(8,128)S(1)}, f32[63,8,128]{2,1,0:T(8,128)S(1)}, u32[]{:S(2)}, u32[]{:S(2)}) collective-permute-start(f32[63,8,128]{2,1,0:T(8,128)S(1)} %get-tuple-element.38), channel_id=1, source_target_pairs={{0,2},{2,0},{4,6},{6,4},{1,3},{3,1},{5,7},{7,5},{8,10},{10,8},{12,... | collective-permute-start | bytes 774152 | tf_op jit(solution)/shard_map/ppermute | solution.py:999
  19.4 7.6 %collective-permute-start.6 = (f32[63,8,128]{2,1,0:T(8,128)S(1)}, f32[63,8,128]{2,1,0:T(8,128)S(1)}, u32[]{:S(2)}, u32[]{:S(2)}) collective-permute-start(f32[63,8,128]{2,1,0:T(8,128)S(1)} %get-tuple-element.39), channel_id=1, source_target_pairs={{2,4},{4,2},{3,5},{5,3},{10,12},{12,10},{11,13},{13,11},{18,20},{2... | collective-permute-start | bytes 774152 | tf_op jit(solution)/shard_map/ppermute | solution.py:998
  21.9 10.7 %collective-permute-start.8 = (f32[16,8,128]{2,1,0:T(8,128)S(1)}, f32[16,8,128]{2,1,0:T(8,128)S(1)}, u32[]{:S(2)}, u32[]{:S(2)}) collective-permute-start(f32[16,8,128]{2,1,0:T(8,128)S(1)} %get-tuple-element.49), channel_id=1, source_target_pairs={{0,2},{2,0},{4,6},{6,4},{1,3},{3,1},{5,7},{7,5},{8,10},{10,8},{12,... | collective-permute-start | bytes 196616 | tf_op jit(solution)/shard_map/ppermute | solution.py:1001
  22.0 10.6 %collective-permute-start.9 = (f32[16,8,128]{2,1,0:T(8,128)S(1)}, f32[16,8,128]{2,1,0:T(8,128)S(1)}, u32[]{:S(2)}, u32[]{:S(2)}) collective-permute-start(f32[16,8,128]{2,1,0:T(8,128)S(1)} %get-tuple-element.50), channel_id=1, source_target_pairs={{2,4},{4,2},{3,5},{5,3},{10,12},{12,10},{11,13},{13,11},{18,20},{2... | collective-permute-start | bytes 196616 | tf_op jit(solution)/shard_map/ppermute | solution.py:1000
  32.5 3.9 %collective-permute-start.7 = (f32[2,24,128]{2,1,0:T(8,128)S(1)}, f32[2,24,128]{2,1,0:T(8,128)S(1)}, u32[]{:S(2)}, u32[]{:S(2)}) collective-permute-start(f32[2,24,128]{2,1,0:T(8,128)S(1)} %get-tuple-element.46), channel_id=1, source_target_pairs={{0,1},{1,0},{2,3},{3,2},{4,5},{5,4},{6,7},{7,6},{8,9},{9,8},{10,11... | collective-permute-start | bytes 73736 | tf_op jit(solution)/shard_map/ppermute | solution.py:1032
  38.6 3.7 %collective-permute-start.10 = (f32[2,8,128]{2,1,0:T(8,128)S(1)}, f32[2,8,128]{2,1,0:T(8,128)S(1)}, u32[]{:S(2)}, u32[]{:S(2)}) collective-permute-start(f32[2,8,128]{2,1,0:T(8,128)S(1)} %get-tuple-element.57), channel_id=1, source_target_pairs={{0,1},{1,0},{2,3},{3,2},{4,5},{5,4},{6,7},{7,6},{8,9},{9,8},{10,11... | collective-permute-start | bytes 24584 | tf_op jit(solution)/shard_map/ppermute | solution.py:1059

commit v8 on v7

--- a/solution.py
+++ b/solution.py
@@ -315,7 +315,7 @@
     return LASER_POWER * along_x * along_y
 
 
-def bulk_kernel(meta, beam, part, in_z, in_d, gy_a, gy_b, out, temp, cond, kx, ky, kz):
+def bulk_kernel(meta, beam, part, in_z, in_d, gy_a, gy_b, out, temp, other, cond, kx, ky, kz, above):
     rows = part.shape[0] // 2
     t, m = part.at[0:rows], part.at[rows : 2 * rows]
     gx, gy, gz = meta[0], meta[1], meta[2]
@@ -330,11 +330,11 @@
     for i in range(n):
         for y in range(col_tiles):
             span = slice(y * SUBL, (y + 1) * SUBL)
-            temp[0, i, span, :] = part_row(i - SKIN, y, t, 0, rows, in_z, in_d, low_z, col_tiles, None)
+            temp[i, span, :] = part_row(i - SKIN, y, t, 0, rows, in_z, in_d, low_z, col_tiles, None)
             cond[i, span, :] = part_row(i - SKIN, y, m, 1, rows, in_z, in_d, low_z, col_tiles, None)
         up = jnp.where(even_y, gy_a[i], gy_b[i])
         low = jnp.where(even_y, gy_b[i], gy_a[i])
-        temp[0, i, cols:size, :] = jnp.where(sub < half, up, low)
+        temp[i, cols:size, :] = jnp.where(sub < half, up, low)
         cond[i, cols:size, :] = turn(jnp.where(sub < half, low, up), half, 0)
 
     lane = iota((size, LANES), 1)
@@ -344,6 +344,7 @@
             kx[i] = 0.5 * (k + cond[i + 1])
         ky[i] = 0.5 * (k + turn(k, -1, 0))
         kz[i] = 0.5 * (k + jnp.where(lane == depth - 1, 0.0, turn(k, -1, 1)))
+        above[i] = 0.5 * (k + jnp.where(lane == 0, 0.0, turn(k, 1, 1)))
 
     col_g = gy * cols + wrapped(iota((size, LANES), 0), cols, size)
     inside_y = jnp.where((col_g >= 0) & (col_g < meta[4] * cols), 1.0, 0.0)
@@ -352,28 +353,28 @@
     first_row = (gx * meta[5] + gz) * rows - SKIN
 
     for s in range(STEPS * SUBSTEPS):
-        src, dst = s % 2, 1 - s % 2
+        src, dst = (temp, other) if s % 2 == 0 else (other, temp)
         last = s == STEPS * SUBSTEPS - 1
         a = beam[s, 0].astype(F32)
         b = beam[s, 1].astype(F32)
         spot = LASER_POWER * fall * jnp.exp(-(((col_f - b) / SPOT_RADIUS) ** 2))
         lo, hi = s + 1, n - 1 - s
-        fx0 = kx[lo - 1] * (temp[src, lo] - temp[src, lo - 1])
+        fx0 = kx[lo - 1] * (src[lo] - src[lo - 1])
         for i in range(lo, hi):
-            v = temp[src, i]
-            fx = kx[i] * (temp[src, i + 1] - v)
+            v = src[i]
+            fx = kx[i] * (src[i + 1] - v)
             fy = ky[i] * (turn(v, -1, 0) - v)
-            fz = kz[i] * (jnp.where(lane == depth - 1, 0.0, turn(v, -1, 1)) - v)
-            above = jnp.where(lane == 0, 0.5 * cond[i] * v, turn(fz, 1, 1))
+            down = kz[i] * (jnp.where(lane == depth - 1, 0.0, turn(v, -1, 1)) - v)
+            up = above[i] * (jnp.where(lane == 0, 0.0, turn(v, 1, 1)) - v)
             row = first_row + i
             along_x = jnp.exp(-((jnp.full((1, LANES), row.astype(F32) - a) / SPOT_RADIUS) ** 2))
-            change = (fx - fx0) + (fy - turn(fy, 1, 0)) + (fz - above) + spot * along_x
+            change = (fx - fx0) + (fy - turn(fy, 1, 0)) + (down + up) + spot * along_x
             new = v + HEAT_STEP * change
             if last:
                 out[i - SKIN] = new[:cols]
             else:
                 ok = (row >= 0) & (row < meta[3] * meta[5] * rows)
-                temp[dst, i] = new * (inside_y * jnp.where(ok, 1.0, 0.0))
+                dst[i] = new * (inside_y * jnp.where(ok, 1.0, 0.0))
             fx0 = fx
 
 
@@ -641,6 +642,7 @@
     deep = TOP - 1 - first
     kx = [0.5 * (v + turn(v, -1, 0)) for v in k[:deep]]
     ky = [0.5 * (v + turn(v, -1, 1)) for v in k[:deep]]
+    ky_low = [0.5 * (v + turn(v, 1, 1)) for v in k[:deep]]
     kz = [0.5 * (k[d] + k[d + 1]) for d in range(deep)]
     for s in range(SUBSTEPS):
         beam_xy = heat_source(row, col, beam, first + s)
@@ -648,10 +650,10 @@
         new = []
         for d in range(TOP - 1 - first - s):
             fx = kx[d] * (turn(t[d], -1, 0) - t[d])
-            fy = ky[d] * (turn(t[d], -1, 1) - t[d])
+            fy = ky[d] * (turn(t[d], -1, 1) - t[d]) + ky_low[d] * (turn(t[d], 1, 1) - t[d])
             fz = kz[d] * (t[d + 1] - t[d])
             factor = jnp.exp(jnp.full(shape, -d / ABSORB_DEPTH, F32))
-            change = (fx - turn(fx, 1, 0)) + (fy - turn(fy, 1, 1)) + (fz - before) + beam_xy * factor
+            change = (fx - turn(fx, 1, 0)) + fy + (fz - before) + beam_xy * factor
             if d == 0:
                 change = change - LATENT_HEAT * softplus(t[0] - BOIL_LEVEL - BACK_PRESSURE * fine)
             new.append(jnp.where(k[d] > 0, t[d] + HEAT_STEP * change, 0.0))
@@ -713,7 +715,7 @@
     mask_of = grid_masks(meta, n, size, rows_x, own_y)
     halo_stepped(h0, h1, g, low_z, mask_of, SUBL, own_y, fh, 0)
     height_terms(g, 1, n - 1, height_matrix(), diff, total, SUBL)
-    first_stage(meta, g, h0, [(SUBL, own_y, diff, total, SUBL, 0)], f, mask_of, 4)
+    first_stage(meta, g, h0, [(SUBL, own_y, diff, total, SUBL, 0)], f, mask_of, True)
 
 
 def unpack_group(packed, b, rows_x, reach, low_z, h0, h1, start, size):
@@ -792,10 +794,10 @@
         halo_stepped(h, h1, g, low_z, mask_of, start, SUBL, fh, start)
         height_terms(g, 1, n - 1, height_matrix(), d, t, start)
         windows.append((start, SUBL, d, t, start, start))
-    first_stage(meta, g, h, windows, f, mask_of, 4)
+    first_stage(meta, g, h, windows, f, mask_of, True)
     height_terms(f, 1, n - 3, height_matrix(), diff, total)
     two = second_stage(meta, g, f, fh, diff, total, 0, reach - 2, own_y, mask_of, store)
-    lax.fori_loop(4, n - 4, two(tuple(range(COMPS))), 0, unroll=4)
+    lax.fori_loop(4, n - 4, two(tuple(range(COMPS))), 0, unroll=True)
     for i in (2, n - 3):
         two((5,))(i, 0)
     for i in (3, n - 4):
@@ -861,7 +863,7 @@
 
 
 def last_kernel(
-    cells, meta, beam, g, in_m, in_t, in_k, bulk, out_t, out_f, mass, p, h, f, fh, h1, diff, total, skin
+    cells, meta, beam, g, g_diff, g_total, in_m, in_t, in_k, bulk, out_t, out_f, mass, p, h, f, fh, h1, diff, total, skin
 ):
     rows_x, own_y = cells
     n, size = g.shape[1], g.shape[2]
@@ -872,8 +874,7 @@
     matrix = height_matrix()
     halo_stepped(h, h1, g, meta[2] == 0, mask_of, 0, size, fh, -1)
     flow = tuple(range(2, COMPS))
-    height_terms(g, 1, n - 1, matrix, diff, total, 0, flow)
-    first_stage(meta, g, h, [(1, size - 2, diff, total, 0, 0)], f, mask_of, True, flow)
+    first_stage(meta, g, h, [(1, size - 2, g_diff, g_total, 0, 0)], f, mask_of, True, flow)
     height_terms(f, 1, n - 3, matrix, diff, total, 0, (4, 5))
 
     def store(i, new):
@@ -894,13 +895,16 @@
     mass[...] = vapor_mass(t[0], fine)
 
 
-def gas_kernel(meta, g, mass, p, h, flow, fh, out_g, f, diff, total):
+def terms_kernel(meta, g, diff, total):
+    height_terms(g, 1, g.shape[1] - 1, height_matrix(), diff, total)
+
+
+def gas_kernel(meta, g, g_diff, g_total, mass, p, h, flow, fh, out_g, f, diff, total):
     rows_x, own_y = out_g.shape[1], out_g.shape[2]
     n, size = g.shape[1], g.shape[2]
     matrix = height_matrix()
-    height_terms(g, 1, n - 1, matrix, diff, total, 0, (0, 1, 4))
     mask_of = grid_masks(meta, n, size, rows_x, own_y)
-    first_stage(meta, g, h, [(1, size - 2, diff, total, 0, 0)], f, mask_of, True, (0, 1), ())
+    first_stage(meta, g, h, [(1, size - 2, g_diff, g_total, 0, 0)], f, mask_of, True, (0, 1), ())
     both = Joined(f, flow)
     height_terms(both, 2, n - 4, matrix, diff, total, 0, tuple(range(COMPS)))
     masses = mass_rows(meta, h, mass, 0, rows_x, own_y, own_y)
@@ -1032,9 +1036,10 @@
     in_m = lax.ppermute(msg_m, "gz", pairs(nz, 0))
     field = (rows + 2 * SKIN, cols + SUBL, depth)
     (bulk,) = call(
-        bulk_kernel, [t.shape], scratch=[(2, *field), field, field, field, field], scalars=1, count=5
+        bulk_kernel, [t.shape], scratch=[field] * 7, scalars=1, count=5
     )(beam, part, in_z, in_d, part_a, part_b)
     low_row = (small, LANES)
+    g_diff, g_total = call(terms_kernel, [(COMPS, n2 - 1, *low_row)] * 2, count=1)(g2)
     mine, other, mass, p, h, f, fh = call(
         functools.partial(last_kernel, (rows_x, own_y)),
         [
@@ -1048,14 +1053,14 @@
         ],
         scratch=[(n2, *low_row)] + [(COMPS, n2 - 1, *low_row)] * 2 + [(part_rows, *block)],
         scalars=1,
-        count=5,
-    )(beam, g2, in_m, top_t, top_k, bulk)
+        count=7,
+    )(beam, g2, g_diff, g_total, in_m, top_t, top_k, bulk)
     (gas,) = call(
         gas_kernel,
         [u.shape],
         scratch=[(2, n2 - 2, *low_row)] + [(COMPS, n2 - 1, *low_row)] * 2,
-        count=6,
-    )(g2, mass, p, h, f, fh)
+        count=8,
+    )(g2, g_diff, g_total, mass, p, h, f, fh)
     given = lax.ppermute(other, "gz", pairs(nz, 0))
     (out,) = call(seal_kernel, [t.shape], count=3)(bulk, mine, given)
     return gas, jnp.transpose(out, (2, 0, 1))

time: 43.4 us -> 42.4 us (0.977)
  Pallas kernels: 17.3 us -> 15 us
  waiting for transfers between devices: 5.05 us -> 7.25 us
  starting transfers between devices: 17.9 us -> 17 us
    ppermute x1, waiting for transfers between devices: 0.89 us -> 1.91 us  [shards(): given = lax.ppermute(other, 'gz', pairs(nz, 0))]
    pallas_call x1, Pallas kernels: 5.46 us -> 4.53 us  [shards(): call(functools.partial(first_kernel, (rows_x, REACH)), [(COMPS, n2, small...]
    ppermute x1, starting transfers between devices: 1.19 us -> 0.36 us  [shards(): given = lax.ppermute(other, 'gz', pairs(nz, 0))]
    pallas_call x1 -> x2, Pallas kernels: 2.9 us -> 2.07 us  [the longest x1 1.63 us: shards(): call(bulk_kernel, [t.shape], scratch=[field] * 7, scalars=1, count=5)]
    ppermute x1, waiting for transfers between devices: 0.89 us -> 1.72 us  [shards(): in_m = lax.ppermute(msg_m, 'gz', pairs(nz, 0))]
  transfers between devices with their start and end apart: 11 -> 11, of which waited for: 5 -> 5; matrix products, arithmetic and copies ran while one was open for 0% -> 0% of each run, Pallas kernels for 27% -> 22%
where the time goes in v8:
time: 42.4 us; the launch traced here: 42.1 us
  starting transfers between devices  17 us (40%)
  Pallas kernels  15 us (35%)
  waiting for transfers between devices  7.25 us (17%)
  local copies, waits for them, and re-layouts  2.04 us (5%)
  between operations  0.8 us (2%)
    pallas_call x1, Pallas kernels, shards(): call(functools.partial(first_kernel, (rows_x, REACH)), [(COMPS, n2, small...  4.53 us
    ppermute x1, starting transfers between devices, shards(): in_d = lax.ppermute(msg_d, ('gx', 'gz'), cross(nx, nz, True))  3.85 us
    ppermute x1, starting transfers between devices, shards(): part_b = lax.ppermute(part_b, 'gy', pairs(ny, 1))  3.03 us
    ppermute x1, waiting for transfers between devices, shards(): in_h = lax.ppermute(msg_h, ('gx', 'gz'), cross(nx, nz, False))  2.81 us
    pallas_call x1, Pallas kernels, shards(): pl.pallas_call(pack, out_shape=[jax.ShapeDtypeStruct(v, F32) for v in sha...  2.55 us
    ppermute x1, starting transfers between devices, shards(): gy_b = lax.ppermute(msg_b, 'gy', pairs(ny, 1))  2.53 us
    pallas_call x1, Pallas kernels, shards(): call(functools.partial(last_kernel, (rows_x, own_y)), [(n_top // 2, *bloc...  2.15 us
    unnamed x7, local copies, waits for them, and re-layouts  2.04 us
  transfers between devices with their start and end apart: 11, of which 5 were waited for; matrix products, arithmetic and copies ran while one was open for 0% of the time, Pallas kernels for 22%

profile of v8, /device:TPU:18, one launch (start us, length us, event | category | flops | bytes accessed | tf_op | source)
XLA Modules:
  0.0 42.1 jit_solution(18427564419324332013)
XLA Ops:
  0.6 2.6 %shard_map.68 = (f32[32,16,128]{2,1,0:T(8,128)}, f32[32,16,128]{2,1,0:T(8,128)}, f32[38,8,128]{2,1,0:T(8,128)}, f32[38,8,128]{2,1,0:T(8,128)}, f32[2,8,128]{2,1,0:T(8,128)}, /*index=5*/f32[17,32,128]{2,1,0:T(8,128)}) custom-call(f32[6,8,16,128]{3,2,1,0:T(8,128)} %refs_0_.6, f32[8,32,128]{2,1,0:T(8,128)} %bitcast.3, s32[8,32,128]{2,1,0:T(8,128)} %bitcast.4, ...), custom_call_target="tpu_custom_call" | custom-call | tf_op jit(solution)/shard_map/pallas_call | solution.py:981
  3.2 1.6 %collective-permute-start = (f32[32,16,128]{2,1,0:T(8,128)}, f32[32,16,128]{2,1,0:T(8,128)S(1)}, u32[]{:S(2)}, u32[]{:S(2)}) collective-permute-start(f32[32,16,128]{2,1,0:T(8,128)} %get-tuple-element.34), channel_id=1, source_target_pairs={{0,8},{8,0},{16,24},{24,16},{1,9},{9,1},{17,25},{25,17},{2,10},{10... | collective-permute-start | bytes 786440 | tf_op jit(solution)/shard_map/ppermute | solution.py:992
  4.8 1.9 %collective-permute-start.1 = (f32[32,16,128]{2,1,0:T(8,128)}, f32[32,16,128]{2,1,0:T(8,128)S(1)}, u32[]{:S(2)}, u32[]{:S(2)}) collective-permute-start(f32[32,16,128]{2,1,0:T(8,128)} %get-tuple-element.35), channel_id=1, source_target_pairs={{8,16},{16,8},{9,17},{17,9},{10,18},{18,10},{11,19},{19,11},{12,20... | collective-permute-start | bytes 786440 | tf_op jit(solution)/shard_map/ppermute | solution.py:993
  6.8 1.6 %collective-permute-start.2 = (f32[38,8,128]{2,1,0:T(8,128)}, f32[38,8,128]{2,1,0:T(8,128)S(1)}, u32[]{:S(2)}, u32[]{:S(2)}) collective-permute-start(f32[38,8,128]{2,1,0:T(8,128)} %get-tuple-element.36), channel_id=1, source_target_pairs={{0,1},{1,0},{2,3},{3,2},{4,5},{5,4},{6,7},{7,6},{8,9},{9,8},{10,11... | collective-permute-start | bytes 466952 | tf_op jit(solution)/shard_map/ppermute | solution.py:994
  8.3 3.9 %collective-permute-start.3 = (f32[38,8,128]{2,1,0:T(8,128)}, f32[38,8,128]{2,1,0:T(8,128)S(1)}, u32[]{:S(2)}, u32[]{:S(2)}) collective-permute-start(f32[38,8,128]{2,1,0:T(8,128)} %get-tuple-element.37), channel_id=1, source_target_pairs={{1,8},{8,1},{9,16},{16,9},{17,24},{24,17},{3,10},{10,3},{11,18},{1... | collective-permute-start | bytes 466952 | tf_op jit(solution)/shard_map/ppermute | solution.py:995
  12.2 1.9 %collective-permute-start.4 = (f32[2,8,128]{2,1,0:T(8,128)}, f32[2,8,128]{2,1,0:T(8,128)S(1)}, u32[]{:S(2)}, u32[]{:S(2)}) collective-permute-start(f32[2,8,128]{2,1,0:T(8,128)} %get-tuple-element.39), channel_id=1, source_target_pairs={{0,9},{9,0},{8,17},{17,8},{16,25},{25,16},{2,11},{11,2},{10,19},{1... | collective-permute-start | bytes 24584 | tf_op jit(solution)/shard_map/ppermute | solution.py:996
  14.1 1.0 %copy-done = f32[6,8,16,128]{3,2,1,0:T(8,128)S(1)} copy-done((f32[6,8,16,128]{3,2,1,0:T(8,128)S(1)}, f32[6,8,16,128]{3,2,1,0:T(8,128)}, u32[]{:S(2)}) %copy-start) | copy-done | bytes 393240
  15.1 1.0 %copy-done.1 = f32[17,32,128]{2,1,0:T(8,128)S(1)} copy-done((f32[17,32,128]{2,1,0:T(8,128)S(1)}, f32[17,32,128]{2,1,0:T(8,128)}, u32[]{:S(2)}) %copy-start.1) | copy-done | bytes 278552
  16.1 2.8 %collective-permute-done.4.refs_6_.refs_5_ = f32[2,8,128]{2,1,0:T(8,128)S(1)} collective-permute-done((f32[2,8,128]{2,1,0:T(8,128)}, f32[2,8,128]{2,1,0:T(8,128)S(1)}, u32[]{:S(2)}, u32[]{:S(2)}) %collective-permute-start.4) | collective-permute-done | bytes 8224 | tf_op jit(solution)/shard_map/ppermute | solution.py:996
  18.9 0.1 collective-permute-done.3.refs_5_.refs_4_.refs_3_
  19.1 0.2 shard_map.70
  19.4 2.5 %collective-permute-start.6 = (f32[63,8,128]{2,1,0:T(8,128)S(1)}, f32[63,8,128]{2,1,0:T(8,128)S(1)}, u32[]{:S(2)}, u32[]{:S(2)}) collective-permute-start(f32[63,8,128]{2,1,0:T(8,128)S(1)} %get-tuple-element.41), channel_id=1, source_target_pairs={{2,4},{4,2},{3,5},{5,3},{10,12},{12,10},{11,13},{13,11},{18,20},{2... | collective-permute-start | bytes 774152 | tf_op jit(solution)/shard_map/ppermute | solution.py:1002
  22.0 3.0 %collective-permute-start.9 = (f32[16,8,128]{2,1,0:T(8,128)S(1)}, f32[16,8,128]{2,1,0:T(8,128)S(1)}, u32[]{:S(2)}, u32[]{:S(2)}) collective-permute-start(f32[16,8,128]{2,1,0:T(8,128)S(1)} %get-tuple-element.54), channel_id=1, source_target_pairs={{2,4},{4,2},{3,5},{5,3},{10,12},{12,10},{11,13},{13,11},{18,20},{2... | collective-permute-start | bytes 196616 | tf_op jit(solution)/shard_map/ppermute | solution.py:1004
  25.1 1.2 %shard_map.71 = (f32[6,20,32,128]{3,2,1,0:T(8,128)S(1)}, f32[6,18,16,128]{3,2,1,0:T(8,128)S(1)}, f32[20,32,128]{2,1,0:T(8,128)S(1)}, f32[20,32,128]{2,1,0:T(8,128)S(1)}, f32[18,16,128]{2,1,0:T(8,128)S(1)}) custom-call(f32[6,8,16,128]{3,2,1,0:T(8,128)S(1)} %get-tuple-element.38.refs_0_, f32[32,16,128]{2,1,0:T(8,128)S(1)} %collective-permute-done.refs_2_.refs_1_, ...), custom_call_target="tpu_custom_call" | custom-call | tf_op jit(solution)/shard_map/pallas_call | solution.py:1015
  26.3 0.7 %collective-permute-done.6.refs_7_ = f32[63,8,128]{2,1,0:T(8,128)S(1)} collective-permute-done((f32[63,8,128]{2,1,0:T(8,128)S(1)}, f32[63,8,128]{2,1,0:T(8,128)S(1)}, u32[]{:S(2)}, u32[]{:S(2)}) %collective-permute-start.6) | collective-permute-done | bytes 258080 | tf_op jit(solution)/shard_map/ppermute | solution.py:1002
  27.0 4.5 %shard_map.72 = (f32[6,14,24,128]{3,2,1,0:T(8,128)S(1)}, f32[2,24,128]{2,1,0:T(8,128)S(1)}, f32[6,32,128]{2,1,0:T(8,128)S(1)}, f32[6,32,128]{2,1,0:T(8,128)S(1)}) custom-call(s32[4,2]{1,0:T(4,128)S(1)} %copy.7.refs_0_, f32[17,32,128]{2,1,0:T(8,128)S(1)} %get-tuple-element.33.refs_1_, f32[32,16,128]{2,1,0:T(8,128)S(1)} %collective-permute-done.refs_2_.refs_1_, ...), custom_call_target="tpu_custom_call" | custom-call | tf_op jit(solution)/shard_map/pallas_call | solution.py:1021
  31.7 1.6 %shard_map.74.refs_7_.refs_0_ = f32[8,32,128]{2,1,0:T(8,128)S(1)} custom-call(s32[4,2]{1,0:T(4,128)S(1)} %copy.7.refs_0_, f32[17,32,128]{2,1,0:T(8,128)S(1)} %get-tuple-element.33.refs_1_, f32[38,8,128]{2,1,0:T(8,128)S(1)} %collective-permute-done.2.refs_4_.refs_3_.refs_2_, f32[38,8,128]{2,1,0:T(8,128)S(1)} %collective-permute-done.3.refs_5_.refs_4_.refs_3_, ...), custom_call_target="tpu_custom_call" | custom-call | tf_op jit(solution)/shard_map/pallas_call | solution.py:1038
  33.3 0.4 %shard_map.73 = (f32[6,13,24,128]{3,2,1,0:T(8,128)S(1)}, f32[6,13,24,128]{3,2,1,0:T(8,128)S(1)}) custom-call(f32[6,14,24,128]{3,2,1,0:T(8,128)S(1)} %get-tuple-element.47.refs_0_.refs_1_), custom_call_target="tpu_custom_call" | custom-call | tf_op jit(solution)/shard_map/pallas_call | solution.py:1042
  33.7 1.7 %collective-permute-done.7.refs_4_ = f32[2,24,128]{2,1,0:T(8,128)S(1)} collective-permute-done((f32[2,24,128]{2,1,0:T(8,128)S(1)}, f32[2,24,128]{2,1,0:T(8,128)S(1)}, u32[]{:S(2)}, u32[]{:S(2)}) %collective-permute-start.7) | collective-permute-done | bytes 24608 | tf_op jit(solution)/shard_map/ppermute | solution.py:1036
  35.4 2.1 %shard_map.75 = (f32[2,8,128]{2,1,0:T(8,128)S(1)}, f32[2,8,128]{2,1,0:T(8,128)S(1)}, f32[32,128]{1,0:T(8,128)S(1)}, f32[10,18,128]{2,1,0:T(8,128)S(1)}, f32[14,2...) custom-call(s32[4,2]{1,0:T(4,128)S(1)} %copy.7.refs_0_, ...), custom_call_target="tpu_custom_call" | custom-call | tf_op jit(solution)/shard_map/pallas_call | solution.py:1043
  37.6 0.4 collective-permute-start.10
  38.0 1.5 %shard_map.76 = f32[6,8,16,128]{3,2,1,0:T(8,128)} custom-call(f32[6,14,24,128]{3,2,1,0:T(8,128)S(1)} %get-tuple-element.47.refs_0_.refs_1_, f32[6,13,24,128]{3,2,1,0:T(8,128)S(1)} %get-tuple-element.48.refs_2_.refs_1_, f32[6,13,24,128]{3,2,1,0:T(8,128)S(1)} %get-tuple-element.49.refs_3_.refs_2_, f32[32,128]{1,0:T(8,128)S(1)} %get-tuple-element.55.refs_3_, ...), custom_call_target="tpu_custom_call" | custom-call | tf_op jit(solution)/shard_map/pallas_call | solution.py:1058
  39.4 1.9 %collective-permute-done.10.refs_2_ = f32[2,8,128]{2,1,0:T(8,128)S(1)} collective-permute-done((f32[2,8,128]{2,1,0:T(8,128)S(1)}, f32[2,8,128]{2,1,0:T(8,128)S(1)}, u32[]{:S(2)}, u32[]{:S(2)}) %collective-permute-start.10) | collective-permute-done | bytes 8224 | tf_op jit(solution)/shard_map/ppermute | solution.py:1064
  41.3 0.8 %shard_map.77 = f32[8,32,128]{2,1,0:T(8,128)} custom-call(f32[8,32,128]{2,1,0:T(8,128)S(1)} %shard_map.74.refs_7_.refs_0_, f32[2,8,128]{2,1,0:T(8,128)S(1)} %get-tuple-element.60.refs_1_, f32[2,8,128]{2,1,0:T(8,128)S(1)} %collective-permute-done.10.refs_2_), custom_call_target="tpu_custom_call" | custom-call | tf_op jit(solution)/shard_map/pallas_call | solution.py:1065
  (15 shorter events, 0.4 us)
Async XLA Ops:
  0.6 24.4 %copy-start.2 = (s32[4,2]{0,1:T(2,128)S(1)}, s32[4,2]{0,1:T(2,128)}, u32[]{:S(2)}) copy-start(s32[4,2]{0,1:T(2,128)} %param.9) | copy-start | bytes 100
  3.2 15.9 %collective-permute-start = (f32[32,16,128]{2,1,0:T(8,128)}, f32[32,16,128]{2,1,0:T(8,128)S(1)}, u32[]{:S(2)}, u32[]{:S(2)}) collective-permute-start(f32[32,16,128]{2,1,0:T(8,128)} %get-tuple-element.34), channel_id=1, source_target_pairs={{0,8},{8,0},{16,24},{24,16},{1,9},{9,1},{17,25},{25,17},{2,10},{10... | collective-permute-start | bytes 786440 | tf_op jit(solution)/shard_map/ppermute | solution.py:992
  4.8 14.2 %collective-permute-start.1 = (f32[32,16,128]{2,1,0:T(8,128)}, f32[32,16,128]{2,1,0:T(8,128)S(1)}, u32[]{:S(2)}, u32[]{:S(2)}) collective-permute-start(f32[32,16,128]{2,1,0:T(8,128)} %get-tuple-element.35), channel_id=1, source_target_pairs={{8,16},{16,8},{9,17},{17,9},{10,18},{18,10},{11,19},{19,11},{12,20... | collective-permute-start | bytes 786440 | tf_op jit(solution)/shard_map/ppermute | solution.py:993
  6.8 12.2 %collective-permute-start.2 = (f32[38,8,128]{2,1,0:T(8,128)}, f32[38,8,128]{2,1,0:T(8,128)S(1)}, u32[]{:S(2)}, u32[]{:S(2)}) collective-permute-start(f32[38,8,128]{2,1,0:T(8,128)} %get-tuple-element.36), channel_id=1, source_target_pairs={{0,1},{1,0},{2,3},{3,2},{4,5},{5,4},{6,7},{7,6},{8,9},{9,8},{10,11... | collective-permute-start | bytes 466952 | tf_op jit(solution)/shard_map/ppermute | solution.py:994
  8.3 10.7 %collective-permute-start.3 = (f32[38,8,128]{2,1,0:T(8,128)}, f32[38,8,128]{2,1,0:T(8,128)S(1)}, u32[]{:S(2)}, u32[]{:S(2)}) collective-permute-start(f32[38,8,128]{2,1,0:T(8,128)} %get-tuple-element.37), channel_id=1, source_target_pairs={{1,8},{8,1},{9,16},{16,9},{17,24},{24,17},{3,10},{10,3},{11,18},{1... | collective-permute-start | bytes 466952 | tf_op jit(solution)/shard_map/ppermute | solution.py:995
  12.2 6.7 %collective-permute-start.4 = (f32[2,8,128]{2,1,0:T(8,128)}, f32[2,8,128]{2,1,0:T(8,128)S(1)}, u32[]{:S(2)}, u32[]{:S(2)}) collective-permute-start(f32[2,8,128]{2,1,0:T(8,128)} %get-tuple-element.39), channel_id=1, source_target_pairs={{0,9},{9,0},{8,17},{17,8},{16,25},{25,16},{2,11},{11,2},{10,19},{1... | collective-permute-start | bytes 24584 | tf_op jit(solution)/shard_map/ppermute | solution.py:996
  14.1 1.0 %copy-start = (f32[6,8,16,128]{3,2,1,0:T(8,128)S(1)}, f32[6,8,16,128]{3,2,1,0:T(8,128)}, u32[]{:S(2)}) copy-start(f32[6,8,16,128]{3,2,1,0:T(8,128)} %refs_0_.6) | copy-start | bytes 1179652
  15.1 1.0 %copy-start.1 = (f32[17,32,128]{2,1,0:T(8,128)S(1)}, f32[17,32,128]{2,1,0:T(8,128)}, u32[]{:S(2)}) copy-start(f32[17,32,128]{2,1,0:T(8,128)} %get-tuple-element.32.refs_1_) | copy-start | bytes 835588
  19.3 7.0 %collective-permute-start.5 = (f32[63,8,128]{2,1,0:T(8,128)S(1)}, f32[63,8,128]{2,1,0:T(8,128)S(1)}, u32[]{:S(2)}, u32[]{:S(2)}) collective-permute-start(f32[63,8,128]{2,1,0:T(8,128)S(1)} %get-tuple-element.40), channel_id=1, source_target_pairs={{0,2},{2,0},{4,6},{6,4},{1,3},{3,1},{5,7},{7,5},{8,10},{10,8},{12,... | collective-permute-start | bytes 774152 | tf_op jit(solution)/shard_map/ppermute | solution.py:1003
  19.4 7.6 %collective-permute-start.6 = (f32[63,8,128]{2,1,0:T(8,128)S(1)}, f32[63,8,128]{2,1,0:T(8,128)S(1)}, u32[]{:S(2)}, u32[]{:S(2)}) collective-permute-start(f32[63,8,128]{2,1,0:T(8,128)S(1)} %get-tuple-element.41), channel_id=1, source_target_pairs={{2,4},{4,2},{3,5},{5,3},{10,12},{12,10},{11,13},{13,11},{18,20},{2... | collective-permute-start | bytes 774152 | tf_op jit(solution)/shard_map/ppermute | solution.py:1002
  21.9 9.7 %collective-permute-start.8 = (f32[16,8,128]{2,1,0:T(8,128)S(1)}, f32[16,8,128]{2,1,0:T(8,128)S(1)}, u32[]{:S(2)}, u32[]{:S(2)}) collective-permute-start(f32[16,8,128]{2,1,0:T(8,128)S(1)} %get-tuple-element.53), channel_id=1, source_target_pairs={{0,2},{2,0},{4,6},{6,4},{1,3},{3,1},{5,7},{7,5},{8,10},{10,8},{12,... | collective-permute-start | bytes 196616 | tf_op jit(solution)/shard_map/ppermute | solution.py:1005
  22.0 9.7 %collective-permute-start.9 = (f32[16,8,128]{2,1,0:T(8,128)S(1)}, f32[16,8,128]{2,1,0:T(8,128)S(1)}, u32[]{:S(2)}, u32[]{:S(2)}) collective-permute-start(f32[16,8,128]{2,1,0:T(8,128)S(1)} %get-tuple-element.54), channel_id=1, source_target_pairs={{2,4},{4,2},{3,5},{5,3},{10,12},{12,10},{11,13},{13,11},{18,20},{2... | collective-permute-start | bytes 196616 | tf_op jit(solution)/shard_map/ppermute | solution.py:1004
  31.6 3.9 %collective-permute-start.7 = (f32[2,24,128]{2,1,0:T(8,128)S(1)}, f32[2,24,128]{2,1,0:T(8,128)S(1)}, u32[]{:S(2)}, u32[]{:S(2)}) collective-permute-start(f32[2,24,128]{2,1,0:T(8,128)S(1)} %get-tuple-element.50), channel_id=1, source_target_pairs={{0,1},{1,0},{2,3},{3,2},{4,5},{5,4},{6,7},{7,6},{8,9},{9,8},{10,11... | collective-permute-start | bytes 73736 | tf_op jit(solution)/shard_map/ppermute | solution.py:1036
  37.6 3.7 %collective-permute-start.10 = (f32[2,8,128]{2,1,0:T(8,128)S(1)}, f32[2,8,128]{2,1,0:T(8,128)S(1)}, u32[]{:S(2)}, u32[]{:S(2)}) collective-permute-start(f32[2,8,128]{2,1,0:T(8,128)S(1)} %get-tuple-element.61), channel_id=1, source_target_pairs={{0,1},{1,0},{2,3},{3,2},{4,5},{5,4},{6,7},{7,6},{8,9},{9,8},{10,11... | collective-permute-start | bytes 24584 | tf_op jit(solution)/shard_map/ppermute | solution.py:1064

commit v9 on v8

--- a/solution.py
+++ b/solution.py
@@ -1021,7 +1021,7 @@
     g2, msg_m, top_t, top_k = call(
         functools.partial(first_kernel, (rows_x, REACH)),
         [
-            (COMPS, n2, small, LANES),
+            (COMPS + 1, n2, small, LANES),
             (n_m, small, LANES),
             (TOP - SUBSTEPS, part_rows, LANES),
             (TOP - SUBSTEPS, part_rows, LANES),
@@ -1039,7 +1039,7 @@
         bulk_kernel, [t.shape], scratch=[field] * 7, scalars=1, count=5
     )(beam, part, in_z, in_d, part_a, part_b)
     low_row = (small, LANES)
-    g_diff, g_total = call(terms_kernel, [(COMPS, n2 - 1, *low_row)] * 2, count=1)(g2)
+    g_diff, g_total = call(terms_kernel, [(COMPS + 1, n2 - 1, *low_row)] * 2, count=1)(g2)
     mine, other, mass, p, h, f, fh = call(
         functools.partial(last_kernel, (rows_x, own_y)),
         [
@@ -1048,10 +1048,10 @@
             (part_rows, LANES),
             (n2 - 4, own_y + 2 * (REACH_LAST - 2), LANES),
             (n2, *low_row),
-            (COMPS, n2 - 2, *low_row),
+            (COMPS + 1, n2 - 2, *low_row),
             (n2 - 2, *low_row),
         ],
-        scratch=[(n2, *low_row)] + [(COMPS, n2 - 1, *low_row)] * 2 + [(part_rows, *block)],
+        scratch=[(n2, *low_row)] + [(COMPS + 1, n2 - 1, *low_row)] * 2 + [(part_rows, *block)],
         scalars=1,
         count=7,
     )(beam, g2, g_diff, g_total, in_m, top_t, top_k, bulk)

time: 42.4 us -> 42.4 us (level)
  no operation moved by 1% of the time
where the time goes in v9:
time: 42.4 us; the launch traced here: 42.1 us
  starting transfers between devices  17 us (40%)
  Pallas kernels  15 us (35%)
  waiting for transfers between devices  7.27 us (17%)
  local copies, waits for them, and re-layouts  2.05 us (5%)
  between operations  0.79 us (2%)
    pallas_call x1, Pallas kernels, shards(): call(functools.partial(first_kernel, (rows_x, REACH)), [(COMPS + 1, n2, s...  4.56 us
    ppermute x1, starting transfers between devices, shards(): in_d = lax.ppermute(msg_d, ('gx', 'gz'), cross(nx, nz, True))  3.85 us
    ppermute x1, starting transfers between devices, shards(): part_b = lax.ppermute(part_b, 'gy', pairs(ny, 1))  3.03 us
    ppermute x1, waiting for transfers between devices, shards(): in_h = lax.ppermute(msg_h, ('gx', 'gz'), cross(nx, nz, False))  2.81 us
    pallas_call x1, Pallas kernels, shards(): pl.pallas_call(pack, out_shape=[jax.ShapeDtypeStruct(v, F32) for v in sha...  2.55 us
    ppermute x1, starting transfers between devices, shards(): gy_b = lax.ppermute(msg_b, 'gy', pairs(ny, 1))  2.53 us
    pallas_call x1, Pallas kernels, shards(): call(functools.partial(last_kernel, (rows_x, own_y)), [(n_top // 2, *bloc...  2.14 us
    unnamed x7, local copies, waits for them, and re-layouts  2.05 us
  transfers between devices with their start and end apart: 11, of which 5 were waited for; matrix products, arithmetic and copies ran while one was open for 0% of the time, Pallas kernels for 22%

profile of v9, /device:TPU:18, one launch (start us, length us, event | category | flops | bytes accessed | tf_op | source)
XLA Modules:
  0.0 42.1 jit_solution(2977751983667514873)
XLA Ops:
  0.6 2.6 %shard_map.68 = (f32[32,16,128]{2,1,0:T(8,128)}, f32[32,16,128]{2,1,0:T(8,128)}, f32[38,8,128]{2,1,0:T(8,128)}, f32[38,8,128]{2,1,0:T(8,128)}, f32[2,8,128]{2,1,0:T(8,128)}, /*index=5*/f32[17,32,128]{2,1,0:T(8,128)}) custom-call(f32[6,8,16,128]{3,2,1,0:T(8,128)} %refs_0_.6, f32[8,32,128]{2,1,0:T(8,128)} %bitcast.3, s32[8,32,128]{2,1,0:T(8,128)} %bitcast.4, ...), custom_call_target="tpu_custom_call" | custom-call | tf_op jit(solution)/shard_map/pallas_call | solution.py:981
  3.2 1.6 %collective-permute-start = (f32[32,16,128]{2,1,0:T(8,128)}, f32[32,16,128]{2,1,0:T(8,128)S(1)}, u32[]{:S(2)}, u32[]{:S(2)}) collective-permute-start(f32[32,16,128]{2,1,0:T(8,128)} %get-tuple-element.34), channel_id=1, source_target_pairs={{0,8},{8,0},{16,24},{24,16},{1,9},{9,1},{17,25},{25,17},{2,10},{10... | collective-permute-start | bytes 786440 | tf_op jit(solution)/shard_map/ppermute | solution.py:992
  4.8 1.9 %collective-permute-start.1 = (f32[32,16,128]{2,1,0:T(8,128)}, f32[32,16,128]{2,1,0:T(8,128)S(1)}, u32[]{:S(2)}, u32[]{:S(2)}) collective-permute-start(f32[32,16,128]{2,1,0:T(8,128)} %get-tuple-element.35), channel_id=1, source_target_pairs={{8,16},{16,8},{9,17},{17,9},{10,18},{18,10},{11,19},{19,11},{12,20... | collective-permute-start | bytes 786440 | tf_op jit(solution)/shard_map/ppermute | solution.py:993
  6.8 1.6 %collective-permute-start.2 = (f32[38,8,128]{2,1,0:T(8,128)}, f32[38,8,128]{2,1,0:T(8,128)S(1)}, u32[]{:S(2)}, u32[]{:S(2)}) collective-permute-start(f32[38,8,128]{2,1,0:T(8,128)} %get-tuple-element.36), channel_id=1, source_target_pairs={{0,1},{1,0},{2,3},{3,2},{4,5},{5,4},{6,7},{7,6},{8,9},{9,8},{10,11... | collective-permute-start | bytes 466952 | tf_op jit(solution)/shard_map/ppermute | solution.py:994
  8.3 3.9 %collective-permute-start.3 = (f32[38,8,128]{2,1,0:T(8,128)}, f32[38,8,128]{2,1,0:T(8,128)S(1)}, u32[]{:S(2)}, u32[]{:S(2)}) collective-permute-start(f32[38,8,128]{2,1,0:T(8,128)} %get-tuple-element.37), channel_id=1, source_target_pairs={{1,8},{8,1},{9,16},{16,9},{17,24},{24,17},{3,10},{10,3},{11,18},{1... | collective-permute-start | bytes 466952 | tf_op jit(solution)/shard_map/ppermute | solution.py:995
  12.2 1.9 %collective-permute-start.4 = (f32[2,8,128]{2,1,0:T(8,128)}, f32[2,8,128]{2,1,0:T(8,128)S(1)}, u32[]{:S(2)}, u32[]{:S(2)}) collective-permute-start(f32[2,8,128]{2,1,0:T(8,128)} %get-tuple-element.39), channel_id=1, source_target_pairs={{0,9},{9,0},{8,17},{17,8},{16,25},{25,16},{2,11},{11,2},{10,19},{1... | collective-permute-start | bytes 24584 | tf_op jit(solution)/shard_map/ppermute | solution.py:996
  14.1 1.0 %copy-done = f32[6,8,16,128]{3,2,1,0:T(8,128)S(1)} copy-done((f32[6,8,16,128]{3,2,1,0:T(8,128)S(1)}, f32[6,8,16,128]{3,2,1,0:T(8,128)}, u32[]{:S(2)}) %copy-start) | copy-done | bytes 393240
  15.1 1.0 %copy-done.1 = f32[17,32,128]{2,1,0:T(8,128)S(1)} copy-done((f32[17,32,128]{2,1,0:T(8,128)S(1)}, f32[17,32,128]{2,1,0:T(8,128)}, u32[]{:S(2)}) %copy-start.1) | copy-done | bytes 278552
  16.1 2.8 %collective-permute-done.4.refs_6_.refs_5_ = f32[2,8,128]{2,1,0:T(8,128)S(1)} collective-permute-done((f32[2,8,128]{2,1,0:T(8,128)}, f32[2,8,128]{2,1,0:T(8,128)S(1)}, u32[]{:S(2)}, u32[]{:S(2)}) %collective-permute-start.4) | collective-permute-done | bytes 8224 | tf_op jit(solution)/shard_map/ppermute | solution.py:996
  18.9 0.1 collective-permute-done.3.refs_5_.refs_4_.refs_3_
  19.1 0.2 shard_map.70
  19.4 2.5 %collective-permute-start.6 = (f32[63,8,128]{2,1,0:T(8,128)S(1)}, f32[63,8,128]{2,1,0:T(8,128)S(1)}, u32[]{:S(2)}, u32[]{:S(2)}) collective-permute-start(f32[63,8,128]{2,1,0:T(8,128)S(1)} %get-tuple-element.41), channel_id=1, source_target_pairs={{2,4},{4,2},{3,5},{5,3},{10,12},{12,10},{11,13},{13,11},{18,20},{2... | collective-permute-start | bytes 774152 | tf_op jit(solution)/shard_map/ppermute | solution.py:1002
  22.0 3.0 %collective-permute-start.9 = (f32[16,8,128]{2,1,0:T(8,128)S(1)}, f32[16,8,128]{2,1,0:T(8,128)S(1)}, u32[]{:S(2)}, u32[]{:S(2)}) collective-permute-start(f32[16,8,128]{2,1,0:T(8,128)S(1)} %get-tuple-element.54), channel_id=1, source_target_pairs={{2,4},{4,2},{3,5},{5,3},{10,12},{12,10},{11,13},{13,11},{18,20},{2... | collective-permute-start | bytes 196616 | tf_op jit(solution)/shard_map/ppermute | solution.py:1004
  25.1 1.2 %shard_map.71 = (f32[6,20,32,128]{3,2,1,0:T(8,128)S(1)}, f32[6,18,16,128]{3,2,1,0:T(8,128)S(1)}, f32[20,32,128]{2,1,0:T(8,128)S(1)}, f32[20,32,128]{2,1,0:T(8,128)S(1)}, f32[18,16,128]{2,1,0:T(8,128)S(1)}) custom-call(f32[6,8,16,128]{3,2,1,0:T(8,128)S(1)} %get-tuple-element.38.refs_0_, f32[32,16,128]{2,1,0:T(8,128)S(1)} %collective-permute-done.refs_2_.refs_1_, ...), custom_call_target="tpu_custom_call" | custom-call | tf_op jit(solution)/shard_map/pallas_call | solution.py:1015
  26.3 0.7 %collective-permute-done.6.refs_7_ = f32[63,8,128]{2,1,0:T(8,128)S(1)} collective-permute-done((f32[63,8,128]{2,1,0:T(8,128)S(1)}, f32[63,8,128]{2,1,0:T(8,128)S(1)}, u32[]{:S(2)}, u32[]{:S(2)}) %collective-permute-start.6) | collective-permute-done | bytes 258080 | tf_op jit(solution)/shard_map/ppermute | solution.py:1002
  27.0 4.6 %shard_map.72 = (f32[7,14,24,128]{3,2,1,0:T(8,128)S(1)}, f32[2,24,128]{2,1,0:T(8,128)S(1)}, f32[6,32,128]{2,1,0:T(8,128)S(1)}, f32[6,32,128]{2,1,0:T(8,128)S(1)}) custom-call(s32[4,2]{1,0:T(4,128)S(1)} %copy.7.refs_0_, f32[17,32,128]{2,1,0:T(8,128)S(1)} %get-tuple-element.33.refs_1_, f32[32,16,128]{2,1,0:T(8,128)S(1)} %collective-permute-done.refs_2_.refs_1_, ...), custom_call_target="tpu_custom_call" | custom-call | tf_op jit(solution)/shard_map/pallas_call | solution.py:1021
  31.7 1.6 %shard_map.74.refs_7_.refs_0_ = f32[8,32,128]{2,1,0:T(8,128)S(1)} custom-call(s32[4,2]{1,0:T(4,128)S(1)} %copy.7.refs_0_, f32[17,32,128]{2,1,0:T(8,128)S(1)} %get-tuple-element.33.refs_1_, f32[38,8,128]{2,1,0:T(8,128)S(1)} %collective-permute-done.2.refs_4_.refs_3_.refs_2_, f32[38,8,128]{2,1,0:T(8,128)S(1)} %collective-permute-done.3.refs_5_.refs_4_.refs_3_, ...), custom_call_target="tpu_custom_call" | custom-call | tf_op jit(solution)/shard_map/pallas_call | solution.py:1038
  33.3 0.4 %shard_map.73 = (f32[7,13,24,128]{3,2,1,0:T(8,128)S(1)}, f32[7,13,24,128]{3,2,1,0:T(8,128)S(1)}) custom-call(f32[7,14,24,128]{3,2,1,0:T(8,128)S(1)} %get-tuple-element.47.refs_0_.refs_1_), custom_call_target="tpu_custom_call" | custom-call | tf_op jit(solution)/shard_map/pallas_call | solution.py:1042
  33.8 1.7 %collective-permute-done.7.refs_4_ = f32[2,24,128]{2,1,0:T(8,128)S(1)} collective-permute-done((f32[2,24,128]{2,1,0:T(8,128)S(1)}, f32[2,24,128]{2,1,0:T(8,128)S(1)}, u32[]{:S(2)}, u32[]{:S(2)}) %collective-permute-start.7) | collective-permute-done | bytes 24608 | tf_op jit(solution)/shard_map/ppermute | solution.py:1036
  35.5 2.1 %shard_map.75 = (f32[2,8,128]{2,1,0:T(8,128)S(1)}, f32[2,8,128]{2,1,0:T(8,128)S(1)}, f32[32,128]{1,0:T(8,128)S(1)}, f32[10,18,128]{2,1,0:T(8,128)S(1)}, f32[14,2...) custom-call(s32[4,2]{1,0:T(4,128)S(1)} %copy.7.refs_0_, ...), custom_call_target="tpu_custom_call" | custom-call | tf_op jit(solution)/shard_map/pallas_call | solution.py:1043
  37.6 0.4 collective-permute-start.10
  38.0 1.4 %shard_map.76 = f32[6,8,16,128]{3,2,1,0:T(8,128)} custom-call(f32[7,14,24,128]{3,2,1,0:T(8,128)S(1)} %get-tuple-element.47.refs_0_.refs_1_, f32[7,13,24,128]{3,2,1,0:T(8,128)S(1)} %get-tuple-element.48.refs_2_.refs_1_, f32[7,13,24,128]{3,2,1,0:T(8,128)S(1)} %get-tuple-element.49.refs_3_.refs_2_, f32[32,128]{1,0:T(8,128)S(1)} %get-tuple-element.55.refs_3_, ...), custom_call_target="tpu_custom_call" | custom-call | tf_op jit(solution)/shard_map/pallas_call | solution.py:1058
  39.4 1.9 %collective-permute-done.10.refs_2_ = f32[2,8,128]{2,1,0:T(8,128)S(1)} collective-permute-done((f32[2,8,128]{2,1,0:T(8,128)S(1)}, f32[2,8,128]{2,1,0:T(8,128)S(1)}, u32[]{:S(2)}, u32[]{:S(2)}) %collective-permute-start.10) | collective-permute-done | bytes 8224 | tf_op jit(solution)/shard_map/ppermute | solution.py:1064
  41.3 0.8 %shard_map.77 = f32[8,32,128]{2,1,0:T(8,128)} custom-call(f32[8,32,128]{2,1,0:T(8,128)S(1)} %shard_map.74.refs_7_.refs_0_, f32[2,8,128]{2,1,0:T(8,128)S(1)} %get-tuple-element.60.refs_1_, f32[2,8,128]{2,1,0:T(8,128)S(1)} %collective-permute-done.10.refs_2_), custom_call_target="tpu_custom_call" | custom-call | tf_op jit(solution)/shard_map/pallas_call | solution.py:1065
  (15 shorter events, 0.4 us)
Async XLA Ops:
  3.2 21.8 %copy-start.2 = (s32[4,2]{0,1:T(2,128)S(1)}, s32[4,2]{0,1:T(2,128)}, u32[]{:S(2)}) copy-start(s32[4,2]{0,1:T(2,128)} %param.9) | copy-start | bytes 100
  3.2 15.9 %collective-permute-start = (f32[32,16,128]{2,1,0:T(8,128)}, f32[32,16,128]{2,1,0:T(8,128)S(1)}, u32[]{:S(2)}, u32[]{:S(2)}) collective-permute-start(f32[32,16,128]{2,1,0:T(8,128)} %get-tuple-element.34), channel_id=1, source_target_pairs={{0,8},{8,0},{16,24},{24,16},{1,9},{9,1},{17,25},{25,17},{2,10},{10... | collective-permute-start | bytes 786440 | tf_op jit(solution)/shard_map/ppermute | solution.py:992
  4.8 14.2 %collective-permute-start.1 = (f32[32,16,128]{2,1,0:T(8,128)}, f32[32,16,128]{2,1,0:T(8,128)S(1)}, u32[]{:S(2)}, u32[]{:S(2)}) collective-permute-start(f32[32,16,128]{2,1,0:T(8,128)} %get-tuple-element.35), channel_id=1, source_target_pairs={{8,16},{16,8},{9,17},{17,9},{10,18},{18,10},{11,19},{19,11},{12,20... | collective-permute-start | bytes 786440 | tf_op jit(solution)/shard_map/ppermute | solution.py:993
  6.8 12.2 %collective-permute-start.2 = (f32[38,8,128]{2,1,0:T(8,128)}, f32[38,8,128]{2,1,0:T(8,128)S(1)}, u32[]{:S(2)}, u32[]{:S(2)}) collective-permute-start(f32[38,8,128]{2,1,0:T(8,128)} %get-tuple-element.36), channel_id=1, source_target_pairs={{0,1},{1,0},{2,3},{3,2},{4,5},{5,4},{6,7},{7,6},{8,9},{9,8},{10,11... | collective-permute-start | bytes 466952 | tf_op jit(solution)/shard_map/ppermute | solution.py:994
  8.3 10.7 %collective-permute-start.3 = (f32[38,8,128]{2,1,0:T(8,128)}, f32[38,8,128]{2,1,0:T(8,128)S(1)}, u32[]{:S(2)}, u32[]{:S(2)}) collective-permute-start(f32[38,8,128]{2,1,0:T(8,128)} %get-tuple-element.37), channel_id=1, source_target_pairs={{1,8},{8,1},{9,16},{16,9},{17,24},{24,17},{3,10},{10,3},{11,18},{1... | collective-permute-start | bytes 466952 | tf_op jit(solution)/shard_map/ppermute | solution.py:995
  12.2 6.7 %collective-permute-start.4 = (f32[2,8,128]{2,1,0:T(8,128)}, f32[2,8,128]{2,1,0:T(8,128)S(1)}, u32[]{:S(2)}, u32[]{:S(2)}) collective-permute-start(f32[2,8,128]{2,1,0:T(8,128)} %get-tuple-element.39), channel_id=1, source_target_pairs={{0,9},{9,0},{8,17},{17,8},{16,25},{25,16},{2,11},{11,2},{10,19},{1... | collective-permute-start | bytes 24584 | tf_op jit(solution)/shard_map/ppermute | solution.py:996
  14.1 1.0 %copy-start = (f32[6,8,16,128]{3,2,1,0:T(8,128)S(1)}, f32[6,8,16,128]{3,2,1,0:T(8,128)}, u32[]{:S(2)}) copy-start(f32[6,8,16,128]{3,2,1,0:T(8,128)} %refs_0_.6) | copy-start | bytes 1179652
  15.1 1.0 %copy-start.1 = (f32[17,32,128]{2,1,0:T(8,128)S(1)}, f32[17,32,128]{2,1,0:T(8,128)}, u32[]{:S(2)}) copy-start(f32[17,32,128]{2,1,0:T(8,128)} %get-tuple-element.32.refs_1_) | copy-start | bytes 835588
  19.3 7.0 %collective-permute-start.5 = (f32[63,8,128]{2,1,0:T(8,128)S(1)}, f32[63,8,128]{2,1,0:T(8,128)S(1)}, u32[]{:S(2)}, u32[]{:S(2)}) collective-permute-start(f32[63,8,128]{2,1,0:T(8,128)S(1)} %get-tuple-element.40), channel_id=1, source_target_pairs={{0,2},{2,0},{4,6},{6,4},{1,3},{3,1},{5,7},{7,5},{8,10},{10,8},{12,... | collective-permute-start | bytes 774152 | tf_op jit(solution)/shard_map/ppermute | solution.py:1003
  19.4 7.6 %collective-permute-start.6 = (f32[63,8,128]{2,1,0:T(8,128)S(1)}, f32[63,8,128]{2,1,0:T(8,128)S(1)}, u32[]{:S(2)}, u32[]{:S(2)}) collective-permute-start(f32[63,8,128]{2,1,0:T(8,128)S(1)} %get-tuple-element.41), channel_id=1, source_target_pairs={{2,4},{4,2},{3,5},{5,3},{10,12},{12,10},{11,13},{13,11},{18,20},{2... | collective-permute-start | bytes 774152 | tf_op jit(solution)/shard_map/ppermute | solution.py:1002
  21.9 9.8 %collective-permute-start.8 = (f32[16,8,128]{2,1,0:T(8,128)S(1)}, f32[16,8,128]{2,1,0:T(8,128)S(1)}, u32[]{:S(2)}, u32[]{:S(2)}) collective-permute-start(f32[16,8,128]{2,1,0:T(8,128)S(1)} %get-tuple-element.53), channel_id=1, source_target_pairs={{0,2},{2,0},{4,6},{6,4},{1,3},{3,1},{5,7},{7,5},{8,10},{10,8},{12,... | collective-permute-start | bytes 196616 | tf_op jit(solution)/shard_map/ppermute | solution.py:1005
  22.0 9.7 %collective-permute-start.9 = (f32[16,8,128]{2,1,0:T(8,128)S(1)}, f32[16,8,128]{2,1,0:T(8,128)S(1)}, u32[]{:S(2)}, u32[]{:S(2)}) collective-permute-start(f32[16,8,128]{2,1,0:T(8,128)S(1)} %get-tuple-element.54), channel_id=1, source_target_pairs={{2,4},{4,2},{3,5},{5,3},{10,12},{12,10},{11,13},{13,11},{18,20},{2... | collective-permute-start | bytes 196616 | tf_op jit(solution)/shard_map/ppermute | solution.py:1004
  31.6 3.9 %collective-permute-start.7 = (f32[2,24,128]{2,1,0:T(8,128)S(1)}, f32[2,24,128]{2,1,0:T(8,128)S(1)}, u32[]{:S(2)}, u32[]{:S(2)}) collective-permute-start(f32[2,24,128]{2,1,0:T(8,128)S(1)} %get-tuple-element.50), channel_id=1, source_target_pairs={{0,1},{1,0},{2,3},{3,2},{4,5},{5,4},{6,7},{7,6},{8,9},{9,8},{10,11... | collective-permute-start | bytes 73736 | tf_op jit(solution)/shard_map/ppermute | solution.py:1036
  37.6 3.7 %collective-permute-start.10 = (f32[2,8,128]{2,1,0:T(8,128)S(1)}, f32[2,8,128]{2,1,0:T(8,128)S(1)}, u32[]{:S(2)}, u32[]{:S(2)}) collective-permute-start(f32[2,8,128]{2,1,0:T(8,128)S(1)} %get-tuple-element.61), channel_id=1, source_target_pairs={{0,1},{1,0},{2,3},{3,2},{4,5},{5,4},{6,7},{7,6},{8,9},{9,8},{10,11... | collective-permute-start | bytes 24584 | tf_op jit(solution)/shard_map/ppermute | solution.py:1064

commit v10 on v9

--- a/solution.py
+++ b/solution.py
@@ -489,14 +489,14 @@
     shape = (6 * LANES, LANES)
     k = iota(shape, 0)
     j = iota(shape, 1)
-    axis = k // (2 * LANES)
+    axis = lax.shift_right_logical(k, (2 * LANES).bit_length() - 1)
     lane = k & (LANES - 1)
     spread = (lane == 4 + 2 * axis) & ((j == 0) | (j == 2) | (j == 10))
     slope = (lane == 10) & (j == 4 + 2 * axis)
     return jnp.where(spread | slope, 1.0, 0.0).astype(jnp.bfloat16)
 
 
-def halo_stepped(h0, h1, g, low_z, mask_of, start, size, out, at):
+def halo_stepped(h0, h1, g, low_z, mask_of, start, size, out, at, couple):
     n = h0.shape[0]
     span = slice(start, start + size)
     rows = (n - 2) * size
@@ -518,7 +518,7 @@
     behind = h1[1 : n - 1, span].reshape(rows, LANES)
     slopes = [east - west, north - south, jnp.where(low_z, 1.0, -1.0) * (behind - touch)]
     coupled = jnp.dot(
-        jnp.concatenate([split(v) for v in slopes], axis=1), couple_matrix(), preferred_element_type=F32
+        jnp.concatenate([split(v) for v in slopes], axis=1), couple, preferred_element_type=F32
     )
     up = by_comp(lane, [GAS_STEP * (v - 0.5 * DRIFT_SPEED) for v in VISCOSITY])
     down = by_comp(lane, [GAS_STEP * (v + 0.5 * DRIFT_SPEED) for v in VISCOSITY])
@@ -713,7 +713,7 @@
                 parts.append(jnp.where(low_z, in_h[y], in_d[base + y]))
         unpack_group(jnp.concatenate(parts, axis=0), b, rows_x, reach, low_z, h0, h1, SUBL, own_y)
     mask_of = grid_masks(meta, n, size, rows_x, own_y)
-    halo_stepped(h0, h1, g, low_z, mask_of, SUBL, own_y, fh, 0)
+    halo_stepped(h0, h1, g, low_z, mask_of, SUBL, own_y, fh, 0, couple_matrix())
     height_terms(g, 1, n - 1, height_matrix(), diff, total, SUBL)
     first_stage(meta, g, h0, [(SUBL, own_y, diff, total, SUBL, 0)], f, mask_of, True)
 
@@ -790,12 +790,13 @@
     fh[:, inner, :] = fh_in[...]
     upper_at = size - SUBL - 1
     windows = []
+    matrix, couple = height_matrix(), couple_matrix()
     for start, d, t in ((1, diff_lo, total_lo), (upper_at, diff_hi, total_hi)):
-        halo_stepped(h, h1, g, low_z, mask_of, start, SUBL, fh, start)
-        height_terms(g, 1, n - 1, height_matrix(), d, t, start)
+        halo_stepped(h, h1, g, low_z, mask_of, start, SUBL, fh, start, couple)
+        height_terms(g, 1, n - 1, matrix, d, t, start)
         windows.append((start, SUBL, d, t, start, start))
     first_stage(meta, g, h, windows, f, mask_of, True)
-    height_terms(f, 1, n - 3, height_matrix(), diff, total)
+    height_terms(f, 1, n - 3, matrix, diff, total)
     two = second_stage(meta, g, f, fh, diff, total, 0, reach - 2, own_y, mask_of, store)
     lax.fori_loop(4, n - 4, two(tuple(range(COMPS))), 0, unroll=True)
     for i in (2, n - 3):
@@ -872,7 +873,7 @@
         unpack_heights(in_m[j], GROUP * q, meta[2] == 0, h, h1, i)
     mask_of = grid_masks(meta, n, size, rows_x, own_y)
     matrix = height_matrix()
-    halo_stepped(h, h1, g, meta[2] == 0, mask_of, 0, size, fh, -1)
+    halo_stepped(h, h1, g, meta[2] == 0, mask_of, 0, size, fh, -1, couple_matrix())
     flow = tuple(range(2, COMPS))
     first_stage(meta, g, h, [(1, size - 2, g_diff, g_total, 0, 0)], f, mask_of, True, flow)
     height_terms(f, 1, n - 3, matrix, diff, total, 0, (4, 5))

time: 42.4 us -> 42.4 us (level)
  no operation moved by 1% of the time
where the time goes in v10:
time: 42.4 us; the launch traced here: 42.1 us
  starting transfers between devices  17.1 us (40%)
  Pallas kernels  15 us (35%)
  waiting for transfers between devices  7.26 us (17%)
  local copies, waits for them, and re-layouts  2.05 us (5%)
  between operations  0.79 us (2%)
    pallas_call x1, Pallas kernels, shards(): call(functools.partial(first_kernel, (rows_x, REACH)), [(COMPS + 1, n2, s...  4.56 us
    ppermute x1, starting transfers between devices, shards(): in_d = lax.ppermute(msg_d, ('gx', 'gz'), cross(nx, nz, True))  3.85 us
    ppermute x1, starting transfers between devices, shards(): part_b = lax.ppermute(part_b, 'gy', pairs(ny, 1))  3.03 us
    ppermute x1, waiting for transfers between devices, shards(): in_h = lax.ppermute(msg_h, ('gx', 'gz'), cross(nx, nz, False))  2.81 us
    pallas_call x1, Pallas kernels, shards(): pl.pallas_call(pack, out_shape=[jax.ShapeDtypeStruct(v, F32) for v in sha...  2.55 us
    ppermute x1, starting transfers between devices, shards(): gy_b = lax.ppermute(msg_b, 'gy', pairs(ny, 1))  2.53 us
    pallas_call x1, Pallas kernels, shards(): call(functools.partial(last_kernel, (rows_x, own_y)), [(n_top // 2, *bloc...  2.14 us
    unnamed x7, local copies, waits for them, and re-layouts  2.05 us
  transfers between devices with their start and end apart: 11, of which 5 were waited for; matrix products, arithmetic and copies ran while one was open for 0% of the time, Pallas kernels for 22%

profile of v10, /device:TPU:18, one launch (start us, length us, event | category | flops | bytes accessed | tf_op | source)
XLA Modules:
  0.0 42.1 jit_solution(1296502708507861928)
XLA Ops:
  0.6 2.6 %shard_map.68 = (f32[32,16,128]{2,1,0:T(8,128)}, f32[32,16,128]{2,1,0:T(8,128)}, f32[38,8,128]{2,1,0:T(8,128)}, f32[38,8,128]{2,1,0:T(8,128)}, f32[2,8,128]{2,1,0:T(8,128)}, /*index=5*/f32[17,32,128]{2,1,0:T(8,128)}) custom-call(f32[6,8,16,128]{3,2,1,0:T(8,128)} %refs_0_.6, f32[8,32,128]{2,1,0:T(8,128)} %bitcast.3, s32[8,32,128]{2,1,0:T(8,128)} %bitcast.4, ...), custom_call_target="tpu_custom_call" | custom-call | tf_op jit(solution)/shard_map/pallas_call | solution.py:982
  3.2 1.6 %collective-permute-start = (f32[32,16,128]{2,1,0:T(8,128)}, f32[32,16,128]{2,1,0:T(8,128)S(1)}, u32[]{:S(2)}, u32[]{:S(2)}) collective-permute-start(f32[32,16,128]{2,1,0:T(8,128)} %get-tuple-element.34), channel_id=1, source_target_pairs={{0,8},{8,0},{16,24},{24,16},{1,9},{9,1},{17,25},{25,17},{2,10},{10... | collective-permute-start | bytes 786440 | tf_op jit(solution)/shard_map/ppermute | solution.py:993
  4.8 1.9 %collective-permute-start.1 = (f32[32,16,128]{2,1,0:T(8,128)}, f32[32,16,128]{2,1,0:T(8,128)S(1)}, u32[]{:S(2)}, u32[]{:S(2)}) collective-permute-start(f32[32,16,128]{2,1,0:T(8,128)} %get-tuple-element.35), channel_id=1, source_target_pairs={{8,16},{16,8},{9,17},{17,9},{10,18},{18,10},{11,19},{19,11},{12,20... | collective-permute-start | bytes 786440 | tf_op jit(solution)/shard_map/ppermute | solution.py:994
  6.8 1.6 %collective-permute-start.2 = (f32[38,8,128]{2,1,0:T(8,128)}, f32[38,8,128]{2,1,0:T(8,128)S(1)}, u32[]{:S(2)}, u32[]{:S(2)}) collective-permute-start(f32[38,8,128]{2,1,0:T(8,128)} %get-tuple-element.36), channel_id=1, source_target_pairs={{0,1},{1,0},{2,3},{3,2},{4,5},{5,4},{6,7},{7,6},{8,9},{9,8},{10,11... | collective-permute-start | bytes 466952 | tf_op jit(solution)/shard_map/ppermute | solution.py:995
  8.3 3.9 %collective-permute-start.3 = (f32[38,8,128]{2,1,0:T(8,128)}, f32[38,8,128]{2,1,0:T(8,128)S(1)}, u32[]{:S(2)}, u32[]{:S(2)}) collective-permute-start(f32[38,8,128]{2,1,0:T(8,128)} %get-tuple-element.37), channel_id=1, source_target_pairs={{1,8},{8,1},{9,16},{16,9},{17,24},{24,17},{3,10},{10,3},{11,18},{1... | collective-permute-start | bytes 466952 | tf_op jit(solution)/shard_map/ppermute | solution.py:996
  12.2 1.9 %collective-permute-start.4 = (f32[2,8,128]{2,1,0:T(8,128)}, f32[2,8,128]{2,1,0:T(8,128)S(1)}, u32[]{:S(2)}, u32[]{:S(2)}) collective-permute-start(f32[2,8,128]{2,1,0:T(8,128)} %get-tuple-element.39), channel_id=1, source_target_pairs={{0,9},{9,0},{8,17},{17,8},{16,25},{25,16},{2,11},{11,2},{10,19},{1... | collective-permute-start | bytes 24584 | tf_op jit(solution)/shard_map/ppermute | solution.py:997
  14.1 1.0 %copy-done = f32[6,8,16,128]{3,2,1,0:T(8,128)S(1)} copy-done((f32[6,8,16,128]{3,2,1,0:T(8,128)S(1)}, f32[6,8,16,128]{3,2,1,0:T(8,128)}, u32[]{:S(2)}) %copy-start) | copy-done | bytes 393240
  15.1 1.0 %copy-done.1 = f32[17,32,128]{2,1,0:T(8,128)S(1)} copy-done((f32[17,32,128]{2,1,0:T(8,128)S(1)}, f32[17,32,128]{2,1,0:T(8,128)}, u32[]{:S(2)}) %copy-start.1) | copy-done | bytes 278552
  16.1 2.8 %collective-permute-done.4.refs_6_.refs_5_ = f32[2,8,128]{2,1,0:T(8,128)S(1)} collective-permute-done((f32[2,8,128]{2,1,0:T(8,128)}, f32[2,8,128]{2,1,0:T(8,128)S(1)}, u32[]{:S(2)}, u32[]{:S(2)}) %collective-permute-start.4) | collective-permute-done | bytes 8224 | tf_op jit(solution)/shard_map/ppermute | solution.py:997
  18.9 0.1 collective-permute-done.3.refs_5_.refs_4_.refs_3_
  19.1 0.2 shard_map.70
  19.4 2.5 %collective-permute-start.6 = (f32[63,8,128]{2,1,0:T(8,128)S(1)}, f32[63,8,128]{2,1,0:T(8,128)S(1)}, u32[]{:S(2)}, u32[]{:S(2)}) collective-permute-start(f32[63,8,128]{2,1,0:T(8,128)S(1)} %get-tuple-element.41), channel_id=1, source_target_pairs={{2,4},{4,2},{3,5},{5,3},{10,12},{12,10},{11,13},{13,11},{18,20},{2... | collective-permute-start | bytes 774152 | tf_op jit(solution)/shard_map/ppermute | solution.py:1003
  22.0 3.0 %collective-permute-start.9 = (f32[16,8,128]{2,1,0:T(8,128)S(1)}, f32[16,8,128]{2,1,0:T(8,128)S(1)}, u32[]{:S(2)}, u32[]{:S(2)}) collective-permute-start(f32[16,8,128]{2,1,0:T(8,128)S(1)} %get-tuple-element.54), channel_id=1, source_target_pairs={{2,4},{4,2},{3,5},{5,3},{10,12},{12,10},{11,13},{13,11},{18,20},{2... | collective-permute-start | bytes 196616 | tf_op jit(solution)/shard_map/ppermute | solution.py:1005
  25.1 1.2 %shard_map.71 = (f32[6,20,32,128]{3,2,1,0:T(8,128)S(1)}, f32[6,18,16,128]{3,2,1,0:T(8,128)S(1)}, f32[20,32,128]{2,1,0:T(8,128)S(1)}, f32[20,32,128]{2,1,0:T(8,128)S(1)}, f32[18,16,128]{2,1,0:T(8,128)S(1)}) custom-call(f32[6,8,16,128]{3,2,1,0:T(8,128)S(1)} %get-tuple-element.38.refs_0_, f32[32,16,128]{2,1,0:T(8,128)S(1)} %collective-permute-done.refs_2_.refs_1_, ...), custom_call_target="tpu_custom_call" | custom-call | tf_op jit(solution)/shard_map/pallas_call | solution.py:1016
  26.3 0.7 %collective-permute-done.6.refs_7_ = f32[63,8,128]{2,1,0:T(8,128)S(1)} collective-permute-done((f32[63,8,128]{2,1,0:T(8,128)S(1)}, f32[63,8,128]{2,1,0:T(8,128)S(1)}, u32[]{:S(2)}, u32[]{:S(2)}) %collective-permute-start.6) | collective-permute-done | bytes 258080 | tf_op jit(solution)/shard_map/ppermute | solution.py:1003
  27.0 4.6 %shard_map.72 = (f32[7,14,24,128]{3,2,1,0:T(8,128)S(1)}, f32[2,24,128]{2,1,0:T(8,128)S(1)}, f32[6,32,128]{2,1,0:T(8,128)S(1)}, f32[6,32,128]{2,1,0:T(8,128)S(1)}) custom-call(s32[4,2]{1,0:T(4,128)S(1)} %copy.7.refs_0_, f32[17,32,128]{2,1,0:T(8,128)S(1)} %get-tuple-element.33.refs_1_, f32[32,16,128]{2,1,0:T(8,128)S(1)} %collective-permute-done.refs_2_.refs_1_, ...), custom_call_target="tpu_custom_call" | custom-call | tf_op jit(solution)/shard_map/pallas_call | solution.py:1022
  31.7 1.6 %shard_map.74.refs_7_.refs_0_ = f32[8,32,128]{2,1,0:T(8,128)S(1)} custom-call(s32[4,2]{1,0:T(4,128)S(1)} %copy.7.refs_0_, f32[17,32,128]{2,1,0:T(8,128)S(1)} %get-tuple-element.33.refs_1_, f32[38,8,128]{2,1,0:T(8,128)S(1)} %collective-permute-done.2.refs_4_.refs_3_.refs_2_, f32[38,8,128]{2,1,0:T(8,128)S(1)} %collective-permute-done.3.refs_5_.refs_4_.refs_3_, ...), custom_call_target="tpu_custom_call" | custom-call | tf_op jit(solution)/shard_map/pallas_call | solution.py:1039
  33.3 0.4 %shard_map.73 = (f32[7,13,24,128]{3,2,1,0:T(8,128)S(1)}, f32[7,13,24,128]{3,2,1,0:T(8,128)S(1)}) custom-call(f32[7,14,24,128]{3,2,1,0:T(8,128)S(1)} %get-tuple-element.47.refs_0_.refs_1_), custom_call_target="tpu_custom_call" | custom-call | tf_op jit(solution)/shard_map/pallas_call | solution.py:1043
  33.8 1.7 %collective-permute-done.7.refs_4_ = f32[2,24,128]{2,1,0:T(8,128)S(1)} collective-permute-done((f32[2,24,128]{2,1,0:T(8,128)S(1)}, f32[2,24,128]{2,1,0:T(8,128)S(1)}, u32[]{:S(2)}, u32[]{:S(2)}) %collective-permute-start.7) | collective-permute-done | bytes 24608 | tf_op jit(solution)/shard_map/ppermute | solution.py:1037
  35.5 2.1 %shard_map.75 = (f32[2,8,128]{2,1,0:T(8,128)S(1)}, f32[2,8,128]{2,1,0:T(8,128)S(1)}, f32[32,128]{1,0:T(8,128)S(1)}, f32[10,18,128]{2,1,0:T(8,128)S(1)}, f32[14,2...) custom-call(s32[4,2]{1,0:T(4,128)S(1)} %copy.7.refs_0_, ...), custom_call_target="tpu_custom_call" | custom-call | tf_op jit(solution)/shard_map/pallas_call | solution.py:1044
  37.6 0.4 collective-permute-start.10
  38.0 1.4 %shard_map.76 = f32[6,8,16,128]{3,2,1,0:T(8,128)} custom-call(f32[7,14,24,128]{3,2,1,0:T(8,128)S(1)} %get-tuple-element.47.refs_0_.refs_1_, f32[7,13,24,128]{3,2,1,0:T(8,128)S(1)} %get-tuple-element.48.refs_2_.refs_1_, f32[7,13,24,128]{3,2,1,0:T(8,128)S(1)} %get-tuple-element.49.refs_3_.refs_2_, f32[32,128]{1,0:T(8,128)S(1)} %get-tuple-element.55.refs_3_, ...), custom_call_target="tpu_custom_call" | custom-call | tf_op jit(solution)/shard_map/pallas_call | solution.py:1059
  39.4 1.9 %collective-permute-done.10.refs_2_ = f32[2,8,128]{2,1,0:T(8,128)S(1)} collective-permute-done((f32[2,8,128]{2,1,0:T(8,128)S(1)}, f32[2,8,128]{2,1,0:T(8,128)S(1)}, u32[]{:S(2)}, u32[]{:S(2)}) %collective-permute-start.10) | collective-permute-done | bytes 8224 | tf_op jit(solution)/shard_map/ppermute | solution.py:1065
  41.3 0.8 %shard_map.77 = f32[8,32,128]{2,1,0:T(8,128)} custom-call(f32[8,32,128]{2,1,0:T(8,128)S(1)} %shard_map.74.refs_7_.refs_0_, f32[2,8,128]{2,1,0:T(8,128)S(1)} %get-tuple-element.60.refs_1_, f32[2,8,128]{2,1,0:T(8,128)S(1)} %collective-permute-done.10.refs_2_), custom_call_target="tpu_custom_call" | custom-call | tf_op jit(solution)/shard_map/pallas_call | solution.py:1066
  (15 shorter events, 0.4 us)
Async XLA Ops:
  3.2 21.8 %copy-start.2 = (s32[4,2]{0,1:T(2,128)S(1)}, s32[4,2]{0,1:T(2,128)}, u32[]{:S(2)}) copy-start(s32[4,2]{0,1:T(2,128)} %param.9) | copy-start | bytes 100
  3.2 15.9 %collective-permute-start = (f32[32,16,128]{2,1,0:T(8,128)}, f32[32,16,128]{2,1,0:T(8,128)S(1)}, u32[]{:S(2)}, u32[]{:S(2)}) collective-permute-start(f32[32,16,128]{2,1,0:T(8,128)} %get-tuple-element.34), channel_id=1, source_target_pairs={{0,8},{8,0},{16,24},{24,16},{1,9},{9,1},{17,25},{25,17},{2,10},{10... | collective-permute-start | bytes 786440 | tf_op jit(solution)/shard_map/ppermute | solution.py:993
  4.8 14.2 %collective-permute-start.1 = (f32[32,16,128]{2,1,0:T(8,128)}, f32[32,16,128]{2,1,0:T(8,128)S(1)}, u32[]{:S(2)}, u32[]{:S(2)}) collective-permute-start(f32[32,16,128]{2,1,0:T(8,128)} %get-tuple-element.35), channel_id=1, source_target_pairs={{8,16},{16,8},{9,17},{17,9},{10,18},{18,10},{11,19},{19,11},{12,20... | collective-permute-start | bytes 786440 | tf_op jit(solution)/shard_map/ppermute | solution.py:994
  6.8 12.2 %collective-permute-start.2 = (f32[38,8,128]{2,1,0:T(8,128)}, f32[38,8,128]{2,1,0:T(8,128)S(1)}, u32[]{:S(2)}, u32[]{:S(2)}) collective-permute-start(f32[38,8,128]{2,1,0:T(8,128)} %get-tuple-element.36), channel_id=1, source_target_pairs={{0,1},{1,0},{2,3},{3,2},{4,5},{5,4},{6,7},{7,6},{8,9},{9,8},{10,11... | collective-permute-start | bytes 466952 | tf_op jit(solution)/shard_map/ppermute | solution.py:995
  8.3 10.7 %collective-permute-start.3 = (f32[38,8,128]{2,1,0:T(8,128)}, f32[38,8,128]{2,1,0:T(8,128)S(1)}, u32[]{:S(2)}, u32[]{:S(2)}) collective-permute-start(f32[38,8,128]{2,1,0:T(8,128)} %get-tuple-element.37), channel_id=1, source_target_pairs={{1,8},{8,1},{9,16},{16,9},{17,24},{24,17},{3,10},{10,3},{11,18},{1... | collective-permute-start | bytes 466952 | tf_op jit(solution)/shard_map/ppermute | solution.py:996
  12.2 6.7 %collective-permute-start.4 = (f32[2,8,128]{2,1,0:T(8,128)}, f32[2,8,128]{2,1,0:T(8,128)S(1)}, u32[]{:S(2)}, u32[]{:S(2)}) collective-permute-start(f32[2,8,128]{2,1,0:T(8,128)} %get-tuple-element.39), channel_id=1, source_target_pairs={{0,9},{9,0},{8,17},{17,8},{16,25},{25,16},{2,11},{11,2},{10,19},{1... | collective-permute-start | bytes 24584 | tf_op jit(solution)/shard_map/ppermute | solution.py:997
  14.1 1.0 %copy-start = (f32[6,8,16,128]{3,2,1,0:T(8,128)S(1)}, f32[6,8,16,128]{3,2,1,0:T(8,128)}, u32[]{:S(2)}) copy-start(f32[6,8,16,128]{3,2,1,0:T(8,128)} %refs_0_.6) | copy-start | bytes 1179652
  15.1 1.0 %copy-start.1 = (f32[17,32,128]{2,1,0:T(8,128)S(1)}, f32[17,32,128]{2,1,0:T(8,128)}, u32[]{:S(2)}) copy-start(f32[17,32,128]{2,1,0:T(8,128)} %get-tuple-element.32.refs_1_) | copy-start | bytes 835588
  19.3 7.0 %collective-permute-start.5 = (f32[63,8,128]{2,1,0:T(8,128)S(1)}, f32[63,8,128]{2,1,0:T(8,128)S(1)}, u32[]{:S(2)}, u32[]{:S(2)}) collective-permute-start(f32[63,8,128]{2,1,0:T(8,128)S(1)} %get-tuple-element.40), channel_id=1, source_target_pairs={{0,2},{2,0},{4,6},{6,4},{1,3},{3,1},{5,7},{7,5},{8,10},{10,8},{12,... | collective-permute-start | bytes 774152 | tf_op jit(solution)/shard_map/ppermute | solution.py:1004
  19.4 7.6 %collective-permute-start.6 = (f32[63,8,128]{2,1,0:T(8,128)S(1)}, f32[63,8,128]{2,1,0:T(8,128)S(1)}, u32[]{:S(2)}, u32[]{:S(2)}) collective-permute-start(f32[63,8,128]{2,1,0:T(8,128)S(1)} %get-tuple-element.41), channel_id=1, source_target_pairs={{2,4},{4,2},{3,5},{5,3},{10,12},{12,10},{11,13},{13,11},{18,20},{2... | collective-permute-start | bytes 774152 | tf_op jit(solution)/shard_map/ppermute | solution.py:1003
  21.9 9.8 %collective-permute-start.8 = (f32[16,8,128]{2,1,0:T(8,128)S(1)}, f32[16,8,128]{2,1,0:T(8,128)S(1)}, u32[]{:S(2)}, u32[]{:S(2)}) collective-permute-start(f32[16,8,128]{2,1,0:T(8,128)S(1)} %get-tuple-element.53), channel_id=1, source_target_pairs={{0,2},{2,0},{4,6},{6,4},{1,3},{3,1},{5,7},{7,5},{8,10},{10,8},{12,... | collective-permute-start | bytes 196616 | tf_op jit(solution)/shard_map/ppermute | solution.py:1006
  22.0 9.7 %collective-permute-start.9 = (f32[16,8,128]{2,1,0:T(8,128)S(1)}, f32[16,8,128]{2,1,0:T(8,128)S(1)}, u32[]{:S(2)}, u32[]{:S(2)}) collective-permute-start(f32[16,8,128]{2,1,0:T(8,128)S(1)} %get-tuple-element.54), channel_id=1, source_target_pairs={{2,4},{4,2},{3,5},{5,3},{10,12},{12,10},{11,13},{13,11},{18,20},{2... | collective-permute-start | bytes 196616 | tf_op jit(solution)/shard_map/ppermute | solution.py:1005
  31.6 3.9 %collective-permute-start.7 = (f32[2,24,128]{2,1,0:T(8,128)S(1)}, f32[2,24,128]{2,1,0:T(8,128)S(1)}, u32[]{:S(2)}, u32[]{:S(2)}) collective-permute-start(f32[2,24,128]{2,1,0:T(8,128)S(1)} %get-tuple-element.50), channel_id=1, source_target_pairs={{0,1},{1,0},{2,3},{3,2},{4,5},{5,4},{6,7},{7,6},{8,9},{9,8},{10,11... | collective-permute-start | bytes 73736 | tf_op jit(solution)/shard_map/ppermute | solution.py:1037
  37.6 3.7 %collective-permute-start.10 = (f32[2,8,128]{2,1,0:T(8,128)S(1)}, f32[2,8,128]{2,1,0:T(8,128)S(1)}, u32[]{:S(2)}, u32[]{:S(2)}) collective-permute-start(f32[2,8,128]{2,1,0:T(8,128)S(1)} %get-tuple-element.61), channel_id=1, source_target_pairs={{0,1},{1,0},{2,3},{3,2},{4,5},{5,4},{6,7},{7,6},{8,9},{9,8},{10,11... | collective-permute-start | bytes 24584 | tf_op jit(solution)/shard_map/ppermute | solution.py:1065

commit v11 on v9

--- a/solution.py
+++ b/solution.py
@@ -863,7 +863,7 @@
 
 
 def last_kernel(
-    cells, meta, beam, g, g_diff, g_total, in_m, in_t, in_k, bulk, out_t, out_f, mass, p, h, f, fh, h1, diff, total, skin
+    cells, meta, beam, g, g_diff, g_total, in_m, in_t, in_k, bulk, out_t, out_f, top, fine_out, p, h, f, fh, h1, diff, total, skin
 ):
     rows_x, own_y = cells
     n, size = g.shape[1], g.shape[2]
@@ -882,7 +882,7 @@
 
     two = second_stage(meta, g, f, fh, diff, total, 1, REACH_LAST - 2, own_y, mask_of, store)
     lax.fori_loop(2, n - 2, two((COMPS - 1,)), 0, unroll=True)
-    fine = fine_pressure(meta, p, h, rows_x, own_y, mass.shape[0])
+    fine = fine_pressure(meta, p, h, rows_x, own_y, top.shape[0])
     cols = LANES // 4
     t = [in_t[d] for d in range(TOP - SUBSTEPS)]
     k = [in_k[d] for d in range(TOP - SUBSTEPS)]
@@ -892,14 +892,15 @@
         skin[:, d, :] = t[d]
     pack_skin(t, 0, cols, skin, out_t)
     pack_skin(t, SUBL, cols, skin, out_f)
-    mass[...] = vapor_mass(t[0], fine)
+    top[...] = t[0]
+    fine_out[...] = fine
 
 
 def terms_kernel(meta, g, diff, total):
     height_terms(g, 1, g.shape[1] - 1, height_matrix(), diff, total)
 
 
-def gas_kernel(meta, g, g_diff, g_total, mass, p, h, flow, fh, out_g, f, diff, total):
+def gas_kernel(meta, g, g_diff, g_total, top, fine, p, h, flow, fh, out_g, f, diff, total, mass):
     rows_x, own_y = out_g.shape[1], out_g.shape[2]
     n, size = g.shape[1], g.shape[2]
     matrix = height_matrix()
@@ -907,6 +908,7 @@
     first_stage(meta, g, h, [(1, size - 2, g_diff, g_total, 0, 0)], f, mask_of, True, (0, 1), ())
     both = Joined(f, flow)
     height_terms(both, 2, n - 4, matrix, diff, total, 0, tuple(range(COMPS)))
+    mass[...] = vapor_mass(top[...], fine[...])
     masses = mass_rows(meta, h, mass, 0, rows_x, own_y, own_y)
     loads = {0: VAPOR_SOURCE, 4: RECOIL_PUSH, 5: RECOIL_PRESSURE}
 
@@ -1040,11 +1042,12 @@
     )(beam, part, in_z, in_d, part_a, part_b)
     low_row = (small, LANES)
     g_diff, g_total = call(terms_kernel, [(COMPS + 1, n2 - 1, *low_row)] * 2, count=1)(g2)
-    mine, other, mass, p, h, f, fh = call(
+    mine, other, top_last, fine, p, h, f, fh = call(
         functools.partial(last_kernel, (rows_x, own_y)),
         [
             (n_top // 2, *block),
             (n_top // 2, *block),
+            (part_rows, LANES),
             (part_rows, LANES),
             (n2 - 4, own_y + 2 * (REACH_LAST - 2), LANES),
             (n2, *low_row),
@@ -1058,9 +1061,9 @@
     (gas,) = call(
         gas_kernel,
         [u.shape],
-        scratch=[(2, n2 - 2, *low_row)] + [(COMPS, n2 - 1, *low_row)] * 2,
-        count=8,
-    )(g2, g_diff, g_total, mass, p, h, f, fh)
+        scratch=[(2, n2 - 2, *low_row)] + [(COMPS, n2 - 1, *low_row)] * 2 + [(part_rows, LANES)],
+        count=9,
+    )(g2, g_diff, g_total, top_last, fine, p, h, f, fh)
     given = lax.ppermute(other, "gz", pairs(nz, 0))
     (out,) = call(seal_kernel, [t.shape], count=3)(bulk, mine, given)
     return gas, jnp.transpose(out, (2, 0, 1))

time: 42.4 us -> 42.4 us (level)
  no operation moved by 1% of the time
where the time goes in v11:
time: 42.4 us; the launch traced here: 42.1 us
  starting transfers between devices  17 us (40%)
  Pallas kernels  14.9 us (35%)
  waiting for transfers between devices  7.28 us (17%)
  local copies, waits for them, and re-layouts  2.05 us (5%)
  between operations  0.79 us (2%)
    pallas_call x1, Pallas kernels, shards(): call(functools.partial(first_kernel, (rows_x, REACH)), [(COMPS + 1, n2, s...  4.55 us
    ppermute x1, starting transfers between devices, shards(): in_d = lax.ppermute(msg_d, ('gx', 'gz'), cross(nx, nz, True))  3.85 us
    ppermute x1, starting transfers between devices, shards(): part_b = lax.ppermute(part_b, 'gy', pairs(ny, 1))  3.03 us
    ppermute x1, waiting for transfers between devices, shards(): in_h = lax.ppermute(msg_h, ('gx', 'gz'), cross(nx, nz, False))  2.81 us
    pallas_call x1, Pallas kernels, shards(): pl.pallas_call(pack, out_shape=[jax.ShapeDtypeStruct(v, F32) for v in sha...  2.55 us
    ppermute x1, starting transfers between devices, shards(): gy_b = lax.ppermute(msg_b, 'gy', pairs(ny, 1))  2.53 us
    pallas_call x1, Pallas kernels, shards(): call(functools.partial(last_kernel, (rows_x, own_y)), [(n_top // 2, *bloc...  2.1 us
    unnamed x7, local copies, waits for them, and re-layouts  2.05 us
  transfers between devices with their start and end apart: 11, of which 5 were waited for; matrix products, arithmetic and copies ran while one was open for 0% of the time, Pallas kernels for 22%

profile of v11, /device:TPU:18, one launch (start us, length us, event | category | flops | bytes accessed | tf_op | source)
XLA Modules:
  0.0 42.1 jit_solution(17968180451554688879)
XLA Ops:
  0.6 2.6 %shard_map.68 = (f32[32,16,128]{2,1,0:T(8,128)}, f32[32,16,128]{2,1,0:T(8,128)}, f32[38,8,128]{2,1,0:T(8,128)}, f32[38,8,128]{2,1,0:T(8,128)}, f32[2,8,128]{2,1,0:T(8,128)}, /*index=5*/f32[17,32,128]{2,1,0:T(8,128)}) custom-call(f32[6,8,16,128]{3,2,1,0:T(8,128)} %refs_0_.6, f32[8,32,128]{2,1,0:T(8,128)} %bitcast.3, s32[8,32,128]{2,1,0:T(8,128)} %bitcast.4, ...), custom_call_target="tpu_custom_call" | custom-call | tf_op jit(solution)/shard_map/pallas_call | solution.py:983
  3.2 1.6 %collective-permute-start = (f32[32,16,128]{2,1,0:T(8,128)}, f32[32,16,128]{2,1,0:T(8,128)S(1)}, u32[]{:S(2)}, u32[]{:S(2)}) collective-permute-start(f32[32,16,128]{2,1,0:T(8,128)} %get-tuple-element.35), channel_id=1, source_target_pairs={{0,8},{8,0},{16,24},{24,16},{1,9},{9,1},{17,25},{25,17},{2,10},{10... | collective-permute-start | bytes 786440 | tf_op jit(solution)/shard_map/ppermute | solution.py:994
  4.8 1.9 %collective-permute-start.1 = (f32[32,16,128]{2,1,0:T(8,128)}, f32[32,16,128]{2,1,0:T(8,128)S(1)}, u32[]{:S(2)}, u32[]{:S(2)}) collective-permute-start(f32[32,16,128]{2,1,0:T(8,128)} %get-tuple-element.36), channel_id=1, source_target_pairs={{8,16},{16,8},{9,17},{17,9},{10,18},{18,10},{11,19},{19,11},{12,20... | collective-permute-start | bytes 786440 | tf_op jit(solution)/shard_map/ppermute | solution.py:995
  6.8 1.6 %collective-permute-start.2 = (f32[38,8,128]{2,1,0:T(8,128)}, f32[38,8,128]{2,1,0:T(8,128)S(1)}, u32[]{:S(2)}, u32[]{:S(2)}) collective-permute-start(f32[38,8,128]{2,1,0:T(8,128)} %get-tuple-element.37), channel_id=1, source_target_pairs={{0,1},{1,0},{2,3},{3,2},{4,5},{5,4},{6,7},{7,6},{8,9},{9,8},{10,11... | collective-permute-start | bytes 466952 | tf_op jit(solution)/shard_map/ppermute | solution.py:996
  8.3 3.9 %collective-permute-start.3 = (f32[38,8,128]{2,1,0:T(8,128)}, f32[38,8,128]{2,1,0:T(8,128)S(1)}, u32[]{:S(2)}, u32[]{:S(2)}) collective-permute-start(f32[38,8,128]{2,1,0:T(8,128)} %get-tuple-element.38), channel_id=1, source_target_pairs={{1,8},{8,1},{9,16},{16,9},{17,24},{24,17},{3,10},{10,3},{11,18},{1... | collective-permute-start | bytes 466952 | tf_op jit(solution)/shard_map/ppermute | solution.py:997
  12.2 1.9 %collective-permute-start.4 = (f32[2,8,128]{2,1,0:T(8,128)}, f32[2,8,128]{2,1,0:T(8,128)S(1)}, u32[]{:S(2)}, u32[]{:S(2)}) collective-permute-start(f32[2,8,128]{2,1,0:T(8,128)} %get-tuple-element.40), channel_id=1, source_target_pairs={{0,9},{9,0},{8,17},{17,8},{16,25},{25,16},{2,11},{11,2},{10,19},{1... | collective-permute-start | bytes 24584 | tf_op jit(solution)/shard_map/ppermute | solution.py:998
  14.1 1.0 %copy-done = f32[6,8,16,128]{3,2,1,0:T(8,128)S(1)} copy-done((f32[6,8,16,128]{3,2,1,0:T(8,128)S(1)}, f32[6,8,16,128]{3,2,1,0:T(8,128)}, u32[]{:S(2)}) %copy-start) | copy-done | bytes 393240
  15.1 1.0 %copy-done.1 = f32[17,32,128]{2,1,0:T(8,128)S(1)} copy-done((f32[17,32,128]{2,1,0:T(8,128)S(1)}, f32[17,32,128]{2,1,0:T(8,128)}, u32[]{:S(2)}) %copy-start.1) | copy-done | bytes 278552
  16.1 2.8 %collective-permute-done.4.refs_6_.refs_5_ = f32[2,8,128]{2,1,0:T(8,128)S(1)} collective-permute-done((f32[2,8,128]{2,1,0:T(8,128)}, f32[2,8,128]{2,1,0:T(8,128)S(1)}, u32[]{:S(2)}, u32[]{:S(2)}) %collective-permute-start.4) | collective-permute-done | bytes 8224 | tf_op jit(solution)/shard_map/ppermute | solution.py:998
  18.9 0.1 collective-permute-done.3.refs_5_.refs_4_.refs_3_
  19.1 0.2 shard_map.70
  19.4 2.5 %collective-permute-start.6 = (f32[63,8,128]{2,1,0:T(8,128)S(1)}, f32[63,8,128]{2,1,0:T(8,128)S(1)}, u32[]{:S(2)}, u32[]{:S(2)}) collective-permute-start(f32[63,8,128]{2,1,0:T(8,128)S(1)} %get-tuple-element.42), channel_id=1, source_target_pairs={{2,4},{4,2},{3,5},{5,3},{10,12},{12,10},{11,13},{13,11},{18,20},{2... | collective-permute-start | bytes 774152 | tf_op jit(solution)/shard_map/ppermute | solution.py:1004
  22.0 3.0 %collective-permute-start.9 = (f32[16,8,128]{2,1,0:T(8,128)S(1)}, f32[16,8,128]{2,1,0:T(8,128)S(1)}, u32[]{:S(2)}, u32[]{:S(2)}) collective-permute-start(f32[16,8,128]{2,1,0:T(8,128)S(1)} %get-tuple-element.55), channel_id=1, source_target_pairs={{2,4},{4,2},{3,5},{5,3},{10,12},{12,10},{11,13},{13,11},{18,20},{2... | collective-permute-start | bytes 196616 | tf_op jit(solution)/shard_map/ppermute | solution.py:1006
  25.1 1.2 %shard_map.71 = (f32[6,20,32,128]{3,2,1,0:T(8,128)S(1)}, f32[6,18,16,128]{3,2,1,0:T(8,128)S(1)}, f32[20,32,128]{2,1,0:T(8,128)S(1)}, f32[20,32,128]{2,1,0:T(8,128)S(1)}, f32[18,16,128]{2,1,0:T(8,128)S(1)}) custom-call(f32[6,8,16,128]{3,2,1,0:T(8,128)S(1)} %get-tuple-element.39.refs_0_, f32[32,16,128]{2,1,0:T(8,128)S(1)} %collective-permute-done.refs_2_.refs_1_, ...), custom_call_target="tpu_custom_call" | custom-call | tf_op jit(solution)/shard_map/pallas_call | solution.py:1017
  26.3 0.7 %collective-permute-done.6.refs_7_ = f32[63,8,128]{2,1,0:T(8,128)S(1)} collective-permute-done((f32[63,8,128]{2,1,0:T(8,128)S(1)}, f32[63,8,128]{2,1,0:T(8,128)S(1)}, u32[]{:S(2)}, u32[]{:S(2)}) %collective-permute-start.6) | collective-permute-done | bytes 258080 | tf_op jit(solution)/shard_map/ppermute | solution.py:1004
  27.0 4.5 %shard_map.72 = (f32[7,14,24,128]{3,2,1,0:T(8,128)S(1)}, f32[2,24,128]{2,1,0:T(8,128)S(1)}, f32[6,32,128]{2,1,0:T(8,128)S(1)}, f32[6,32,128]{2,1,0:T(8,128)S(1)}) custom-call(s32[4,2]{1,0:T(4,128)S(1)} %copy.7.refs_0_, f32[17,32,128]{2,1,0:T(8,128)S(1)} %get-tuple-element.34.refs_1_, f32[32,16,128]{2,1,0:T(8,128)S(1)} %collective-permute-done.refs_2_.refs_1_, ...), custom_call_target="tpu_custom_call" | custom-call | tf_op jit(solution)/shard_map/pallas_call | solution.py:1023
  31.7 1.6 %shard_map.74.refs_7_.refs_0_ = f32[8,32,128]{2,1,0:T(8,128)S(1)} custom-call(s32[4,2]{1,0:T(4,128)S(1)} %copy.7.refs_0_, f32[17,32,128]{2,1,0:T(8,128)S(1)} %get-tuple-element.34.refs_1_, f32[38,8,128]{2,1,0:T(8,128)S(1)} %collective-permute-done.2.refs_4_.refs_3_.refs_2_, f32[38,8,128]{2,1,0:T(8,128)S(1)} %collective-permute-done.3.refs_5_.refs_4_.refs_3_, ...), custom_call_target="tpu_custom_call" | custom-call | tf_op jit(solution)/shard_map/pallas_call | solution.py:1040
  33.3 0.4 %shard_map.73 = (f32[7,13,24,128]{3,2,1,0:T(8,128)S(1)}, f32[7,13,24,128]{3,2,1,0:T(8,128)S(1)}) custom-call(f32[7,14,24,128]{3,2,1,0:T(8,128)S(1)} %get-tuple-element.48.refs_0_.refs_1_), custom_call_target="tpu_custom_call" | custom-call | tf_op jit(solution)/shard_map/pallas_call | solution.py:1044
  33.7 1.7 %collective-permute-done.7.refs_4_ = f32[2,24,128]{2,1,0:T(8,128)S(1)} collective-permute-done((f32[2,24,128]{2,1,0:T(8,128)S(1)}, f32[2,24,128]{2,1,0:T(8,128)S(1)}, u32[]{:S(2)}, u32[]{:S(2)}) %collective-permute-start.7) | collective-permute-done | bytes 24608 | tf_op jit(solution)/shard_map/ppermute | solution.py:1038
  35.5 2.1 %shard_map.75 = (f32[2,8,128]{2,1,0:T(8,128)S(1)}, f32[2,8,128]{2,1,0:T(8,128)S(1)}, f32[32,128]{1,0:T(8,128)S(1)}, f32[32,128]{1,0:T(8,128)S(1)}, f32[10,18,128...) custom-call(s32[4,2]{1,0:T(4,128)S(1)} %copy.7.refs_0_, ...), custom_call_target="tpu_custom_call" | custom-call | tf_op jit(solution)/shard_map/pallas_call | solution.py:1045
  37.6 0.3 collective-permute-start.10
  37.9 1.4 %shard_map.76 = f32[6,8,16,128]{3,2,1,0:T(8,128)} custom-call(f32[7,14,24,128]{3,2,1,0:T(8,128)S(1)} %get-tuple-element.48.refs_0_.refs_1_, f32[7,13,24,128]{3,2,1,0:T(8,128)S(1)} %get-tuple-element.49.refs_2_.refs_1_, f32[7,13,24,128]{3,2,1,0:T(8,128)S(1)} %get-tuple-element.50.refs_3_.refs_2_, f32[32,128]{1,0:T(8,128)S(1)} %get-tuple-element.56.refs_3_, ...), custom_call_target="tpu_custom_call" | custom-call | tf_op jit(solution)/shard_map/pallas_call | solution.py:1061
  39.3 1.9 %collective-permute-done.10.refs_2_ = f32[2,8,128]{2,1,0:T(8,128)S(1)} collective-permute-done((f32[2,8,128]{2,1,0:T(8,128)S(1)}, f32[2,8,128]{2,1,0:T(8,128)S(1)}, u32[]{:S(2)}, u32[]{:S(2)}) %collective-permute-start.10) | collective-permute-done | bytes 8224 | tf_op jit(solution)/shard_map/ppermute | solution.py:1067
  41.3 0.8 %shard_map.77 = f32[8,32,128]{2,1,0:T(8,128)} custom-call(f32[8,32,128]{2,1,0:T(8,128)S(1)} %shard_map.74.refs_7_.refs_0_, f32[2,8,128]{2,1,0:T(8,128)S(1)} %get-tuple-element.62.refs_1_, f32[2,8,128]{2,1,0:T(8,128)S(1)} %collective-permute-done.10.refs_2_), custom_call_target="tpu_custom_call" | custom-call | tf_op jit(solution)/shard_map/pallas_call | solution.py:1068
  (15 shorter events, 0.4 us)
Async XLA Ops:
  3.2 21.8 %copy-start.2 = (s32[4,2]{0,1:T(2,128)S(1)}, s32[4,2]{0,1:T(2,128)}, u32[]{:S(2)}) copy-start(s32[4,2]{0,1:T(2,128)} %param.9) | copy-start | bytes 100
  3.2 15.9 %collective-permute-start = (f32[32,16,128]{2,1,0:T(8,128)}, f32[32,16,128]{2,1,0:T(8,128)S(1)}, u32[]{:S(2)}, u32[]{:S(2)}) collective-permute-start(f32[32,16,128]{2,1,0:T(8,128)} %get-tuple-element.35), channel_id=1, source_target_pairs={{0,8},{8,0},{16,24},{24,16},{1,9},{9,1},{17,25},{25,17},{2,10},{10... | collective-permute-start | bytes 786440 | tf_op jit(solution)/shard_map/ppermute | solution.py:994
  4.8 14.2 %collective-permute-start.1 = (f32[32,16,128]{2,1,0:T(8,128)}, f32[32,16,128]{2,1,0:T(8,128)S(1)}, u32[]{:S(2)}, u32[]{:S(2)}) collective-permute-start(f32[32,16,128]{2,1,0:T(8,128)} %get-tuple-element.36), channel_id=1, source_target_pairs={{8,16},{16,8},{9,17},{17,9},{10,18},{18,10},{11,19},{19,11},{12,20... | collective-permute-start | bytes 786440 | tf_op jit(solution)/shard_map/ppermute | solution.py:995
  6.8 12.2 %collective-permute-start.2 = (f32[38,8,128]{2,1,0:T(8,128)}, f32[38,8,128]{2,1,0:T(8,128)S(1)}, u32[]{:S(2)}, u32[]{:S(2)}) collective-permute-start(f32[38,8,128]{2,1,0:T(8,128)} %get-tuple-element.37), channel_id=1, source_target_pairs={{0,1},{1,0},{2,3},{3,2},{4,5},{5,4},{6,7},{7,6},{8,9},{9,8},{10,11... | collective-permute-start | bytes 466952 | tf_op jit(solution)/shard_map/ppermute | solution.py:996
  8.3 10.7 %collective-permute-start.3 = (f32[38,8,128]{2,1,0:T(8,128)}, f32[38,8,128]{2,1,0:T(8,128)S(1)}, u32[]{:S(2)}, u32[]{:S(2)}) collective-permute-start(f32[38,8,128]{2,1,0:T(8,128)} %get-tuple-element.38), channel_id=1, source_target_pairs={{1,8},{8,1},{9,16},{16,9},{17,24},{24,17},{3,10},{10,3},{11,18},{1... | collective-permute-start | bytes 466952 | tf_op jit(solution)/shard_map/ppermute | solution.py:997
  12.2 6.7 %collective-permute-start.4 = (f32[2,8,128]{2,1,0:T(8,128)}, f32[2,8,128]{2,1,0:T(8,128)S(1)}, u32[]{:S(2)}, u32[]{:S(2)}) collective-permute-start(f32[2,8,128]{2,1,0:T(8,128)} %get-tuple-element.40), channel_id=1, source_target_pairs={{0,9},{9,0},{8,17},{17,8},{16,25},{25,16},{2,11},{11,2},{10,19},{1... | collective-permute-start | bytes 24584 | tf_op jit(solution)/shard_map/ppermute | solution.py:998
  14.1 1.0 %copy-start = (f32[6,8,16,128]{3,2,1,0:T(8,128)S(1)}, f32[6,8,16,128]{3,2,1,0:T(8,128)}, u32[]{:S(2)}) copy-start(f32[6,8,16,128]{3,2,1,0:T(8,128)} %refs_0_.6) | copy-start | bytes 1179652
  15.1 1.0 %copy-start.1 = (f32[17,32,128]{2,1,0:T(8,128)S(1)}, f32[17,32,128]{2,1,0:T(8,128)}, u32[]{:S(2)}) copy-start(f32[17,32,128]{2,1,0:T(8,128)} %get-tuple-element.33.refs_1_) | copy-start | bytes 835588
  19.3 7.0 %collective-permute-start.5 = (f32[63,8,128]{2,1,0:T(8,128)S(1)}, f32[63,8,128]{2,1,0:T(8,128)S(1)}, u32[]{:S(2)}, u32[]{:S(2)}) collective-permute-start(f32[63,8,128]{2,1,0:T(8,128)S(1)} %get-tuple-element.41), channel_id=1, source_target_pairs={{0,2},{2,0},{4,6},{6,4},{1,3},{3,1},{5,7},{7,5},{8,10},{10,8},{12,... | collective-permute-start | bytes 774152 | tf_op jit(solution)/shard_map/ppermute | solution.py:1005
  19.4 7.6 %collective-permute-start.6 = (f32[63,8,128]{2,1,0:T(8,128)S(1)}, f32[63,8,128]{2,1,0:T(8,128)S(1)}, u32[]{:S(2)}, u32[]{:S(2)}) collective-permute-start(f32[63,8,128]{2,1,0:T(8,128)S(1)} %get-tuple-element.42), channel_id=1, source_target_pairs={{2,4},{4,2},{3,5},{5,3},{10,12},{12,10},{11,13},{13,11},{18,20},{2... | collective-permute-start | bytes 774152 | tf_op jit(solution)/shard_map/ppermute | solution.py:1004
  21.9 9.7 %collective-permute-start.8 = (f32[16,8,128]{2,1,0:T(8,128)S(1)}, f32[16,8,128]{2,1,0:T(8,128)S(1)}, u32[]{:S(2)}, u32[]{:S(2)}) collective-permute-start(f32[16,8,128]{2,1,0:T(8,128)S(1)} %get-tuple-element.54), channel_id=1, source_target_pairs={{0,2},{2,0},{4,6},{6,4},{1,3},{3,1},{5,7},{7,5},{8,10},{10,8},{12,... | collective-permute-start | bytes 196616 | tf_op jit(solution)/shard_map/ppermute | solution.py:1007
  22.0 9.7 %collective-permute-start.9 = (f32[16,8,128]{2,1,0:T(8,128)S(1)}, f32[16,8,128]{2,1,0:T(8,128)S(1)}, u32[]{:S(2)}, u32[]{:S(2)}) collective-permute-start(f32[16,8,128]{2,1,0:T(8,128)S(1)} %get-tuple-element.55), channel_id=1, source_target_pairs={{2,4},{4,2},{3,5},{5,3},{10,12},{12,10},{11,13},{13,11},{18,20},{2... | collective-permute-start | bytes 196616 | tf_op jit(solution)/shard_map/ppermute | solution.py:1006
  31.6 3.9 %collective-permute-start.7 = (f32[2,24,128]{2,1,0:T(8,128)S(1)}, f32[2,24,128]{2,1,0:T(8,128)S(1)}, u32[]{:S(2)}, u32[]{:S(2)}) collective-permute-start(f32[2,24,128]{2,1,0:T(8,128)S(1)} %get-tuple-element.51), channel_id=1, source_target_pairs={{0,1},{1,0},{2,3},{3,2},{4,5},{5,4},{6,7},{7,6},{8,9},{9,8},{10,11... | collective-permute-start | bytes 73736 | tf_op jit(solution)/shard_map/ppermute | solution.py:1038
  37.6 3.7 %collective-permute-start.10 = (f32[2,8,128]{2,1,0:T(8,128)S(1)}, f32[2,8,128]{2,1,0:T(8,128)S(1)}, u32[]{:S(2)}, u32[]{:S(2)}) collective-permute-start(f32[2,8,128]{2,1,0:T(8,128)S(1)} %get-tuple-element.63), channel_id=1, source_target_pairs={{0,1},{1,0},{2,3},{3,2},{4,5},{5,4},{6,7},{7,6},{8,9},{9,8},{10,11... | collective-permute-start | bytes 24584 | tf_op jit(solution)/shard_map/ppermute | solution.py:1067
